TPU v7x, 32 devices: a whole 2x2x4 slice. The times are simulated.
32 devices in a mesh: tm: 16 (over z, x, core), head: 2 (over y).
Axes of the slice: x: 2, y: 2, z: 4, core: 2. Of those that a mesh axis runs over, the one named last changes fastest.
Arguments:
- query_proj: bfloat16 [2048, 768], P('tm', 'head'), may hold values from -80 to 80
- key_proj: bfloat16 [2048, 768], P('tm', 'head'), may hold values from -80 to 80
- value_proj: bfloat16 [2048, 768], P('tm', 'head'), may hold values from -12 to 12
- query_gain: float32 [768], P('head'), may hold values from 0.25 to 1.75
- key_gain: float32 [768], P('head'), may hold values from 0.25 to 1.75
- gate_table: float32 [50, 768], P(None, 'head'), may hold values from 0.5 to 2
- frame_step: int32 [2], replicated, may hold values from 0 to 49
- far_blocks: int32 [16, 16], P('tm'), may hold values from -1 to 1, as said below
Outputs:
- attended: bfloat16 [2048, 768], P('tm', 'head')
Inputs may be any that keep to these rules, and one draw needn't show every extreme that they name: `far_blocks`: entry [i, j] is the index of the key block of 64 tokens that query block i takes from query block j's tokens, or -1 for none; it is -1 wherever |i - j| <= 1.
All inputs are finite; a program needn't handle non-finite values.
Results may differ from a plain program's by a relative error of at most 0.007.
The roundings to bfloat16 on the way count: a program that leaves them out, or rounds other values in their place, can miss the bound.
Values may be sent and summed in bfloat16 or wider, within the bound.
No kernel may reach another device: no remote copies, remote signals or barrier semaphores. Data moves between devices by JAX's collectives and lax.ppermute only.
A program may use at most 64 MiB of HBM per device.

v0:
```python
import jax
import jax.numpy as jnp
from jax import lax
from jax.sharding import PartitionSpec as P

HD = 128
BLK = 64
FRAME_TOK = 1560


epsilon = 1e-06


def extended(block, sides, width):
    for axis, dim in sides:
        count = lax.axis_size(axis)
        forward = [(i, i + 1) for i in range(count - 1)]
        backward = [(target, source) for source, target in forward]
        low = lax.ppermute(
            lax.slice_in_dim(block, block.shape[dim] - width, None, axis=dim), axis, forward
        )
        high = lax.ppermute(lax.slice_in_dim(block, 0, width, axis=dim), axis, backward)
        block = jnp.concatenate([low, block, high], axis=dim)
    return block


def softmax_update(carry, query_part, key_part, value_part, key_mask, score_scale):
    run_max, run_sum, accum = carry
    scores = (
        lax.dot_general(
            query_part, key_part, (((1,), (1,)), ((), ())), preferred_element_type=jnp.float32
        )
        * score_scale
    )
    scores = jnp.where(key_mask[None, :], scores, -jnp.inf)
    new_max = jnp.max(scores, axis=-1)
    fading = jnp.exp(run_max - new_max)
    weights = jnp.exp(scores - new_max[:, None])
    run_sum = run_sum * fading + jnp.sum(weights, axis=-1)
    accum = accum * fading[:, None] + jnp.dot(
        weights.astype(jnp.bfloat16), value_part, preferred_element_type=jnp.float32
    )
    return (new_max, run_sum, accum)


def local(
    query_proj, key_proj, value_proj, query_gain, key_gain, gate_table, frame_step, far_blocks
):
    row_count, feat_width = query_proj.shape
    head_count = feat_width // HD
    full_width = feat_width * lax.axis_size("head")
    query_f = query_proj.astype(jnp.float32)
    key_f = key_proj.astype(jnp.float32)
    query_sq, key_sq = lax.psum(
        (jnp.sum(query_f * query_f, axis=-1), jnp.sum(key_f * key_f, axis=-1)), "head"
    )
    query_norm = (
        query_f * lax.rsqrt(query_sq / full_width + epsilon)[:, None] * query_gain
    ).astype(jnp.bfloat16)
    key_norm = (key_f * lax.rsqrt(key_sq / full_width + epsilon)[:, None] * key_gain).astype(
        jnp.bfloat16
    )
    device_index = lax.axis_index("tm")
    device_total = lax.axis_size("tm")
    band = extended(jnp.stack([key_norm, value_proj]), (("tm", 1),), row_count)
    segment = jnp.arange(3 * row_count, dtype=jnp.int32) // row_count
    band_mask = (
        (segment == 1)
        | (segment == 0) & (device_index > 0)
        | (segment == 2) & (device_index < device_total - 1)
    )
    requests = lax.all_to_all(far_blocks, "tm", split_axis=1, concat_axis=0, tiled=True)[:, 0]
    block_count = row_count // BLK
    key_blocks = key_norm.reshape(block_count, BLK, feat_width)
    value_blocks = value_proj.reshape(block_count, BLK, feat_width)
    picked = jnp.maximum(requests, 0)
    served = (requests >= 0)[:, None, None]
    send_keys = jnp.where(served, key_blocks[picked], jnp.zeros((), jnp.bfloat16))
    send_values = jnp.where(served, value_blocks[picked], jnp.zeros((), jnp.bfloat16))
    far_keys, far_values = (
        lax.all_to_all(send_keys, "tm", split_axis=0, concat_axis=0, tiled=True),
        lax.all_to_all(send_values, "tm", split_axis=0, concat_axis=0, tiled=True),
    )
    wanted = far_blocks[0] >= 0
    positions = device_index * row_count + jnp.arange(row_count, dtype=jnp.int32)
    frame_ids = positions // FRAME_TOK
    frame_hit = frame_ids[:, None] == jnp.arange(frame_step.shape[0], dtype=jnp.int32)[None, :]
    step_rows = jnp.sum(jnp.where(frame_hit, frame_step[None, :], 0), axis=-1)
    step_hit = (
        step_rows[:, None] == jnp.arange(gate_table.shape[0], dtype=jnp.int32)[None, :]
    ).astype(jnp.float32)
    gates = jnp.dot(step_hit, gate_table, precision=lax.Precision.HIGHEST)
    score_scale = HD ** (-0.5)
    query_block = min(row_count, 512)
    far_rows = device_total * BLK
    all_keys = jnp.concatenate([band[0], far_keys.reshape(far_rows, feat_width)], axis=0)
    all_values = jnp.concatenate([band[1], far_values.reshape(far_rows, feat_width)], axis=0)
    all_mask = jnp.concatenate([band_mask, jnp.repeat(wanted, BLK)], axis=0)
    head_outputs = []
    for head_id in range(head_count):
        low = head_id * HD
        high = low + HD
        query_part = query_norm[0:query_block, low:high]
        initial = (
            jnp.full((query_block,), -jnp.inf, jnp.float32),
            jnp.zeros((query_block,), jnp.float32),
            jnp.zeros((query_block, HD), jnp.float32),
        )
        carry = softmax_update(
            initial,
            query_part,
            all_keys[:, low:high],
            all_values[:, low:high],
            all_mask,
            score_scale,
        )
        context = carry[2] / carry[1][:, None]
        row_outputs = (context * gates[0:query_block, low:high]).astype(jnp.bfloat16)
        head_outputs.append(row_outputs)
    return jnp.concatenate(head_outputs, axis=1)


def solution(mesh):
    return jax.shard_map(
        local,
        mesh=mesh,
        in_specs=(
            P("tm", "head"),
            P("tm", "head"),
            P("tm", "head"),
            P("head"),
            P("head"),
            P(None, "head"),
            P(),
            P("tm", None),
        ),
        out_specs=P("tm", "head"),
        check_vma=False,
    )
```

profile of v0, /device:TPU:0, one launch (start us, length us, event | category | flops | bytes accessed | tf_op | source)
XLA Modules:
  0.0 79.8 jit_solution(8007571006981916896)
XLA Ops:
  0.0 0.0 copy-start
  0.0 0.0 copy-start.11
  0.0 1.1 %fusion.34 = (f32[128]{0:T(128)S(1)}, f32[128]{0:T(128)S(1)}) fusion(bf16[128,384]{1,0:T(8,128)(2,1)} %param.8, bf16[128,384]{1,0:T(8,128)(2,1)} %param.9), kind=kLoop, calls=%fused_computation.57 | loop fusion | flops 294656 | bytes 197632 | tf_op jit(solution)/shard_map/reduce_sum | solution.py:55
  1.1 5.9 %all-reduce = (f32[128]{0:T(128)S(1)}, f32[128]{0:T(128)S(1)}) all-reduce(f32[128]{0:T(128)S(1)} %get-tuple-element.24, f32[128]{0:T(128)S(1)} %get-tuple-element.23), channel_id=1, replica_groups=mesh['tm'=16,'head'=2] {'head'}, use_global_device_ids=true, to_apply=%region_3.0 | all-reduce | flops 256 | bytes 2048 | tf_op jit(solution)/shard_map/psum | solution.py:54
  7.1 1.0 %fusion.69 = bf16[1,128,384]{2,1,0:T(8,128)(2,1)S(1)} fusion(f32[384]{0:T(512)} %param.12, f32[128]{0:T(128)S(1)} %add_rsqrt_fusion, bf16[128,384]{1,0:T(8,128)(2,1)} %param.9), kind=kLoop, calls=%fused_computation.110 | loop fusion | flops 196608 | bytes 198656 | tf_op jit(solution)/shard_map/stack | solution.py:65
  8.1 0.9 %pad_maximum_fusion.5 = bf16[2,128,384]{2,1,0:T(8,128)(2,1)S(1)} fusion(bf16[1,128,384]{2,1,0:T(8,128)(2,1)} %bitcast.21, bf16[1,128,384]{2,1,0:T(8,128)(2,1)S(1)} %fusion.69), kind=kLoop, calls=%fused_computation.63 | loop fusion | flops 98304 | bytes 393216 | tf_op jit(solution)/shard_map/stack | solution.py:65
  9.0 1.3 %collective-permute-start.1 = (bf16[2,128,384]{2,1,0:T(8,128)(2,1)S(1)}, bf16[2,128,384]{2,1,0:T(8,128)(2,1)S(1)}, u32[]{:S(2)}, u32[]{:S(2)}) collective-permute-start(bf16[2,128,384]{2,1,0:T(8,128)(2,1)S(1)} %pad_maximum_fusion.5), channel_id=1, source_target_pairs={{2,0},{4,2},{6,4},{8,6},{10,8},{12,10},{14,12},{16,14},{18,16},{20... | collective-permute-start | bytes 589832 | tf_op jit(solution)/shard_map/ppermute | solution.py:22
  10.3 3.0 %collective-permute-start = (bf16[2,128,384]{2,1,0:T(8,128)(2,1)S(1)}, bf16[2,128,384]{2,1,0:T(8,128)(2,1)S(1)}, u32[]{:S(2)}, u32[]{:S(2)}) collective-permute-start(bf16[2,128,384]{2,1,0:T(8,128)(2,1)S(1)} %pad_maximum_fusion.5), channel_id=1, source_target_pairs={{0,2},{2,4},{4,6},{6,8},{8,10},{10,12},{12,14},{14,16},{16,18},{18... | collective-permute-start | bytes 589832 | tf_op jit(solution)/shard_map/ppermute | solution.py:19
  13.3 0.0 copy-done.11
  13.3 0.7 copy.23
  14.0 6.4 %all-to-all-start = ((s32[1,16,1]{2,0,1:T(1,128)}), s32[1,16,1]{2,0,1:T(1,128)S(1)}, u32[]{:S(2)}, u32[]{:S(2)}) async-start(s32[1,16,1]{2,0,1:T(1,128)} %copy.23), calls=%async_computation | async-start | bytes 16384 | tf_op jit(solution)/shard_map/all_to_all | solution.py:72
  20.5 0.0 copy-done.5
  20.5 0.0 copy-done.9
  20.5 0.1 fusion.39
  20.6 0.1 broadcast_in_dim.75
  20.7 0.1 reshape.96
  20.8 6.0 %all-to-all-done = s32[1,16,1]{2,0,1:T(1,128)S(1)} async-done(((s32[1,16,1]{2,0,1:T(1,128)}), s32[1,16,1]{2,0,1:T(1,128)S(1)}, u32[]{:S(2)}, u32[]{:S(2)}) %all-to-all-start) | async-done | bytes 96 | tf_op jit(solution)/shard_map/all_to_all | solution.py:72
  26.8 0.4 maximum_reduce_fusion
  27.2 0.0 copy-done.1
  27.2 0.7 gather_fusion.1
  27.9 0.7 gather_fusion
  28.6 0.4 compare_reduce_fusion
  29.0 1.4 %broadcast_select_fusion = (bf16[16,64,384]{2,1,0:T(8,128)(2,1)}, bf16[16,64,384]{2,1,0:T(8,128)(2,1)}) fusion(bf16[16,64,384]{2,1,0:T(8,128)(2,1)S(1)} %gather_fusion.1, pred[16]{0:T(512)(128)(4,1)S(1)} %compare_reduce_fusion, bf16[16,64,384]{2,1,0:T(8,128)(2,1)S(1)} %gather_fusion), kind=kLoop, calls=%fused_computation.28 | loop fusion | flops 786432 | bytes 3145744 | tf_op jit(solution)/shard_map/jit(_where)/select_n | solution.py:79
  30.4 3.7 %all-to-all-start.1 = ((bf16[16,64,384]{2,1,0:T(8,128)(2,1)}), bf16[16,64,384]{2,1,0:T(8,128)(2,1)S(1)}, u32[]{:S(2)}, u32[]{:S(2)}) async-start(bf16[16,64,384]{2,1,0:T(8,128)(2,1)} %get-tuple-element.16), calls=%async_computation.1 | async-start | bytes 1572864 | tf_op jit(solution)/shard_map/all_to_all | solution.py:81
  34.2 0.0 copy-done.12
  34.2 0.1 fusion.55
  34.3 0.0 copy-done
  34.3 1.1 %fusion.40 = f32[128,384]{0,1:T(8,128)} fusion(f32[50,384]{1,0:T(8,128)S(1)} %copy-done, s32[128]{0:T(128)S(1)} %fusion.55), kind=kOutput, calls=%fused_computation.66 | convolution fusion | flops 29497600 | bytes 273920 | tf_op jit(solution)/shard_map/dot_general | solution.py:92
  35.4 0.0 copy-done.8
  35.4 0.1 fusion.36
  35.5 0.0 copy-start.7
  35.5 0.0 collective-permute-done.1
  35.5 0.0 collective-permute-done
  35.5 0.1 pad_maximum_fusion
  35.6 0.8 slice_bitcast_fusion
  36.4 16.5 %all-to-all-done.1 = bf16[16,64,384]{2,1,0:T(8,128)(2,1)S(1)} async-done(((bf16[16,64,384]{2,1,0:T(8,128)(2,1)}), bf16[16,64,384]{2,1,0:T(8,128)(2,1)S(1)}, u32[]{:S(2)}, u32[]{:S(2)}) %all-to-all-start.1) | async-done | bytes 786464 | tf_op jit(solution)/shard_map/all_to_all | solution.py:81
  52.8 5.4 %all-to-all-start.2 = ((bf16[16,64,384]{2,1,0:T(8,128)(2,1)}), bf16[16,64,384]{2,1,0:T(8,128)(2,1)S(1)}, u32[]{:S(2)}, u32[]{:S(2)}) async-start(bf16[16,64,384]{2,1,0:T(8,128)(2,1)} %get-tuple-element.15), calls=%async_computation.2 | async-start | bytes 1572864 | tf_op jit(solution)/shard_map/all_to_all | solution.py:82
  58.3 0.3 fusion.65
  58.6 0.3 fusion.16
  58.9 1.1 %fusion.66 = (f32[128]{0:T(128)S(1)}, f32[128,1408]{1,0:T(8,128)S(1)}) fusion(bf16[1024,384]{1,0:T(8,128)(2,1)S(1)} %bitcast.16, bf16[384,384]{1,0:T(8,128)(2,1)S(1)} %get-tuple-element.8, bf16[128,384]{1,0:T(8,128)(2,1)} %copy-done.7, pred[1408]{0:T(1024)(128)(4,1)S(1)} %pad_add_fusion), kind=kOutput, calls=%fused_computation.108 | convolution fusion | flops 47398784 | bytes 1836928 | tf_op jit(solution)/shard_map/dot_general | solution.py:30
  60.0 0.3 fusion.14
  60.2 1.1 %fusion.67 = (f32[128]{0:T(128)S(1)}, f32[128,1408]{1,0:T(8,128)S(1)}) fusion(bf16[1024,384]{1,0:T(8,128)(2,1)S(1)} %bitcast.17, bf16[384,384]{1,0:T(8,128)(2,1)S(1)} %get-tuple-element.8, bf16[128,384]{1,0:T(8,128)(2,1)} %copy-done.7, pred[1408]{0:T(1024)(128)(4,1)S(1)} %pad_add_fusion), kind=kOutput, calls=%fused_computation.109 | convolution fusion | flops 47398784 | bytes 1836928 | tf_op jit(solution)/shard_map/dot_general | solution.py:30
  61.4 0.3 fusion.12
  61.7 15.3 %all-to-all-done.2 = bf16[16,64,384]{2,1,0:T(8,128)(2,1)S(1)} async-done(((bf16[16,64,384]{2,1,0:T(8,128)(2,1)}), bf16[16,64,384]{2,1,0:T(8,128)(2,1)S(1)}, u32[]{:S(2)}, u32[]{:S(2)}) %all-to-all-start.2) | async-done | bytes 786464 | tf_op jit(solution)/shard_map/all_to_all | solution.py:82
  77.0 1.3 %fusion.11 = bf16[128,128]{0,1:T(8,128)(2,1)S(1)} fusion(f32[128,1408]{1,0:T(8,128)S(1)} %copy-done.3, bf16[1024,384]{1,0:T(8,128)(2,1)S(1)} %bitcast.18, bf16[384,384]{1,0:T(8,128)(2,1)} %get-tuple-element.7, f32[128]{0:T(128)S(1)} %get-tuple-element.17, f32[128,384]{0,1:T(8,128)} %fusion.40, f32[128]{0:T(128)S(1)} %get-tuple-element.14, ...), kind=kOutput, calls=%fused_computation.23 | convolution fusion | flops 47284224 | bytes 1902080 | tf_op jit(solution)/shard_map/dot_general | solution.py:40
  78.3 0.4 fusion.10
  78.7 0.4 fusion.9
  79.1 0.8 copy.27
  (27 shorter events, 0.1 us)
Async XLA Ops:
  0.0 34.3 %copy-start = (f32[50,384]{1,0:T(8,128)S(1)}, f32[50,384]{1,0:T(8,128)}, u32[]{:S(2)}) copy-start(f32[50,384]{1,0:T(8,128)} %param.13) | copy-start | bytes 230404
  0.0 20.5 %copy-start.5 = (bf16[128,384]{1,0:T(8,128)(2,1)S(1)}, bf16[128,384]{1,0:T(8,128)(2,1)}, u32[]{:S(2)}) copy-start(bf16[128,384]{1,0:T(8,128)(2,1)} %param.9) | copy-start | bytes 294916
  0.0 20.5 %copy-start.9 = (f32[384]{0:T(512)S(1)}, f32[384]{0:T(512)}, u32[]{:S(2)}) copy-start(f32[384]{0:T(512)} %param.12) | copy-start | bytes 4612
  0.0 27.2 %copy-start.1 = (bf16[128,384]{1,0:T(8,128)(2,1)S(1)}, bf16[128,384]{1,0:T(8,128)(2,1)}, u32[]{:S(2)}) copy-start(bf16[128,384]{1,0:T(8,128)(2,1)} %param.10) | copy-start | bytes 294916
  0.0 13.3 %copy-start.11 = (s32[1,16]{1,0:T(1,128)S(1)}, s32[1,16]{1,0:T(1,128)}, u32[]{:S(2)}) copy-start(s32[1,16]{1,0:T(1,128)} %param.15) | copy-start | bytes 196
  9.0 26.5 %collective-permute-start.1 = (bf16[2,128,384]{2,1,0:T(8,128)(2,1)S(1)}, bf16[2,128,384]{2,1,0:T(8,128)(2,1)S(1)}, u32[]{:S(2)}, u32[]{:S(2)}) collective-permute-start(bf16[2,128,384]{2,1,0:T(8,128)(2,1)S(1)} %pad_maximum_fusion.5), channel_id=1, source_target_pairs={{2,0},{4,2},{6,4},{8,6},{10,8},{12,10},{14,12},{16,14},{18,16},{20... | collective-permute-start | bytes 589832 | tf_op jit(solution)/shard_map/ppermute | solution.py:22
  10.3 25.2 %collective-permute-start = (bf16[2,128,384]{2,1,0:T(8,128)(2,1)S(1)}, bf16[2,128,384]{2,1,0:T(8,128)(2,1)S(1)}, u32[]{:S(2)}, u32[]{:S(2)}) collective-permute-start(bf16[2,128,384]{2,1,0:T(8,128)(2,1)S(1)} %pad_maximum_fusion.5), channel_id=1, source_target_pairs={{0,2},{2,4},{4,6},{6,8},{8,10},{10,12},{12,14},{14,16},{16,18},{18... | collective-permute-start | bytes 589832 | tf_op jit(solution)/shard_map/ppermute | solution.py:19
  14.0 12.8 %all-to-all-start = ((s32[1,16,1]{2,0,1:T(1,128)}), s32[1,16,1]{2,0,1:T(1,128)S(1)}, u32[]{:S(2)}, u32[]{:S(2)}) async-start(s32[1,16,1]{2,0,1:T(1,128)} %copy.23), calls=%async_computation | async-start | bytes 16384 | tf_op jit(solution)/shard_map/all_to_all | solution.py:72
  30.4 3.8 %copy-start.12 = (s32[2]{0:T(128)S(1)}, s32[2]{0:T(128)}, u32[]{:S(2)}) copy-start(s32[2]{0:T(128)} %param.14) | copy-start | bytes 28
  30.4 5.0 %copy-start.8 = (bf16[128,384]{1,0:T(8,128)(2,1)S(1)}, bf16[128,384]{1,0:T(8,128)(2,1)}, u32[]{:S(2)}) copy-start(bf16[128,384]{1,0:T(8,128)(2,1)} %param.8) | copy-start | bytes 294916
  30.4 5.0 %copy-start.10 = (f32[384]{0:T(512)S(1)}, f32[384]{0:T(512)}, u32[]{:S(2)}) copy-start(f32[384]{0:T(512)} %param.11) | copy-start | bytes 4612
  30.4 22.4 %all-to-all-start.1 = ((bf16[16,64,384]{2,1,0:T(8,128)(2,1)}), bf16[16,64,384]{2,1,0:T(8,128)(2,1)S(1)}, u32[]{:S(2)}, u32[]{:S(2)}) async-start(bf16[16,64,384]{2,1,0:T(8,128)(2,1)} %get-tuple-element.16), calls=%async_computation.1 | async-start | bytes 1572864 | tf_op jit(solution)/shard_map/all_to_all | solution.py:81
  35.5 22.8 %copy-start.7 = (bf16[128,384]{1,0:T(8,128)(2,1)}, bf16[128,384]{1,0:T(8,128)(2,1)S(1)}, u32[]{:S(2)}) copy-start(bf16[128,384]{1,0:T(8,128)(2,1)S(1)} %fusion.36) | copy-start | bytes 294916
  52.8 24.1 %all-to-all-start.2 = ((bf16[16,64,384]{2,1,0:T(8,128)(2,1)}), bf16[16,64,384]{2,1,0:T(8,128)(2,1)S(1)}, u32[]{:S(2)}, u32[]{:S(2)}) async-start(bf16[16,64,384]{2,1,0:T(8,128)(2,1)} %get-tuple-element.15), calls=%async_computation.2 | async-start | bytes 1572864 | tf_op jit(solution)/shard_map/all_to_all | solution.py:82
  58.6 1.4 %copy-start.2 = (f32[128,1408]{1,0:T(8,128)}, f32[128,1408]{1,0:T(8,128)S(1)}, u32[]{:S(2)}) copy-start(f32[128,1408]{1,0:T(8,128)S(1)} %get-tuple-element.18) | copy-start | bytes 2162692
  61.4 15.6 %copy-start.3 = (f32[128,1408]{1,0:T(8,128)S(1)}, f32[128,1408]{1,0:T(8,128)}, u32[]{:S(2)}) copy-start(f32[128,1408]{1,0:T(8,128)} %copy-done.2) | copy-start | bytes 2162692
  77.0 1.3 %copy-start.4 = (bf16[384,384]{1,0:T(8,128)(2,1)S(1)}, bf16[384,384]{1,0:T(8,128)(2,1)}, u32[]{:S(2)}) copy-start(bf16[384,384]{1,0:T(8,128)(2,1)} %get-tuple-element.7) | copy-start | bytes 884740
  77.0 1.4 %copy-start.6 = (f32[128,384]{0,1:T(8,128)S(1)}, f32[128,384]{0,1:T(8,128)}, u32[]{:S(2)}) copy-start(f32[128,384]{0,1:T(8,128)} %fusion.40) | copy-start | bytes 589828
where the time goes:
time: 80.6 us; the launch traced here: 79.8 us
  waiting for transfers between devices  37.8 us (47%)
  starting transfers between devices  19.9 us (25%)
  other arithmetic  6.33 us (8%)
  blocking collectives  5.91 us (7%)
  matrix products  5.71 us (7%)
  local copies, waits for them, and re-layouts  3.85 us (5%)
    all_to_all x1, waiting for transfers between devices, local(): lax.all_to_all(send_keys, 'tm', split_axis=0, concat_axis=0, tiled=True)  16.5 us
    all_to_all x1, waiting for transfers between devices, local(): lax.all_to_all(send_values, 'tm', split_axis=0, concat_axis=0, tiled=True)  15.3 us
    all_to_all x1, starting transfers between devices, local(): lax.all_to_all(far_blocks, 'tm', split_axis=1, concat_axis=0, tiled=True)  6.43 us
    all_to_all x1, waiting for transfers between devices, local(): lax.all_to_all(far_blocks, 'tm', split_axis=1, concat_axis=0, tiled=True)  6.04 us
    psum x1, blocking collectives, local(): lax.psum((jnp.sum(query_f * query_f, axis=-1), jnp.sum(key_f * key_f, axi...  5.91 us
    all_to_all x1, starting transfers between devices, local(): lax.all_to_all(send_values, 'tm', split_axis=0, concat_axis=0, tiled=True)  5.43 us
    all_to_all x1, starting transfers between devices, local(): lax.all_to_all(send_keys, 'tm', split_axis=0, concat_axis=0, tiled=True)  3.74 us
    ppermute x1, starting transfers between devices, extended(): lax.ppermute(lax.slice_in_dim(block, block.shape[dim] - width, None, axis...  3.04 us
  transfers between devices with their start and end apart: 5, of which 3 were waited for; matrix products, arithmetic and copies ran while one was open for 12% of the time, Pallas kernels for 0%

commit v1 on v0

v1 whole, which is shorter than its diff:
```python
import functools

import jax
import jax.numpy as jnp
from jax import lax
from jax.experimental import pallas as pl
from jax.experimental.pallas import tpu as pltpu
from jax.sharding import PartitionSpec as P

HD = 128
BLK = 64
FRAME_TOK = 1560
EPSILON = 1e-06
LOG2E = 1.4426950408889634
MASKED = -1e30


def sums_kernel(query_ref, key_ref, out_ref):
    rows = query_ref.shape[0]
    for place, ref in enumerate((query_ref, key_ref)):
        wide = ref[...].astype(jnp.float32)
        out_ref[0:1, place * rows : (place + 1) * rows] = jnp.sum(
            (wide * wide).T, axis=0, keepdims=True
        )


def attention_kernel(
    far_ref,
    step_ref,
    query_ref,
    keys_ref,
    values_ref,
    sums_ref,
    query_gain_ref,
    key_gain_ref,
    gate_ref,
    out_ref,
    key_buf,
    value_buf,
    factor_buf,
):
    rows, width = query_ref.shape
    blocks = keys_ref.shape[0] // rows
    splits = sums_ref.shape[0] // blocks
    heads = width // HD
    full_width = width * splits
    me = lax.axis_index("tm")

    sums = jnp.sum(sums_ref[...].reshape(blocks, splits, 2 * rows), axis=1)
    factors = lax.rsqrt(sums / full_width + EPSILON)
    key_factors = factors[:, rows:]
    pad = -blocks % rows
    if pad:
        key_factors = jnp.concatenate([key_factors, jnp.zeros((pad, rows), jnp.float32)], axis=0)
    factor_buf[...] = key_factors.T[:, :blocks]
    block_ids = lax.broadcasted_iota(jnp.int32, (blocks, rows), 0)
    query_factor = jnp.sum(
        jnp.where(block_ids == me, factors[:, :rows], 0.0), axis=0, keepdims=True
    )
    query_factor = jnp.broadcast_to(query_factor, (rows, rows)).T[:, :1]

    query = (
        query_ref[...].astype(jnp.float32) * query_factor * query_gain_ref[...]
    ).astype(jnp.bfloat16)

    def place_block(slot, start, factor):
        wide = keys_ref[pl.ds(start, BLK), :].astype(jnp.float32)
        key_buf[slot * BLK : (slot + 1) * BLK, :] = (
            wide * factor * key_gain_ref[...]
        ).astype(jnp.bfloat16)
        value_buf[slot * BLK : (slot + 1) * BLK, :] = values_ref[pl.ds(start, BLK), :]

    wanted = []
    for j in range(blocks):
        choice = far_ref[0, j]
        first = jnp.maximum(choice, 0) * BLK
        place_block(
            j,
            pl.multiple_of(j * rows + first, BLK),
            factor_buf[pl.ds(pl.multiple_of(first, BLK), BLK), j : j + 1],
        )
        wanted.append((choice >= 0) | (jnp.abs(me - j) <= 1))
    lanes = lax.broadcasted_iota(jnp.int32, (BLK, blocks), 1)
    for side in range(3):
        near = me + side - 1
        held = jnp.clip(near, 0, blocks - 1)
        factor = jnp.sum(
            jnp.where(lanes == held, factor_buf[BLK:, :], 0.0), axis=1, keepdims=True
        )
        place_block(blocks + side, pl.multiple_of(held * rows + BLK, BLK), factor)
        wanted.append((near >= 0) & (near < blocks))
    slots = len(wanted)
    total = key_buf.shape[0] // BLK
    for slot in range(slots, total):
        key_buf[slot * BLK : (slot + 1) * BLK, :] = jnp.zeros((BLK, width), jnp.bfloat16)
        value_buf[slot * BLK : (slot + 1) * BLK, :] = jnp.zeros((BLK, width), jnp.bfloat16)
        wanted.append(jnp.bool_(False))

    half = lax.broadcasted_iota(jnp.int32, (1, 2 * BLK), 1) < BLK
    bias = jnp.concatenate(
        [
            jnp.where(
                half,
                jnp.where(wanted[2 * pair], 0.0, MASKED),
                jnp.where(wanted[2 * pair + 1], 0.0, MASKED),
            )
            for pair in range(total // 2)
        ],
        axis=1,
    )

    start = me * rows
    first_frame = start // FRAME_TOK
    last_frame = (start + rows - 1) // FRAME_TOK
    row_ids = lax.broadcasted_iota(jnp.int32, (rows, 1), 0)
    gate = jnp.where(
        row_ids < (first_frame + 1) * FRAME_TOK - start,
        gate_ref[pl.ds(step_ref[first_frame], 1), :],
        gate_ref[pl.ds(step_ref[last_frame], 1), :],
    )

    scale = HD ** (-0.5) * LOG2E
    for head in range(heads):
        low, high = head * HD, (head + 1) * HD
        scores = (
            lax.dot_general(
                query[:, low:high],
                key_buf[:, low:high],
                (((1,), (1,)), ((), ())),
                preferred_element_type=jnp.float32,
            )
            * scale
            + bias
        )
        weights = jnp.exp2(scores - jnp.max(scores, axis=1, keepdims=True))
        totals = jnp.sum(weights, axis=1, keepdims=True)
        context = jnp.dot(
            weights.astype(jnp.bfloat16),
            value_buf[:, low:high],
            preferred_element_type=jnp.float32,
        )
        out_ref[:, low:high] = (context / totals * gate[:, low:high]).astype(jnp.bfloat16)


def local(
    query_proj, key_proj, value_proj, query_gain, key_gain, gate_table, frame_step, far_blocks
):
    rows, width = query_proj.shape
    blocks = lax.axis_size("tm")
    smem = pl.BlockSpec(memory_space=pltpu.SMEM)
    vmem = pl.BlockSpec(memory_space=pltpu.VMEM)
    sums = pl.pallas_call(
        sums_kernel,
        out_shape=jax.ShapeDtypeStruct((1, 2 * rows), jnp.float32),
        in_specs=[vmem, vmem],
        out_specs=vmem,
    )(query_proj, key_proj)
    all_sums = lax.all_gather(sums, ("tm", "head"), axis=0, tiled=True)
    all_keys = lax.all_gather(key_proj, "tm", axis=0, tiled=True)
    all_values = lax.all_gather(value_proj, "tm", axis=0, tiled=True)
    slots = blocks + 3
    key_rows = (slots + slots % 2) * BLK
    return pl.pallas_call(
        attention_kernel,
        out_shape=jax.ShapeDtypeStruct((rows, width), jnp.bfloat16),
        in_specs=[smem, smem] + [vmem] * 7,
        out_specs=vmem,
        scratch_shapes=[
            pltpu.VMEM((key_rows, width), jnp.bfloat16),
            pltpu.VMEM((key_rows, width), jnp.bfloat16),
            pltpu.VMEM((rows, blocks), jnp.float32),
        ],
        compiler_params=pltpu.CompilerParams(vmem_limit_bytes=48 * 2**20),
    )(
        far_blocks,
        frame_step,
        query_proj,
        all_keys,
        all_values,
        all_sums,
        query_gain.reshape(1, width),
        key_gain.reshape(1, width),
        gate_table,
    )


def solution(mesh):
    return jax.shard_map(
        local,
        mesh=mesh,
        in_specs=(
            P("tm", "head"),
            P("tm", "head"),
            P("tm", "head"),
            P("head"),
            P("head"),
            P(None, "head"),
            P(),
            P("tm", None),
        ),
        out_specs=P("tm", "head"),
        check_vma=False,
    )
```

time: 80.6 us -> 109 us (1.35)
  blocking collectives: 5.91 us -> 70.1 us
  waiting for transfers between devices: 37.8 us -> 13.2 us
  starting transfers between devices: 19.9 us -> 0.04 us
  between operations: 0.29 us -> 13.4 us
  other arithmetic: 6.33 us -> 0 us
  matrix products: 5.71 us -> 0 us
  Pallas kernels: 0 us -> 4.88 us
  local copies, waits for them, and re-layouts: 3.85 us -> 7.27 us
    all_gather x0 -> x1, blocking collectives: none -> 70.1 us  [local(): all_sums = lax.all_gather(sums, ('tm', 'head'), axis=0, tiled=True)]
    all_to_all x3 -> x0, waiting for transfers between devices: 37.8 us -> none  [the longest x1 16.5 us: local(): lax.all_to_all(send_keys, 'tm', split_axis=0, concat_axis=0, tiled=True)]
    all_to_all x3 -> x0, starting transfers between devices: 15.6 us -> none  [the longest x1 6.43 us: local(): lax.all_to_all(far_blocks, 'tm', split_axis=1, concat_axis=0, tiled=True)]
    all_gather x0 -> x2, waiting for transfers between devices: none -> 11.8 us  [the longest x1 11.8 us: local(): all_keys = lax.all_gather(key_proj, 'tm', axis=0, tiled=True)]
    psum x1 -> x0, blocking collectives: 5.91 us -> none  [local(): lax.psum((jnp.sum(query_f * query_f, axis=-1), jnp.sum(key_f * key_f, axi...]
    unnamed x26 -> x13, local copies, waits for them, and re-layouts: 0.05 us -> 5.91 us
    dot_general x7 -> x0, matrix products: 5.71 us -> none  [the longest x3 2.56 us: softmax_update(): lax.dot_general(query_part, key_part, (((1,), (1,)), ((), ())), preferred...]
    pallas_call x0 -> x2, Pallas kernels: none -> 4.88 us  [the longest x1 3.19 us: local(): pl.pallas_call(attention_kernel, out_shape=jax.ShapeDtypeStruct((rows, wi...]
  transfers between devices with their start and end apart: 5 -> 2, of which waited for: 3 -> 1; matrix products, arithmetic and copies ran while one was open for 12% -> 1% of each run, Pallas kernels for 0% -> 2%
where the time goes in v1:
time: 109 us
  blocking collectives  70.1 us (64%)
  between operations  13.4 us (12%)
  waiting for transfers between devices  13.2 us (12%)
  local copies, waits for them, and re-layouts  7.27 us (7%)
  Pallas kernels  4.88 us (4%)
    all_gather x1, blocking collectives, local(): all_sums = lax.all_gather(sums, ('tm', 'head'), axis=0, tiled=True)  70.1 us
    all_gather x1, waiting for transfers between devices, local(): all_keys = lax.all_gather(key_proj, 'tm', axis=0, tiled=True)  11.8 us
    unnamed x13, local copies, waits for them, and re-layouts  5.91 us
    pallas_call x1, Pallas kernels, local(): pl.pallas_call(attention_kernel, out_shape=jax.ShapeDtypeStruct((rows, wi...  3.19 us
  transfers between devices with their start and end apart: 2, of which 1 were waited for; matrix products, arithmetic and copies ran while one was open for 1% of the time, Pallas kernels for 2%

profile of v1, /device:TPU:0, one launch (start us, length us, event | category | flops | bytes accessed | tf_op | source)
XLA Modules:
  0.0 108.9 jit_solution(13071055551204879911)
XLA Ops:
  6.5 0.0 all-gather.6.cloned.1.call-start
  6.5 0.7 all-gather.6.cloned.1.call-update
  7.3 0.0 all-gather.4.cloned.1.call-start
  7.3 0.7 all-gather.4.cloned.1.call-update
  8.0 1.7 %shard_map.82 = f32[1,256]{1,0:T(1,128)} custom-call(bf16[128,384]{1,0:T(8,128)(2,1)} %query_ref.3, bf16[128,384]{1,0:T(8,128)(2,1)} %key_ref.1), custom_call_target="tpu_custom_call" | custom-call | tf_op jit(solution)/shard_map/pallas_call | solution.py:152
  9.7 0.7 reshape.6.query_gain_ref
  10.4 0.7 reshape.7.key_gain_ref
  11.1 70.1 %all-gather = f32[32,1,256]{2,1,0:T(1,128)S(1)} all-gather(f32[1,1,256]{2,1,0:T(1,128)} %bitcast.5), channel_id=1, replica_groups=mesh['tm'=16,'head'=2] {'tm','head'}, dimensions={0}, use_global_device_ids=true | all-gather | bytes 33792 | tf_op jit(solution)/shard_map/all_gather | solution.py:158
  81.2 0.0 all-gather.6.cloned.1.call-done.values_ref
  81.2 11.8 %all-gather.4.cloned.1.call-done.keys_ref = bf16[2048,384]{1,0:T(8,128)(2,1)} async-done(((bf16[128,384]{1,0:T(8,128)(2,1)}), bf16[2048,384]{1,0:T(8,128)(2,1)}) %all-gather.4.cloned.1.call-update) | async-done | bytes 1572880 | tf_op jit(solution)/shard_map/all_gather | solution.py:159
  93.0 0.0 copy-start
  93.0 1.4 %copy-done = bf16[2048,384]{1,0:T(8,128)(2,1)S(1)} copy-done((bf16[2048,384]{1,0:T(8,128)(2,1)S(1)}, bf16[2048,384]{1,0:T(8,128)(2,1)}, u32[]{:S(2)}) %copy-start) | copy-done | bytes 1572888
  94.4 0.0 copy-start.1
  94.4 1.4 %copy-done.1 = bf16[2048,384]{1,0:T(8,128)(2,1)S(1)} copy-done((bf16[2048,384]{1,0:T(8,128)(2,1)S(1)}, bf16[2048,384]{1,0:T(8,128)(2,1)}, u32[]{:S(2)}) %copy-start.1) | copy-done | bytes 1572888
  95.8 0.0 copy-start.2
  95.8 0.9 copy-done.2
  96.7 0.0 copy-start.3
  96.7 0.9 copy-done.3
  97.6 0.0 copy-start.4
  97.6 0.7 copy-done.4
  98.2 0.0 copy-start.5
  98.2 0.7 copy-done.5
  98.9 3.2 %shard_map.83 = bf16[128,384]{1,0:T(8,128)(2,1)} custom-call(s32[1,16]{1,0:T(1,128)S(1)} %copy-done.4, s32[2]{0:T(128)S(1)} %copy-done.5, bf16[128,384]{1,0:T(8,128)(2,1)S(1)} %copy-done.2, bf16[2048,384]{1,0:T(8,128)(2,1)S(1)} %copy-done.1, bf16[2048,384]{1,0:T(8,128)(2,1)S(1)} %copy-done, f32[32,256]{1,0:T(8,128)S(1)} %bitcast.4, ...), custom_call_target="tpu_custom_call" | custom-call | tf_op jit(solution)/shard_map/pallas_call | solution.py:163
  (1 shorter events, 0.0 us)
Async XLA Ops:
  6.5 74.7 %all-gather.6.cloned.1.call-start = ((), (), s32[]{:S(2)}) async-start(), calls=%async_computation.1 | async-start | bytes 1671168 | tf_op jit(solution)/shard_map/all_gather | solution.py:160
  7.3 85.7 %all-gather.4.cloned.1.call-start = ((), (), s32[]{:S(2)}) async-start(), calls=%async_computation | async-start | bytes 1671168 | tf_op jit(solution)/shard_map/all_gather | solution.py:159
  93.0 1.4 %copy-start = (bf16[2048,384]{1,0:T(8,128)(2,1)S(1)}, bf16[2048,384]{1,0:T(8,128)(2,1)}, u32[]{:S(2)}) copy-start(bf16[2048,384]{1,0:T(8,128)(2,1)} %all-gather.6.cloned.1.call-done.values_ref) | copy-start | bytes 4718596
  94.4 1.4 %copy-start.1 = (bf16[2048,384]{1,0:T(8,128)(2,1)S(1)}, bf16[2048,384]{1,0:T(8,128)(2,1)}, u32[]{:S(2)}) copy-start(bf16[2048,384]{1,0:T(8,128)(2,1)} %all-gather.4.cloned.1.call-done.keys_ref) | copy-start | bytes 4718596
  95.8 0.9 copy-start.2
  96.7 0.9 copy-start.3
  97.6 0.7 copy-start.4
  98.2 0.7 copy-start.5
Sparse Core Ops, SparseCore 0:
  9.6 42.3 all-gather.5
  54.3 38.5 all-gather.3

commit v2 on v0

v2 whole, which is shorter than its diff:
```python
import functools

import jax
import jax.numpy as jnp
from jax import lax
from jax.experimental import pallas as pl
from jax.experimental.pallas import tpu as pltpu
from jax.sharding import PartitionSpec as P

HD = 128
BLK = 64
FRAME_TOK = 1560
EPSILON = 1e-06
LOG2E = 1.4426950408889634
MASKED = -1e30
EXTRA = 16
QUERY_MASKS = (0, 2, 4, 6)
ANY = pl.BlockSpec(memory_space=pl.ANY)
VMEM = pl.BlockSpec(memory_space=pltpu.VMEM)


def sums_kernel(query_hbm, key_hbm, out_ref, query_ref, key_ref, sems):
    copies = [
        pltpu.make_async_copy(query_hbm, query_ref, sems.at[0]),
        pltpu.make_async_copy(key_hbm, key_ref, sems.at[1]),
    ]
    for copy in copies:
        copy.start()
    for place, ref in enumerate((query_ref, key_ref)):
        copies[place].wait()
        wide = ref[...].astype(jnp.float32)
        square = wide * wide
        part = square[:, :HD]
        for low in range(HD, square.shape[1], HD):
            part = part + square[:, low : low + HD]
        out_ref[place : place + 1, :] = jnp.sum(part.T, axis=0, keepdims=True)


def norm_kernel(
    full_width,
    query_hbm,
    key_hbm,
    value_hbm,
    query_gain_ref,
    key_gain_ref,
    far_ref,
    own_ref,
    other_ref,
    query_out,
    pair_out,
    query_ref,
    key_ref,
    sems,
):
    rows, width = query_ref.shape
    copies = [
        pltpu.make_async_copy(query_hbm, query_ref, sems.at[0]),
        pltpu.make_async_copy(key_hbm, key_ref, sems.at[1]),
        pltpu.make_async_copy(value_hbm, pair_out.at[rows:, :], sems.at[2]),
    ]
    for copy in copies:
        copy.start()
    factors = lax.rsqrt((own_ref[...] + other_ref[...]) / full_width + EPSILON)
    columns = [
        jnp.broadcast_to(factors[place : place + 1, :], (rows, rows)).T[:, :1]
        for place in range(2)
    ]
    far = far_ref[...].astype(jnp.float32).astype(jnp.bfloat16)
    pad = jnp.zeros((1, HD - far.shape[1]), jnp.bfloat16)
    far = jnp.concatenate([far, pad], axis=1).astype(jnp.float32)
    query_out[rows:, :HD] = jnp.broadcast_to(far, (EXTRA, HD)).astype(jnp.bfloat16)
    query_out[rows:, HD:] = jnp.zeros((EXTRA, width - HD), jnp.bfloat16)
    copies[1].wait()
    pair_out[:rows, :] = (
        key_ref[...].astype(jnp.float32) * columns[1] * key_gain_ref[...]
    ).astype(jnp.bfloat16)
    copies[0].wait()
    query_out[:rows, :] = (
        query_ref[...].astype(jnp.float32) * columns[0] * query_gain_ref[...]
    ).astype(jnp.bfloat16)
    copies[2].wait()


def attention_kernel(key_masks, *refs):
    queries = refs[: len(QUERY_MASKS)]
    pairs = refs[len(QUERY_MASKS) : len(QUERY_MASKS) + len(key_masks)]
    own_out, sums_out, *packets = refs[len(QUERY_MASKS) + len(key_masks) :]
    rows, width = own_out.shape
    heads = width // HD
    me = lax.axis_index("tm")
    lane = lax.broadcasted_iota(jnp.int32, (1, HD), 1)
    half = (lane >= BLK).astype(jnp.float32)
    biases = []
    for query_mask, query_ref in zip(QUERY_MASKS, queries):
        far = query_ref[rows:, :HD].astype(jnp.float32)[:1]
        parts = []
        for key_mask in key_masks:
            query_id, key_id = me ^ query_mask, me ^ key_mask
            choice = jnp.sum(jnp.where(lane == key_id, far, 0.0), axis=1, keepdims=True)
            taken = (choice == half) | (jnp.abs(query_id - key_id) <= 1)
            parts.append(jnp.where(taken, 0.0, MASKED))
        biases.append(jnp.concatenate(parts, axis=1))

    scale = HD ** (-0.5) * LOG2E
    logs = jnp.zeros((rows, HD), jnp.float32)
    for head in range(heads):
        low, high = head * HD, (head + 1) * HD
        keys = jnp.concatenate([pair[:rows, low:high] for pair in pairs], axis=0)
        values = jnp.concatenate([pair[rows:, low:high] for pair in pairs], axis=0)
        for place, query_ref in enumerate(queries):
            scores = (
                lax.dot_general(
                    query_ref[:rows, low:high],
                    keys,
                    (((1,), (1,)), ((), ())),
                    preferred_element_type=jnp.float32,
                )
                * scale
                + biases[place]
            )
            top = jnp.max(scores, axis=1, keepdims=True)
            weights = jnp.exp2(scores - top)
            totals = jnp.sum(weights, axis=1, keepdims=True)
            context = (
                jnp.dot(
                    weights.astype(jnp.bfloat16), values, preferred_element_type=jnp.float32
                )
                / totals
            )
            logs = jnp.where(lane == place * heads + head, top + jnp.log2(totals), logs)
            if place == 0:
                own_out[:, low:high] = context
            else:
                packets[place - 1][:rows, low:high] = context.astype(jnp.bfloat16)
    rows_form = logs.T
    sub = lax.broadcasted_iota(jnp.int32, (EXTRA, HD), 0)
    for place in range(len(queries)):
        for head in range(heads):
            low, high = head * HD, (head + 1) * HD
            line = place * heads + head
            value = rows_form[line : line + 1, :]
            if place == 0:
                sums_out[:, low:high] = jnp.broadcast_to(value, (8, HD))
            else:
                first = value.astype(jnp.bfloat16).astype(jnp.float32)
                second = (value - first).astype(jnp.bfloat16).astype(jnp.float32)
                third = value - first - second
                packets[place - 1][rows:, low:high] = jnp.where(
                    sub == 0, first, jnp.where(sub == 1, second, third)
                ).astype(jnp.bfloat16)


def merge_kernel(own_ref, sums_ref, *refs):
    *packets, gate_ref, out_ref = refs
    rows, width = own_ref.shape
    heads = width // HD
    logs = [sums_ref[:1, :]]
    for packet in packets:
        pieces = packet[rows:, :].astype(jnp.float32)
        logs.append(pieces[0:1] + pieces[1:2] + pieces[2:3])
    top = functools.reduce(jnp.maximum, logs)
    weights = [jnp.exp2(log - top) for log in logs]
    total = sum(weights)
    weights = [weight / total for weight in weights]
    lines = [weight[:, h * HD : (h + 1) * HD] for weight in weights for h in range(heads)]
    lines += [jnp.zeros((1, HD), jnp.float32)] * (-len(lines) % 8)
    columns = jnp.concatenate(lines, axis=0).T
    start = lax.axis_index("tm") * rows
    first_rows = (start // FRAME_TOK + 1) * FRAME_TOK - start
    row_ids = lax.broadcasted_iota(jnp.int32, (rows, 1), 0)
    for head in range(heads):
        low, high = head * HD, (head + 1) * HD
        context = own_ref[:, low:high] * columns[:, head : head + 1]
        for place, packet in enumerate(packets):
            line = (place + 1) * heads + head
            context += packet[:rows, low:high].astype(jnp.float32) * columns[:, line : line + 1]
        gate = jnp.where(
            row_ids < first_rows, gate_ref[0:1, low:high], gate_ref[1:2, low:high]
        )
        out_ref[:, low:high] = (context * gate).astype(jnp.bfloat16)


def exchange(array, mask):
    count = lax.axis_size("tm")
    return lax.ppermute(array, "tm", [(i, i ^ mask) for i in range(count)])


def local(
    query_proj, key_proj, value_proj, query_gain, key_gain, gate_table, frame_step, far_blocks
):
    rows, width = query_proj.shape
    count = lax.axis_size("tm")
    splits = lax.axis_size("head")
    heads = width // HD
    params = pltpu.CompilerParams(vmem_limit_bytes=(8 + count // 4) * 2**20)

    sums = pl.pallas_call(
        sums_kernel,
        out_shape=jax.ShapeDtypeStruct((2, rows), jnp.float32),
        in_specs=[ANY, ANY],
        out_specs=VMEM,
        scratch_shapes=[
            pltpu.VMEM((rows, width), jnp.bfloat16),
            pltpu.VMEM((rows, width), jnp.bfloat16),
            pltpu.SemaphoreType.DMA((2,)),
        ],
        compiler_params=params,
    )(query_proj, key_proj)
    if splits == 2:
        others = lax.ppermute(sums, "head", [(0, 1), (1, 0)])
    else:
        sums = lax.psum(sums, "head")
        others = jnp.zeros_like(sums)

    query_pack, pair_pack = pl.pallas_call(
        functools.partial(norm_kernel, width * splits),
        out_shape=(
            jax.ShapeDtypeStruct((rows + EXTRA, width), jnp.bfloat16),
            jax.ShapeDtypeStruct((2 * rows, width), jnp.bfloat16),
        ),
        in_specs=[ANY, ANY, ANY, VMEM, VMEM, VMEM, VMEM, VMEM],
        out_specs=(VMEM, VMEM),
        scratch_shapes=[
            pltpu.VMEM((rows, width), jnp.bfloat16),
            pltpu.VMEM((rows, width), jnp.bfloat16),
            pltpu.SemaphoreType.DMA((3,)),
        ],
        compiler_params=params,
    )(
        query_proj,
        key_proj,
        value_proj,
        query_gain.reshape(1, width),
        key_gain.reshape(1, width),
        far_blocks,
        sums,
        others,
    )

    pairs = {0: pair_pack}
    key_bits = [1 << bit for bit in range(3, count.bit_length() - 1)] + [1]
    for mask in key_bits:
        for held in list(pairs):
            pairs[held ^ mask] = exchange(pairs[held], mask)
    key_masks = sorted(pairs)
    queries = [query_pack] + [exchange(query_pack, mask) for mask in QUERY_MASKS[1:]]

    partial = pl.pallas_call(
        functools.partial(attention_kernel, key_masks),
        out_shape=[
            jax.ShapeDtypeStruct((rows, width), jnp.float32),
            jax.ShapeDtypeStruct((8, width), jnp.float32),
        ]
        + [jax.ShapeDtypeStruct((rows + EXTRA, width), jnp.bfloat16)] * 3,
        in_specs=[VMEM] * (len(QUERY_MASKS) + len(key_masks)),
        out_specs=[VMEM] * 5,
        compiler_params=params,
    )(*queries, *[pairs[mask] for mask in key_masks])
    own, own_logs, *packets = partial
    packets = [exchange(packet, mask) for packet, mask in zip(packets, QUERY_MASKS[1:])]

    start = lax.axis_index("tm") * rows
    steps = [frame_step[start // FRAME_TOK], frame_step[(start + rows - 1) // FRAME_TOK]]
    gates = jnp.concatenate(
        [lax.dynamic_slice_in_dim(gate_table, step, 1, axis=0) for step in steps], axis=0
    )
    return pl.pallas_call(
        merge_kernel,
        out_shape=jax.ShapeDtypeStruct((rows, width), jnp.bfloat16),
        in_specs=[VMEM] * 6,
        out_specs=VMEM,
        compiler_params=params,
    )(own, own_logs, *packets, gates)


def solution(mesh):
    return jax.shard_map(
        local,
        mesh=mesh,
        in_specs=(
            P("tm", "head"),
            P("tm", "head"),
            P("tm", "head"),
            P("head"),
            P("head"),
            P(None, "head"),
            P(),
            P("tm", None),
        ),
        out_specs=P("tm", "head"),
        check_vma=False,
    )
```

time: 80.6 us -> 45.5 us (0.56)
  waiting for transfers between devices: 37.8 us -> 18.8 us
  starting transfers between devices: 19.9 us -> 13.3 us
  other arithmetic: 6.33 us -> 0.01 us
  blocking collectives: 5.91 us -> 0 us
  matrix products: 5.71 us -> 0 us
  Pallas kernels: 0 us -> 5.59 us
  between operations: 0.29 us -> 3.68 us
    all_to_all x3 -> x0, waiting for transfers between devices: 37.8 us -> none  [the longest x1 16.5 us: local(): lax.all_to_all(send_keys, 'tm', split_axis=0, concat_axis=0, tiled=True)]
    ppermute x2 -> x10, waiting for transfers between devices: 0.01 us -> 18.8 us  [the longest x9 17.3 us: exchange(): return lax.ppermute(array, 'tm', [(i, i ^ mask) for i in range(count)])]
    all_to_all x3 -> x0, starting transfers between devices: 15.6 us -> none  [the longest x1 6.43 us: local(): lax.all_to_all(far_blocks, 'tm', split_axis=1, concat_axis=0, tiled=True)]
    ppermute x2 -> x10, starting transfers between devices: 4.33 us -> 13.3 us  [the longest x9 10.3 us: exchange(): return lax.ppermute(array, 'tm', [(i, i ^ mask) for i in range(count)])]
    psum x1 -> x0, blocking collectives: 5.91 us -> none  [local(): lax.psum((jnp.sum(query_f * query_f, axis=-1), jnp.sum(key_f * key_f, axi...]
    dot_general x7 -> x0, matrix products: 5.71 us -> none  [the longest x3 2.56 us: softmax_update(): lax.dot_general(query_part, key_part, (((1,), (1,)), ((), ())), preferred...]
    pallas_call x0 -> x4, Pallas kernels: none -> 5.59 us  [the longest x1 3.32 us: local(): pl.pallas_call(functools.partial(attention_kernel, key_masks), out_shape=...]
    unnamed x26 -> x14, local copies, waits for them, and re-layouts: 0.05 us -> 2.46 us
  transfers between devices with their start and end apart: 5 -> 10, of which waited for: 3 -> 8; matrix products, arithmetic and copies ran while one was open for 12% -> 3% of each run, Pallas kernels for 0% -> 0%
where the time goes in v2:
time: 45.5 us; the launch traced here: 45.3 us
  waiting for transfers between devices  18.8 us (41%)
  starting transfers between devices  13.3 us (29%)
  Pallas kernels  5.59 us (12%)
  local copies, waits for them, and re-layouts  3.84 us (8%)
  between operations  3.68 us (8%)
    ppermute x9, waiting for transfers between devices, exchange(): return lax.ppermute(array, 'tm', [(i, i ^ mask) for i in range(count)])  17.3 us
    ppermute x9, starting transfers between devices, exchange(): return lax.ppermute(array, 'tm', [(i, i ^ mask) for i in range(count)])  10.3 us
    pallas_call x1, Pallas kernels, local(): pl.pallas_call(functools.partial(attention_kernel, key_masks), out_shape=...  3.32 us
    ppermute x1, starting transfers between devices, local(): others = lax.ppermute(sums, 'head', [(0, 1), (1, 0)])  3.03 us
    unnamed x14, local copies, waits for them, and re-layouts  2.46 us
    ppermute x1, waiting for transfers between devices, local(): others = lax.ppermute(sums, 'head', [(0, 1), (1, 0)])  1.52 us
    pallas_call x1, Pallas kernels, local(): pl.pallas_call(merge_kernel, out_shape=jax.ShapeDtypeStruct((rows, width)...  1.1 us
  transfers between devices with their start and end apart: 10, of which 8 were waited for; matrix products, arithmetic and copies ran while one was open for 3% of the time, Pallas kernels for 0%

profile of v2, /device:TPU:0, one launch (start us, length us, event | category | flops | bytes accessed | tf_op | source)
XLA Modules:
  0.0 45.3 jit_solution(8560128024901362876)
XLA Ops:
  0.0 0.0 copy-start
  0.0 0.9 %copy-done = bf16[128,384]{1,0:T(8,128)(2,1)S(1)} copy-done((bf16[128,384]{1,0:T(8,128)(2,1)S(1)}, bf16[128,384]{1,0:T(8,128)(2,1)}, u32[]{:S(2)}) %copy-start) | copy-done | bytes 98328
  0.9 0.0 copy-start.1
  0.9 0.9 %copy-done.1 = bf16[128,384]{1,0:T(8,128)(2,1)S(1)} copy-done((bf16[128,384]{1,0:T(8,128)(2,1)S(1)}, bf16[128,384]{1,0:T(8,128)(2,1)}, u32[]{:S(2)}) %copy-start.1) | copy-done | bytes 98328
  1.8 0.0 copy-start.5
  1.8 0.0 copy-start.2
  1.8 0.5 %shard_map.82.own_ref = f32[2,128]{1,0:T(2,128)S(1)} custom-call(bf16[128,384]{1,0:T(8,128)(2,1)S(1)} %copy-done, bf16[128,384]{1,0:T(8,128)(2,1)S(1)} %copy-done.1), custom_call_target="tpu_custom_call" | custom-call | tf_op jit(solution)/shard_map/pallas_call | solution.py:197
  2.3 0.0 copy-start.6
  2.3 3.0 %collective-permute-start = (f32[2,128]{1,0:T(2,128)S(1)}, f32[2,128]{1,0:T(2,128)S(1)}, u32[]{:S(2)}, u32[]{:S(2)}) collective-permute-start(f32[2,128]{1,0:T(2,128)S(1)} %shard_map.82.own_ref), channel_id=1, source_target_pairs={{0,1},{1,0},{2,3},{3,2},{4,5},{5,4},{6,7},{7,6},{8,9},{9,8},{10,11... | collective-permute-start | bytes 3080 | tf_op jit(solution)/shard_map/ppermute | solution.py:210
  5.3 0.0 copy-done.5
  5.3 0.0 copy-done.6
  5.3 0.0 copy-start.3
  5.3 1.5 %collective-permute-done.other_ref = f32[2,128]{1,0:T(2,128)S(1)} collective-permute-done((f32[2,128]{1,0:T(2,128)S(1)}, f32[2,128]{1,0:T(2,128)S(1)}, u32[]{:S(2)}, u32[]{:S(2)}) %collective-permute-start) | collective-permute-done | bytes 1056 | tf_op jit(solution)/shard_map/ppermute | solution.py:210
  6.9 0.0 copy-done.2
  6.9 0.0 copy-done.3
  6.9 0.7 %shard_map.83 = (bf16[144,384]{1,0:T(8,128)(2,1)S(1)}, bf16[256,384]{1,0:T(8,128)(2,1)S(1)}) custom-call(bf16[128,384]{1,0:T(8,128)(2,1)S(1)} %copy-done, bf16[128,384]{1,0:T(8,128)(2,1)S(1)} %copy-done.1, bf16[128,384]{1,0:T(8,128)(2,1)S(1)} %copy-done.2, f32[1,384]{1,0:T(1,128)S(1)} %reshape.6.query_gain_ref, f32[1,384]{1,0:T(1,128)S(1)} %reshape.7.key_gain_ref, ...), custom_call_target="tpu_custom_call" | custom-call | tf_op jit(solution)/shard_map/pallas_call | solution.py:215
  7.6 3.2 %collective-permute-start.5 = (bf16[256,384]{1,0:T(8,128)(2,1)S(1)}, bf16[256,384]{1,0:T(8,128)(2,1)S(1)}, u32[]{:S(2)}, u32[]{:S(2)}) collective-permute-start(bf16[256,384]{1,0:T(8,128)(2,1)S(1)} %get-tuple-element.13.refs_4_), channel_id=1, source_target_pairs={{0,16},{2,18},{4,20},{6,22},{8,24},{10,26},{12,28},{14,30},{16,0},... | collective-permute-start | bytes 589832 | tf_op jit(solution)/shard_map/ppermute | solution.py:185
  10.7 0.0 collective-permute-start.4
  10.7 8.0 %collective-permute-done.5.refs_6_ = bf16[256,384]{1,0:T(8,128)(2,1)S(1)} collective-permute-done((bf16[256,384]{1,0:T(8,128)(2,1)S(1)}, bf16[256,384]{1,0:T(8,128)(2,1)S(1)}, u32[]{:S(2)}, u32[]{:S(2)}) %collective-permute-start.5) | collective-permute-done | bytes 196640 | tf_op jit(solution)/shard_map/ppermute | solution.py:185
  18.7 0.0 collective-permute-start.6
  18.7 0.0 copy-start.4
  18.7 0.7 %copy-done.4 = s32[2]{0:T(128)S(1)} copy-done((s32[2]{0:T(128)S(1)}, s32[2]{0:T(128)}, u32[]{:S(2)}) %copy-start.4) | copy-done | bytes 32
  19.3 0.6 %fusion = (s32[1]{0:T(128)}, s32[1]{0:T(128)}) fusion(s32[2]{0:T(128)S(1)} %copy-done.4, s32[]{:T(128)S(6)} %select_n.21, s32[]{:T(128)S(6)} %select_n.24), kind=kLoop, calls=%fused_computation.3 | loop fusion | bytes 24 | tf_op jit(solution)/shard_map/dynamic_slice | solution.py:263
  23.6 1.6 %collective-permute-start.1 = (bf16[144,384]{1,0:T(8,128)(2,1)S(1)}, bf16[144,384]{1,0:T(8,128)(2,1)S(1)}, u32[]{:S(2)}, u32[]{:S(2)}) collective-permute-start(bf16[144,384]{1,0:T(8,128)(2,1)S(1)} %get-tuple-element.12.refs_0_), channel_id=1, source_target_pairs={{0,4},{2,6},{4,0},{6,2},{8,12},{10,14},{12,8},{14,10},{16,20},{18,... | collective-permute-start | bytes 331784 | tf_op jit(solution)/shard_map/ppermute | solution.py:185
  25.2 0.7 %collective-permute-start.2 = (bf16[144,384]{1,0:T(8,128)(2,1)S(1)}, bf16[144,384]{1,0:T(8,128)(2,1)S(1)}, u32[]{:S(2)}, u32[]{:S(2)}) collective-permute-start(bf16[144,384]{1,0:T(8,128)(2,1)S(1)} %get-tuple-element.12.refs_0_), channel_id=1, source_target_pairs={{0,8},{2,10},{4,12},{6,14},{8,0},{10,2},{12,4},{14,6},{16,24},{18,... | collective-permute-start | bytes 331784 | tf_op jit(solution)/shard_map/ppermute | solution.py:185
  25.8 1.3 %collective-permute-start.3 = (bf16[144,384]{1,0:T(8,128)(2,1)S(1)}, bf16[144,384]{1,0:T(8,128)(2,1)S(1)}, u32[]{:S(2)}, u32[]{:S(2)}) collective-permute-start(bf16[144,384]{1,0:T(8,128)(2,1)S(1)} %get-tuple-element.12.refs_0_), channel_id=1, source_target_pairs={{0,12},{2,14},{4,8},{6,10},{8,4},{10,6},{12,0},{14,2},{16,28},{18,... | collective-permute-start | bytes 331784 | tf_op jit(solution)/shard_map/ppermute | solution.py:185
  27.1 0.8 %constant_dynamic-slice_fusion.1 = (f32[1,384]{1,0:T(1,128)S(1)}, f32[1,384]{1,0:T(1,128)S(1)}) fusion(f32[50,384]{1,0:T(8,128)} %param.13, s32[]{:T(128)S(6)} %select_n.22, s32[]{:T(128)S(6)} %select_n.25), kind=kLoop, calls=%fused_computation.2 | loop fusion | bytes 6152 | tf_op jit(solution)/shard_map/dynamic_slice | solution.py:265
  27.9 1.2 %collective-permute-done.1.refs_1_ = bf16[144,384]{1,0:T(8,128)(2,1)S(1)} collective-permute-done((bf16[144,384]{1,0:T(8,128)(2,1)S(1)}, bf16[144,384]{1,0:T(8,128)(2,1)S(1)}, u32[]{:S(2)}, u32[]{:S(2)}) %collective-permute-start.1) | collective-permute-done | bytes 110624 | tf_op jit(solution)/shard_map/ppermute | solution.py:185
  29.1 2.0 %collective-permute-done.2.refs_2_ = bf16[144,384]{1,0:T(8,128)(2,1)S(1)} collective-permute-done((bf16[144,384]{1,0:T(8,128)(2,1)S(1)}, bf16[144,384]{1,0:T(8,128)(2,1)S(1)}, u32[]{:S(2)}, u32[]{:S(2)}) %collective-permute-start.2) | collective-permute-done | bytes 110624 | tf_op jit(solution)/shard_map/ppermute | solution.py:185
  31.1 1.6 %collective-permute-done.3.refs_3_ = bf16[144,384]{1,0:T(8,128)(2,1)S(1)} collective-permute-done((bf16[144,384]{1,0:T(8,128)(2,1)S(1)}, bf16[144,384]{1,0:T(8,128)(2,1)S(1)}, u32[]{:S(2)}, u32[]{:S(2)}) %collective-permute-start.3) | collective-permute-done | bytes 110624 | tf_op jit(solution)/shard_map/ppermute | solution.py:185
  32.6 0.0 collective-permute-done.4.refs_5_
  32.6 0.0 collective-permute-done.6.refs_7_
  32.6 3.3 %shard_map.84 = (f32[128,384]{1,0:T(8,128)S(1)}, f32[8,384]{1,0:T(8,128)S(1)}, bf16[144,384]{1,0:T(8,128)(2,1)S(1)}, bf16[144,384]{1,0:T(8,128)(2,1)S(1)}, bf16[144,384]{1,0:T(8,128)(2,1)S(1)}) custom-call(bf16[144,384]{1,0:T(8,128)(2,1)S(1)} %get-tuple-element.12.refs_0_, bf16[144,384]{1,0:T(8,128)(2,1)S(1)} %collective-permute-done.1.refs_1_, ...), custom_call_target="tpu_custom_call" | custom-call | tf_op jit(solution)/shard_map/pallas_call | solution.py:248
  36.0 1.6 %collective-permute-start.7 = (bf16[144,384]{1,0:T(8,128)(2,1)S(1)}, bf16[144,384]{1,0:T(8,128)(2,1)S(1)}, u32[]{:S(2)}, u32[]{:S(2)}) collective-permute-start(bf16[144,384]{1,0:T(8,128)(2,1)S(1)} %get-tuple-element.16), channel_id=1, source_target_pairs={{0,4},{2,6},{4,0},{6,2},{8,12},{10,14},{12,8},{14,10},{16,20},{18,... | collective-permute-start | bytes 331784 | tf_op jit(solution)/shard_map/ppermute | solution.py:185
  37.6 0.7 %collective-permute-start.8 = (bf16[144,384]{1,0:T(8,128)(2,1)S(1)}, bf16[144,384]{1,0:T(8,128)(2,1)S(1)}, u32[]{:S(2)}, u32[]{:S(2)}) collective-permute-start(bf16[144,384]{1,0:T(8,128)(2,1)S(1)} %get-tuple-element.17), channel_id=1, source_target_pairs={{0,8},{2,10},{4,12},{6,14},{8,0},{10,2},{12,4},{14,6},{16,24},{18,... | collective-permute-start | bytes 331784 | tf_op jit(solution)/shard_map/ppermute | solution.py:185
  38.3 1.3 %collective-permute-start.9 = (bf16[144,384]{1,0:T(8,128)(2,1)S(1)}, bf16[144,384]{1,0:T(8,128)(2,1)S(1)}, u32[]{:S(2)}, u32[]{:S(2)}) collective-permute-start(bf16[144,384]{1,0:T(8,128)(2,1)S(1)} %get-tuple-element.18), channel_id=1, source_target_pairs={{0,12},{2,14},{4,8},{6,10},{8,4},{10,6},{12,0},{14,2},{16,28},{18,... | collective-permute-start | bytes 331784 | tf_op jit(solution)/shard_map/ppermute | solution.py:185
  39.5 1.8 %collective-permute-done.7.refs_0_ = bf16[144,384]{1,0:T(8,128)(2,1)S(1)} collective-permute-done((bf16[144,384]{1,0:T(8,128)(2,1)S(1)}, bf16[144,384]{1,0:T(8,128)(2,1)S(1)}, u32[]{:S(2)}, u32[]{:S(2)}) %collective-permute-start.7) | collective-permute-done | bytes 110624 | tf_op jit(solution)/shard_map/ppermute | solution.py:185
  41.4 1.5 %collective-permute-done.8.refs_1_ = bf16[144,384]{1,0:T(8,128)(2,1)S(1)} collective-permute-done((bf16[144,384]{1,0:T(8,128)(2,1)S(1)}, bf16[144,384]{1,0:T(8,128)(2,1)S(1)}, u32[]{:S(2)}, u32[]{:S(2)}) %collective-permute-start.8) | collective-permute-done | bytes 110624 | tf_op jit(solution)/shard_map/ppermute | solution.py:185
  42.9 1.3 %collective-permute-done.9.refs_2_ = bf16[144,384]{1,0:T(8,128)(2,1)S(1)} collective-permute-done((bf16[144,384]{1,0:T(8,128)(2,1)S(1)}, bf16[144,384]{1,0:T(8,128)(2,1)S(1)}, u32[]{:S(2)}, u32[]{:S(2)}) %collective-permute-start.9) | collective-permute-done | bytes 110624 | tf_op jit(solution)/shard_map/ppermute | solution.py:185
  44.2 1.1 %shard_map.85 = bf16[128,384]{1,0:T(8,128)(2,1)} custom-call(f32[128,384]{1,0:T(8,128)S(1)} %get-tuple-element.14.own_ref, f32[8,384]{1,0:T(8,128)S(1)} %get-tuple-element.15.sums_ref, bf16[144,384]{1,0:T(8,128)(2,1)S(1)} %collective-permute-done.7.refs_0_, bf16[144,384]{1,0:T(8,128)(2,1)S(1)} %collective-permute-done.8.refs_1_, ...), custom_call_target="tpu_custom_call" | custom-call | tf_op jit(solution)/shard_map/pallas_call | solution.py:267
  (3 shorter events, 0.0 us)
Async XLA Ops:
  0.0 0.9 %copy-start = (bf16[128,384]{1,0:T(8,128)(2,1)S(1)}, bf16[128,384]{1,0:T(8,128)(2,1)}, u32[]{:S(2)}) copy-start(bf16[128,384]{1,0:T(8,128)(2,1)} %query_hbm.3) | copy-start | bytes 294916
  0.9 0.9 %copy-start.1 = (bf16[128,384]{1,0:T(8,128)(2,1)S(1)}, bf16[128,384]{1,0:T(8,128)(2,1)}, u32[]{:S(2)}) copy-start(bf16[128,384]{1,0:T(8,128)(2,1)} %key_hbm.3) | copy-start | bytes 294916
  1.8 3.5 %copy-start.5 = (f32[384]{0:T(512)S(1)}, f32[384]{0:T(512)}, u32[]{:S(2)}) copy-start(f32[384]{0:T(512)} %param.11) | copy-start | bytes 4612
  1.8 5.1 %copy-start.2 = (bf16[128,384]{1,0:T(8,128)(2,1)S(1)}, bf16[128,384]{1,0:T(8,128)(2,1)}, u32[]{:S(2)}) copy-start(bf16[128,384]{1,0:T(8,128)(2,1)} %value_hbm.1) | copy-start | bytes 294916
  2.3 3.1 %copy-start.6 = (f32[384]{0:T(512)S(1)}, f32[384]{0:T(512)}, u32[]{:S(2)}) copy-start(f32[384]{0:T(512)} %param.12) | copy-start | bytes 4612
  2.3 4.6 %collective-permute-start = (f32[2,128]{1,0:T(2,128)S(1)}, f32[2,128]{1,0:T(2,128)S(1)}, u32[]{:S(2)}, u32[]{:S(2)}) collective-permute-start(f32[2,128]{1,0:T(2,128)S(1)} %shard_map.82.own_ref), channel_id=1, source_target_pairs={{0,1},{1,0},{2,3},{3,2},{4,5},{5,4},{6,7},{7,6},{8,9},{9,8},{10,11... | collective-permute-start | bytes 3080 | tf_op jit(solution)/shard_map/ppermute | solution.py:210
  5.3 1.5 %copy-start.3 = (s32[1,16]{1,0:T(1,128)S(1)}, s32[1,16]{1,0:T(1,128)}, u32[]{:S(2)}) copy-start(s32[1,16]{1,0:T(1,128)} %far_ref.1) | copy-start | bytes 196
  7.6 11.1 %collective-permute-start.5 = (bf16[256,384]{1,0:T(8,128)(2,1)S(1)}, bf16[256,384]{1,0:T(8,128)(2,1)S(1)}, u32[]{:S(2)}, u32[]{:S(2)}) collective-permute-start(bf16[256,384]{1,0:T(8,128)(2,1)S(1)} %get-tuple-element.13.refs_4_), channel_id=1, source_target_pairs={{0,16},{2,18},{4,20},{6,22},{8,24},{10,26},{12,28},{14,30},{16,0},... | collective-permute-start | bytes 589832 | tf_op jit(solution)/shard_map/ppermute | solution.py:185
  10.7 21.9 %collective-permute-start.4 = (bf16[256,384]{1,0:T(8,128)(2,1)S(1)}, bf16[256,384]{1,0:T(8,128)(2,1)S(1)}, u32[]{:S(2)}, u32[]{:S(2)}) collective-permute-start(bf16[256,384]{1,0:T(8,128)(2,1)S(1)} %get-tuple-element.13.refs_4_), channel_id=1, source_target_pairs={{0,2},{2,0},{4,6},{6,4},{8,10},{10,8},{12,14},{14,12},{16,18},{18,... | collective-permute-start | bytes 589832 | tf_op jit(solution)/shard_map/ppermute | solution.py:185
  18.7 14.0 %collective-permute-start.6 = (bf16[256,384]{1,0:T(8,128)(2,1)S(1)}, bf16[256,384]{1,0:T(8,128)(2,1)S(1)}, u32[]{:S(2)}, u32[]{:S(2)}) collective-permute-start(bf16[256,384]{1,0:T(8,128)(2,1)S(1)} %collective-permute-done.5.refs_6_), channel_id=1, source_target_pairs={{0,2},{2,0},{4,6},{6,4},{8,10},{10,8},{12,14},{14,12},{16,18},{18,... | collective-permute-start | bytes 589832 | tf_op jit(solution)/shard_map/ppermute | solution.py:185
  18.7 0.7 %copy-start.4 = (s32[2]{0:T(128)S(1)}, s32[2]{0:T(128)}, u32[]{:S(2)}) copy-start(s32[2]{0:T(128)} %param.14) | copy-start | bytes 28
  23.6 5.5 %collective-permute-start.1 = (bf16[144,384]{1,0:T(8,128)(2,1)S(1)}, bf16[144,384]{1,0:T(8,128)(2,1)S(1)}, u32[]{:S(2)}, u32[]{:S(2)}) collective-permute-start(bf16[144,384]{1,0:T(8,128)(2,1)S(1)} %get-tuple-element.12.refs_0_), channel_id=1, source_target_pairs={{0,4},{2,6},{4,0},{6,2},{8,12},{10,14},{12,8},{14,10},{16,20},{18,... | collective-permute-start | bytes 331784 | tf_op jit(solution)/shard_map/ppermute | solution.py:185
  25.2 5.9 %collective-permute-start.2 = (bf16[144,384]{1,0:T(8,128)(2,1)S(1)}, bf16[144,384]{1,0:T(8,128)(2,1)S(1)}, u32[]{:S(2)}, u32[]{:S(2)}) collective-permute-start(bf16[144,384]{1,0:T(8,128)(2,1)S(1)} %get-tuple-element.12.refs_0_), channel_id=1, source_target_pairs={{0,8},{2,10},{4,12},{6,14},{8,0},{10,2},{12,4},{14,6},{16,24},{18,... | collective-permute-start | bytes 331784 | tf_op jit(solution)/shard_map/ppermute | solution.py:185
  25.8 6.8 %collective-permute-start.3 = (bf16[144,384]{1,0:T(8,128)(2,1)S(1)}, bf16[144,384]{1,0:T(8,128)(2,1)S(1)}, u32[]{:S(2)}, u32[]{:S(2)}) collective-permute-start(bf16[144,384]{1,0:T(8,128)(2,1)S(1)} %get-tuple-element.12.refs_0_), channel_id=1, source_target_pairs={{0,12},{2,14},{4,8},{6,10},{8,4},{10,6},{12,0},{14,2},{16,28},{18,... | collective-permute-start | bytes 331784 | tf_op jit(solution)/shard_map/ppermute | solution.py:185
  36.0 5.4 %collective-permute-start.7 = (bf16[144,384]{1,0:T(8,128)(2,1)S(1)}, bf16[144,384]{1,0:T(8,128)(2,1)S(1)}, u32[]{:S(2)}, u32[]{:S(2)}) collective-permute-start(bf16[144,384]{1,0:T(8,128)(2,1)S(1)} %get-tuple-element.16), channel_id=1, source_target_pairs={{0,4},{2,6},{4,0},{6,2},{8,12},{10,14},{12,8},{14,10},{16,20},{18,... | collective-permute-start | bytes 331784 | tf_op jit(solution)/shard_map/ppermute | solution.py:185
  37.6 5.3 %collective-permute-start.8 = (bf16[144,384]{1,0:T(8,128)(2,1)S(1)}, bf16[144,384]{1,0:T(8,128)(2,1)S(1)}, u32[]{:S(2)}, u32[]{:S(2)}) collective-permute-start(bf16[144,384]{1,0:T(8,128)(2,1)S(1)} %get-tuple-element.17), channel_id=1, source_target_pairs={{0,8},{2,10},{4,12},{6,14},{8,0},{10,2},{12,4},{14,6},{16,24},{18,... | collective-permute-start | bytes 331784 | tf_op jit(solution)/shard_map/ppermute | solution.py:185
  38.3 5.9 %collective-permute-start.9 = (bf16[144,384]{1,0:T(8,128)(2,1)S(1)}, bf16[144,384]{1,0:T(8,128)(2,1)S(1)}, u32[]{:S(2)}, u32[]{:S(2)}) collective-permute-start(bf16[144,384]{1,0:T(8,128)(2,1)S(1)} %get-tuple-element.18), channel_id=1, source_target_pairs={{0,12},{2,14},{4,8},{6,10},{8,4},{10,6},{12,0},{14,2},{16,28},{18,... | collective-permute-start | bytes 331784 | tf_op jit(solution)/shard_map/ppermute | solution.py:185

commit v3 on v2

--- a/solution.py
+++ b/solution.py
@@ -17,6 +17,7 @@
 QUERY_MASKS = (0, 2, 4, 6)
 ANY = pl.BlockSpec(memory_space=pl.ANY)
 VMEM = pl.BlockSpec(memory_space=pltpu.VMEM)
+SMEM = pl.BlockSpec(memory_space=pltpu.SMEM)
 
 
 def sums_kernel(query_hbm, key_hbm, out_ref, query_ref, key_ref, sems):
@@ -38,55 +39,50 @@
 
 def norm_kernel(
     full_width,
-    query_hbm,
-    key_hbm,
-    value_hbm,
+    query_ref,
+    key_ref,
     query_gain_ref,
     key_gain_ref,
     far_ref,
     own_ref,
     other_ref,
     query_out,
-    pair_out,
-    query_ref,
-    key_ref,
-    sems,
+    key_out,
 ):
     rows, width = query_ref.shape
-    copies = [
-        pltpu.make_async_copy(query_hbm, query_ref, sems.at[0]),
-        pltpu.make_async_copy(key_hbm, key_ref, sems.at[1]),
-        pltpu.make_async_copy(value_hbm, pair_out.at[rows:, :], sems.at[2]),
-    ]
-    for copy in copies:
-        copy.start()
     factors = lax.rsqrt((own_ref[...] + other_ref[...]) / full_width + EPSILON)
     columns = [
         jnp.broadcast_to(factors[place : place + 1, :], (rows, rows)).T[:, :1]
         for place in range(2)
     ]
-    far = far_ref[...].astype(jnp.float32).astype(jnp.bfloat16)
-    pad = jnp.zeros((1, HD - far.shape[1]), jnp.bfloat16)
-    far = jnp.concatenate([far, pad], axis=1).astype(jnp.float32)
+    far = far_ref[...].astype(jnp.float32)
+    far = jnp.concatenate([far, jnp.zeros((1, HD - far.shape[1]), jnp.float32)], axis=1)
     query_out[rows:, :HD] = jnp.broadcast_to(far, (EXTRA, HD)).astype(jnp.bfloat16)
     query_out[rows:, HD:] = jnp.zeros((EXTRA, width - HD), jnp.bfloat16)
-    copies[1].wait()
-    pair_out[:rows, :] = (
+    key_out[...] = (
         key_ref[...].astype(jnp.float32) * columns[1] * key_gain_ref[...]
     ).astype(jnp.bfloat16)
-    copies[0].wait()
     query_out[:rows, :] = (
         query_ref[...].astype(jnp.float32) * columns[0] * query_gain_ref[...]
     ).astype(jnp.bfloat16)
-    copies[2].wait()
-
-
-def attention_kernel(key_masks, *refs):
-    queries = refs[: len(QUERY_MASKS)]
-    pairs = refs[len(QUERY_MASKS) : len(QUERY_MASKS) + len(key_masks)]
-    own_out, sums_out, *packets = refs[len(QUERY_MASKS) + len(key_masks) :]
-    rows, width = own_out.shape
-    heads = width // HD
+
+
+def masked_scores(queries, keys, key_masks, low, high, biases):
+    rows = keys[0].shape[0]
+    scores = lax.dot_general(
+        jnp.concatenate([query[:rows, low:high] for query in queries], axis=0),
+        jnp.concatenate([key[:, low:high] for key in keys], axis=0),
+        (((1,), (1,)), ((), ())),
+        preferred_element_type=jnp.float32,
+    )
+    scale = HD ** (-0.5) * LOG2E
+    return [
+        scores[place * rows : (place + 1) * rows] * scale + bias
+        for place, bias in enumerate(biases)
+    ]
+
+
+def key_biases(queries, key_masks, rows):
     me = lax.axis_index("tm")
     lane = lax.broadcasted_iota(jnp.int32, (1, HD), 1)
     half = (lane >= BLK).astype(jnp.float32)
@@ -100,41 +96,87 @@
             taken = (choice == half) | (jnp.abs(query_id - key_id) <= 1)
             parts.append(jnp.where(taken, 0.0, MASKED))
         biases.append(jnp.concatenate(parts, axis=1))
-
-    scale = HD ** (-0.5) * LOG2E
+    return biases
+
+
+def near_kernel(key_masks, step_ref, gate_ref, *refs):
+    count, held = len(QUERY_MASKS), len(key_masks)
+    queries, keys = refs[:count], refs[count : count + held]
+    values = refs[count + held : count + 2 * held]
+    context_out, stats_out, gate_out = refs[count + 2 * held :]
+    rows, width = keys[0].shape
+    start = lax.axis_index("tm") * rows
+    first = step_ref[start // FRAME_TOK]
+    last = step_ref[(start + rows - 1) // FRAME_TOK]
+    gate_out[0:1, :] = gate_ref[pl.ds(first, 1), :]
+    gate_out[1:2, :] = gate_ref[pl.ds(last, 1), :]
+    biases = key_biases(queries, key_masks, rows)
+    lane = lax.broadcasted_iota(jnp.int32, (1, HD), 1)
+    stats = [jnp.zeros((rows, HD), jnp.float32)] * count
+    for head in range(width // HD):
+        low, high = head * HD, (head + 1) * HD
+        scores = masked_scores(queries, keys, key_masks, low, high, biases)
+        rounded = []
+        for place in range(count):
+            top = jnp.max(scores[place], axis=1, keepdims=True)
+            weights = jnp.exp2(scores[place] - top)
+            total = jnp.sum(weights, axis=1, keepdims=True)
+            rounded.append(weights.astype(jnp.bfloat16))
+            stats[place] = jnp.where(
+                lane == 2 * head,
+                top,
+                jnp.where(lane == 2 * head + 1, total, stats[place]),
+            )
+        context_out[:, low:high] = jnp.dot(
+            jnp.concatenate(rounded, axis=0),
+            jnp.concatenate([value[:, low:high] for value in values], axis=0),
+            preferred_element_type=jnp.float32,
+        )
+    for place in range(count):
+        stats_out[place * rows : (place + 1) * rows, :] = stats[place]
+
+
+def far_kernel(key_masks, *refs):
+    count, held = len(QUERY_MASKS), len(key_masks)
+    queries, keys = refs[:count], refs[count : count + held]
+    values = refs[count + held : count + 2 * held]
+    context_ref, stats_ref, own_out, sums_out, *packets = refs[count + 2 * held :]
+    rows, width = own_out.shape
+    heads = width // HD
+    biases = key_biases(queries, key_masks, rows)
+    lane = lax.broadcasted_iota(jnp.int32, (1, HD), 1)
     logs = jnp.zeros((rows, HD), jnp.float32)
     for head in range(heads):
         low, high = head * HD, (head + 1) * HD
-        keys = jnp.concatenate([pair[:rows, low:high] for pair in pairs], axis=0)
-        values = jnp.concatenate([pair[rows:, low:high] for pair in pairs], axis=0)
-        for place, query_ref in enumerate(queries):
-            scores = (
-                lax.dot_general(
-                    query_ref[:rows, low:high],
-                    keys,
-                    (((1,), (1,)), ((), ())),
-                    preferred_element_type=jnp.float32,
-                )
-                * scale
-                + biases[place]
-            )
-            top = jnp.max(scores, axis=1, keepdims=True)
-            weights = jnp.exp2(scores - top)
-            totals = jnp.sum(weights, axis=1, keepdims=True)
-            context = (
-                jnp.dot(
-                    weights.astype(jnp.bfloat16), values, preferred_element_type=jnp.float32
-                )
-                / totals
-            )
-            logs = jnp.where(lane == place * heads + head, top + jnp.log2(totals), logs)
+        scores = masked_scores(queries, keys, key_masks, low, high, biases)
+        rounded, totals, fades = [], [], []
+        for place in range(count):
+            part = slice(place * rows, (place + 1) * rows)
+            old_top = stats_ref[part, 2 * head : 2 * head + 1]
+            old_total = stats_ref[part, 2 * head + 1 : 2 * head + 2]
+            top = jnp.maximum(old_top, jnp.max(scores[place], axis=1, keepdims=True))
+            weights = jnp.exp2(scores[place] - top)
+            fade = jnp.exp2(old_top - top)
+            total = old_total * fade + jnp.sum(weights, axis=1, keepdims=True)
+            rounded.append(weights.astype(jnp.bfloat16))
+            totals.append(total)
+            fades.append(fade)
+            logs = jnp.where(lane == place * heads + head, top + jnp.log2(total), logs)
+        added = jnp.dot(
+            jnp.concatenate(rounded, axis=0),
+            jnp.concatenate([value[:, low:high] for value in values], axis=0),
+            preferred_element_type=jnp.float32,
+        )
+        for place in range(count):
+            part = slice(place * rows, (place + 1) * rows)
+            context = (context_ref[part, low:high] * fades[place] + added[part]) / totals[place]
             if place == 0:
                 own_out[:, low:high] = context
             else:
                 packets[place - 1][:rows, low:high] = context.astype(jnp.bfloat16)
     rows_form = logs.T
     sub = lax.broadcasted_iota(jnp.int32, (EXTRA, HD), 0)
-    for place in range(len(queries)):
+    for place in range(count):
         for head in range(heads):
             low, high = head * HD, (head + 1) * HD
             line = place * heads + head
@@ -191,8 +233,13 @@
     rows, width = query_proj.shape
     count = lax.axis_size("tm")
     splits = lax.axis_size("head")
-    heads = width // HD
     params = pltpu.CompilerParams(vmem_limit_bytes=(8 + count // 4) * 2**20)
+    far_bits = [1 << bit for bit in range(3, count.bit_length() - 1)]
+
+    values = {0: value_proj}
+    for mask in far_bits + [1]:
+        for held in list(values):
+            values[held ^ mask] = exchange(values[held], mask)
 
     sums = pl.pallas_call(
         sums_kernel,
@@ -204,7 +251,6 @@
             pltpu.VMEM((rows, width), jnp.bfloat16),
             pltpu.SemaphoreType.DMA((2,)),
         ],
-        compiler_params=params,
     )(query_proj, key_proj)
     if splits == 2:
         others = lax.ppermute(sums, "head", [(0, 1), (1, 0)])
@@ -212,24 +258,18 @@
         sums = lax.psum(sums, "head")
         others = jnp.zeros_like(sums)
 
-    query_pack, pair_pack = pl.pallas_call(
+    query_pack, key_norm = pl.pallas_call(
         functools.partial(norm_kernel, width * splits),
         out_shape=(
             jax.ShapeDtypeStruct((rows + EXTRA, width), jnp.bfloat16),
-            jax.ShapeDtypeStruct((2 * rows, width), jnp.bfloat16),
+            jax.ShapeDtypeStruct((rows, width), jnp.bfloat16),
         ),
-        in_specs=[ANY, ANY, ANY, VMEM, VMEM, VMEM, VMEM, VMEM],
+        in_specs=[VMEM] * 7,
         out_specs=(VMEM, VMEM),
-        scratch_shapes=[
-            pltpu.VMEM((rows, width), jnp.bfloat16),
-            pltpu.VMEM((rows, width), jnp.bfloat16),
-            pltpu.SemaphoreType.DMA((3,)),
-        ],
         compiler_params=params,
     )(
         query_proj,
         key_proj,
-        value_proj,
         query_gain.reshape(1, width),
         key_gain.reshape(1, width),
         far_blocks,
@@ -237,33 +277,57 @@
         others,
     )
 
-    pairs = {0: pair_pack}
-    key_bits = [1 << bit for bit in range(3, count.bit_length() - 1)] + [1]
-    for mask in key_bits:
-        for held in list(pairs):
-            pairs[held ^ mask] = exchange(pairs[held], mask)
-    key_masks = sorted(pairs)
+    keys = {0: key_norm}
+    for mask in far_bits + [1]:
+        for held in list(keys):
+            keys[held ^ mask] = exchange(keys[held], mask)
     queries = [query_pack] + [exchange(query_pack, mask) for mask in QUERY_MASKS[1:]]
-
-    partial = pl.pallas_call(
-        functools.partial(attention_kernel, key_masks),
+    near = [0, 1]
+    far = [mask for mask in sorted(keys) if mask not in near]
+
+    stacked = len(QUERY_MASKS) * rows
+    context, stats, gates = pl.pallas_call(
+        functools.partial(near_kernel, near),
+        out_shape=[
+            jax.ShapeDtypeStruct((stacked, width), jnp.float32),
+            jax.ShapeDtypeStruct((stacked, HD), jnp.float32),
+            jax.ShapeDtypeStruct((8, width), jnp.float32),
+        ],
+        in_specs=[SMEM] + [VMEM] * (1 + len(QUERY_MASKS) + 2 * len(near)),
+        out_specs=[VMEM] * 3,
+        compiler_params=params,
+        cost_estimate=pl.CostEstimate(
+            flops=4 * stacked * len(near) * rows * width,
+            bytes_accessed=8 * 2**20,
+            transcendentals=0,
+        ),
+    )(
+        frame_step,
+        gate_table,
+        *queries,
+        *[keys[mask] for mask in near],
+        *[values[mask] for mask in near],
+    )
+
+    own, own_logs, *packets = pl.pallas_call(
+        functools.partial(far_kernel, far),
         out_shape=[
             jax.ShapeDtypeStruct((rows, width), jnp.float32),
             jax.ShapeDtypeStruct((8, width), jnp.float32),
         ]
         + [jax.ShapeDtypeStruct((rows + EXTRA, width), jnp.bfloat16)] * 3,
-        in_specs=[VMEM] * (len(QUERY_MASKS) + len(key_masks)),
+        in_specs=[VMEM] * (len(QUERY_MASKS) + 2 * len(far) + 2),
         out_specs=[VMEM] * 5,
         compiler_params=params,
-    )(*queries, *[pairs[mask] for mask in key_masks])
-    own, own_logs, *packets = partial
+    )(
+        *queries,
+        *[keys[mask] for mask in far],
+        *[values[mask] for mask in far],
+        context,
+        stats,
+    )
     packets = [exchange(packet, mask) for packet, mask in zip(packets, QUERY_MASKS[1:])]
 
-    start = lax.axis_index("tm") * rows
-    steps = [frame_step[start // FRAME_TOK], frame_step[(start + rows - 1) // FRAME_TOK]]
-    gates = jnp.concatenate(
-        [lax.dynamic_slice_in_dim(gate_table, step, 1, axis=0) for step in steps], axis=0
-    )
     return pl.pallas_call(
         merge_kernel,
         out_shape=jax.ShapeDtypeStruct((rows, width), jnp.bfloat16),

time: 45.5 us -> 38.1 us (0.84)
  waiting for transfers between devices: 18.8 us -> 13.9 us
  Pallas kernels: 5.59 us -> 10.3 us
  between operations: 3.68 us -> 0.13 us
  local copies, waits for them, and re-layouts: 3.84 us -> 0.72 us
    ppermute x9 -> x12, waiting for transfers between devices: 17.3 us -> 12.3 us  [exchange(): return lax.ppermute(array, 'tm', [(i, i ^ mask) for i in range(count)])]
    pallas_call x1 -> x2, Pallas kernels: 3.32 us -> 7.34 us  [the longest x1 5.99 us: local(): pl.pallas_call(functools.partial(far_kernel, far), out_shape=[jax.ShapeDt...]
    unnamed x14 -> x16, local copies, waits for them, and re-layouts: 2.46 us -> 0.04 us
    ppermute x1, starting transfers between devices: 3.03 us -> 1.58 us  [local(): others = lax.ppermute(sums, 'head', [(0, 1), (1, 0)])]
    dynamic_slice x2 -> x0, local copies, waits for them, and re-layouts: 1.38 us -> none  [the longest x1 0.79 us: local(): lax.dynamic_slice_in_dim(gate_table, step, 1, axis=0)]
    pallas_call x1, Pallas kernels: 0.48 us -> 1.69 us  [local(): pl.pallas_call(sums_kernel, out_shape=jax.ShapeDtypeStruct((2, rows), jnp...]
    ppermute x9 -> x12, starting transfers between devices: 10.3 us -> 11.3 us  [exchange(): return lax.ppermute(array, 'tm', [(i, i ^ mask) for i in range(count)])]
    reshape x1, local copies, waits for them, and re-layouts: 0.01 us -> 0.68 us  [local(): query_gain.reshape(1, width)]
  transfers between devices with their start and end apart: 10 -> 13, of which waited for: 8 -> 6; matrix products, arithmetic and copies ran while one was open for 3% -> 2% of each run, Pallas kernels for 0% -> 9%
where the time goes in v3:
time: 38.1 us; the launch traced here: 37.9 us
  waiting for transfers between devices  13.9 us (36%)
  starting transfers between devices  12.9 us (34%)
  Pallas kernels  10.3 us (27%)
  local copies, waits for them, and re-layouts  0.72 us (2%)
    ppermute x12, waiting for transfers between devices, exchange(): return lax.ppermute(array, 'tm', [(i, i ^ mask) for i in range(count)])  12.3 us
    ppermute x12, starting transfers between devices, exchange(): return lax.ppermute(array, 'tm', [(i, i ^ mask) for i in range(count)])  11.3 us
    pallas_call x1, Pallas kernels, local(): pl.pallas_call(functools.partial(far_kernel, far), out_shape=[jax.ShapeDt...  5.99 us
    pallas_call x1, Pallas kernels, local(): pl.pallas_call(sums_kernel, out_shape=jax.ShapeDtypeStruct((2, rows), jnp...  1.69 us
    ppermute x1, starting transfers between devices, local(): others = lax.ppermute(sums, 'head', [(0, 1), (1, 0)])  1.58 us
    ppermute x1, waiting for transfers between devices, local(): others = lax.ppermute(sums, 'head', [(0, 1), (1, 0)])  1.54 us
    pallas_call x1, Pallas kernels, local(): pl.pallas_call(functools.partial(near_kernel, near), out_shape=[jax.Shape...  1.35 us
    pallas_call x1, Pallas kernels, local(): pl.pallas_call(merge_kernel, out_shape=jax.ShapeDtypeStruct((rows, width)...  1.1 us
  transfers between devices with their start and end apart: 13, of which 6 were waited for; matrix products, arithmetic and copies ran while one was open for 2% of the time, Pallas kernels for 9%

profile of v3, /device:TPU:0, one launch (start us, length us, event | category | flops | bytes accessed | tf_op | source)
XLA Modules:
  0.0 37.9 jit_solution(16522062976771781868)
XLA Ops:
  0.0 0.0 copy-start.1
  0.0 0.0 copy-start
  0.0 4.0 %collective-permute-start.6 = (bf16[128,384]{1,0:T(8,128)(2,1)}, bf16[128,384]{1,0:T(8,128)(2,1)S(1)}, u32[]{:S(2)}, u32[]{:S(2)}) collective-permute-start(bf16[128,384]{1,0:T(8,128)(2,1)} %refs_6_.1), channel_id=1, source_target_pairs={{0,16},{2,18},{4,20},{6,22},{8,24},{10,26},{12,28},{14,30},{16,0},... | collective-permute-start | bytes 294920 | tf_op jit(solution)/shard_map/ppermute | solution.py:227
  4.0 0.0 collective-permute-start.9
  4.0 1.7 %shard_map.82.own_ref = f32[2,128]{1,0:T(2,128)} custom-call(bf16[128,384]{1,0:T(8,128)(2,1)} %query_ref.1, bf16[128,384]{1,0:T(8,128)(2,1)} %key_ref.1), custom_call_target="tpu_custom_call" | custom-call | tf_op jit(solution)/shard_map/pallas_call | solution.py:244
  5.7 0.0 copy-start.7
  5.8 1.6 %collective-permute-start = (f32[2,128]{1,0:T(2,128)}, f32[2,128]{1,0:T(2,128)S(1)}, u32[]{:S(2)}, u32[]{:S(2)}) collective-permute-start(f32[2,128]{1,0:T(2,128)} %shard_map.82.own_ref), channel_id=1, source_target_pairs={{0,1},{1,0},{2,3},{3,2},{4,5},{5,4},{6,7},{7,6},{8,9},{9,8},{10,11... | collective-permute-start | bytes 3080 | tf_op jit(solution)/shard_map/ppermute | solution.py:256
  7.3 0.7 %reshape.6.query_gain_ref = f32[1,384]{1,0:T(1,128)S(1)} reshape(f32[384]{0:T(512)} %param.11) | data formatting | bytes 3072 | tf_op jit(solution)/shard_map/reshape | solution.py:273
  8.0 0.0 copy-done.7
  8.0 0.0 copy-start.4
  8.0 0.0 copy-start.5
  8.0 0.0 copy-start.2
  8.1 0.0 copy-start.3
  8.1 1.5 %collective-permute-done.other_ref = f32[2,128]{1,0:T(2,128)S(1)} collective-permute-done((f32[2,128]{1,0:T(2,128)}, f32[2,128]{1,0:T(2,128)S(1)}, u32[]{:S(2)}, u32[]{:S(2)}) %collective-permute-start) | collective-permute-done | bytes 1056 | tf_op jit(solution)/shard_map/ppermute | solution.py:256
  9.6 0.0 copy-done.1
  9.6 0.0 copy-done
  9.6 0.0 copy-done.4
  9.6 0.0 copy-done.5
  9.6 0.2 shard_map.83
  9.8 0.0 copy-start.6
  9.8 0.1 collective-permute-start.8
  9.9 0.2 collective-permute-start.4
  10.1 2.8 %collective-permute-start.3 = (bf16[144,384]{1,0:T(8,128)(2,1)S(1)}, bf16[144,384]{1,0:T(8,128)(2,1)S(1)}, u32[]{:S(2)}, u32[]{:S(2)}) collective-permute-start(bf16[144,384]{1,0:T(8,128)(2,1)S(1)} %get-tuple-element.15.refs_0_), channel_id=1, source_target_pairs={{0,12},{2,14},{4,8},{6,10},{8,4},{10,6},{12,0},{14,2},{16,28},{18,... | collective-permute-start | bytes 331784 | tf_op jit(solution)/shard_map/ppermute | solution.py:227
  12.8 0.0 collective-permute-done.6.refs_6_
  12.8 0.5 %collective-permute-start.2 = (bf16[144,384]{1,0:T(8,128)(2,1)S(1)}, bf16[144,384]{1,0:T(8,128)(2,1)S(1)}, u32[]{:S(2)}, u32[]{:S(2)}) collective-permute-start(bf16[144,384]{1,0:T(8,128)(2,1)S(1)} %get-tuple-element.15.refs_0_), channel_id=1, source_target_pairs={{0,8},{2,10},{4,12},{6,14},{8,0},{10,2},{12,4},{14,6},{16,24},{18,... | collective-permute-start | bytes 331784 | tf_op jit(solution)/shard_map/ppermute | solution.py:227
  13.3 0.0 collective-permute-done.9.refs_7_
  13.3 0.3 collective-permute-start.1
  13.6 0.0 collective-permute-done.8.refs_5_
  13.6 0.0 collective-permute-start.7
  13.6 4.7 %collective-permute-done.4.refs_4_ = bf16[128,384]{1,0:T(8,128)(2,1)S(1)} collective-permute-done((bf16[128,384]{1,0:T(8,128)(2,1)S(1)}, bf16[128,384]{1,0:T(8,128)(2,1)S(1)}, u32[]{:S(2)}, u32[]{:S(2)}) %collective-permute-start.4) | collective-permute-done | bytes 98336 | tf_op jit(solution)/shard_map/ppermute | solution.py:227
  18.2 0.0 collective-permute-start.5
  18.2 0.0 collective-permute-done.3.refs_3_
  18.2 2.6 %collective-permute-done.2.refs_2_ = bf16[144,384]{1,0:T(8,128)(2,1)S(1)} collective-permute-done((bf16[144,384]{1,0:T(8,128)(2,1)S(1)}, bf16[144,384]{1,0:T(8,128)(2,1)S(1)}, u32[]{:S(2)}, u32[]{:S(2)}) %collective-permute-start.2) | collective-permute-done | bytes 110624 | tf_op jit(solution)/shard_map/ppermute | solution.py:227
  20.8 0.0 collective-permute-done.1.refs_1_
  20.8 0.0 copy-done.2
  20.8 0.0 copy-done.3
  20.8 0.0 copy-done.6
  20.8 1.3 %shard_map.84 = (f32[512,384]{1,0:T(8,128)S(1)}, f32[512,128]{1,0:T(8,128)S(1)}, f32[8,384]{1,0:T(8,128)S(1)}) custom-call(s32[2]{0:T(128)S(1)} %copy-done.6, f32[50,384]{1,0:T(8,128)S(1)} %copy-done.3, bf16[144,384]{1,0:T(8,128)(2,1)S(1)} %get-tuple-element.15.refs_0_, bf16[144,384]{1,0:T(8,128)(2,1)S(1)} %collective-permute-done.1.refs_1_, ...), custom_call_target="tpu_custom_call" | custom-call | flops 201326592 | bytes 8388608 | tf_op jit(solution)/shard_map/pallas_call | solution.py:289
  22.2 0.0 collective-permute-done.7.refs_7_
  22.2 0.0 collective-permute-done.5.refs_5_
  22.2 6.0 %shard_map.85 = (f32[128,384]{1,0:T(8,128)S(1)}, f32[8,384]{1,0:T(8,128)S(1)}, bf16[144,384]{1,0:T(8,128)(2,1)S(1)}, bf16[144,384]{1,0:T(8,128)(2,1)S(1)}, bf16[144,384]{1,0:T(8,128)(2,1)S(1)}) custom-call(bf16[144,384]{1,0:T(8,128)(2,1)S(1)} %get-tuple-element.15.refs_0_, bf16[144,384]{1,0:T(8,128)(2,1)S(1)} %collective-permute-done.1.refs_1_, ...), custom_call_target="tpu_custom_call" | custom-call | tf_op jit(solution)/shard_map/pallas_call | solution.py:312
  28.2 0.6 %collective-permute-start.10 = (bf16[144,384]{1,0:T(8,128)(2,1)S(1)}, bf16[144,384]{1,0:T(8,128)(2,1)S(1)}, u32[]{:S(2)}, u32[]{:S(2)}) collective-permute-start(bf16[144,384]{1,0:T(8,128)(2,1)S(1)} %get-tuple-element.21), channel_id=1, source_target_pairs={{0,4},{2,6},{4,0},{6,2},{8,12},{10,14},{12,8},{14,10},{16,20},{18,... | collective-permute-start | bytes 331784 | tf_op jit(solution)/shard_map/ppermute | solution.py:227
  28.8 0.5 %collective-permute-start.11 = (bf16[144,384]{1,0:T(8,128)(2,1)S(1)}, bf16[144,384]{1,0:T(8,128)(2,1)S(1)}, u32[]{:S(2)}, u32[]{:S(2)}) collective-permute-start(bf16[144,384]{1,0:T(8,128)(2,1)S(1)} %get-tuple-element.22), channel_id=1, source_target_pairs={{0,8},{2,10},{4,12},{6,14},{8,0},{10,2},{12,4},{14,6},{16,24},{18,... | collective-permute-start | bytes 331784 | tf_op jit(solution)/shard_map/ppermute | solution.py:227
  29.2 2.5 %collective-permute-start.12 = (bf16[144,384]{1,0:T(8,128)(2,1)S(1)}, bf16[144,384]{1,0:T(8,128)(2,1)S(1)}, u32[]{:S(2)}, u32[]{:S(2)}) collective-permute-start(bf16[144,384]{1,0:T(8,128)(2,1)S(1)} %get-tuple-element.23), channel_id=1, source_target_pairs={{0,12},{2,14},{4,8},{6,10},{8,4},{10,6},{12,0},{14,2},{16,28},{18,... | collective-permute-start | bytes 331784 | tf_op jit(solution)/shard_map/ppermute | solution.py:227
  31.8 1.5 %collective-permute-done.10.refs_0_ = bf16[144,384]{1,0:T(8,128)(2,1)S(1)} collective-permute-done((bf16[144,384]{1,0:T(8,128)(2,1)S(1)}, bf16[144,384]{1,0:T(8,128)(2,1)S(1)}, u32[]{:S(2)}, u32[]{:S(2)}) %collective-permute-start.10) | collective-permute-done | bytes 110624 | tf_op jit(solution)/shard_map/ppermute | solution.py:227
  33.3 1.3 %collective-permute-done.11.refs_1_ = bf16[144,384]{1,0:T(8,128)(2,1)S(1)} collective-permute-done((bf16[144,384]{1,0:T(8,128)(2,1)S(1)}, bf16[144,384]{1,0:T(8,128)(2,1)S(1)}, u32[]{:S(2)}, u32[]{:S(2)}) %collective-permute-start.11) | collective-permute-done | bytes 110624 | tf_op jit(solution)/shard_map/ppermute | solution.py:227
  34.5 2.3 %collective-permute-done.12.refs_2_ = bf16[144,384]{1,0:T(8,128)(2,1)S(1)} collective-permute-done((bf16[144,384]{1,0:T(8,128)(2,1)S(1)}, bf16[144,384]{1,0:T(8,128)(2,1)S(1)}, u32[]{:S(2)}, u32[]{:S(2)}) %collective-permute-start.12) | collective-permute-done | bytes 110624 | tf_op jit(solution)/shard_map/ppermute | solution.py:227
  36.8 1.1 %shard_map.86 = bf16[128,384]{1,0:T(8,128)(2,1)} custom-call(f32[128,384]{1,0:T(8,128)S(1)} %get-tuple-element.19.own_ref, f32[8,384]{1,0:T(8,128)S(1)} %get-tuple-element.20.sums_ref, bf16[144,384]{1,0:T(8,128)(2,1)S(1)} %collective-permute-done.10.refs_0_, bf16[144,384]{1,0:T(8,128)(2,1)S(1)} %collective-permute-done.11.refs_1_, ...), custom_call_target="tpu_custom_call" | custom-call | tf_op jit(solution)/shard_map/pallas_call | solution.py:331
  (1 shorter events, 0.0 us)
Async XLA Ops:
  0.0 9.6 %copy-start.1 = (bf16[128,384]{1,0:T(8,128)(2,1)S(1)}, bf16[128,384]{1,0:T(8,128)(2,1)}, u32[]{:S(2)}) copy-start(bf16[128,384]{1,0:T(8,128)(2,1)} %key_ref.1) | copy-start | bytes 294916
  0.0 9.6 %copy-start = (bf16[128,384]{1,0:T(8,128)(2,1)S(1)}, bf16[128,384]{1,0:T(8,128)(2,1)}, u32[]{:S(2)}) copy-start(bf16[128,384]{1,0:T(8,128)(2,1)} %query_ref.1) | copy-start | bytes 294916
  0.0 12.8 %collective-permute-start.6 = (bf16[128,384]{1,0:T(8,128)(2,1)}, bf16[128,384]{1,0:T(8,128)(2,1)S(1)}, u32[]{:S(2)}, u32[]{:S(2)}) collective-permute-start(bf16[128,384]{1,0:T(8,128)(2,1)} %refs_6_.1), channel_id=1, source_target_pairs={{0,16},{2,18},{4,20},{6,22},{8,24},{10,26},{12,28},{14,30},{16,0},... | collective-permute-start | bytes 294920 | tf_op jit(solution)/shard_map/ppermute | solution.py:227
  4.0 9.2 %collective-permute-start.9 = (bf16[128,384]{1,0:T(8,128)(2,1)}, bf16[128,384]{1,0:T(8,128)(2,1)S(1)}, u32[]{:S(2)}, u32[]{:S(2)}) collective-permute-start(bf16[128,384]{1,0:T(8,128)(2,1)} %refs_6_.1), channel_id=1, source_target_pairs={{0,2},{2,0},{4,6},{6,4},{8,10},{10,8},{12,14},{14,12},{16,18},{18,... | collective-permute-start | bytes 294920 | tf_op jit(solution)/shard_map/ppermute | solution.py:227
  5.7 2.3 %copy-start.7 = (f32[384]{0:T(512)S(1)}, f32[384]{0:T(512)}, u32[]{:S(2)}) copy-start(f32[384]{0:T(512)} %param.12) | copy-start | bytes 4612
  5.8 3.8 %collective-permute-start = (f32[2,128]{1,0:T(2,128)}, f32[2,128]{1,0:T(2,128)S(1)}, u32[]{:S(2)}, u32[]{:S(2)}) collective-permute-start(f32[2,128]{1,0:T(2,128)} %shard_map.82.own_ref), channel_id=1, source_target_pairs={{0,1},{1,0},{2,3},{3,2},{4,5},{5,4},{6,7},{7,6},{8,9},{9,8},{10,11... | collective-permute-start | bytes 3080 | tf_op jit(solution)/shard_map/ppermute | solution.py:256
  8.0 1.6 %copy-start.4 = (f32[2,128]{1,0:T(2,128)S(1)}, f32[2,128]{1,0:T(2,128)}, u32[]{:S(2)}) copy-start(f32[2,128]{1,0:T(2,128)} %shard_map.82.own_ref) | copy-start | bytes 3076
  8.0 1.6 %copy-start.5 = (s32[1,16]{1,0:T(1,128)S(1)}, s32[1,16]{1,0:T(1,128)}, u32[]{:S(2)}) copy-start(s32[1,16]{1,0:T(1,128)} %far_ref.1) | copy-start | bytes 196
  8.0 12.8 %copy-start.2 = (bf16[128,384]{1,0:T(8,128)(2,1)S(1)}, bf16[128,384]{1,0:T(8,128)(2,1)}, u32[]{:S(2)}) copy-start(bf16[128,384]{1,0:T(8,128)(2,1)} %refs_6_.1) | copy-start | bytes 294916
  8.1 12.8 %copy-start.3 = (f32[50,384]{1,0:T(8,128)S(1)}, f32[50,384]{1,0:T(8,128)}, u32[]{:S(2)}) copy-start(f32[50,384]{1,0:T(8,128)} %gate_ref.1) | copy-start | bytes 230404
  9.8 11.0 %copy-start.6 = (s32[2]{0:T(128)S(1)}, s32[2]{0:T(128)}, u32[]{:S(2)}) copy-start(s32[2]{0:T(128)} %step_ref.1) | copy-start | bytes 28
  9.8 3.7 %collective-permute-start.8 = (bf16[128,384]{1,0:T(8,128)(2,1)S(1)}, bf16[128,384]{1,0:T(8,128)(2,1)S(1)}, u32[]{:S(2)}, u32[]{:S(2)}) collective-permute-start(bf16[128,384]{1,0:T(8,128)(2,1)S(1)} %get-tuple-element.16.refs_4_), channel_id=1, source_target_pairs={{0,2},{2,0},{4,6},{6,4},{8,10},{10,8},{12,14},{14,12},{16,18},{18,... | collective-permute-start | bytes 294920 | tf_op jit(solution)/shard_map/ppermute | solution.py:227
  9.9 8.3 %collective-permute-start.4 = (bf16[128,384]{1,0:T(8,128)(2,1)S(1)}, bf16[128,384]{1,0:T(8,128)(2,1)S(1)}, u32[]{:S(2)}, u32[]{:S(2)}) collective-permute-start(bf16[128,384]{1,0:T(8,128)(2,1)S(1)} %get-tuple-element.16.refs_4_), channel_id=1, source_target_pairs={{0,16},{2,18},{4,20},{6,22},{8,24},{10,26},{12,28},{14,30},{16,0},... | collective-permute-start | bytes 294920 | tf_op jit(solution)/shard_map/ppermute | solution.py:227
  10.1 8.2 %collective-permute-start.3 = (bf16[144,384]{1,0:T(8,128)(2,1)S(1)}, bf16[144,384]{1,0:T(8,128)(2,1)S(1)}, u32[]{:S(2)}, u32[]{:S(2)}) collective-permute-start(bf16[144,384]{1,0:T(8,128)(2,1)S(1)} %get-tuple-element.15.refs_0_), channel_id=1, source_target_pairs={{0,12},{2,14},{4,8},{6,10},{8,4},{10,6},{12,0},{14,2},{16,28},{18,... | collective-permute-start | bytes 331784 | tf_op jit(solution)/shard_map/ppermute | solution.py:227
  12.8 8.0 %collective-permute-start.2 = (bf16[144,384]{1,0:T(8,128)(2,1)S(1)}, bf16[144,384]{1,0:T(8,128)(2,1)S(1)}, u32[]{:S(2)}, u32[]{:S(2)}) collective-permute-start(bf16[144,384]{1,0:T(8,128)(2,1)S(1)} %get-tuple-element.15.refs_0_), channel_id=1, source_target_pairs={{0,8},{2,10},{4,12},{6,14},{8,0},{10,2},{12,4},{14,6},{16,24},{18,... | collective-permute-start | bytes 331784 | tf_op jit(solution)/shard_map/ppermute | solution.py:227
  13.3 7.5 %collective-permute-start.1 = (bf16[144,384]{1,0:T(8,128)(2,1)S(1)}, bf16[144,384]{1,0:T(8,128)(2,1)S(1)}, u32[]{:S(2)}, u32[]{:S(2)}) collective-permute-start(bf16[144,384]{1,0:T(8,128)(2,1)S(1)} %get-tuple-element.15.refs_0_), channel_id=1, source_target_pairs={{0,4},{2,6},{4,0},{6,2},{8,12},{10,14},{12,8},{14,10},{16,20},{18,... | collective-permute-start | bytes 331784 | tf_op jit(solution)/shard_map/ppermute | solution.py:227
  13.6 8.6 %collective-permute-start.7 = (bf16[128,384]{1,0:T(8,128)(2,1)S(1)}, bf16[128,384]{1,0:T(8,128)(2,1)S(1)}, u32[]{:S(2)}, u32[]{:S(2)}) collective-permute-start(bf16[128,384]{1,0:T(8,128)(2,1)S(1)} %collective-permute-done.6.refs_6_), channel_id=1, source_target_pairs={{0,2},{2,0},{4,6},{6,4},{8,10},{10,8},{12,14},{14,12},{16,18},{18,... | collective-permute-start | bytes 294920 | tf_op jit(solution)/shard_map/ppermute | solution.py:227
  18.2 4.0 %collective-permute-start.5 = (bf16[128,384]{1,0:T(8,128)(2,1)S(1)}, bf16[128,384]{1,0:T(8,128)(2,1)S(1)}, u32[]{:S(2)}, u32[]{:S(2)}) collective-permute-start(bf16[128,384]{1,0:T(8,128)(2,1)S(1)} %collective-permute-done.4.refs_4_), channel_id=1, source_target_pairs={{0,2},{2,0},{4,6},{6,4},{8,10},{10,8},{12,14},{14,12},{16,18},{18,... | collective-permute-start | bytes 294920 | tf_op jit(solution)/shard_map/ppermute | solution.py:227
  28.2 5.1 %collective-permute-start.10 = (bf16[144,384]{1,0:T(8,128)(2,1)S(1)}, bf16[144,384]{1,0:T(8,128)(2,1)S(1)}, u32[]{:S(2)}, u32[]{:S(2)}) collective-permute-start(bf16[144,384]{1,0:T(8,128)(2,1)S(1)} %get-tuple-element.21), channel_id=1, source_target_pairs={{0,4},{2,6},{4,0},{6,2},{8,12},{10,14},{12,8},{14,10},{16,20},{18,... | collective-permute-start | bytes 331784 | tf_op jit(solution)/shard_map/ppermute | solution.py:227
  28.8 5.8 %collective-permute-start.11 = (bf16[144,384]{1,0:T(8,128)(2,1)S(1)}, bf16[144,384]{1,0:T(8,128)(2,1)S(1)}, u32[]{:S(2)}, u32[]{:S(2)}) collective-permute-start(bf16[144,384]{1,0:T(8,128)(2,1)S(1)} %get-tuple-element.22), channel_id=1, source_target_pairs={{0,8},{2,10},{4,12},{6,14},{8,0},{10,2},{12,4},{14,6},{16,24},{18,... | collective-permute-start | bytes 331784 | tf_op jit(solution)/shard_map/ppermute | solution.py:227
  29.2 7.6 %collective-permute-start.12 = (bf16[144,384]{1,0:T(8,128)(2,1)S(1)}, bf16[144,384]{1,0:T(8,128)(2,1)S(1)}, u32[]{:S(2)}, u32[]{:S(2)}) collective-permute-start(bf16[144,384]{1,0:T(8,128)(2,1)S(1)} %get-tuple-element.23), channel_id=1, source_target_pairs={{0,12},{2,14},{4,8},{6,10},{8,4},{10,6},{12,0},{14,2},{16,28},{18,... | collective-permute-start | bytes 331784 | tf_op jit(solution)/shard_map/ppermute | solution.py:227

commit v4 on v0

v4 whole, which is shorter than its diff:
```python
import functools

import jax
import jax.numpy as jnp
from jax import lax
from jax.experimental import pallas as pl
from jax.experimental.pallas import tpu as pltpu
from jax.sharding import PartitionSpec as P

HD = 128
BLK = 64
FRAME_TOK = 1560
EPSILON = 1e-06
LOG2E = 1.4426950408889634
SCALE = HD ** (-0.5) * LOG2E
MASKED = -1e30
EXTRA = 16
ANY = pl.BlockSpec(memory_space=pl.ANY)
VMEM = pl.BlockSpec(memory_space=pltpu.VMEM)
SMEM = pl.BlockSpec(memory_space=pltpu.SMEM)


def spread(row):
    return jnp.broadcast_to(row, (row.shape[1], row.shape[1])).T


def squares(source_ref):
    wide = source_ref[...].astype(jnp.float32)
    square = wide * wide
    part = square[:, :HD]
    for low in range(HD, square.shape[1], HD):
        part = part + square[:, low : low + HD]
    return jnp.sum(part.T, axis=0, keepdims=True)


def own_sums_kernel(query_hbm, key_hbm, out_ref, query_ref, key_ref, sems):
    copies = [
        pltpu.make_async_copy(query_hbm, query_ref, sems.at[0]),
        pltpu.make_async_copy(key_hbm, key_ref, sems.at[1]),
    ]
    for copy in copies:
        copy.start()
    out_ref[...] = jnp.zeros_like(out_ref)
    for place, ref in enumerate((query_ref, key_ref)):
        copies[place].wait()
        out_ref[place : place + 1, :] = squares(ref)


def sums_kernel(own_ref, *refs):
    *sources, out_ref = refs
    out_ref[...] = jnp.zeros_like(out_ref)
    out_ref[0:2, :] = own_ref[0:2, :]
    for place, source_ref in enumerate(sources, start=2):
        out_ref[place : place + 1, :] = squares(source_ref)


def normed(source_ref, own_ref, other_ref, line, gain_ref, full_width):
    total = own_ref[line : line + 1, :] + other_ref[line : line + 1, :]
    factor = spread(lax.rsqrt(total / full_width + EPSILON))
    parts = []
    for low in range(0, source_ref.shape[1], HD):
        wide = source_ref[:, low : low + HD].astype(jnp.float32)
        parts.append((wide * factor * gain_ref[:, low : low + HD]).astype(jnp.bfloat16))
    return jnp.concatenate(parts, axis=1)


def pack_kernel(full_width, held, gain_ref, own_ref, other_ref, *refs):
    keys, values, pack_out = refs[:held], refs[held : 2 * held], refs[2 * held]
    rows = keys[0].shape[0]
    for place, key_ref in enumerate(keys):
        pack_out[place * rows : (place + 1) * rows, :] = normed(
            key_ref, own_ref, other_ref, 1 + place + (place > 0), gain_ref, full_width
        )
    for place, value_ref in enumerate(values, start=held):
        pack_out[place * rows : (place + 1) * rows, :] = value_ref[...]


def key_bias(far_ref, query_mask, key_masks):
    me = lax.axis_index("tm")
    lane = lax.broadcasted_iota(jnp.int32, (1, HD), 1)
    half = (lane >= BLK).astype(jnp.float32)
    far = far_ref[...].astype(jnp.float32)
    far = jnp.concatenate([far, jnp.full((1, HD - far.shape[1]), -1.0)], axis=1)
    parts = []
    for key_mask in key_masks:
        query_id, key_id = me ^ query_mask, me ^ key_mask
        choice = jnp.sum(jnp.where(lane == key_id, far, 0.0), axis=1, keepdims=True)
        taken = (choice == half) | (jnp.abs(query_id - key_id) <= 1)
        parts.append(jnp.where(taken, 0.0, MASKED))
    return jnp.concatenate(parts, axis=1)


def columns_of(pack, second, low, high):
    half = pack.shape[0] // 2
    return pack[half * second : half * (second + 1), low:high]


def absorb(query, keys, values, bias, old):
    rows = query.shape[0]
    logits = (
        lax.dot_general(
            query, keys, (((1,), (1,)), ((), ())), preferred_element_type=jnp.float32
        )
        * SCALE
        + bias
    )
    top = jnp.broadcast_to(jnp.max(logits, axis=1, keepdims=True), (rows, HD))
    if old is not None:
        top = jnp.maximum(top, old[0])
    weights = [
        jnp.exp2(logits[:, left : left + HD] - top) for left in range(0, logits.shape[1], HD)
    ]
    total = jnp.sum(functools.reduce(jnp.add, weights), axis=1, keepdims=True)
    total = jnp.broadcast_to(total, (rows, HD))
    context = jnp.dot(
        jnp.concatenate([weight.astype(jnp.bfloat16) for weight in weights], axis=1),
        values,
        preferred_element_type=jnp.float32,
    )
    if old is not None:
        fade = jnp.exp2(old[0] - top)
        total = total + old[1] * fade
        context = context + old[2] * fade
    return top, total, context


def own_attention(full_width, query_masks, key_masks, gain_ref, own_ref, other_ref, *refs):
    queries, far, pack = refs[:2], refs[2:4], refs[4]
    query_out, context_out, stats_out = refs[5:]
    rows, width = queries[0].shape
    for place, mask in enumerate(query_masks):
        part = slice(place * rows, (place + 1) * rows)
        bias = key_bias(far[place], mask, key_masks)
        query = normed(queries[place], own_ref, other_ref, 2 * place, gain_ref, full_width)
        query_out[part, :] = query
        for low in range(0, width, HD):
            high, wide = low + HD, 2 * low
            top, total, context = absorb(
                query[:, low:high],
                columns_of(pack, 0, low, high),
                columns_of(pack, 1, low, high),
                bias,
                None,
            )
            context_out[part, low:high] = context
            stats_out[part, wide : wide + HD] = top
            stats_out[part, wide + HD : wide + 2 * HD] = total


def last_attention(place, query_mask, key_masks, query_ref, far_ref, *refs):
    pack, context_ref, stats_ref, *outs = refs
    rows, width = query_ref.shape[0] // 2, query_ref.shape[1]
    heads = width // HD
    part = slice(place * rows, (place + 1) * rows)
    bias = key_bias(far_ref, query_mask, key_masks)
    lane = lax.broadcasted_iota(jnp.int32, (1, HD), 1)
    logs = jnp.zeros((rows, HD), jnp.float32)
    for head in range(heads):
        low, high = head * HD, (head + 1) * HD
        wide = 2 * low
        top, total, context = absorb(
            query_ref[part, low:high],
            columns_of(pack, 0, low, high),
            columns_of(pack, 1, low, high),
            bias,
            (
                stats_ref[part, wide : wide + HD],
                stats_ref[part, wide + HD : wide + 2 * HD],
                context_ref[part, low:high],
            ),
        )
        outs[0][:rows, low:high] = (context * (1.0 / total)).astype(outs[0].dtype)
        logs = jnp.where(lane == head, top + jnp.log2(total), logs)
    lines = logs.T
    sub = lax.broadcasted_iota(jnp.int32, (EXTRA, HD), 0)
    for head in range(heads):
        low, high = head * HD, (head + 1) * HD
        value = lines[head : head + 1, :]
        if place == 0:
            outs[1][:, low:high] = jnp.broadcast_to(value, (8, HD))
        else:
            first = value.astype(jnp.bfloat16).astype(jnp.float32)
            second = (value - first).astype(jnp.bfloat16).astype(jnp.float32)
            third = value - first - second
            outs[0][rows:, low:high] = jnp.where(
                sub == 0, first, jnp.where(sub == 1, second, third)
            ).astype(jnp.bfloat16)


def gate_kernel(step_ref, table_ref, out_ref):
    rows = out_ref.shape[0] // 2
    start = lax.axis_index("tm") * HD
    first = step_ref[start // FRAME_TOK]
    last = step_ref[(start + HD - 1) // FRAME_TOK]
    out_ref[:rows, :] = jnp.broadcast_to(table_ref[pl.ds(first, 1), :], (rows, out_ref.shape[1]))
    out_ref[rows:, :] = jnp.broadcast_to(table_ref[pl.ds(last, 1), :], (rows, out_ref.shape[1]))


def merge_kernel(own_ref, logs_ref, packet_ref, gate_ref, out_ref):
    rows, width = own_ref.shape
    pieces = packet_ref[rows:, :].astype(jnp.float32)
    other = pieces[0:1] + pieces[1:2] + pieces[2:3]
    top = jnp.maximum(logs_ref[:1, :], other)
    own_weight = jnp.exp2(logs_ref[:1, :] - top)
    other_weight = jnp.exp2(other - top)
    share = own_weight / (own_weight + other_weight)
    start = lax.axis_index("tm") * rows
    first_rows = (start // FRAME_TOK + 1) * FRAME_TOK - start
    row_ids = lax.broadcasted_iota(jnp.int32, (rows, 1), 0)
    for low in range(0, width, HD):
        high = low + HD
        column = spread(share[:, low:high])
        other_part = packet_ref[:rows, low:high].astype(jnp.float32)
        context = own_ref[:, low:high] * column + other_part * (1.0 - column)
        gate = jnp.where(
            row_ids < first_rows, gate_ref[0:1, low:high], gate_ref[8:9, low:high]
        )
        out_ref[:, low:high] = (context * gate).astype(jnp.bfloat16)


def exchange(array, mask):
    count = lax.axis_size("tm")
    return lax.ppermute(array, "tm", [(i, i ^ mask) for i in range(count)])


def gathered(array, bits):
    held = {0: array}
    for bit in bits:
        for mask in list(held):
            held[mask ^ bit] = exchange(held[mask], bit)
    return held


def local(
    query_proj, key_proj, value_proj, query_gain, key_gain, gate_table, frame_step, far_blocks
):
    rows, width = query_proj.shape
    count = lax.axis_size("tm")
    splits = lax.axis_size("head")
    full_width = width * splits
    params = pltpu.CompilerParams(vmem_limit_bytes=(8 + count // 2) * 2**20)
    bits = [1 << place for place in range(1, count.bit_length() - 2)]
    query_mask = count // 2
    query_gain = query_gain.reshape(1, width)
    key_gain = key_gain.reshape(1, width)

    keys = gathered(key_proj, bits[::-1])
    values = gathered(value_proj, bits)
    queries = [query_proj, exchange(query_proj, query_mask)]
    far = [far_blocks, exchange(far_blocks, query_mask)]
    masks = sorted(keys, key=lambda mask: (mask.bit_count(), mask))

    own_sums = pl.pallas_call(
        own_sums_kernel,
        out_shape=jax.ShapeDtypeStruct((8, rows), jnp.float32),
        in_specs=[ANY, ANY],
        out_specs=VMEM,
        scratch_shapes=[
            pltpu.VMEM((rows, width), jnp.bfloat16),
            pltpu.VMEM((rows, width), jnp.bfloat16),
            pltpu.SemaphoreType.DMA((2,)),
        ],
    )(query_proj, key_proj)
    sources = queries[1:] + [keys[mask] for mask in masks[1:]]
    lines = len(sources) + 2
    sums = pl.pallas_call(
        sums_kernel,
        out_shape=jax.ShapeDtypeStruct((lines + -lines % 8, rows), jnp.float32),
        in_specs=[VMEM] * (1 + len(sources)),
        out_specs=VMEM,
        compiler_params=params,
    )(own_sums, *sources)
    if splits == 2:
        others = lax.ppermute(sums, "head", [(0, 1), (1, 0)])
    else:
        sums = lax.psum(sums, "head")
        others = jnp.zeros_like(sums)

    pack = pl.pallas_call(
        functools.partial(pack_kernel, full_width, len(masks)),
        out_shape=jax.ShapeDtypeStruct((2 * len(masks) * rows, width), jnp.bfloat16),
        in_specs=[VMEM] * (3 + 2 * len(masks)),
        out_specs=VMEM,
        compiler_params=params,
    )(
        key_gain,
        sums,
        others,
        *[keys[mask] for mask in masks],
        *[values[mask] for mask in masks],
    )
    other_pack = exchange(pack, 1)

    query_norm, context, stats = pl.pallas_call(
        functools.partial(own_attention, full_width, [0, query_mask], masks),
        out_shape=[
            jax.ShapeDtypeStruct((2 * rows, width), jnp.bfloat16),
            jax.ShapeDtypeStruct((2 * rows, width), jnp.float32),
            jax.ShapeDtypeStruct((2 * rows, 2 * width), jnp.float32),
        ],
        in_specs=[VMEM] * 8,
        out_specs=[VMEM] * 3,
        compiler_params=params,
    )(query_gain, sums, others, *queries, *far, pack)

    def last_part(place, out_shape):
        return pl.pallas_call(
            functools.partial(
                last_attention, place, place * query_mask, [mask ^ 1 for mask in masks]
            ),
            out_shape=out_shape,
            in_specs=[VMEM] * 5,
            out_specs=[VMEM] * len(out_shape),
            compiler_params=params,
        )(query_norm, far[place], other_pack, context, stats)

    (packet,) = last_part(1, [jax.ShapeDtypeStruct((rows + EXTRA, width), jnp.bfloat16)])
    own, own_logs = last_part(
        0,
        [
            jax.ShapeDtypeStruct((rows, width), jnp.float32),
            jax.ShapeDtypeStruct((8, width), jnp.float32),
        ],
    )
    gates = pl.pallas_call(
        gate_kernel,
        out_shape=jax.ShapeDtypeStruct((16, width), jnp.float32),
        in_specs=[SMEM, VMEM],
        out_specs=VMEM,
        compiler_params=params,
    )(frame_step, gate_table)
    packet = exchange(packet, query_mask)

    return pl.pallas_call(
        merge_kernel,
        out_shape=jax.ShapeDtypeStruct((rows, width), jnp.bfloat16),
        in_specs=[VMEM] * 4,
        out_specs=VMEM,
        compiler_params=params,
    )(own, own_logs, packet, gates)


def solution(mesh):
    return jax.shard_map(
        local,
        mesh=mesh,
        in_specs=(
            P("tm", "head"),
            P("tm", "head"),
            P("tm", "head"),
            P("head"),
            P("head"),
            P(None, "head"),
            P(),
            P("tm", None),
        ),
        out_specs=P("tm", "head"),
        check_vma=False,
    )
```

time: 80.6 us -> 33.5 us (0.42)
  waiting for transfers between devices: 37.8 us -> 8.41 us
  Pallas kernels: 0 us -> 7.16 us
  other arithmetic: 6.33 us -> 0 us
  blocking collectives: 5.91 us -> 0 us
  matrix products: 5.71 us -> 0 us
  local copies, waits for them, and re-layouts: 3.85 us -> 0.77 us
  starting transfers between devices: 19.9 us -> 16.9 us
    all_to_all x3 -> x0, waiting for transfers between devices: 37.8 us -> none  [the longest x1 16.5 us: local(): lax.all_to_all(send_keys, 'tm', split_axis=0, concat_axis=0, tiled=True)]
    all_to_all x3 -> x0, starting transfers between devices: 15.6 us -> none  [the longest x1 6.43 us: local(): lax.all_to_all(far_blocks, 'tm', split_axis=1, concat_axis=0, tiled=True)]
    ppermute x2 -> x11, starting transfers between devices: 4.33 us -> 16.9 us  [the longest x10 15.3 us: exchange(): return lax.ppermute(array, 'tm', [(i, i ^ mask) for i in range(count)])]
    ppermute x2 -> x11, waiting for transfers between devices: 0.01 us -> 8.41 us  [the longest x10 6.85 us: exchange(): return lax.ppermute(array, 'tm', [(i, i ^ mask) for i in range(count)])]
    pallas_call x0 -> x8, Pallas kernels: none -> 7.16 us  [the longest x2 1.95 us: last_part(): pl.pallas_call(functools.partial(last_attention, place, place * query_mas...]
    psum x1 -> x0, blocking collectives: 5.91 us -> none  [local(): lax.psum((jnp.sum(query_f * query_f, axis=-1), jnp.sum(key_f * key_f, axi...]
    dot_general x7 -> x0, matrix products: 5.71 us -> none  [the longest x3 2.56 us: softmax_update(): lax.dot_general(query_part, key_part, (((1,), (1,)), ((), ())), preferred...]
    reduce_sum x5 -> x0, other arithmetic: 1.95 us -> none  [the longest x1 1.11 us: local(): jnp.sum(query_f * query_f, axis=-1)]
  transfers between devices with their start and end apart: 5 -> 11, of which waited for: 3 -> 4; matrix products, arithmetic and copies ran while one was open for 12% -> 0% of each run, Pallas kernels for 0% -> 16%
where the time goes in v4:
time: 33.5 us; the launch traced here: 33.4 us
  starting transfers between devices  16.9 us (50%)
  waiting for transfers between devices  8.41 us (25%)
  Pallas kernels  7.16 us (21%)
  local copies, waits for them, and re-layouts  0.77 us (2%)
    ppermute x10, starting transfers between devices, exchange(): return lax.ppermute(array, 'tm', [(i, i ^ mask) for i in range(count)])  15.3 us
    ppermute x10, waiting for transfers between devices, exchange(): return lax.ppermute(array, 'tm', [(i, i ^ mask) for i in range(count)])  6.85 us
    pallas_call x2, Pallas kernels, last_part(): pl.pallas_call(functools.partial(last_attention, place, place * query_mas...  1.95 us
    pallas_call x1, Pallas kernels, local(): pl.pallas_call(functools.partial(own_attention, full_width, [0, query_mas...  1.76 us
    pallas_call x1, Pallas kernels, local(): pl.pallas_call(own_sums_kernel, out_shape=jax.ShapeDtypeStruct((8, rows),...  1.74 us
    ppermute x1, starting transfers between devices, local(): others = lax.ppermute(sums, 'head', [(0, 1), (1, 0)])  1.58 us
    ppermute x1, waiting for transfers between devices, local(): others = lax.ppermute(sums, 'head', [(0, 1), (1, 0)])  1.56 us
    pallas_call x1, Pallas kernels, local(): pl.pallas_call(merge_kernel, out_shape=jax.ShapeDtypeStruct((rows, width)...  0.81 us
  transfers between devices with their start and end apart: 11, of which 4 were waited for; matrix products, arithmetic and copies ran while one was open for 0% of the time, Pallas kernels for 16%

profile of v4, /device:TPU:0, one launch (start us, length us, event | category | flops | bytes accessed | tf_op | source)
XLA Modules:
  0.0 33.4 jit_solution(16827336703688168511)
XLA Ops:
  0.0 3.0 %collective-permute-start.2 = (bf16[128,384]{1,0:T(8,128)(2,1)}, bf16[128,384]{1,0:T(8,128)(2,1)S(1)}, u32[]{:S(2)}, u32[]{:S(2)}) collective-permute-start(bf16[128,384]{1,0:T(8,128)(2,1)} %refs_0_.2), channel_id=1, source_target_pairs={{0,8},{2,10},{4,12},{6,14},{8,0},{10,2},{12,4},{14,6},{16,24},{18,... | collective-permute-start | bytes 294920 | tf_op jit(solution)/shard_map/ppermute | solution.py:223
  3.0 1.5 %collective-permute-start.6 = (bf16[128,384]{1,0:T(8,128)(2,1)}, bf16[128,384]{1,0:T(8,128)(2,1)S(1)}, u32[]{:S(2)}, u32[]{:S(2)}) collective-permute-start(bf16[128,384]{1,0:T(8,128)(2,1)} %refs_4_.1), channel_id=1, source_target_pairs={{0,4},{2,6},{4,0},{6,2},{8,12},{10,14},{12,8},{14,10},{16,20},{18,... | collective-permute-start | bytes 294920 | tf_op jit(solution)/shard_map/ppermute | solution.py:223
  4.5 0.5 %collective-permute-start.1 = (bf16[128,384]{1,0:T(8,128)(2,1)}, bf16[128,384]{1,0:T(8,128)(2,1)S(1)}, u32[]{:S(2)}, u32[]{:S(2)}) collective-permute-start(bf16[128,384]{1,0:T(8,128)(2,1)} %refs_0_.2), channel_id=1, source_target_pairs={{0,4},{2,6},{4,0},{6,2},{8,12},{10,14},{12,8},{14,10},{16,20},{18,... | collective-permute-start | bytes 294920 | tf_op jit(solution)/shard_map/ppermute | solution.py:223
  5.1 2.6 %collective-permute-start = (bf16[128,384]{1,0:T(8,128)(2,1)}, bf16[128,384]{1,0:T(8,128)(2,1)S(1)}, u32[]{:S(2)}, u32[]{:S(2)}) collective-permute-start(bf16[128,384]{1,0:T(8,128)(2,1)} %refs_0_.3), channel_id=1, source_target_pairs={{0,16},{2,18},{4,20},{6,22},{8,24},{10,26},{12,28},{14,30},{16,0},... | collective-permute-start | bytes 294920 | tf_op jit(solution)/shard_map/ppermute | solution.py:223
  7.6 0.0 collective-permute-done.2.refs_2_
  7.6 1.5 %collective-permute-start.3 = (bf16[128,384]{1,0:T(8,128)(2,1)S(1)}, bf16[128,384]{1,0:T(8,128)(2,1)S(1)}, u32[]{:S(2)}, u32[]{:S(2)}) collective-permute-start(bf16[128,384]{1,0:T(8,128)(2,1)S(1)} %collective-permute-done.2.refs_2_), channel_id=1, source_target_pairs={{0,4},{2,6},{4,0},{6,2},{8,12},{10,14},{12,8},{14,10},{16,20},{18,... | collective-permute-start | bytes 294920 | tf_op jit(solution)/shard_map/ppermute | solution.py:223
  9.1 0.4 %collective-permute-start.7 = (bf16[128,384]{1,0:T(8,128)(2,1)}, bf16[128,384]{1,0:T(8,128)(2,1)S(1)}, u32[]{:S(2)}, u32[]{:S(2)}) collective-permute-start(bf16[128,384]{1,0:T(8,128)(2,1)} %refs_4_.1), channel_id=1, source_target_pairs={{0,8},{2,10},{4,12},{6,14},{8,0},{10,2},{12,4},{14,6},{16,24},{18,... | collective-permute-start | bytes 294920 | tf_op jit(solution)/shard_map/ppermute | solution.py:223
  9.6 0.0 collective-permute-done.6.refs_5_
  9.6 1.6 %collective-permute-start.8 = (bf16[128,384]{1,0:T(8,128)(2,1)S(1)}, bf16[128,384]{1,0:T(8,128)(2,1)S(1)}, u32[]{:S(2)}, u32[]{:S(2)}) collective-permute-start(bf16[128,384]{1,0:T(8,128)(2,1)S(1)} %collective-permute-done.6.refs_5_), channel_id=1, source_target_pairs={{0,8},{2,10},{4,12},{6,14},{8,0},{10,2},{12,4},{14,6},{16,24},{18,... | collective-permute-start | bytes 294920 | tf_op jit(solution)/shard_map/ppermute | solution.py:223
  11.2 0.0 copy-start.7
  11.2 1.7 %shard_map.82.own_ref = f32[8,128]{1,0:T(8,128)} custom-call(bf16[128,384]{1,0:T(8,128)(2,1)} %refs_0_.3, bf16[128,384]{1,0:T(8,128)(2,1)} %refs_0_.2), custom_call_target="tpu_custom_call" | custom-call | tf_op jit(solution)/shard_map/pallas_call | solution.py:253
  12.9 0.0 copy-start
  12.9 0.0 copy-start.2
  12.9 0.0 collective-permute-done.refs_0_.refs_1_
  12.9 0.0 collective-permute-done.1.refs_1_
  13.0 0.0 collective-permute-done.3.refs_3_
  13.0 0.0 copy-start.4
  13.0 0.7 %copy-done.4 = f32[8,128]{1,0:T(8,128)S(1)} copy-done((f32[8,128]{1,0:T(8,128)S(1)}, f32[8,128]{1,0:T(8,128)}, u32[]{:S(2)}) %copy-start.4) | copy-done | bytes 4120
  13.7 0.1 shard_map.83.own_ref
  13.8 1.6 %collective-permute-start.4 = (f32[8,128]{1,0:T(8,128)S(1)}, f32[8,128]{1,0:T(8,128)S(1)}, u32[]{:S(2)}, u32[]{:S(2)}) collective-permute-start(f32[8,128]{1,0:T(8,128)S(1)} %shard_map.83.own_ref), channel_id=1, source_target_pairs={{0,1},{1,0},{2,3},{3,2},{4,5},{5,4},{6,7},{7,6},{8,9},{9,8},{10,11... | collective-permute-start | bytes 12296 | tf_op jit(solution)/shard_map/ppermute | solution.py:274
  15.4 0.0 copy-done.7
  15.4 0.0 copy-start.5
  15.4 0.0 copy-start.8
  15.4 0.0 copy-start.1
  15.5 0.0 collective-permute-done.7.refs_6_
  15.5 0.5 %collective-permute-done.8.refs_7_ = bf16[128,384]{1,0:T(8,128)(2,1)S(1)} collective-permute-done((bf16[128,384]{1,0:T(8,128)(2,1)S(1)}, bf16[128,384]{1,0:T(8,128)(2,1)S(1)}, u32[]{:S(2)}, u32[]{:S(2)}) %collective-permute-start.8) | collective-permute-done | bytes 98336 | tf_op jit(solution)/shard_map/ppermute | solution.py:223
  16.0 1.6 %collective-permute-done.4.other_ref = f32[8,128]{1,0:T(8,128)S(1)} collective-permute-done((f32[8,128]{1,0:T(8,128)S(1)}, f32[8,128]{1,0:T(8,128)S(1)}, u32[]{:S(2)}, u32[]{:S(2)}) %collective-permute-start.4) | collective-permute-done | bytes 4128 | tf_op jit(solution)/shard_map/ppermute | solution.py:274
  17.5 0.0 copy-done
  17.5 0.0 copy-done.2
  17.5 0.2 shard_map.84.refs_4_
  17.7 0.1 collective-permute-start.9
  17.8 0.0 copy-done.5
  17.8 2.0 %collective-permute-start.5 = (s32[1,16]{1,0:T(1,128)S(1)}, s32[1,16]{1,0:T(1,128)S(1)}, u32[]{:S(2)}, u32[]{:S(2)}) collective-permute-start(s32[1,16]{1,0:T(1,128)S(1)} %copy-done.5), channel_id=1, source_target_pairs={{0,16},{2,18},{4,20},{6,22},{8,24},{10,26},{12,28},{14,30},{16,0},... | collective-permute-start | bytes 200 | tf_op jit(solution)/shard_map/ppermute | solution.py:223
  19.8 0.0 copy-done.8
  19.8 2.5 %collective-permute-done.5.refs_3_.far_ref = s32[1,16]{1,0:T(1,128)S(1)} collective-permute-done((s32[1,16]{1,0:T(1,128)S(1)}, s32[1,16]{1,0:T(1,128)S(1)}, u32[]{:S(2)}, u32[]{:S(2)}) %collective-permute-start.5) | collective-permute-done | bytes 96 | tf_op jit(solution)/shard_map/ppermute | solution.py:223
  22.3 0.0 copy-done.1
  22.3 1.8 %shard_map.85 = (bf16[256,384]{1,0:T(8,128)(2,1)S(1)}, f32[256,384]{1,0:T(8,128)S(1)}, f32[256,768]{1,0:T(8,128)S(1)}) custom-call(f32[1,384]{1,0:T(1,128)S(1)} %reshape.6.gain_ref, f32[8,128]{1,0:T(8,128)S(1)} %shard_map.83.own_ref, f32[8,128]{1,0:T(8,128)S(1)} %collective-permute-done.4.other_ref, bf16[128,384]{1,0:T(8,128)(2,1)S(1)} %copy-done.1, ...), custom_call_target="tpu_custom_call" | custom-call | tf_op jit(solution)/shard_map/pallas_call | solution.py:294
  24.1 0.0 collective-permute-done.9.refs_0_
  24.1 0.0 copy-start.3
  24.1 0.0 copy-start.6
  24.1 1.0 %shard_map.87 = bf16[144,384]{1,0:T(8,128)(2,1)S(1)} custom-call(bf16[256,384]{1,0:T(8,128)(2,1)S(1)} %get-tuple-element.10.query_ref, s32[1,16]{1,0:T(1,128)S(1)} %collective-permute-done.5.refs_3_.far_ref, bf16[1024,384]{1,0:T(8,128)(2,1)S(1)} %collective-permute-done.9.refs_0_, f32[256,384]{1,0:T(8,128)S(1)} %get-tuple-element.11.refs_1_, ...), custom_call_target="tpu_custom_call" | custom-call | tf_op jit(solution)/shard_map/pallas_call | solution.py:307
  25.1 2.0 %collective-permute-start.10 = (bf16[144,384]{1,0:T(8,128)(2,1)S(1)}, bf16[144,384]{1,0:T(8,128)(2,1)S(1)}, u32[]{:S(2)}, u32[]{:S(2)}) collective-permute-start(bf16[144,384]{1,0:T(8,128)(2,1)S(1)} %shard_map.87), channel_id=1, source_target_pairs={{0,16},{2,18},{4,20},{6,22},{8,24},{10,26},{12,28},{14,30},{16,0},... | collective-permute-start | bytes 331784 | tf_op jit(solution)/shard_map/ppermute | solution.py:223
  27.1 0.0 copy-done.3
  27.1 0.0 copy-done.6
  27.1 0.6 %shard_map.88.gate_ref = f32[16,384]{1,0:T(8,128)S(1)} custom-call(s32[2]{0:T(128)S(1)} %copy-done.6, f32[50,384]{1,0:T(8,128)S(1)} %copy-done.3), custom_call_target="tpu_custom_call" | custom-call | tf_op jit(solution)/shard_map/pallas_call | solution.py:325
  27.7 1.0 %shard_map.86 = (f32[128,384]{1,0:T(8,128)S(1)}, f32[8,384]{1,0:T(8,128)S(1)}) custom-call(bf16[256,384]{1,0:T(8,128)(2,1)S(1)} %get-tuple-element.10.query_ref, s32[1,16]{1,0:T(1,128)S(1)} %copy-done.5, bf16[1024,384]{1,0:T(8,128)(2,1)S(1)} %collective-permute-done.9.refs_0_, f32[256,384]{1,0:T(8,128)S(1)} %get-tuple-element.11.refs_1_, ...), custom_call_target="tpu_custom_call" | custom-call | tf_op jit(solution)/shard_map/pallas_call | solution.py:307
  28.7 3.9 %collective-permute-done.10.packet_ref = bf16[144,384]{1,0:T(8,128)(2,1)S(1)} collective-permute-done((bf16[144,384]{1,0:T(8,128)(2,1)S(1)}, bf16[144,384]{1,0:T(8,128)(2,1)S(1)}, u32[]{:S(2)}, u32[]{:S(2)}) %collective-permute-start.10) | collective-permute-done | bytes 110624 | tf_op jit(solution)/shard_map/ppermute | solution.py:223
  32.6 0.8 %shard_map.89 = bf16[128,384]{1,0:T(8,128)(2,1)} custom-call(f32[128,384]{1,0:T(8,128)S(1)} %get-tuple-element.13.own_ref, f32[8,384]{1,0:T(8,128)S(1)} %get-tuple-element.14.logs_ref, bf16[144,384]{1,0:T(8,128)(2,1)S(1)} %collective-permute-done.10.packet_ref, f32[16,384]{1,0:T(8,128)S(1)} %shard_map.88.gate_ref), custom_call_target="tpu_custom_call" | custom-call | tf_op jit(solution)/shard_map/pallas_call | solution.py:334
  (2 shorter events, 0.0 us)
Async XLA Ops:
  0.0 7.6 %collective-permute-start.2 = (bf16[128,384]{1,0:T(8,128)(2,1)}, bf16[128,384]{1,0:T(8,128)(2,1)S(1)}, u32[]{:S(2)}, u32[]{:S(2)}) collective-permute-start(bf16[128,384]{1,0:T(8,128)(2,1)} %refs_0_.2), channel_id=1, source_target_pairs={{0,8},{2,10},{4,12},{6,14},{8,0},{10,2},{12,4},{14,6},{16,24},{18,... | collective-permute-start | bytes 294920 | tf_op jit(solution)/shard_map/ppermute | solution.py:223
  3.0 6.6 %collective-permute-start.6 = (bf16[128,384]{1,0:T(8,128)(2,1)}, bf16[128,384]{1,0:T(8,128)(2,1)S(1)}, u32[]{:S(2)}, u32[]{:S(2)}) collective-permute-start(bf16[128,384]{1,0:T(8,128)(2,1)} %refs_4_.1), channel_id=1, source_target_pairs={{0,4},{2,6},{4,0},{6,2},{8,12},{10,14},{12,8},{14,10},{16,20},{18,... | collective-permute-start | bytes 294920 | tf_op jit(solution)/shard_map/ppermute | solution.py:223
  4.5 8.4 %collective-permute-start.1 = (bf16[128,384]{1,0:T(8,128)(2,1)}, bf16[128,384]{1,0:T(8,128)(2,1)S(1)}, u32[]{:S(2)}, u32[]{:S(2)}) collective-permute-start(bf16[128,384]{1,0:T(8,128)(2,1)} %refs_0_.2), channel_id=1, source_target_pairs={{0,4},{2,6},{4,0},{6,2},{8,12},{10,14},{12,8},{14,10},{16,20},{18,... | collective-permute-start | bytes 294920 | tf_op jit(solution)/shard_map/ppermute | solution.py:223
  5.1 7.9 %collective-permute-start = (bf16[128,384]{1,0:T(8,128)(2,1)}, bf16[128,384]{1,0:T(8,128)(2,1)S(1)}, u32[]{:S(2)}, u32[]{:S(2)}) collective-permute-start(bf16[128,384]{1,0:T(8,128)(2,1)} %refs_0_.3), channel_id=1, source_target_pairs={{0,16},{2,18},{4,20},{6,22},{8,24},{10,26},{12,28},{14,30},{16,0},... | collective-permute-start | bytes 294920 | tf_op jit(solution)/shard_map/ppermute | solution.py:223
  7.6 5.3 %collective-permute-start.3 = (bf16[128,384]{1,0:T(8,128)(2,1)S(1)}, bf16[128,384]{1,0:T(8,128)(2,1)S(1)}, u32[]{:S(2)}, u32[]{:S(2)}) collective-permute-start(bf16[128,384]{1,0:T(8,128)(2,1)S(1)} %collective-permute-done.2.refs_2_), channel_id=1, source_target_pairs={{0,4},{2,6},{4,0},{6,2},{8,12},{10,14},{12,8},{14,10},{16,20},{18,... | collective-permute-start | bytes 294920 | tf_op jit(solution)/shard_map/ppermute | solution.py:223
  9.1 6.3 %collective-permute-start.7 = (bf16[128,384]{1,0:T(8,128)(2,1)}, bf16[128,384]{1,0:T(8,128)(2,1)S(1)}, u32[]{:S(2)}, u32[]{:S(2)}) collective-permute-start(bf16[128,384]{1,0:T(8,128)(2,1)} %refs_4_.1), channel_id=1, source_target_pairs={{0,8},{2,10},{4,12},{6,14},{8,0},{10,2},{12,4},{14,6},{16,24},{18,... | collective-permute-start | bytes 294920 | tf_op jit(solution)/shard_map/ppermute | solution.py:223
  9.6 6.4 %collective-permute-start.8 = (bf16[128,384]{1,0:T(8,128)(2,1)S(1)}, bf16[128,384]{1,0:T(8,128)(2,1)S(1)}, u32[]{:S(2)}, u32[]{:S(2)}) collective-permute-start(bf16[128,384]{1,0:T(8,128)(2,1)S(1)} %collective-permute-done.6.refs_5_), channel_id=1, source_target_pairs={{0,8},{2,10},{4,12},{6,14},{8,0},{10,2},{12,4},{14,6},{16,24},{18,... | collective-permute-start | bytes 294920 | tf_op jit(solution)/shard_map/ppermute | solution.py:223
  11.2 4.3 %copy-start.7 = (f32[384]{0:T(512)S(1)}, f32[384]{0:T(512)}, u32[]{:S(2)}) copy-start(f32[384]{0:T(512)} %param.12) | copy-start | bytes 4612
  12.9 4.6 %copy-start = (bf16[128,384]{1,0:T(8,128)(2,1)S(1)}, bf16[128,384]{1,0:T(8,128)(2,1)}, u32[]{:S(2)}) copy-start(bf16[128,384]{1,0:T(8,128)(2,1)} %refs_0_.2) | copy-start | bytes 294916
  12.9 4.6 %copy-start.2 = (bf16[128,384]{1,0:T(8,128)(2,1)S(1)}, bf16[128,384]{1,0:T(8,128)(2,1)}, u32[]{:S(2)}) copy-start(bf16[128,384]{1,0:T(8,128)(2,1)} %refs_4_.1) | copy-start | bytes 294916
  13.0 0.7 %copy-start.4 = (f32[8,128]{1,0:T(8,128)S(1)}, f32[8,128]{1,0:T(8,128)}, u32[]{:S(2)}) copy-start(f32[8,128]{1,0:T(8,128)} %shard_map.82.own_ref) | copy-start | bytes 12292
  13.8 3.7 %collective-permute-start.4 = (f32[8,128]{1,0:T(8,128)S(1)}, f32[8,128]{1,0:T(8,128)S(1)}, u32[]{:S(2)}, u32[]{:S(2)}) collective-permute-start(f32[8,128]{1,0:T(8,128)S(1)} %shard_map.83.own_ref), channel_id=1, source_target_pairs={{0,1},{1,0},{2,3},{3,2},{4,5},{5,4},{6,7},{7,6},{8,9},{9,8},{10,11... | collective-permute-start | bytes 12296 | tf_op jit(solution)/shard_map/ppermute | solution.py:274
  15.4 2.4 %copy-start.5 = (s32[1,16]{1,0:T(1,128)S(1)}, s32[1,16]{1,0:T(1,128)}, u32[]{:S(2)}) copy-start(s32[1,16]{1,0:T(1,128)} %far_ref.1) | copy-start | bytes 196
  15.4 4.4 %copy-start.8 = (f32[384]{0:T(512)S(1)}, f32[384]{0:T(512)}, u32[]{:S(2)}) copy-start(f32[384]{0:T(512)} %param.11) | copy-start | bytes 4612
  15.4 6.9 %copy-start.1 = (bf16[128,384]{1,0:T(8,128)(2,1)S(1)}, bf16[128,384]{1,0:T(8,128)(2,1)}, u32[]{:S(2)}) copy-start(bf16[128,384]{1,0:T(8,128)(2,1)} %refs_0_.3) | copy-start | bytes 294916
  17.7 6.4 %collective-permute-start.9 = (bf16[1024,384]{1,0:T(8,128)(2,1)S(1)}, bf16[1024,384]{1,0:T(8,128)(2,1)S(1)}, u32[]{:S(2)}, u32[]{:S(2)}) collective-permute-start(bf16[1024,384]{1,0:T(8,128)(2,1)S(1)} %shard_map.84.refs_4_), channel_id=1, source_target_pairs={{0,2},{2,0},{4,6},{6,4},{8,10},{10,8},{12,14},{14,12},{16,18},{18,... | collective-permute-start | bytes 2359304 | tf_op jit(solution)/shard_map/ppermute | solution.py:223
  17.8 4.5 %collective-permute-start.5 = (s32[1,16]{1,0:T(1,128)S(1)}, s32[1,16]{1,0:T(1,128)S(1)}, u32[]{:S(2)}, u32[]{:S(2)}) collective-permute-start(s32[1,16]{1,0:T(1,128)S(1)} %copy-done.5), channel_id=1, source_target_pairs={{0,16},{2,18},{4,20},{6,22},{8,24},{10,26},{12,28},{14,30},{16,0},... | collective-permute-start | bytes 200 | tf_op jit(solution)/shard_map/ppermute | solution.py:223
  24.1 3.0 %copy-start.3 = (f32[50,384]{1,0:T(8,128)S(1)}, f32[50,384]{1,0:T(8,128)}, u32[]{:S(2)}) copy-start(f32[50,384]{1,0:T(8,128)} %table_ref.1) | copy-start | bytes 230404
  24.1 3.0 %copy-start.6 = (s32[2]{0:T(128)S(1)}, s32[2]{0:T(128)}, u32[]{:S(2)}) copy-start(s32[2]{0:T(128)} %step_ref.1) | copy-start | bytes 28
  25.1 7.5 %collective-permute-start.10 = (bf16[144,384]{1,0:T(8,128)(2,1)S(1)}, bf16[144,384]{1,0:T(8,128)(2,1)S(1)}, u32[]{:S(2)}, u32[]{:S(2)}) collective-permute-start(bf16[144,384]{1,0:T(8,128)(2,1)S(1)} %shard_map.87), channel_id=1, source_target_pairs={{0,16},{2,18},{4,20},{6,22},{8,24},{10,26},{12,28},{14,30},{16,0},... | collective-permute-start | bytes 331784 | tf_op jit(solution)/shard_map/ppermute | solution.py:223

commit v5 on v4

--- a/solution.py
+++ b/solution.py
@@ -25,7 +25,7 @@
 
 
 def squares(source_ref):
-    wide = source_ref[...].astype(jnp.float32)
+    wide = source_ref[:HD, :].astype(jnp.float32)
     square = wide * wide
     part = square[:, :HD]
     for low in range(HD, square.shape[1], HD):
@@ -33,17 +33,24 @@
     return jnp.sum(part.T, axis=0, keepdims=True)
 
 
-def own_sums_kernel(query_hbm, key_hbm, out_ref, query_ref, key_ref, sems):
+def own_kernel(query_hbm, key_hbm, far_ref, query_out, key_out, sums_out, query_ref, sems):
+    rows, width = query_ref.shape
     copies = [
         pltpu.make_async_copy(query_hbm, query_ref, sems.at[0]),
-        pltpu.make_async_copy(key_hbm, key_ref, sems.at[1]),
+        pltpu.make_async_copy(key_hbm, key_out, sems.at[1]),
     ]
     for copy in copies:
         copy.start()
-    out_ref[...] = jnp.zeros_like(out_ref)
-    for place, ref in enumerate((query_ref, key_ref)):
-        copies[place].wait()
-        out_ref[place : place + 1, :] = squares(ref)
+    far = far_ref[...].astype(jnp.float32)
+    far = jnp.concatenate([far, jnp.full((1, HD - far.shape[1]), -1.0)], axis=1)
+    query_out[rows:, :HD] = jnp.broadcast_to(far, (EXTRA, HD)).astype(jnp.bfloat16)
+    query_out[rows:, HD:] = jnp.zeros((EXTRA, width - HD), jnp.bfloat16)
+    sums_out[...] = jnp.zeros_like(sums_out)
+    copies[0].wait()
+    query_out[:rows, :] = query_ref[...]
+    sums_out[0:1, :] = squares(query_ref)
+    copies[1].wait()
+    sums_out[1:2, :] = squares(key_out)
 
 
 def sums_kernel(own_ref, *refs):
@@ -59,7 +66,7 @@
     factor = spread(lax.rsqrt(total / full_width + EPSILON))
     parts = []
     for low in range(0, source_ref.shape[1], HD):
-        wide = source_ref[:, low : low + HD].astype(jnp.float32)
+        wide = source_ref[:HD, low : low + HD].astype(jnp.float32)
         parts.append((wide * factor * gain_ref[:, low : low + HD]).astype(jnp.bfloat16))
     return jnp.concatenate(parts, axis=1)
 
@@ -75,12 +82,11 @@
         pack_out[place * rows : (place + 1) * rows, :] = value_ref[...]
 
 
-def key_bias(far_ref, query_mask, key_masks):
+def key_bias(query_ref, query_mask, key_masks):
     me = lax.axis_index("tm")
     lane = lax.broadcasted_iota(jnp.int32, (1, HD), 1)
     half = (lane >= BLK).astype(jnp.float32)
-    far = far_ref[...].astype(jnp.float32)
-    far = jnp.concatenate([far, jnp.full((1, HD - far.shape[1]), -1.0)], axis=1)
+    far = query_ref[HD:, :HD].astype(jnp.float32)[:1]
     parts = []
     for key_mask in key_masks:
         query_id, key_id = me ^ query_mask, me ^ key_mask
@@ -125,12 +131,12 @@
 
 
 def own_attention(full_width, query_masks, key_masks, gain_ref, own_ref, other_ref, *refs):
-    queries, far, pack = refs[:2], refs[2:4], refs[4]
-    query_out, context_out, stats_out = refs[5:]
-    rows, width = queries[0].shape
+    queries, pack = refs[:2], refs[2]
+    query_out, context_out, stats_out = refs[3:]
+    rows, width = query_out.shape[0] // 2, query_out.shape[1]
     for place, mask in enumerate(query_masks):
         part = slice(place * rows, (place + 1) * rows)
-        bias = key_bias(far[place], mask, key_masks)
+        bias = key_bias(queries[place], mask, key_masks)
         query = normed(queries[place], own_ref, other_ref, 2 * place, gain_ref, full_width)
         query_out[part, :] = query
         for low in range(0, width, HD):
@@ -147,12 +153,12 @@
             stats_out[part, wide + HD : wide + 2 * HD] = total
 
 
-def last_attention(place, query_mask, key_masks, query_ref, far_ref, *refs):
+def last_attention(place, query_mask, key_masks, query_ref, raw_ref, *refs):
     pack, context_ref, stats_ref, *outs = refs
     rows, width = query_ref.shape[0] // 2, query_ref.shape[1]
     heads = width // HD
     part = slice(place * rows, (place + 1) * rows)
-    bias = key_bias(far_ref, query_mask, key_masks)
+    bias = key_bias(raw_ref, query_mask, key_masks)
     lane = lax.broadcasted_iota(jnp.int32, (1, HD), 1)
     logs = jnp.zeros((rows, HD), jnp.float32)
     for head in range(heads):
@@ -239,28 +245,32 @@
     splits = lax.axis_size("head")
     full_width = width * splits
     params = pltpu.CompilerParams(vmem_limit_bytes=(8 + count // 2) * 2**20)
-    bits = [1 << place for place in range(1, count.bit_length() - 2)]
-    query_mask = count // 2
+    query_mask = count // 4
+    bits = [1 << place for place in range(1, count.bit_length() - 1)]
+    bits = [bit for bit in bits[::-1] if bit != query_mask]
     query_gain = query_gain.reshape(1, width)
     key_gain = key_gain.reshape(1, width)
 
-    keys = gathered(key_proj, bits[::-1])
-    values = gathered(value_proj, bits)
-    queries = [query_proj, exchange(query_proj, query_mask)]
-    far = [far_blocks, exchange(far_blocks, query_mask)]
-    masks = sorted(keys, key=lambda mask: (mask.bit_count(), mask))
-
-    own_sums = pl.pallas_call(
-        own_sums_kernel,
-        out_shape=jax.ShapeDtypeStruct((8, rows), jnp.float32),
-        in_specs=[ANY, ANY],
-        out_specs=VMEM,
+    query_packet, own_key, own_sums = pl.pallas_call(
+        own_kernel,
+        out_shape=[
+            jax.ShapeDtypeStruct((rows + EXTRA, width), jnp.bfloat16),
+            jax.ShapeDtypeStruct((rows, width), jnp.bfloat16),
+            jax.ShapeDtypeStruct((8, rows), jnp.float32),
+        ],
+        in_specs=[ANY, ANY, VMEM],
+        out_specs=[VMEM] * 3,
         scratch_shapes=[
-            pltpu.VMEM((rows, width), jnp.bfloat16),
             pltpu.VMEM((rows, width), jnp.bfloat16),
             pltpu.SemaphoreType.DMA((2,)),
         ],
-    )(query_proj, key_proj)
+    )(query_proj, key_proj, far_blocks)
+    keys = gathered(key_proj, bits)
+    keys[0] = own_key
+    values = gathered(value_proj, bits)
+    queries = [query_packet, exchange(query_packet, query_mask)]
+    masks = sorted(keys, key=lambda mask: (mask.bit_count(), mask))
+
     sources = queries[1:] + [keys[mask] for mask in masks[1:]]
     lines = len(sources) + 2
     sums = pl.pallas_call(
@@ -298,10 +308,10 @@
             jax.ShapeDtypeStruct((2 * rows, width), jnp.float32),
             jax.ShapeDtypeStruct((2 * rows, 2 * width), jnp.float32),
         ],
-        in_specs=[VMEM] * 8,
+        in_specs=[VMEM] * 6,
         out_specs=[VMEM] * 3,
         compiler_params=params,
-    )(query_gain, sums, others, *queries, *far, pack)
+    )(query_gain, sums, others, *queries, pack)
 
     def last_part(place, out_shape):
         return pl.pallas_call(
@@ -312,7 +322,7 @@
             in_specs=[VMEM] * 5,
             out_specs=[VMEM] * len(out_shape),
             compiler_params=params,
-        )(query_norm, far[place], other_pack, context, stats)
+        )(query_norm, queries[place], other_pack, context, stats)
 
     (packet,) = last_part(1, [jax.ShapeDtypeStruct((rows + EXTRA, width), jnp.bfloat16)])
     own, own_logs = last_part(

time: 33.5 us -> 31.7 us (0.946)
  starting transfers between devices: 16.9 us -> 13 us
  waiting for transfers between devices: 8.41 us -> 9.21 us
  Pallas kernels: 7.16 us -> 7.8 us
  local copies, waits for them, and re-layouts: 0.77 us -> 1.35 us
    ppermute x10 -> x9, starting transfers between devices: 15.3 us -> 11.6 us  [exchange(): return lax.ppermute(array, 'tm', [(i, i ^ mask) for i in range(count)])]
    ppermute x1, waiting for transfers between devices: 1.56 us -> 2.23 us  [local(): others = lax.ppermute(sums, 'head', [(0, 1), (1, 0)])]
    pallas_call x1, Pallas kernels: 1.74 us -> 2.38 us  [local(): pl.pallas_call(own_kernel, out_shape=[jax.ShapeDtypeStruct((rows + EXTRA,...]
    unnamed x18, local copies, waits for them, and re-layouts: 0.76 us -> 1.35 us
    ppermute x10 -> x9, waiting for transfers between devices: 6.85 us -> 6.98 us  [exchange(): return lax.ppermute(array, 'tm', [(i, i ^ mask) for i in range(count)])]
  transfers between devices with their start and end apart: 11 -> 10, of which waited for: 4 -> 4; matrix products, arithmetic and copies ran while one was open for 0% -> 0% of each run, Pallas kernels for 16% -> 18%
where the time goes in v5:
time: 31.7 us; the launch traced here: 31.5 us
  starting transfers between devices  13 us (41%)
  waiting for transfers between devices  9.21 us (29%)
  Pallas kernels  7.8 us (25%)
  local copies, waits for them, and re-layouts  1.35 us (4%)
    ppermute x9, starting transfers between devices, exchange(): return lax.ppermute(array, 'tm', [(i, i ^ mask) for i in range(count)])  11.6 us
    ppermute x9, waiting for transfers between devices, exchange(): return lax.ppermute(array, 'tm', [(i, i ^ mask) for i in range(count)])  6.98 us
    pallas_call x1, Pallas kernels, local(): pl.pallas_call(own_kernel, out_shape=[jax.ShapeDtypeStruct((rows + EXTRA,...  2.38 us
    ppermute x1, waiting for transfers between devices, local(): others = lax.ppermute(sums, 'head', [(0, 1), (1, 0)])  2.23 us
    pallas_call x2, Pallas kernels, last_part(): pl.pallas_call(functools.partial(last_attention, place, place * query_mas...  1.95 us
    pallas_call x1, Pallas kernels, local(): pl.pallas_call(functools.partial(own_attention, full_width, [0, query_mas...  1.76 us
    ppermute x1, starting transfers between devices, local(): others = lax.ppermute(sums, 'head', [(0, 1), (1, 0)])  1.42 us
    unnamed x18, local copies, waits for them, and re-layouts  1.35 us
  transfers between devices with their start and end apart: 10, of which 4 were waited for; matrix products, arithmetic and copies ran while one was open for 0% of the time, Pallas kernels for 18%

profile of v5, /device:TPU:0, one launch (start us, length us, event | category | flops | bytes accessed | tf_op | source)
XLA Modules:
  0.0 31.5 jit_solution(1103070846200695349)
XLA Ops:
  0.0 0.0 copy-start.6
  0.0 0.0 copy-start.1
  0.0 4.0 %collective-permute-start.2 = (bf16[128,384]{1,0:T(8,128)(2,1)}, bf16[128,384]{1,0:T(8,128)(2,1)S(1)}, u32[]{:S(2)}, u32[]{:S(2)}) collective-permute-start(bf16[128,384]{1,0:T(8,128)(2,1)} %key_hbm.1), channel_id=1, source_target_pairs={{0,16},{2,18},{4,20},{6,22},{8,24},{10,26},{12,28},{14,30},{16,0},... | collective-permute-start | bytes 294920 | tf_op jit(solution)/shard_map/ppermute | solution.py:229
  4.0 0.1 collective-permute-start.6
  4.1 2.4 %shard_map.82 = (bf16[144,384]{1,0:T(8,128)(2,1)}, bf16[128,384]{1,0:T(8,128)(2,1)}, f32[8,128]{1,0:T(8,128)}) custom-call(bf16[128,384]{1,0:T(8,128)(2,1)} %query_hbm.1, bf16[128,384]{1,0:T(8,128)(2,1)} %key_hbm.1, s32[1,16]{1,0:T(1,128)} %far_ref.1), custom_call_target="tpu_custom_call" | custom-call | tf_op jit(solution)/shard_map/pallas_call | solution.py:254
  6.5 1.9 %collective-permute-start = (bf16[144,384]{1,0:T(8,128)(2,1)}, bf16[144,384]{1,0:T(8,128)(2,1)S(1)}, u32[]{:S(2)}, u32[]{:S(2)}) collective-permute-start(bf16[144,384]{1,0:T(8,128)(2,1)} %get-tuple-element.14.refs_0_.raw_ref), channel_id=1, source_target_pairs={{0,8},{2,10},{4,12},{6,14},{8,0},{10,2},{12,4},{14,6},{16,24},{18,... | collective-permute-start | bytes 331784 | tf_op jit(solution)/shard_map/ppermute | solution.py:229
  8.4 0.0 copy-done.6
  8.4 1.5 %collective-permute-start.1 = (bf16[128,384]{1,0:T(8,128)(2,1)S(1)}, bf16[128,384]{1,0:T(8,128)(2,1)S(1)}, u32[]{:S(2)}, u32[]{:S(2)}) collective-permute-start(bf16[128,384]{1,0:T(8,128)(2,1)S(1)} %copy-done.6), channel_id=1, source_target_pairs={{0,4},{2,6},{4,0},{6,2},{8,12},{10,14},{12,8},{14,10},{16,20},{18,... | collective-permute-start | bytes 294920 | tf_op jit(solution)/shard_map/ppermute | solution.py:229
  9.9 2.4 %collective-permute-done.2.refs_2_ = bf16[128,384]{1,0:T(8,128)(2,1)S(1)} collective-permute-done((bf16[128,384]{1,0:T(8,128)(2,1)}, bf16[128,384]{1,0:T(8,128)(2,1)S(1)}, u32[]{:S(2)}, u32[]{:S(2)}) %collective-permute-start.2) | collective-permute-done | bytes 98336 | tf_op jit(solution)/shard_map/ppermute | solution.py:229
  12.3 1.7 %collective-permute-start.3 = (bf16[128,384]{1,0:T(8,128)(2,1)S(1)}, bf16[128,384]{1,0:T(8,128)(2,1)S(1)}, u32[]{:S(2)}, u32[]{:S(2)}) collective-permute-start(bf16[128,384]{1,0:T(8,128)(2,1)S(1)} %collective-permute-done.2.refs_2_), channel_id=1, source_target_pairs={{0,4},{2,6},{4,0},{6,2},{8,12},{10,14},{12,8},{14,10},{16,20},{18,... | collective-permute-start | bytes 294920 | tf_op jit(solution)/shard_map/ppermute | solution.py:229
  13.9 0.0 copy-done.1
  13.9 0.4 %collective-permute-start.5 = (bf16[128,384]{1,0:T(8,128)(2,1)S(1)}, bf16[128,384]{1,0:T(8,128)(2,1)S(1)}, u32[]{:S(2)}, u32[]{:S(2)}) collective-permute-start(bf16[128,384]{1,0:T(8,128)(2,1)S(1)} %copy-done.1), channel_id=1, source_target_pairs={{0,4},{2,6},{4,0},{6,2},{8,12},{10,14},{12,8},{14,10},{16,20},{18,... | collective-permute-start | bytes 294920 | tf_op jit(solution)/shard_map/ppermute | solution.py:229
  14.3 0.0 collective-permute-done.6.refs_6_
  14.3 1.7 %collective-permute-start.7 = (bf16[128,384]{1,0:T(8,128)(2,1)S(1)}, bf16[128,384]{1,0:T(8,128)(2,1)S(1)}, u32[]{:S(2)}, u32[]{:S(2)}) collective-permute-start(bf16[128,384]{1,0:T(8,128)(2,1)S(1)} %collective-permute-done.6.refs_6_), channel_id=1, source_target_pairs={{0,4},{2,6},{4,0},{6,2},{8,12},{10,14},{12,8},{14,10},{16,20},{18,... | collective-permute-start | bytes 294920 | tf_op jit(solution)/shard_map/ppermute | solution.py:229
  15.9 0.0 collective-permute-done.1.refs_1_
  15.9 0.0 collective-permute-done.refs_0_.refs_1_.raw_ref
  16.0 1.5 %collective-permute-done.3.refs_3_ = bf16[128,384]{1,0:T(8,128)(2,1)S(1)} collective-permute-done((bf16[128,384]{1,0:T(8,128)(2,1)S(1)}, bf16[128,384]{1,0:T(8,128)(2,1)S(1)}, u32[]{:S(2)}, u32[]{:S(2)}) %collective-permute-start.3) | collective-permute-done | bytes 98336 | tf_op jit(solution)/shard_map/ppermute | solution.py:229
  17.5 0.0 copy-start.4
  17.5 0.7 %copy-done.4 = f32[8,128]{1,0:T(8,128)S(1)} copy-done((f32[8,128]{1,0:T(8,128)S(1)}, f32[8,128]{1,0:T(8,128)}, u32[]{:S(2)}) %copy-start.4) | copy-done | bytes 4120
  18.1 0.0 copy-start.7
  18.1 0.0 copy-start.2
  18.1 0.1 shard_map.83.own_ref
  18.3 1.4 %collective-permute-start.4 = (f32[8,128]{1,0:T(8,128)S(1)}, f32[8,128]{1,0:T(8,128)S(1)}, u32[]{:S(2)}, u32[]{:S(2)}) collective-permute-start(f32[8,128]{1,0:T(8,128)S(1)} %shard_map.83.own_ref), channel_id=1, source_target_pairs={{0,1},{1,0},{2,3},{3,2},{4,5},{5,4},{6,7},{7,6},{8,9},{9,8},{10,11... | collective-permute-start | bytes 12296 | tf_op jit(solution)/shard_map/ppermute | solution.py:284
  19.7 0.0 copy-done.7
  19.7 0.0 collective-permute-done.5.refs_5_
  19.7 0.0 collective-permute-done.7.refs_7_
  19.7 2.2 %collective-permute-done.4.other_ref = f32[8,128]{1,0:T(8,128)S(1)} collective-permute-done((f32[8,128]{1,0:T(8,128)S(1)}, f32[8,128]{1,0:T(8,128)S(1)}, u32[]{:S(2)}, u32[]{:S(2)}) %collective-permute-start.4) | collective-permute-done | bytes 4128 | tf_op jit(solution)/shard_map/ppermute | solution.py:284
  22.0 0.0 copy-done.2
  22.0 0.0 copy-start.8
  22.0 0.0 copy-start
  22.0 0.2 shard_map.84.refs_2_
  22.2 0.1 collective-permute-start.8
  22.2 0.4 %copy-done.8 = f32[384]{0:T(512)S(1)} copy-done((f32[384]{0:T(512)S(1)}, f32[384]{0:T(512)}, u32[]{:S(2)}) %copy-start.8) | copy-done | bytes 1560
  22.7 0.2 copy-done
  22.9 1.8 %shard_map.85 = (bf16[256,384]{1,0:T(8,128)(2,1)S(1)}, f32[256,384]{1,0:T(8,128)S(1)}, f32[256,768]{1,0:T(8,128)S(1)}) custom-call(f32[1,384]{1,0:T(1,128)S(1)} %reshape.6.gain_ref, f32[8,128]{1,0:T(8,128)S(1)} %shard_map.83.own_ref, f32[8,128]{1,0:T(8,128)S(1)} %collective-permute-done.4.other_ref, bf16[144,384]{1,0:T(8,128)(2,1)S(1)} %copy-done, ...), custom_call_target="tpu_custom_call" | custom-call | tf_op jit(solution)/shard_map/pallas_call | solution.py:304
  24.7 0.0 collective-permute-done.8.refs_0_
  24.7 0.0 copy-start.3
  24.7 0.0 copy-start.5
  24.7 1.0 %shard_map.87 = bf16[144,384]{1,0:T(8,128)(2,1)S(1)} custom-call(bf16[256,384]{1,0:T(8,128)(2,1)S(1)} %get-tuple-element.16.query_ref, bf16[144,384]{1,0:T(8,128)(2,1)S(1)} %collective-permute-done.refs_0_.refs_1_.raw_ref, bf16[1024,384]{1,0:T(8,128)(2,1)S(1)} %collective-permute-done.8.refs_0_, f32[256,384]{1,0:T(8,128)S(1)} %get-tuple-element.17.refs_1_, ...), custom_call_target="tpu_custom_call" | custom-call | tf_op jit(solution)/shard_map/pallas_call | solution.py:317
  25.7 0.3 %collective-permute-start.9 = (bf16[144,384]{1,0:T(8,128)(2,1)S(1)}, bf16[144,384]{1,0:T(8,128)(2,1)S(1)}, u32[]{:S(2)}, u32[]{:S(2)}) collective-permute-start(bf16[144,384]{1,0:T(8,128)(2,1)S(1)} %shard_map.87), channel_id=1, source_target_pairs={{0,8},{2,10},{4,12},{6,14},{8,0},{10,2},{12,4},{14,6},{16,24},{18,... | collective-permute-start | bytes 331784 | tf_op jit(solution)/shard_map/ppermute | solution.py:229
  26.0 0.0 copy-done.3
  26.0 0.0 copy-done.5
  26.0 0.6 %shard_map.88.gate_ref = f32[16,384]{1,0:T(8,128)S(1)} custom-call(s32[2]{0:T(128)S(1)} %copy-done.5, f32[50,384]{1,0:T(8,128)S(1)} %copy-done.3), custom_call_target="tpu_custom_call" | custom-call | tf_op jit(solution)/shard_map/pallas_call | solution.py:335
  26.6 1.0 %shard_map.86 = (f32[128,384]{1,0:T(8,128)S(1)}, f32[8,384]{1,0:T(8,128)S(1)}) custom-call(bf16[256,384]{1,0:T(8,128)(2,1)S(1)} %get-tuple-element.16.query_ref, bf16[144,384]{1,0:T(8,128)(2,1)S(1)} %copy-done, bf16[1024,384]{1,0:T(8,128)(2,1)S(1)} %collective-permute-done.8.refs_0_, f32[256,384]{1,0:T(8,128)S(1)} %get-tuple-element.17.refs_1_, ...), custom_call_target="tpu_custom_call" | custom-call | tf_op jit(solution)/shard_map/pallas_call | solution.py:317
  27.6 3.1 %collective-permute-done.9.packet_ref = bf16[144,384]{1,0:T(8,128)(2,1)S(1)} collective-permute-done((bf16[144,384]{1,0:T(8,128)(2,1)S(1)}, bf16[144,384]{1,0:T(8,128)(2,1)S(1)}, u32[]{:S(2)}, u32[]{:S(2)}) %collective-permute-start.9) | collective-permute-done | bytes 110624 | tf_op jit(solution)/shard_map/ppermute | solution.py:229
  30.7 0.8 %shard_map.89 = bf16[128,384]{1,0:T(8,128)(2,1)} custom-call(f32[128,384]{1,0:T(8,128)S(1)} %get-tuple-element.19.own_ref, f32[8,384]{1,0:T(8,128)S(1)} %get-tuple-element.20.logs_ref, bf16[144,384]{1,0:T(8,128)(2,1)S(1)} %collective-permute-done.9.packet_ref, f32[16,384]{1,0:T(8,128)S(1)} %shard_map.88.gate_ref), custom_call_target="tpu_custom_call" | custom-call | tf_op jit(solution)/shard_map/pallas_call | solution.py:344
  (2 shorter events, 0.0 us)
Async XLA Ops:
  0.0 8.4 %copy-start.6 = (bf16[128,384]{1,0:T(8,128)(2,1)S(1)}, bf16[128,384]{1,0:T(8,128)(2,1)}, u32[]{:S(2)}) copy-start(bf16[128,384]{1,0:T(8,128)(2,1)} %key_hbm.1) | copy-start | bytes 294916
  0.0 13.9 %copy-start.1 = (bf16[128,384]{1,0:T(8,128)(2,1)S(1)}, bf16[128,384]{1,0:T(8,128)(2,1)}, u32[]{:S(2)}) copy-start(bf16[128,384]{1,0:T(8,128)(2,1)} %refs_4_.1) | copy-start | bytes 294916
  0.0 12.3 %collective-permute-start.2 = (bf16[128,384]{1,0:T(8,128)(2,1)}, bf16[128,384]{1,0:T(8,128)(2,1)S(1)}, u32[]{:S(2)}, u32[]{:S(2)}) collective-permute-start(bf16[128,384]{1,0:T(8,128)(2,1)} %key_hbm.1), channel_id=1, source_target_pairs={{0,16},{2,18},{4,20},{6,22},{8,24},{10,26},{12,28},{14,30},{16,0},... | collective-permute-start | bytes 294920 | tf_op jit(solution)/shard_map/ppermute | solution.py:229
  4.0 10.2 %collective-permute-start.6 = (bf16[128,384]{1,0:T(8,128)(2,1)}, bf16[128,384]{1,0:T(8,128)(2,1)S(1)}, u32[]{:S(2)}, u32[]{:S(2)}) collective-permute-start(bf16[128,384]{1,0:T(8,128)(2,1)} %refs_4_.1), channel_id=1, source_target_pairs={{0,16},{2,18},{4,20},{6,22},{8,24},{10,26},{12,28},{14,30},{16,0},... | collective-permute-start | bytes 294920 | tf_op jit(solution)/shard_map/ppermute | solution.py:229
  6.5 9.4 %collective-permute-start = (bf16[144,384]{1,0:T(8,128)(2,1)}, bf16[144,384]{1,0:T(8,128)(2,1)S(1)}, u32[]{:S(2)}, u32[]{:S(2)}) collective-permute-start(bf16[144,384]{1,0:T(8,128)(2,1)} %get-tuple-element.14.refs_0_.raw_ref), channel_id=1, source_target_pairs={{0,8},{2,10},{4,12},{6,14},{8,0},{10,2},{12,4},{14,6},{16,24},{18,... | collective-permute-start | bytes 331784 | tf_op jit(solution)/shard_map/ppermute | solution.py:229
  8.4 7.5 %collective-permute-start.1 = (bf16[128,384]{1,0:T(8,128)(2,1)S(1)}, bf16[128,384]{1,0:T(8,128)(2,1)S(1)}, u32[]{:S(2)}, u32[]{:S(2)}) collective-permute-start(bf16[128,384]{1,0:T(8,128)(2,1)S(1)} %copy-done.6), channel_id=1, source_target_pairs={{0,4},{2,6},{4,0},{6,2},{8,12},{10,14},{12,8},{14,10},{16,20},{18,... | collective-permute-start | bytes 294920 | tf_op jit(solution)/shard_map/ppermute | solution.py:229
  12.3 5.2 %collective-permute-start.3 = (bf16[128,384]{1,0:T(8,128)(2,1)S(1)}, bf16[128,384]{1,0:T(8,128)(2,1)S(1)}, u32[]{:S(2)}, u32[]{:S(2)}) collective-permute-start(bf16[128,384]{1,0:T(8,128)(2,1)S(1)} %collective-permute-done.2.refs_2_), channel_id=1, source_target_pairs={{0,4},{2,6},{4,0},{6,2},{8,12},{10,14},{12,8},{14,10},{16,20},{18,... | collective-permute-start | bytes 294920 | tf_op jit(solution)/shard_map/ppermute | solution.py:229
  13.9 5.8 %collective-permute-start.5 = (bf16[128,384]{1,0:T(8,128)(2,1)S(1)}, bf16[128,384]{1,0:T(8,128)(2,1)S(1)}, u32[]{:S(2)}, u32[]{:S(2)}) collective-permute-start(bf16[128,384]{1,0:T(8,128)(2,1)S(1)} %copy-done.1), channel_id=1, source_target_pairs={{0,4},{2,6},{4,0},{6,2},{8,12},{10,14},{12,8},{14,10},{16,20},{18,... | collective-permute-start | bytes 294920 | tf_op jit(solution)/shard_map/ppermute | solution.py:229
  14.3 5.4 %collective-permute-start.7 = (bf16[128,384]{1,0:T(8,128)(2,1)S(1)}, bf16[128,384]{1,0:T(8,128)(2,1)S(1)}, u32[]{:S(2)}, u32[]{:S(2)}) collective-permute-start(bf16[128,384]{1,0:T(8,128)(2,1)S(1)} %collective-permute-done.6.refs_6_), channel_id=1, source_target_pairs={{0,4},{2,6},{4,0},{6,2},{8,12},{10,14},{12,8},{14,10},{16,20},{18,... | collective-permute-start | bytes 294920 | tf_op jit(solution)/shard_map/ppermute | solution.py:229
  17.5 0.7 %copy-start.4 = (f32[8,128]{1,0:T(8,128)S(1)}, f32[8,128]{1,0:T(8,128)}, u32[]{:S(2)}) copy-start(f32[8,128]{1,0:T(8,128)} %get-tuple-element.13.own_ref) | copy-start | bytes 12292
  18.1 1.6 %copy-start.7 = (f32[384]{0:T(512)S(1)}, f32[384]{0:T(512)}, u32[]{:S(2)}) copy-start(f32[384]{0:T(512)} %param.12) | copy-start | bytes 4612
  18.1 3.8 %copy-start.2 = (bf16[128,384]{1,0:T(8,128)(2,1)S(1)}, bf16[128,384]{1,0:T(8,128)(2,1)}, u32[]{:S(2)}) copy-start(bf16[128,384]{1,0:T(8,128)(2,1)} %get-tuple-element.15.refs_0_) | copy-start | bytes 294916
  18.3 3.7 %collective-permute-start.4 = (f32[8,128]{1,0:T(8,128)S(1)}, f32[8,128]{1,0:T(8,128)S(1)}, u32[]{:S(2)}, u32[]{:S(2)}) collective-permute-start(f32[8,128]{1,0:T(8,128)S(1)} %shard_map.83.own_ref), channel_id=1, source_target_pairs={{0,1},{1,0},{2,3},{3,2},{4,5},{5,4},{6,7},{7,6},{8,9},{9,8},{10,11... | collective-permute-start | bytes 12296 | tf_op jit(solution)/shard_map/ppermute | solution.py:284
  22.0 0.7 %copy-start.8 = (f32[384]{0:T(512)S(1)}, f32[384]{0:T(512)}, u32[]{:S(2)}) copy-start(f32[384]{0:T(512)} %param.11) | copy-start | bytes 4612
  22.0 0.9 %copy-start = (bf16[144,384]{1,0:T(8,128)(2,1)S(1)}, bf16[144,384]{1,0:T(8,128)(2,1)}, u32[]{:S(2)}) copy-start(bf16[144,384]{1,0:T(8,128)(2,1)} %get-tuple-element.14.refs_0_.raw_ref) | copy-start | bytes 331780
  22.2 2.5 %collective-permute-start.8 = (bf16[1024,384]{1,0:T(8,128)(2,1)S(1)}, bf16[1024,384]{1,0:T(8,128)(2,1)S(1)}, u32[]{:S(2)}, u32[]{:S(2)}) collective-permute-start(bf16[1024,384]{1,0:T(8,128)(2,1)S(1)} %shard_map.84.refs_2_), channel_id=1, source_target_pairs={{0,2},{2,0},{4,6},{6,4},{8,10},{10,8},{12,14},{14,12},{16,18},{18,... | collective-permute-start | bytes 2359304 | tf_op jit(solution)/shard_map/ppermute | solution.py:229
  24.7 1.4 %copy-start.3 = (f32[50,384]{1,0:T(8,128)S(1)}, f32[50,384]{1,0:T(8,128)}, u32[]{:S(2)}) copy-start(f32[50,384]{1,0:T(8,128)} %table_ref.1) | copy-start | bytes 230404
  24.7 1.3 %copy-start.5 = (s32[2]{0:T(128)S(1)}, s32[2]{0:T(128)}, u32[]{:S(2)}) copy-start(s32[2]{0:T(128)} %step_ref.1) | copy-start | bytes 28
  25.7 5.0 %collective-permute-start.9 = (bf16[144,384]{1,0:T(8,128)(2,1)S(1)}, bf16[144,384]{1,0:T(8,128)(2,1)S(1)}, u32[]{:S(2)}, u32[]{:S(2)}) collective-permute-start(bf16[144,384]{1,0:T(8,128)(2,1)S(1)} %shard_map.87), channel_id=1, source_target_pairs={{0,8},{2,10},{4,12},{6,14},{8,0},{10,2},{12,4},{14,6},{16,24},{18,... | collective-permute-start | bytes 331784 | tf_op jit(solution)/shard_map/ppermute | solution.py:229

commit v6 on v5

--- a/solution.py
+++ b/solution.py
@@ -33,17 +33,28 @@
     return jnp.sum(part.T, axis=0, keepdims=True)
 
 
-def own_kernel(query_hbm, key_hbm, far_ref, query_out, key_out, sums_out, query_ref, sems):
+def own_kernel(
+    query_hbm,
+    key_hbm,
+    value_hbm,
+    far_hbm,
+    query_out,
+    key_out,
+    value_out,
+    sums_out,
+    query_ref,
+    far_ref,
+    sems,
+):
     rows, width = query_ref.shape
     copies = [
         pltpu.make_async_copy(query_hbm, query_ref, sems.at[0]),
         pltpu.make_async_copy(key_hbm, key_out, sems.at[1]),
+        pltpu.make_async_copy(far_hbm, far_ref, sems.at[2]),
+        pltpu.make_async_copy(value_hbm, value_out, sems.at[3]),
     ]
     for copy in copies:
         copy.start()
-    far = far_ref[...].astype(jnp.float32)
-    far = jnp.concatenate([far, jnp.full((1, HD - far.shape[1]), -1.0)], axis=1)
-    query_out[rows:, :HD] = jnp.broadcast_to(far, (EXTRA, HD)).astype(jnp.bfloat16)
     query_out[rows:, HD:] = jnp.zeros((EXTRA, width - HD), jnp.bfloat16)
     sums_out[...] = jnp.zeros_like(sums_out)
     copies[0].wait()
@@ -51,13 +62,17 @@
     sums_out[0:1, :] = squares(query_ref)
     copies[1].wait()
     sums_out[1:2, :] = squares(key_out)
-
-
-def sums_kernel(own_ref, *refs):
+    copies[2].wait()
+    far = far_ref[...].astype(jnp.float32)
+    far = jnp.concatenate([far, jnp.full((1, HD - far.shape[1]), -1.0)], axis=1)
+    query_out[rows:, :HD] = jnp.broadcast_to(far, (EXTRA, HD)).astype(jnp.bfloat16)
+    copies[3].wait()
+
+
+def sums_kernel(first, before_ref, *refs):
     *sources, out_ref = refs
-    out_ref[...] = jnp.zeros_like(out_ref)
-    out_ref[0:2, :] = own_ref[0:2, :]
-    for place, source_ref in enumerate(sources, start=2):
+    out_ref[...] = before_ref[...]
+    for place, source_ref in enumerate(sources, start=first):
         out_ref[place : place + 1, :] = squares(source_ref)
 
 
@@ -251,35 +266,45 @@
     query_gain = query_gain.reshape(1, width)
     key_gain = key_gain.reshape(1, width)
 
-    query_packet, own_key, own_sums = pl.pallas_call(
+    lines = 2 + 2 ** len(bits)
+    lines += -lines % 8
+    query_packet, own_key, own_value, own_sums = pl.pallas_call(
         own_kernel,
         out_shape=[
             jax.ShapeDtypeStruct((rows + EXTRA, width), jnp.bfloat16),
             jax.ShapeDtypeStruct((rows, width), jnp.bfloat16),
-            jax.ShapeDtypeStruct((8, rows), jnp.float32),
+            jax.ShapeDtypeStruct((rows, width), jnp.bfloat16),
+            jax.ShapeDtypeStruct((lines, rows), jnp.float32),
         ],
-        in_specs=[ANY, ANY, VMEM],
-        out_specs=[VMEM] * 3,
+        in_specs=[ANY] * 4,
+        out_specs=[VMEM] * 4,
         scratch_shapes=[
             pltpu.VMEM((rows, width), jnp.bfloat16),
-            pltpu.SemaphoreType.DMA((2,)),
+            pltpu.VMEM(far_blocks.shape, jnp.int32),
+            pltpu.SemaphoreType.DMA((4,)),
         ],
-    )(query_proj, key_proj, far_blocks)
+    )(query_proj, key_proj, value_proj, far_blocks)
     keys = gathered(key_proj, bits)
     keys[0] = own_key
-    values = gathered(value_proj, bits)
+    values = gathered(own_value, bits)
     queries = [query_packet, exchange(query_packet, query_mask)]
     masks = sorted(keys, key=lambda mask: (mask.bit_count(), mask))
 
-    sources = queries[1:] + [keys[mask] for mask in masks[1:]]
-    lines = len(sources) + 2
-    sums = pl.pallas_call(
-        sums_kernel,
-        out_shape=jax.ShapeDtypeStruct((lines + -lines % 8, rows), jnp.float32),
-        in_specs=[VMEM] * (1 + len(sources)),
-        out_specs=VMEM,
-        compiler_params=params,
-    )(own_sums, *sources)
+    sums = own_sums
+    first = 2
+    near = [mask for mask in masks[1:] if mask.bit_count() == 1]
+    for sources in (
+        queries[1:] + [keys[mask] for mask in near],
+        [keys[mask] for mask in masks[1 + len(near) :]],
+    ):
+        sums = pl.pallas_call(
+            functools.partial(sums_kernel, first),
+            out_shape=jax.ShapeDtypeStruct(own_sums.shape, jnp.float32),
+            in_specs=[VMEM] * (1 + len(sources)),
+            out_specs=VMEM,
+            compiler_params=params,
+        )(sums, *sources)
+        first += len(sources)
     if splits == 2:
         others = lax.ppermute(sums, "head", [(0, 1), (1, 0)])
     else:

time: 31.7 us -> 29.4 us (0.927)
  waiting for transfers between devices: 9.21 us -> 6.17 us
  starting transfers between devices: 13 us -> 14.9 us
  local copies, waits for them, and re-layouts: 1.35 us -> 0.68 us
  Pallas kernels: 7.8 us -> 7.39 us
    ppermute x9, waiting for transfers between devices: 6.98 us -> 5.25 us  [exchange(): return lax.ppermute(array, 'tm', [(i, i ^ mask) for i in range(count)])]
    ppermute x9, starting transfers between devices: 11.6 us -> 13.3 us  [exchange(): return lax.ppermute(array, 'tm', [(i, i ^ mask) for i in range(count)])]
    ppermute x1, waiting for transfers between devices: 2.23 us -> 0.92 us  [local(): others = lax.ppermute(sums, 'head', [(0, 1), (1, 0)])]
    unnamed x18, local copies, waits for them, and re-layouts: 1.35 us -> 0.68 us
    pallas_call x1, Pallas kernels: 2.38 us -> 1.88 us  [local(): pl.pallas_call(own_kernel, out_shape=[jax.ShapeDtypeStruct((rows + EXTRA,...]
  transfers between devices with their start and end apart: 10 -> 10, of which waited for: 4 -> 6; matrix products, arithmetic and copies ran while one was open for 0% -> 0% of each run, Pallas kernels for 18% -> 19%
where the time goes in v6:
time: 29.4 us; the launch traced here: 29.2 us
  starting transfers between devices  14.9 us (51%)
  Pallas kernels  7.39 us (25%)
  waiting for transfers between devices  6.17 us (21%)
  local copies, waits for them, and re-layouts  0.68 us (2%)
    ppermute x9, starting transfers between devices, exchange(): return lax.ppermute(array, 'tm', [(i, i ^ mask) for i in range(count)])  13.3 us
    ppermute x9, waiting for transfers between devices, exchange(): return lax.ppermute(array, 'tm', [(i, i ^ mask) for i in range(count)])  5.25 us
    pallas_call x2, Pallas kernels, last_part(): pl.pallas_call(functools.partial(last_attention, place, place * query_mas...  1.95 us
    pallas_call x1, Pallas kernels, local(): pl.pallas_call(own_kernel, out_shape=[jax.ShapeDtypeStruct((rows + EXTRA,...  1.88 us
    pallas_call x1, Pallas kernels, local(): pl.pallas_call(functools.partial(own_attention, full_width, [0, query_mas...  1.76 us
    ppermute x1, starting transfers between devices, local(): others = lax.ppermute(sums, 'head', [(0, 1), (1, 0)])  1.63 us
    ppermute x1, waiting for transfers between devices, local(): others = lax.ppermute(sums, 'head', [(0, 1), (1, 0)])  0.92 us
    pallas_call x1, Pallas kernels, local(): pl.pallas_call(merge_kernel, out_shape=jax.ShapeDtypeStruct((rows, width)...  0.81 us
  transfers between devices with their start and end apart: 10, of which 6 were waited for; matrix products, arithmetic and copies ran while one was open for 0% of the time, Pallas kernels for 19%

profile of v6, /device:TPU:0, one launch (start us, length us, event | category | flops | bytes accessed | tf_op | source)
XLA Modules:
  0.0 29.2 jit_solution(13690140337717149497)
XLA Ops:
  0.0 0.0 copy-start.6
  0.0 4.0 %collective-permute-start.2 = (bf16[128,384]{1,0:T(8,128)(2,1)}, bf16[128,384]{1,0:T(8,128)(2,1)S(1)}, u32[]{:S(2)}, u32[]{:S(2)}) collective-permute-start(bf16[128,384]{1,0:T(8,128)(2,1)} %key_hbm.1), channel_id=1, source_target_pairs={{0,16},{2,18},{4,20},{6,22},{8,24},{10,26},{12,28},{14,30},{16,0},... | collective-permute-start | bytes 294920 | tf_op jit(solution)/shard_map/ppermute | solution.py:244
  4.0 1.9 %shard_map.82 = (bf16[144,384]{1,0:T(8,128)(2,1)}, bf16[128,384]{1,0:T(8,128)(2,1)}, bf16[128,384]{1,0:T(8,128)(2,1)}, f32[8,128]{1,0:T(8,128)}) custom-call(bf16[128,384]{1,0:T(8,128)(2,1)} %query_hbm.1, bf16[128,384]{1,0:T(8,128)(2,1)} %key_hbm.1, bf16[128,384]{1,0:T(8,128)(2,1)} %value_hbm.1, s32[1,16]{1,0:T(1,128)} %far_hbm.1), custom_call_target="tpu_custom_call" | custom-call | tf_op jit(solution)/shard_map/pallas_call | solution.py:271
  5.9 0.0 copy-start.4
  5.9 0.1 collective-permute-start.6
  6.0 1.9 %collective-permute-start = (bf16[144,384]{1,0:T(8,128)(2,1)}, bf16[144,384]{1,0:T(8,128)(2,1)S(1)}, u32[]{:S(2)}, u32[]{:S(2)}) collective-permute-start(bf16[144,384]{1,0:T(8,128)(2,1)} %get-tuple-element.15.refs_0_.raw_ref), channel_id=1, source_target_pairs={{0,8},{2,10},{4,12},{6,14},{8,0},{10,2},{12,4},{14,6},{16,24},{18,... | collective-permute-start | bytes 331784 | tf_op jit(solution)/shard_map/ppermute | solution.py:244
  7.9 0.0 copy-done.6
  7.9 1.5 %collective-permute-start.1 = (bf16[128,384]{1,0:T(8,128)(2,1)S(1)}, bf16[128,384]{1,0:T(8,128)(2,1)S(1)}, u32[]{:S(2)}, u32[]{:S(2)}) collective-permute-start(bf16[128,384]{1,0:T(8,128)(2,1)S(1)} %copy-done.6), channel_id=1, source_target_pairs={{0,4},{2,6},{4,0},{6,2},{8,12},{10,14},{12,8},{14,10},{16,20},{18,... | collective-permute-start | bytes 294920 | tf_op jit(solution)/shard_map/ppermute | solution.py:244
  9.4 0.0 collective-permute-done.2.refs_2_
  9.4 1.4 %collective-permute-start.3 = (bf16[128,384]{1,0:T(8,128)(2,1)S(1)}, bf16[128,384]{1,0:T(8,128)(2,1)S(1)}, u32[]{:S(2)}, u32[]{:S(2)}) collective-permute-start(bf16[128,384]{1,0:T(8,128)(2,1)S(1)} %collective-permute-done.2.refs_2_), channel_id=1, source_target_pairs={{0,4},{2,6},{4,0},{6,2},{8,12},{10,14},{12,8},{14,10},{16,20},{18,... | collective-permute-start | bytes 294920 | tf_op jit(solution)/shard_map/ppermute | solution.py:244
  10.8 0.6 %collective-permute-start.5 = (bf16[128,384]{1,0:T(8,128)(2,1)}, bf16[128,384]{1,0:T(8,128)(2,1)S(1)}, u32[]{:S(2)}, u32[]{:S(2)}) collective-permute-start(bf16[128,384]{1,0:T(8,128)(2,1)} %get-tuple-element.17.refs_4_), channel_id=1, source_target_pairs={{0,4},{2,6},{4,0},{6,2},{8,12},{10,14},{12,8},{14,10},{16,20},{18,... | collective-permute-start | bytes 294920 | tf_op jit(solution)/shard_map/ppermute | solution.py:244
  11.4 1.7 %collective-permute-done.6.refs_6_ = bf16[128,384]{1,0:T(8,128)(2,1)S(1)} collective-permute-done((bf16[128,384]{1,0:T(8,128)(2,1)}, bf16[128,384]{1,0:T(8,128)(2,1)S(1)}, u32[]{:S(2)}, u32[]{:S(2)}) %collective-permute-start.6) | collective-permute-done | bytes 98336 | tf_op jit(solution)/shard_map/ppermute | solution.py:244
  13.1 1.5 %collective-permute-start.7 = (bf16[128,384]{1,0:T(8,128)(2,1)S(1)}, bf16[128,384]{1,0:T(8,128)(2,1)S(1)}, u32[]{:S(2)}, u32[]{:S(2)}) collective-permute-start(bf16[128,384]{1,0:T(8,128)(2,1)S(1)} %collective-permute-done.6.refs_6_), channel_id=1, source_target_pairs={{0,4},{2,6},{4,0},{6,2},{8,12},{10,14},{12,8},{14,10},{16,20},{18,... | collective-permute-start | bytes 294920 | tf_op jit(solution)/shard_map/ppermute | solution.py:244
  14.6 0.0 collective-permute-done.1.refs_1_
  14.6 0.0 collective-permute-done.refs_0_.refs_1_.raw_ref
  14.6 0.0 copy-done.4
  14.6 0.0 copy-start.2
  14.6 0.1 shard_map.83.before_ref
  14.8 0.0 copy-start.7
  14.8 0.0 copy-start.1
  14.8 0.8 %collective-permute-done.3.refs_0_.refs_3_ = bf16[128,384]{1,0:T(8,128)(2,1)S(1)} collective-permute-done((bf16[128,384]{1,0:T(8,128)(2,1)S(1)}, bf16[128,384]{1,0:T(8,128)(2,1)S(1)}, u32[]{:S(2)}, u32[]{:S(2)}) %collective-permute-start.3) | collective-permute-done | bytes 98336 | tf_op jit(solution)/shard_map/ppermute | solution.py:244
  15.6 0.1 shard_map.84.own_ref
  15.7 1.6 %collective-permute-start.4 = (f32[8,128]{1,0:T(8,128)S(1)}, f32[8,128]{1,0:T(8,128)S(1)}, u32[]{:S(2)}, u32[]{:S(2)}) collective-permute-start(f32[8,128]{1,0:T(8,128)S(1)} %shard_map.84.own_ref), channel_id=1, source_target_pairs={{0,1},{1,0},{2,3},{3,2},{4,5},{5,4},{6,7},{7,6},{8,9},{9,8},{10,11... | collective-permute-start | bytes 12296 | tf_op jit(solution)/shard_map/ppermute | solution.py:309
  17.3 0.0 copy-done.7
  17.3 0.1 collective-permute-done.5.refs_5_
  17.4 1.1 %collective-permute-done.7.refs_7_ = bf16[128,384]{1,0:T(8,128)(2,1)S(1)} collective-permute-done((bf16[128,384]{1,0:T(8,128)(2,1)S(1)}, bf16[128,384]{1,0:T(8,128)(2,1)S(1)}, u32[]{:S(2)}, u32[]{:S(2)}) %collective-permute-start.7) | collective-permute-done | bytes 98336 | tf_op jit(solution)/shard_map/ppermute | solution.py:244
  18.5 0.9 %collective-permute-done.4.other_ref = f32[8,128]{1,0:T(8,128)S(1)} collective-permute-done((f32[8,128]{1,0:T(8,128)S(1)}, f32[8,128]{1,0:T(8,128)S(1)}, u32[]{:S(2)}, u32[]{:S(2)}) %collective-permute-start.4) | collective-permute-done | bytes 4128 | tf_op jit(solution)/shard_map/ppermute | solution.py:309
  19.4 0.0 copy-done.2
  19.4 0.0 copy-done.1
  19.4 0.0 copy-start.8
  19.4 0.0 copy-start
  19.4 0.2 shard_map.85.refs_2_
  19.6 0.1 collective-permute-start.8
  19.7 0.4 %copy-done.8 = f32[384]{0:T(512)S(1)} copy-done((f32[384]{0:T(512)S(1)}, f32[384]{0:T(512)}, u32[]{:S(2)}) %copy-start.8) | copy-done | bytes 1560
  20.1 0.2 copy-done
  20.3 1.8 %shard_map.86 = (bf16[256,384]{1,0:T(8,128)(2,1)S(1)}, f32[256,384]{1,0:T(8,128)S(1)}, f32[256,768]{1,0:T(8,128)S(1)}) custom-call(f32[1,384]{1,0:T(1,128)S(1)} %reshape.6.gain_ref, f32[8,128]{1,0:T(8,128)S(1)} %shard_map.84.own_ref, f32[8,128]{1,0:T(8,128)S(1)} %collective-permute-done.4.other_ref, bf16[144,384]{1,0:T(8,128)(2,1)S(1)} %copy-done, ...), custom_call_target="tpu_custom_call" | custom-call | tf_op jit(solution)/shard_map/pallas_call | solution.py:329
  22.1 0.0 collective-permute-done.8.refs_0_
  22.1 0.0 copy-start.3
  22.1 0.0 copy-start.5
  22.1 1.0 %shard_map.88 = bf16[144,384]{1,0:T(8,128)(2,1)S(1)} custom-call(bf16[256,384]{1,0:T(8,128)(2,1)S(1)} %get-tuple-element.18.query_ref, bf16[144,384]{1,0:T(8,128)(2,1)S(1)} %collective-permute-done.refs_0_.refs_1_.raw_ref, bf16[1024,384]{1,0:T(8,128)(2,1)S(1)} %collective-permute-done.8.refs_0_, f32[256,384]{1,0:T(8,128)S(1)} %get-tuple-element.19.refs_1_, ...), custom_call_target="tpu_custom_call" | custom-call | tf_op jit(solution)/shard_map/pallas_call | solution.py:342
  23.1 2.2 %collective-permute-start.9 = (bf16[144,384]{1,0:T(8,128)(2,1)S(1)}, bf16[144,384]{1,0:T(8,128)(2,1)S(1)}, u32[]{:S(2)}, u32[]{:S(2)}) collective-permute-start(bf16[144,384]{1,0:T(8,128)(2,1)S(1)} %shard_map.88), channel_id=1, source_target_pairs={{0,8},{2,10},{4,12},{6,14},{8,0},{10,2},{12,4},{14,6},{16,24},{18,... | collective-permute-start | bytes 331784 | tf_op jit(solution)/shard_map/ppermute | solution.py:244
  25.2 0.0 copy-done.3
  25.2 0.0 copy-done.5
  25.3 0.6 %shard_map.89.gate_ref = f32[16,384]{1,0:T(8,128)S(1)} custom-call(s32[2]{0:T(128)S(1)} %copy-done.5, f32[50,384]{1,0:T(8,128)S(1)} %copy-done.3), custom_call_target="tpu_custom_call" | custom-call | tf_op jit(solution)/shard_map/pallas_call | solution.py:360
  25.8 1.0 %shard_map.87 = (f32[128,384]{1,0:T(8,128)S(1)}, f32[8,384]{1,0:T(8,128)S(1)}) custom-call(bf16[256,384]{1,0:T(8,128)(2,1)S(1)} %get-tuple-element.18.query_ref, bf16[144,384]{1,0:T(8,128)(2,1)S(1)} %copy-done, bf16[1024,384]{1,0:T(8,128)(2,1)S(1)} %collective-permute-done.8.refs_0_, f32[256,384]{1,0:T(8,128)S(1)} %get-tuple-element.19.refs_1_, ...), custom_call_target="tpu_custom_call" | custom-call | tf_op jit(solution)/shard_map/pallas_call | solution.py:342
  26.8 1.6 %collective-permute-done.9.packet_ref = bf16[144,384]{1,0:T(8,128)(2,1)S(1)} collective-permute-done((bf16[144,384]{1,0:T(8,128)(2,1)S(1)}, bf16[144,384]{1,0:T(8,128)(2,1)S(1)}, u32[]{:S(2)}, u32[]{:S(2)}) %collective-permute-start.9) | collective-permute-done | bytes 110624 | tf_op jit(solution)/shard_map/ppermute | solution.py:244
  28.4 0.8 %shard_map.90 = bf16[128,384]{1,0:T(8,128)(2,1)} custom-call(f32[128,384]{1,0:T(8,128)S(1)} %get-tuple-element.21.own_ref, f32[8,384]{1,0:T(8,128)S(1)} %get-tuple-element.22.logs_ref, bf16[144,384]{1,0:T(8,128)(2,1)S(1)} %collective-permute-done.9.packet_ref, f32[16,384]{1,0:T(8,128)S(1)} %shard_map.89.gate_ref), custom_call_target="tpu_custom_call" | custom-call | tf_op jit(solution)/shard_map/pallas_call | solution.py:369
  (2 shorter events, 0.0 us)
Async XLA Ops:
  0.0 7.9 %copy-start.6 = (bf16[128,384]{1,0:T(8,128)(2,1)S(1)}, bf16[128,384]{1,0:T(8,128)(2,1)}, u32[]{:S(2)}) copy-start(bf16[128,384]{1,0:T(8,128)(2,1)} %key_hbm.1) | copy-start | bytes 294916
  0.0 9.4 %collective-permute-start.2 = (bf16[128,384]{1,0:T(8,128)(2,1)}, bf16[128,384]{1,0:T(8,128)(2,1)S(1)}, u32[]{:S(2)}, u32[]{:S(2)}) collective-permute-start(bf16[128,384]{1,0:T(8,128)(2,1)} %key_hbm.1), channel_id=1, source_target_pairs={{0,16},{2,18},{4,20},{6,22},{8,24},{10,26},{12,28},{14,30},{16,0},... | collective-permute-start | bytes 294920 | tf_op jit(solution)/shard_map/ppermute | solution.py:244
  5.9 8.7 %copy-start.4 = (f32[8,128]{1,0:T(8,128)S(1)}, f32[8,128]{1,0:T(8,128)}, u32[]{:S(2)}) copy-start(f32[8,128]{1,0:T(8,128)} %get-tuple-element.14.before_ref) | copy-start | bytes 12292
  5.9 7.2 %collective-permute-start.6 = (bf16[128,384]{1,0:T(8,128)(2,1)}, bf16[128,384]{1,0:T(8,128)(2,1)S(1)}, u32[]{:S(2)}, u32[]{:S(2)}) collective-permute-start(bf16[128,384]{1,0:T(8,128)(2,1)} %get-tuple-element.17.refs_4_), channel_id=1, source_target_pairs={{0,16},{2,18},{4,20},{6,22},{8,24},{10,26},{12,28},{14,30},{16,0},... | collective-permute-start | bytes 294920 | tf_op jit(solution)/shard_map/ppermute | solution.py:244
  6.0 8.6 %collective-permute-start = (bf16[144,384]{1,0:T(8,128)(2,1)}, bf16[144,384]{1,0:T(8,128)(2,1)S(1)}, u32[]{:S(2)}, u32[]{:S(2)}) collective-permute-start(bf16[144,384]{1,0:T(8,128)(2,1)} %get-tuple-element.15.refs_0_.raw_ref), channel_id=1, source_target_pairs={{0,8},{2,10},{4,12},{6,14},{8,0},{10,2},{12,4},{14,6},{16,24},{18,... | collective-permute-start | bytes 331784 | tf_op jit(solution)/shard_map/ppermute | solution.py:244
  7.9 6.7 %collective-permute-start.1 = (bf16[128,384]{1,0:T(8,128)(2,1)S(1)}, bf16[128,384]{1,0:T(8,128)(2,1)S(1)}, u32[]{:S(2)}, u32[]{:S(2)}) collective-permute-start(bf16[128,384]{1,0:T(8,128)(2,1)S(1)} %copy-done.6), channel_id=1, source_target_pairs={{0,4},{2,6},{4,0},{6,2},{8,12},{10,14},{12,8},{14,10},{16,20},{18,... | collective-permute-start | bytes 294920 | tf_op jit(solution)/shard_map/ppermute | solution.py:244
  9.4 6.2 %collective-permute-start.3 = (bf16[128,384]{1,0:T(8,128)(2,1)S(1)}, bf16[128,384]{1,0:T(8,128)(2,1)S(1)}, u32[]{:S(2)}, u32[]{:S(2)}) collective-permute-start(bf16[128,384]{1,0:T(8,128)(2,1)S(1)} %collective-permute-done.2.refs_2_), channel_id=1, source_target_pairs={{0,4},{2,6},{4,0},{6,2},{8,12},{10,14},{12,8},{14,10},{16,20},{18,... | collective-permute-start | bytes 294920 | tf_op jit(solution)/shard_map/ppermute | solution.py:244
  10.8 6.6 %collective-permute-start.5 = (bf16[128,384]{1,0:T(8,128)(2,1)}, bf16[128,384]{1,0:T(8,128)(2,1)S(1)}, u32[]{:S(2)}, u32[]{:S(2)}) collective-permute-start(bf16[128,384]{1,0:T(8,128)(2,1)} %get-tuple-element.17.refs_4_), channel_id=1, source_target_pairs={{0,4},{2,6},{4,0},{6,2},{8,12},{10,14},{12,8},{14,10},{16,20},{18,... | collective-permute-start | bytes 294920 | tf_op jit(solution)/shard_map/ppermute | solution.py:244
  13.1 5.4 %collective-permute-start.7 = (bf16[128,384]{1,0:T(8,128)(2,1)S(1)}, bf16[128,384]{1,0:T(8,128)(2,1)S(1)}, u32[]{:S(2)}, u32[]{:S(2)}) collective-permute-start(bf16[128,384]{1,0:T(8,128)(2,1)S(1)} %collective-permute-done.6.refs_6_), channel_id=1, source_target_pairs={{0,4},{2,6},{4,0},{6,2},{8,12},{10,14},{12,8},{14,10},{16,20},{18,... | collective-permute-start | bytes 294920 | tf_op jit(solution)/shard_map/ppermute | solution.py:244
  14.6 4.8 %copy-start.2 = (bf16[128,384]{1,0:T(8,128)(2,1)S(1)}, bf16[128,384]{1,0:T(8,128)(2,1)}, u32[]{:S(2)}) copy-start(bf16[128,384]{1,0:T(8,128)(2,1)} %get-tuple-element.17.refs_4_) | copy-start | bytes 294916
  14.8 2.6 %copy-start.7 = (f32[384]{0:T(512)S(1)}, f32[384]{0:T(512)}, u32[]{:S(2)}) copy-start(f32[384]{0:T(512)} %param.12) | copy-start | bytes 4612
  14.8 4.6 %copy-start.1 = (bf16[128,384]{1,0:T(8,128)(2,1)S(1)}, bf16[128,384]{1,0:T(8,128)(2,1)}, u32[]{:S(2)}) copy-start(bf16[128,384]{1,0:T(8,128)(2,1)} %get-tuple-element.16.refs_0_) | copy-start | bytes 294916
  15.7 3.7 %collective-permute-start.4 = (f32[8,128]{1,0:T(8,128)S(1)}, f32[8,128]{1,0:T(8,128)S(1)}, u32[]{:S(2)}, u32[]{:S(2)}) collective-permute-start(f32[8,128]{1,0:T(8,128)S(1)} %shard_map.84.own_ref), channel_id=1, source_target_pairs={{0,1},{1,0},{2,3},{3,2},{4,5},{5,4},{6,7},{7,6},{8,9},{9,8},{10,11... | collective-permute-start | bytes 12296 | tf_op jit(solution)/shard_map/ppermute | solution.py:309
  19.4 0.7 %copy-start.8 = (f32[384]{0:T(512)S(1)}, f32[384]{0:T(512)}, u32[]{:S(2)}) copy-start(f32[384]{0:T(512)} %param.11) | copy-start | bytes 4612
  19.4 0.9 %copy-start = (bf16[144,384]{1,0:T(8,128)(2,1)S(1)}, bf16[144,384]{1,0:T(8,128)(2,1)}, u32[]{:S(2)}) copy-start(bf16[144,384]{1,0:T(8,128)(2,1)} %get-tuple-element.15.refs_0_.raw_ref) | copy-start | bytes 331780
  19.6 2.5 %collective-permute-start.8 = (bf16[1024,384]{1,0:T(8,128)(2,1)S(1)}, bf16[1024,384]{1,0:T(8,128)(2,1)S(1)}, u32[]{:S(2)}, u32[]{:S(2)}) collective-permute-start(bf16[1024,384]{1,0:T(8,128)(2,1)S(1)} %shard_map.85.refs_2_), channel_id=1, source_target_pairs={{0,2},{2,0},{4,6},{6,4},{8,10},{10,8},{12,14},{14,12},{16,18},{18,... | collective-permute-start | bytes 2359304 | tf_op jit(solution)/shard_map/ppermute | solution.py:244
  22.1 3.2 %copy-start.3 = (f32[50,384]{1,0:T(8,128)S(1)}, f32[50,384]{1,0:T(8,128)}, u32[]{:S(2)}) copy-start(f32[50,384]{1,0:T(8,128)} %table_ref.1) | copy-start | bytes 230404
  22.1 3.2 %copy-start.5 = (s32[2]{0:T(128)S(1)}, s32[2]{0:T(128)}, u32[]{:S(2)}) copy-start(s32[2]{0:T(128)} %step_ref.1) | copy-start | bytes 28
  23.1 5.4 %collective-permute-start.9 = (bf16[144,384]{1,0:T(8,128)(2,1)S(1)}, bf16[144,384]{1,0:T(8,128)(2,1)S(1)}, u32[]{:S(2)}, u32[]{:S(2)}) collective-permute-start(bf16[144,384]{1,0:T(8,128)(2,1)S(1)} %shard_map.88), channel_id=1, source_target_pairs={{0,8},{2,10},{4,12},{6,14},{8,0},{10,2},{12,4},{14,6},{16,24},{18,... | collective-permute-start | bytes 331784 | tf_op jit(solution)/shard_map/ppermute | solution.py:244

commit v7 on v6

--- a/solution.py
+++ b/solution.py
@@ -260,9 +260,8 @@
     splits = lax.axis_size("head")
     full_width = width * splits
     params = pltpu.CompilerParams(vmem_limit_bytes=(8 + count // 2) * 2**20)
-    query_mask = count // 4
-    bits = [1 << place for place in range(1, count.bit_length() - 1)]
-    bits = [bit for bit in bits[::-1] if bit != query_mask]
+    query_mask = count // 2
+    bits = [1 << place for place in range(1, count.bit_length() - 2)]
     query_gain = query_gain.reshape(1, width)
     key_gain = key_gain.reshape(1, width)
 
@@ -284,7 +283,7 @@
             pltpu.SemaphoreType.DMA((4,)),
         ],
     )(query_proj, key_proj, value_proj, far_blocks)
-    keys = gathered(key_proj, bits)
+    keys = gathered(key_proj, bits[::-1])
     keys[0] = own_key
     values = gathered(own_value, bits)
     queries = [query_packet, exchange(query_packet, query_mask)]

time: 29.4 us -> 31.5 us (1.071)
  waiting for transfers between devices: 6.17 us -> 8.77 us
  starting transfers between devices: 14.9 us -> 14.4 us
    ppermute x9, waiting for transfers between devices: 5.25 us -> 8.41 us  [exchange(): return lax.ppermute(array, 'tm', [(i, i ^ mask) for i in range(count)])]
    ppermute x1, waiting for transfers between devices: 0.92 us -> 0.36 us  [local(): others = lax.ppermute(sums, 'head', [(0, 1), (1, 0)])]
    ppermute x9, starting transfers between devices: 13.3 us -> 12.8 us  [exchange(): return lax.ppermute(array, 'tm', [(i, i ^ mask) for i in range(count)])]
  transfers between devices with their start and end apart: 10 -> 10, of which waited for: 6 -> 7; matrix products, arithmetic and copies ran while one was open for 0% -> 0% of each run, Pallas kernels for 19% -> 17%
where the time goes in v7:
time: 31.5 us; the launch traced here: 31.3 us
  starting transfers between devices  14.4 us (46%)
  waiting for transfers between devices  8.77 us (28%)
  Pallas kernels  7.39 us (23%)
  local copies, waits for them, and re-layouts  0.68 us (2%)
    ppermute x9, starting transfers between devices, exchange(): return lax.ppermute(array, 'tm', [(i, i ^ mask) for i in range(count)])  12.8 us
    ppermute x9, waiting for transfers between devices, exchange(): return lax.ppermute(array, 'tm', [(i, i ^ mask) for i in range(count)])  8.41 us
    pallas_call x2, Pallas kernels, last_part(): pl.pallas_call(functools.partial(last_attention, place, place * query_mas...  1.95 us
    pallas_call x1, Pallas kernels, local(): pl.pallas_call(own_kernel, out_shape=[jax.ShapeDtypeStruct((rows + EXTRA,...  1.88 us
    pallas_call x1, Pallas kernels, local(): pl.pallas_call(functools.partial(own_attention, full_width, [0, query_mas...  1.76 us
    ppermute x1, starting transfers between devices, local(): others = lax.ppermute(sums, 'head', [(0, 1), (1, 0)])  1.58 us
    pallas_call x1, Pallas kernels, local(): pl.pallas_call(merge_kernel, out_shape=jax.ShapeDtypeStruct((rows, width)...  0.81 us
    unnamed x18, local copies, waits for them, and re-layouts  0.67 us
  transfers between devices with their start and end apart: 10, of which 7 were waited for; matrix products, arithmetic and copies ran while one was open for 0% of the time, Pallas kernels for 17%

profile of v7, /device:TPU:0, one launch (start us, length us, event | category | flops | bytes accessed | tf_op | source)
XLA Modules:
  0.0 31.3 jit_solution(8045905076270747071)
XLA Ops:
  0.0 0.0 copy-start.6
  0.0 3.0 %collective-permute-start.2 = (bf16[128,384]{1,0:T(8,128)(2,1)}, bf16[128,384]{1,0:T(8,128)(2,1)S(1)}, u32[]{:S(2)}, u32[]{:S(2)}) collective-permute-start(bf16[128,384]{1,0:T(8,128)(2,1)} %key_hbm.1), channel_id=1, source_target_pairs={{0,8},{2,10},{4,12},{6,14},{8,0},{10,2},{12,4},{14,6},{16,24},{18,... | collective-permute-start | bytes 294920 | tf_op jit(solution)/shard_map/ppermute | solution.py:244
  3.0 1.9 %shard_map.82 = (bf16[144,384]{1,0:T(8,128)(2,1)}, bf16[128,384]{1,0:T(8,128)(2,1)}, bf16[128,384]{1,0:T(8,128)(2,1)}, f32[8,128]{1,0:T(8,128)}) custom-call(bf16[128,384]{1,0:T(8,128)(2,1)} %query_hbm.1, bf16[128,384]{1,0:T(8,128)(2,1)} %key_hbm.1, bf16[128,384]{1,0:T(8,128)(2,1)} %value_hbm.1, s32[1,16]{1,0:T(1,128)} %far_hbm.1), custom_call_target="tpu_custom_call" | custom-call | tf_op jit(solution)/shard_map/pallas_call | solution.py:270
  4.9 0.0 copy-start.4
  4.9 1.6 %collective-permute-start.5 = (bf16[128,384]{1,0:T(8,128)(2,1)}, bf16[128,384]{1,0:T(8,128)(2,1)S(1)}, u32[]{:S(2)}, u32[]{:S(2)}) collective-permute-start(bf16[128,384]{1,0:T(8,128)(2,1)} %get-tuple-element.17.refs_4_), channel_id=1, source_target_pairs={{0,4},{2,6},{4,0},{6,2},{8,12},{10,14},{12,8},{14,10},{16,20},{18,... | collective-permute-start | bytes 294920 | tf_op jit(solution)/shard_map/ppermute | solution.py:244
  6.5 2.6 %collective-permute-start = (bf16[144,384]{1,0:T(8,128)(2,1)}, bf16[144,384]{1,0:T(8,128)(2,1)S(1)}, u32[]{:S(2)}, u32[]{:S(2)}) collective-permute-start(bf16[144,384]{1,0:T(8,128)(2,1)} %get-tuple-element.15.refs_0_.raw_ref), channel_id=1, source_target_pairs={{0,16},{2,18},{4,20},{6,22},{8,24},{10,26},{12,28},{14,30},{16,0},... | collective-permute-start | bytes 331784 | tf_op jit(solution)/shard_map/ppermute | solution.py:244
  9.1 0.0 copy-done.6
  9.1 0.5 %collective-permute-start.1 = (bf16[128,384]{1,0:T(8,128)(2,1)S(1)}, bf16[128,384]{1,0:T(8,128)(2,1)S(1)}, u32[]{:S(2)}, u32[]{:S(2)}) collective-permute-start(bf16[128,384]{1,0:T(8,128)(2,1)S(1)} %copy-done.6), channel_id=1, source_target_pairs={{0,4},{2,6},{4,0},{6,2},{8,12},{10,14},{12,8},{14,10},{16,20},{18,... | collective-permute-start | bytes 294920 | tf_op jit(solution)/shard_map/ppermute | solution.py:244
  9.6 0.0 collective-permute-done.2.refs_2_
  9.6 1.5 %collective-permute-start.3 = (bf16[128,384]{1,0:T(8,128)(2,1)S(1)}, bf16[128,384]{1,0:T(8,128)(2,1)S(1)}, u32[]{:S(2)}, u32[]{:S(2)}) collective-permute-start(bf16[128,384]{1,0:T(8,128)(2,1)S(1)} %collective-permute-done.2.refs_2_), channel_id=1, source_target_pairs={{0,4},{2,6},{4,0},{6,2},{8,12},{10,14},{12,8},{14,10},{16,20},{18,... | collective-permute-start | bytes 294920 | tf_op jit(solution)/shard_map/ppermute | solution.py:244
  11.1 0.4 %collective-permute-start.6 = (bf16[128,384]{1,0:T(8,128)(2,1)}, bf16[128,384]{1,0:T(8,128)(2,1)S(1)}, u32[]{:S(2)}, u32[]{:S(2)}) collective-permute-start(bf16[128,384]{1,0:T(8,128)(2,1)} %get-tuple-element.17.refs_4_), channel_id=1, source_target_pairs={{0,8},{2,10},{4,12},{6,14},{8,0},{10,2},{12,4},{14,6},{16,24},{18,... | collective-permute-start | bytes 294920 | tf_op jit(solution)/shard_map/ppermute | solution.py:244
  11.6 0.0 collective-permute-done.5.refs_5_
  11.6 1.6 %collective-permute-start.7 = (bf16[128,384]{1,0:T(8,128)(2,1)S(1)}, bf16[128,384]{1,0:T(8,128)(2,1)S(1)}, u32[]{:S(2)}, u32[]{:S(2)}) collective-permute-start(bf16[128,384]{1,0:T(8,128)(2,1)S(1)} %collective-permute-done.5.refs_5_), channel_id=1, source_target_pairs={{0,8},{2,10},{4,12},{6,14},{8,0},{10,2},{12,4},{14,6},{16,24},{18,... | collective-permute-start | bytes 294920 | tf_op jit(solution)/shard_map/ppermute | solution.py:244
  13.1 0.7 %collective-permute-done.1.refs_1_ = bf16[128,384]{1,0:T(8,128)(2,1)S(1)} collective-permute-done((bf16[128,384]{1,0:T(8,128)(2,1)S(1)}, bf16[128,384]{1,0:T(8,128)(2,1)S(1)}, u32[]{:S(2)}, u32[]{:S(2)}) %collective-permute-start.1) | collective-permute-done | bytes 98336 | tf_op jit(solution)/shard_map/ppermute | solution.py:244
  13.8 0.4 %collective-permute-done.refs_0_.refs_1_.raw_ref = bf16[144,384]{1,0:T(8,128)(2,1)S(1)} collective-permute-done((bf16[144,384]{1,0:T(8,128)(2,1)}, bf16[144,384]{1,0:T(8,128)(2,1)S(1)}, u32[]{:S(2)}, u32[]{:S(2)}) %collective-permute-start) | collective-permute-done | bytes 110624 | tf_op jit(solution)/shard_map/ppermute | solution.py:244
  14.2 0.0 copy-done.4
  14.2 0.0 copy-start.2
  14.2 0.1 shard_map.83.before_ref
  14.3 0.0 copy-start.7
  14.3 0.0 copy-start.1
  14.4 0.5 %collective-permute-done.3.refs_0_.refs_3_ = bf16[128,384]{1,0:T(8,128)(2,1)S(1)} collective-permute-done((bf16[128,384]{1,0:T(8,128)(2,1)S(1)}, bf16[128,384]{1,0:T(8,128)(2,1)S(1)}, u32[]{:S(2)}, u32[]{:S(2)}) %collective-permute-start.3) | collective-permute-done | bytes 98336 | tf_op jit(solution)/shard_map/ppermute | solution.py:244
  14.9 0.1 shard_map.84.own_ref
  15.0 1.6 %collective-permute-start.4 = (f32[8,128]{1,0:T(8,128)S(1)}, f32[8,128]{1,0:T(8,128)S(1)}, u32[]{:S(2)}, u32[]{:S(2)}) collective-permute-start(f32[8,128]{1,0:T(8,128)S(1)} %shard_map.84.own_ref), channel_id=1, source_target_pairs={{0,1},{1,0},{2,3},{3,2},{4,5},{5,4},{6,7},{7,6},{8,9},{9,8},{10,11... | collective-permute-start | bytes 12296 | tf_op jit(solution)/shard_map/ppermute | solution.py:308
  16.6 0.0 copy-done.7
  16.6 0.5 %collective-permute-done.6.refs_6_ = bf16[128,384]{1,0:T(8,128)(2,1)S(1)} collective-permute-done((bf16[128,384]{1,0:T(8,128)(2,1)}, bf16[128,384]{1,0:T(8,128)(2,1)S(1)}, u32[]{:S(2)}, u32[]{:S(2)}) %collective-permute-start.6) | collective-permute-done | bytes 98336 | tf_op jit(solution)/shard_map/ppermute | solution.py:244
  17.0 1.3 %collective-permute-done.7.refs_7_ = bf16[128,384]{1,0:T(8,128)(2,1)S(1)} collective-permute-done((bf16[128,384]{1,0:T(8,128)(2,1)S(1)}, bf16[128,384]{1,0:T(8,128)(2,1)S(1)}, u32[]{:S(2)}, u32[]{:S(2)}) %collective-permute-start.7) | collective-permute-done | bytes 98336 | tf_op jit(solution)/shard_map/ppermute | solution.py:244
  18.3 0.4 %collective-permute-done.4.other_ref = f32[8,128]{1,0:T(8,128)S(1)} collective-permute-done((f32[8,128]{1,0:T(8,128)S(1)}, f32[8,128]{1,0:T(8,128)S(1)}, u32[]{:S(2)}, u32[]{:S(2)}) %collective-permute-start.4) | collective-permute-done | bytes 4128 | tf_op jit(solution)/shard_map/ppermute | solution.py:308
  18.7 0.0 copy-done.2
  18.7 0.0 copy-done.1
  18.7 0.0 copy-start.8
  18.7 0.0 copy-start
  18.7 0.2 shard_map.85.refs_2_
  18.9 0.1 collective-permute-start.8
  18.9 0.4 %copy-done.8 = f32[384]{0:T(512)S(1)} copy-done((f32[384]{0:T(512)S(1)}, f32[384]{0:T(512)}, u32[]{:S(2)}) %copy-start.8) | copy-done | bytes 1560
  19.3 0.2 copy-done
  19.6 1.8 %shard_map.86 = (bf16[256,384]{1,0:T(8,128)(2,1)S(1)}, f32[256,384]{1,0:T(8,128)S(1)}, f32[256,768]{1,0:T(8,128)S(1)}) custom-call(f32[1,384]{1,0:T(1,128)S(1)} %reshape.6.gain_ref, f32[8,128]{1,0:T(8,128)S(1)} %shard_map.84.own_ref, f32[8,128]{1,0:T(8,128)S(1)} %collective-permute-done.4.other_ref, bf16[144,384]{1,0:T(8,128)(2,1)S(1)} %copy-done, ...), custom_call_target="tpu_custom_call" | custom-call | tf_op jit(solution)/shard_map/pallas_call | solution.py:328
  21.3 0.0 collective-permute-done.8.refs_0_
  21.3 0.0 copy-start.3
  21.4 0.0 copy-start.5
  21.4 1.0 %shard_map.88 = bf16[144,384]{1,0:T(8,128)(2,1)S(1)} custom-call(bf16[256,384]{1,0:T(8,128)(2,1)S(1)} %get-tuple-element.18.query_ref, bf16[144,384]{1,0:T(8,128)(2,1)S(1)} %collective-permute-done.refs_0_.refs_1_.raw_ref, bf16[1024,384]{1,0:T(8,128)(2,1)S(1)} %collective-permute-done.8.refs_0_, f32[256,384]{1,0:T(8,128)S(1)} %get-tuple-element.19.refs_1_, ...), custom_call_target="tpu_custom_call" | custom-call | tf_op jit(solution)/shard_map/pallas_call | solution.py:341
  22.4 1.5 %collective-permute-start.9 = (bf16[144,384]{1,0:T(8,128)(2,1)S(1)}, bf16[144,384]{1,0:T(8,128)(2,1)S(1)}, u32[]{:S(2)}, u32[]{:S(2)}) collective-permute-start(bf16[144,384]{1,0:T(8,128)(2,1)S(1)} %shard_map.88), channel_id=1, source_target_pairs={{0,16},{2,18},{4,20},{6,22},{8,24},{10,26},{12,28},{14,30},{16,0},... | collective-permute-start | bytes 331784 | tf_op jit(solution)/shard_map/ppermute | solution.py:244
  23.8 0.0 copy-done.3
  23.8 0.0 copy-done.5
  23.8 0.6 %shard_map.89.gate_ref = f32[16,384]{1,0:T(8,128)S(1)} custom-call(s32[2]{0:T(128)S(1)} %copy-done.5, f32[50,384]{1,0:T(8,128)S(1)} %copy-done.3), custom_call_target="tpu_custom_call" | custom-call | tf_op jit(solution)/shard_map/pallas_call | solution.py:359
  24.4 1.0 %shard_map.87 = (f32[128,384]{1,0:T(8,128)S(1)}, f32[8,384]{1,0:T(8,128)S(1)}) custom-call(bf16[256,384]{1,0:T(8,128)(2,1)S(1)} %get-tuple-element.18.query_ref, bf16[144,384]{1,0:T(8,128)(2,1)S(1)} %copy-done, bf16[1024,384]{1,0:T(8,128)(2,1)S(1)} %collective-permute-done.8.refs_0_, f32[256,384]{1,0:T(8,128)S(1)} %get-tuple-element.19.refs_1_, ...), custom_call_target="tpu_custom_call" | custom-call | tf_op jit(solution)/shard_map/pallas_call | solution.py:341
  25.4 5.1 %collective-permute-done.9.packet_ref = bf16[144,384]{1,0:T(8,128)(2,1)S(1)} collective-permute-done((bf16[144,384]{1,0:T(8,128)(2,1)S(1)}, bf16[144,384]{1,0:T(8,128)(2,1)S(1)}, u32[]{:S(2)}, u32[]{:S(2)}) %collective-permute-start.9) | collective-permute-done | bytes 110624 | tf_op jit(solution)/shard_map/ppermute | solution.py:244
  30.5 0.8 %shard_map.90 = bf16[128,384]{1,0:T(8,128)(2,1)} custom-call(f32[128,384]{1,0:T(8,128)S(1)} %get-tuple-element.21.own_ref, f32[8,384]{1,0:T(8,128)S(1)} %get-tuple-element.22.logs_ref, bf16[144,384]{1,0:T(8,128)(2,1)S(1)} %collective-permute-done.9.packet_ref, f32[16,384]{1,0:T(8,128)S(1)} %shard_map.89.gate_ref), custom_call_target="tpu_custom_call" | custom-call | tf_op jit(solution)/shard_map/pallas_call | solution.py:368
  (2 shorter events, 0.0 us)
Async XLA Ops:
  0.0 9.1 %copy-start.6 = (bf16[128,384]{1,0:T(8,128)(2,1)S(1)}, bf16[128,384]{1,0:T(8,128)(2,1)}, u32[]{:S(2)}) copy-start(bf16[128,384]{1,0:T(8,128)(2,1)} %key_hbm.1) | copy-start | bytes 294916
  0.0 9.6 %collective-permute-start.2 = (bf16[128,384]{1,0:T(8,128)(2,1)}, bf16[128,384]{1,0:T(8,128)(2,1)S(1)}, u32[]{:S(2)}, u32[]{:S(2)}) collective-permute-start(bf16[128,384]{1,0:T(8,128)(2,1)} %key_hbm.1), channel_id=1, source_target_pairs={{0,8},{2,10},{4,12},{6,14},{8,0},{10,2},{12,4},{14,6},{16,24},{18,... | collective-permute-start | bytes 294920 | tf_op jit(solution)/shard_map/ppermute | solution.py:244
  4.9 9.3 %copy-start.4 = (f32[8,128]{1,0:T(8,128)S(1)}, f32[8,128]{1,0:T(8,128)}, u32[]{:S(2)}) copy-start(f32[8,128]{1,0:T(8,128)} %get-tuple-element.14.before_ref) | copy-start | bytes 12292
  4.9 6.6 %collective-permute-start.5 = (bf16[128,384]{1,0:T(8,128)(2,1)}, bf16[128,384]{1,0:T(8,128)(2,1)S(1)}, u32[]{:S(2)}, u32[]{:S(2)}) collective-permute-start(bf16[128,384]{1,0:T(8,128)(2,1)} %get-tuple-element.17.refs_4_), channel_id=1, source_target_pairs={{0,4},{2,6},{4,0},{6,2},{8,12},{10,14},{12,8},{14,10},{16,20},{18,... | collective-permute-start | bytes 294920 | tf_op jit(solution)/shard_map/ppermute | solution.py:244
  6.5 7.7 %collective-permute-start = (bf16[144,384]{1,0:T(8,128)(2,1)}, bf16[144,384]{1,0:T(8,128)(2,1)S(1)}, u32[]{:S(2)}, u32[]{:S(2)}) collective-permute-start(bf16[144,384]{1,0:T(8,128)(2,1)} %get-tuple-element.15.refs_0_.raw_ref), channel_id=1, source_target_pairs={{0,16},{2,18},{4,20},{6,22},{8,24},{10,26},{12,28},{14,30},{16,0},... | collective-permute-start | bytes 331784 | tf_op jit(solution)/shard_map/ppermute | solution.py:244
  9.1 4.7 %collective-permute-start.1 = (bf16[128,384]{1,0:T(8,128)(2,1)S(1)}, bf16[128,384]{1,0:T(8,128)(2,1)S(1)}, u32[]{:S(2)}, u32[]{:S(2)}) collective-permute-start(bf16[128,384]{1,0:T(8,128)(2,1)S(1)} %copy-done.6), channel_id=1, source_target_pairs={{0,4},{2,6},{4,0},{6,2},{8,12},{10,14},{12,8},{14,10},{16,20},{18,... | collective-permute-start | bytes 294920 | tf_op jit(solution)/shard_map/ppermute | solution.py:244
  9.6 5.3 %collective-permute-start.3 = (bf16[128,384]{1,0:T(8,128)(2,1)S(1)}, bf16[128,384]{1,0:T(8,128)(2,1)S(1)}, u32[]{:S(2)}, u32[]{:S(2)}) collective-permute-start(bf16[128,384]{1,0:T(8,128)(2,1)S(1)} %collective-permute-done.2.refs_2_), channel_id=1, source_target_pairs={{0,4},{2,6},{4,0},{6,2},{8,12},{10,14},{12,8},{14,10},{16,20},{18,... | collective-permute-start | bytes 294920 | tf_op jit(solution)/shard_map/ppermute | solution.py:244
  11.1 5.9 %collective-permute-start.6 = (bf16[128,384]{1,0:T(8,128)(2,1)}, bf16[128,384]{1,0:T(8,128)(2,1)S(1)}, u32[]{:S(2)}, u32[]{:S(2)}) collective-permute-start(bf16[128,384]{1,0:T(8,128)(2,1)} %get-tuple-element.17.refs_4_), channel_id=1, source_target_pairs={{0,8},{2,10},{4,12},{6,14},{8,0},{10,2},{12,4},{14,6},{16,24},{18,... | collective-permute-start | bytes 294920 | tf_op jit(solution)/shard_map/ppermute | solution.py:244
  11.6 6.7 %collective-permute-start.7 = (bf16[128,384]{1,0:T(8,128)(2,1)S(1)}, bf16[128,384]{1,0:T(8,128)(2,1)S(1)}, u32[]{:S(2)}, u32[]{:S(2)}) collective-permute-start(bf16[128,384]{1,0:T(8,128)(2,1)S(1)} %collective-permute-done.5.refs_5_), channel_id=1, source_target_pairs={{0,8},{2,10},{4,12},{6,14},{8,0},{10,2},{12,4},{14,6},{16,24},{18,... | collective-permute-start | bytes 294920 | tf_op jit(solution)/shard_map/ppermute | solution.py:244
  14.2 4.5 %copy-start.2 = (bf16[128,384]{1,0:T(8,128)(2,1)S(1)}, bf16[128,384]{1,0:T(8,128)(2,1)}, u32[]{:S(2)}) copy-start(bf16[128,384]{1,0:T(8,128)(2,1)} %get-tuple-element.17.refs_4_) | copy-start | bytes 294916
  14.3 2.2 %copy-start.7 = (f32[384]{0:T(512)S(1)}, f32[384]{0:T(512)}, u32[]{:S(2)}) copy-start(f32[384]{0:T(512)} %param.12) | copy-start | bytes 4612
  14.3 4.3 %copy-start.1 = (bf16[128,384]{1,0:T(8,128)(2,1)S(1)}, bf16[128,384]{1,0:T(8,128)(2,1)}, u32[]{:S(2)}) copy-start(bf16[128,384]{1,0:T(8,128)(2,1)} %get-tuple-element.16.refs_0_) | copy-start | bytes 294916
  15.0 3.7 %collective-permute-start.4 = (f32[8,128]{1,0:T(8,128)S(1)}, f32[8,128]{1,0:T(8,128)S(1)}, u32[]{:S(2)}, u32[]{:S(2)}) collective-permute-start(f32[8,128]{1,0:T(8,128)S(1)} %shard_map.84.own_ref), channel_id=1, source_target_pairs={{0,1},{1,0},{2,3},{3,2},{4,5},{5,4},{6,7},{7,6},{8,9},{9,8},{10,11... | collective-permute-start | bytes 12296 | tf_op jit(solution)/shard_map/ppermute | solution.py:308
  18.7 0.7 %copy-start.8 = (f32[384]{0:T(512)S(1)}, f32[384]{0:T(512)}, u32[]{:S(2)}) copy-start(f32[384]{0:T(512)} %param.11) | copy-start | bytes 4612
  18.7 0.9 %copy-start = (bf16[144,384]{1,0:T(8,128)(2,1)S(1)}, bf16[144,384]{1,0:T(8,128)(2,1)}, u32[]{:S(2)}) copy-start(bf16[144,384]{1,0:T(8,128)(2,1)} %get-tuple-element.15.refs_0_.raw_ref) | copy-start | bytes 331780
  18.9 2.5 %collective-permute-start.8 = (bf16[1024,384]{1,0:T(8,128)(2,1)S(1)}, bf16[1024,384]{1,0:T(8,128)(2,1)S(1)}, u32[]{:S(2)}, u32[]{:S(2)}) collective-permute-start(bf16[1024,384]{1,0:T(8,128)(2,1)S(1)} %shard_map.85.refs_2_), channel_id=1, source_target_pairs={{0,2},{2,0},{4,6},{6,4},{8,10},{10,8},{12,14},{14,12},{16,18},{18,... | collective-permute-start | bytes 2359304 | tf_op jit(solution)/shard_map/ppermute | solution.py:244
  21.3 2.5 %copy-start.3 = (f32[50,384]{1,0:T(8,128)S(1)}, f32[50,384]{1,0:T(8,128)}, u32[]{:S(2)}) copy-start(f32[50,384]{1,0:T(8,128)} %table_ref.1) | copy-start | bytes 230404
  21.4 2.5 %copy-start.5 = (s32[2]{0:T(128)S(1)}, s32[2]{0:T(128)}, u32[]{:S(2)}) copy-start(s32[2]{0:T(128)} %step_ref.1) | copy-start | bytes 28
  22.4 8.2 %collective-permute-start.9 = (bf16[144,384]{1,0:T(8,128)(2,1)S(1)}, bf16[144,384]{1,0:T(8,128)(2,1)S(1)}, u32[]{:S(2)}, u32[]{:S(2)}) collective-permute-start(bf16[144,384]{1,0:T(8,128)(2,1)S(1)} %shard_map.88), channel_id=1, source_target_pairs={{0,16},{2,18},{4,20},{6,22},{8,24},{10,26},{12,28},{14,30},{16,0},... | collective-permute-start | bytes 331784 | tf_op jit(solution)/shard_map/ppermute | solution.py:244

commit v8 on v6

--- a/solution.py
+++ b/solution.py
@@ -15,6 +15,7 @@
 SCALE = HD ** (-0.5) * LOG2E
 MASKED = -1e30
 EXTRA = 16
+AHEAD = 4 * 10**9
 ANY = pl.BlockSpec(memory_space=pl.ANY)
 VMEM = pl.BlockSpec(memory_space=pltpu.VMEM)
 SMEM = pl.BlockSpec(memory_space=pltpu.SMEM)
@@ -69,16 +70,25 @@
     copies[3].wait()
 
 
-def sums_kernel(first, before_ref, *refs):
+def near_sums_kernel(lines, before_ref, value_ref, *refs):
+    *sources, out_ref, value_out = refs
+    sums_kernel(lines, before_ref, *sources[: len(lines)], out_ref)
+    value_out[...] = value_ref[...]
+
+
+def sums_kernel(lines, before_ref, *refs):
     *sources, out_ref = refs
     out_ref[...] = before_ref[...]
-    for place, source_ref in enumerate(sources, start=first):
-        out_ref[place : place + 1, :] = squares(source_ref)
-
-
-def normed(source_ref, own_ref, other_ref, line, gain_ref, full_width):
-    total = own_ref[line : line + 1, :] + other_ref[line : line + 1, :]
-    factor = spread(lax.rsqrt(total / full_width + EPSILON))
+    for line, source_ref in zip(lines, sources):
+        out_ref[line : line + 1, :] = squares(source_ref)
+
+
+def factor_kernel(full_width, own_ref, other_ref, out_ref):
+    out_ref[...] = lax.rsqrt((own_ref[...] + other_ref[...]) / full_width + EPSILON)
+
+
+def normed(source_ref, factors_ref, line, gain_ref):
+    factor = spread(factors_ref[line : line + 1, :])
     parts = []
     for low in range(0, source_ref.shape[1], HD):
         wide = source_ref[:HD, low : low + HD].astype(jnp.float32)
@@ -86,12 +96,12 @@
     return jnp.concatenate(parts, axis=1)
 
 
-def pack_kernel(full_width, held, gain_ref, own_ref, other_ref, *refs):
+def pack_kernel(held, gain_ref, factors_ref, *refs):
     keys, values, pack_out = refs[:held], refs[held : 2 * held], refs[2 * held]
     rows = keys[0].shape[0]
     for place, key_ref in enumerate(keys):
         pack_out[place * rows : (place + 1) * rows, :] = normed(
-            key_ref, own_ref, other_ref, 1 + place + (place > 0), gain_ref, full_width
+            key_ref, factors_ref, 1 + place + (place > 0), gain_ref
         )
     for place, value_ref in enumerate(values, start=held):
         pack_out[place * rows : (place + 1) * rows, :] = value_ref[...]
@@ -145,14 +155,14 @@
     return top, total, context
 
 
-def own_attention(full_width, query_masks, key_masks, gain_ref, own_ref, other_ref, *refs):
+def own_attention(query_masks, key_masks, gain_ref, factors_ref, *refs):
     queries, pack = refs[:2], refs[2]
     query_out, context_out, stats_out = refs[3:]
     rows, width = query_out.shape[0] // 2, query_out.shape[1]
     for place, mask in enumerate(query_masks):
         part = slice(place * rows, (place + 1) * rows)
         bias = key_bias(queries[place], mask, key_masks)
-        query = normed(queries[place], own_ref, other_ref, 2 * place, gain_ref, full_width)
+        query = normed(queries[place], factors_ref, 2 * place, gain_ref)
         query_out[part, :] = query
         for low in range(0, width, HD):
             high, wide = low + HD, 2 * low
@@ -258,7 +268,6 @@
     rows, width = query_proj.shape
     count = lax.axis_size("tm")
     splits = lax.axis_size("head")
-    full_width = width * splits
     params = pltpu.CompilerParams(vmem_limit_bytes=(8 + count // 2) * 2**20)
     query_mask = count // 4
     bits = [1 << place for place in range(1, count.bit_length() - 1)]
@@ -284,59 +293,78 @@
             pltpu.SemaphoreType.DMA((4,)),
         ],
     )(query_proj, key_proj, value_proj, far_blocks)
+    queries = [query_packet, exchange(query_packet, query_mask)]
     keys = gathered(key_proj, bits)
     keys[0] = own_key
-    values = gathered(own_value, bits)
-    queries = [query_packet, exchange(query_packet, query_mask)]
-    masks = sorted(keys, key=lambda mask: (mask.bit_count(), mask))
-
-    sums = own_sums
-    first = 2
-    near = [mask for mask in masks[1:] if mask.bit_count() == 1]
-    for sources in (
-        queries[1:] + [keys[mask] for mask in near],
-        [keys[mask] for mask in masks[1 + len(near) :]],
-    ):
-        sums = pl.pallas_call(
-            functools.partial(sums_kernel, first),
+    masks = sorted(keys, key=lambda mask: (mask.bit_count(), -mask))
+    near = 1 + len(bits)
+
+    def summed(sums, sources, lines, cost):
+        return pl.pallas_call(
+            functools.partial(sums_kernel, lines),
             out_shape=jax.ShapeDtypeStruct(own_sums.shape, jnp.float32),
             in_specs=[VMEM] * (1 + len(sources)),
             out_specs=VMEM,
             compiler_params=params,
+            cost_estimate=pl.CostEstimate(flops=cost, bytes_accessed=0, transcendentals=0),
         )(sums, *sources)
-        first += len(sources)
+
+    values = gathered(own_value, bits[1:])
+    sums = summed(own_sums, [keys[bits[0]]], [3], AHEAD)
+    sources = [queries[1]] + [keys[mask] for mask in masks[2:near]]
+    sources += [values[bit] for bit in bits[1:]]
+    sums, late_value = pl.pallas_call(
+        functools.partial(near_sums_kernel, [2, *range(4, near + 2)]),
+        out_shape=[
+            jax.ShapeDtypeStruct(own_sums.shape, jnp.float32),
+            jax.ShapeDtypeStruct((rows, width), jnp.bfloat16),
+        ],
+        in_specs=[VMEM] * (2 + len(sources)),
+        out_specs=[VMEM] * 2,
+        compiler_params=params,
+    )(sums, own_value, *sources)
+    late_values = gathered(exchange(late_value, bits[0]), bits[1:])
+    values.update({mask ^ bits[0]: value for mask, value in late_values.items()})
+    sums = summed(sums, [keys[mask] for mask in masks[near:]], range(near + 2, len(masks) + 2), 0)
     if splits == 2:
         others = lax.ppermute(sums, "head", [(0, 1), (1, 0)])
     else:
         sums = lax.psum(sums, "head")
         others = jnp.zeros_like(sums)
 
+    factors = pl.pallas_call(
+        functools.partial(factor_kernel, width * splits),
+        out_shape=jax.ShapeDtypeStruct(sums.shape, jnp.float32),
+        in_specs=[VMEM] * 2,
+        out_specs=VMEM,
+        compiler_params=params,
+        cost_estimate=pl.CostEstimate(flops=AHEAD, bytes_accessed=0, transcendentals=0),
+    )(sums, others)
     pack = pl.pallas_call(
-        functools.partial(pack_kernel, full_width, len(masks)),
+        functools.partial(pack_kernel, len(masks)),
         out_shape=jax.ShapeDtypeStruct((2 * len(masks) * rows, width), jnp.bfloat16),
-        in_specs=[VMEM] * (3 + 2 * len(masks)),
+        in_specs=[VMEM] * (2 + 2 * len(masks)),
         out_specs=VMEM,
         compiler_params=params,
     )(
         key_gain,
-        sums,
-        others,
+        factors,
         *[keys[mask] for mask in masks],
         *[values[mask] for mask in masks],
     )
     other_pack = exchange(pack, 1)
 
     query_norm, context, stats = pl.pallas_call(
-        functools.partial(own_attention, full_width, [0, query_mask], masks),
+        functools.partial(own_attention, [0, query_mask], masks),
         out_shape=[
             jax.ShapeDtypeStruct((2 * rows, width), jnp.bfloat16),
             jax.ShapeDtypeStruct((2 * rows, width), jnp.float32),
             jax.ShapeDtypeStruct((2 * rows, 2 * width), jnp.float32),
         ],
-        in_specs=[VMEM] * 6,
+        in_specs=[VMEM] * 5,
         out_specs=[VMEM] * 3,
         compiler_params=params,
-    )(query_gain, sums, others, *queries, pack)
+    )(query_gain, factors, *queries, pack)
 
     def last_part(place, out_shape):
         return pl.pallas_call(

time: 29.4 us -> 35.1 us (1.19)
  waiting for transfers between devices: 6.17 us -> 14.8 us
  starting transfers between devices: 14.9 us -> 11.9 us
    ppermute x9, waiting for transfers between devices: 5.25 us -> 14.8 us  [exchange(): return lax.ppermute(array, 'tm', [(i, i ^ mask) for i in range(count)])]
    ppermute x9, starting transfers between devices: 13.3 us -> 10.3 us  [exchange(): return lax.ppermute(array, 'tm', [(i, i ^ mask) for i in range(count)])]
    ppermute x1, waiting for transfers between devices: 0.92 us -> 0.01 us  [local(): others = lax.ppermute(sums, 'head', [(0, 1), (1, 0)])]
    pallas_call x4 -> x6, Pallas kernels: 2.19 us -> 2.23 us  [the longest x1 1.74 us: local(): pl.pallas_call(functools.partial(own_attention, [0, query_mask], masks),...]
  transfers between devices with their start and end apart: 10 -> 10, of which waited for: 6 -> 5; matrix products, arithmetic and copies ran while one was open for 0% -> 0% of each run, Pallas kernels for 19% -> 16%
where the time goes in v8:
time: 35.1 us; the launch traced here: 34.9 us
  waiting for transfers between devices  14.8 us (42%)
  starting transfers between devices  11.9 us (34%)
  Pallas kernels  7.41 us (21%)
  local copies, waits for them, and re-layouts  0.69 us (2%)
    ppermute x9, waiting for transfers between devices, exchange(): return lax.ppermute(array, 'tm', [(i, i ^ mask) for i in range(count)])  14.8 us
    ppermute x9, starting transfers between devices, exchange(): return lax.ppermute(array, 'tm', [(i, i ^ mask) for i in range(count)])  10.3 us
    pallas_call x2, Pallas kernels, last_part(): pl.pallas_call(functools.partial(last_attention, place, place * query_mas...  1.93 us
    pallas_call x1, Pallas kernels, local(): pl.pallas_call(own_kernel, out_shape=[jax.ShapeDtypeStruct((rows + EXTRA,...  1.88 us
    pallas_call x1, Pallas kernels, local(): pl.pallas_call(functools.partial(own_attention, [0, query_mask], masks),...  1.74 us
    ppermute x1, starting transfers between devices, local(): others = lax.ppermute(sums, 'head', [(0, 1), (1, 0)])  1.58 us
    pallas_call x1, Pallas kernels, local(): pl.pallas_call(merge_kernel, out_shape=jax.ShapeDtypeStruct((rows, width)...  0.81 us
  transfers between devices with their start and end apart: 10, of which 5 were waited for; matrix products, arithmetic and copies ran while one was open for 0% of the time, Pallas kernels for 16%

profile of v8, /device:TPU:0, one launch (start us, length us, event | category | flops | bytes accessed | tf_op | source)
XLA Modules:
  0.0 34.9 jit_solution(6617795053074396660)
XLA Ops:
  0.0 4.0 %collective-permute-start = (bf16[128,384]{1,0:T(8,128)(2,1)}, bf16[128,384]{1,0:T(8,128)(2,1)S(1)}, u32[]{:S(2)}, u32[]{:S(2)}) collective-permute-start(bf16[128,384]{1,0:T(8,128)(2,1)} %key_hbm.1), channel_id=1, source_target_pairs={{0,16},{2,18},{4,20},{6,22},{8,24},{10,26},{12,28},{14,30},{16,0},... | collective-permute-start | bytes 294920 | tf_op jit(solution)/shard_map/ppermute | solution.py:254
  4.0 1.5 %collective-permute-start.2 = (bf16[128,384]{1,0:T(8,128)(2,1)}, bf16[128,384]{1,0:T(8,128)(2,1)S(1)}, u32[]{:S(2)}, u32[]{:S(2)}) collective-permute-start(bf16[128,384]{1,0:T(8,128)(2,1)} %key_hbm.1), channel_id=1, source_target_pairs={{0,4},{2,6},{4,0},{6,2},{8,12},{10,14},{12,8},{14,10},{16,20},{18,... | collective-permute-start | bytes 294920 | tf_op jit(solution)/shard_map/ppermute | solution.py:254
  5.5 1.9 %shard_map.82 = (bf16[144,384]{1,0:T(8,128)(2,1)}, bf16[128,384]{1,0:T(8,128)(2,1)}, bf16[128,384]{1,0:T(8,128)(2,1)}, f32[8,128]{1,0:T(8,128)}) custom-call(bf16[128,384]{1,0:T(8,128)(2,1)} %query_hbm.1, bf16[128,384]{1,0:T(8,128)(2,1)} %key_hbm.1, bf16[128,384]{1,0:T(8,128)(2,1)} %value_hbm.1, s32[1,16]{1,0:T(1,128)} %far_hbm.1), custom_call_target="tpu_custom_call" | custom-call | tf_op jit(solution)/shard_map/pallas_call | solution.py:280
  7.4 0.0 copy-start.5
  7.4 1.6 %collective-permute-start.1 = (bf16[144,384]{1,0:T(8,128)(2,1)}, bf16[144,384]{1,0:T(8,128)(2,1)S(1)}, u32[]{:S(2)}, u32[]{:S(2)}) collective-permute-start(bf16[144,384]{1,0:T(8,128)(2,1)} %get-tuple-element.18.refs_0_.raw_ref), channel_id=1, source_target_pairs={{0,8},{2,10},{4,12},{6,14},{8,0},{10,2},{12,4},{14,6},{16,24},{18,... | collective-permute-start | bytes 331784 | tf_op jit(solution)/shard_map/ppermute | solution.py:254
  9.1 0.5 %collective-permute-start.3 = (bf16[128,384]{1,0:T(8,128)(2,1)}, bf16[128,384]{1,0:T(8,128)(2,1)S(1)}, u32[]{:S(2)}, u32[]{:S(2)}) collective-permute-start(bf16[128,384]{1,0:T(8,128)(2,1)} %get-tuple-element.17.value_ref.refs_4_), channel_id=1, source_target_pairs={{0,4},{2,6},{4,0},{6,2},{8,12},{10,14},{12,8},{14,10},{16,20},{18,... | collective-permute-start | bytes 294920 | tf_op jit(solution)/shard_map/ppermute | solution.py:254
  9.6 0.0 collective-permute-done.refs_0_.refs_1_
  9.6 1.5 %collective-permute-start.4 = (bf16[128,384]{1,0:T(8,128)(2,1)S(1)}, bf16[128,384]{1,0:T(8,128)(2,1)S(1)}, u32[]{:S(2)}, u32[]{:S(2)}) collective-permute-start(bf16[128,384]{1,0:T(8,128)(2,1)S(1)} %collective-permute-done.refs_0_.refs_1_), channel_id=1, source_target_pairs={{0,4},{2,6},{4,0},{6,2},{8,12},{10,14},{12,8},{14,10},{16,20},{18,... | collective-permute-start | bytes 294920 | tf_op jit(solution)/shard_map/ppermute | solution.py:254
  11.1 0.0 copy-done.5
  11.1 0.0 copy-start.1
  11.1 0.1 shard_map.83.before_ref
  11.2 2.8 %collective-permute-done.3.refs_2_.refs_6_ = bf16[128,384]{1,0:T(8,128)(2,1)S(1)} collective-permute-done((bf16[128,384]{1,0:T(8,128)(2,1)}, bf16[128,384]{1,0:T(8,128)(2,1)S(1)}, u32[]{:S(2)}, u32[]{:S(2)}) %collective-permute-start.3) | collective-permute-done | bytes 98336 | tf_op jit(solution)/shard_map/ppermute | solution.py:254
  14.0 0.0 collective-permute-done.2.refs_1_.refs_2_
  14.0 0.0 collective-permute-done.1.refs_0_.refs_1_.raw_ref
  14.0 0.0 copy-done.1
  14.0 0.1 shard_map.84
  14.2 0.4 %collective-permute-start.6 = (bf16[128,384]{1,0:T(8,128)(2,1)S(1)}, bf16[128,384]{1,0:T(8,128)(2,1)S(1)}, u32[]{:S(2)}, u32[]{:S(2)}) collective-permute-start(bf16[128,384]{1,0:T(8,128)(2,1)S(1)} %get-tuple-element.21), channel_id=1, source_target_pairs={{0,16},{2,18},{4,20},{6,22},{8,24},{10,26},{12,28},{14,30},{16,0},... | collective-permute-start | bytes 294920 | tf_op jit(solution)/shard_map/ppermute | solution.py:254
  14.6 0.5 %collective-permute-done.4.refs_0_.refs_3_ = bf16[128,384]{1,0:T(8,128)(2,1)S(1)} collective-permute-done((bf16[128,384]{1,0:T(8,128)(2,1)S(1)}, bf16[128,384]{1,0:T(8,128)(2,1)S(1)}, u32[]{:S(2)}, u32[]{:S(2)}) %collective-permute-start.4) | collective-permute-done | bytes 98336 | tf_op jit(solution)/shard_map/ppermute | solution.py:254
  15.1 0.0 copy-start.6
  15.1 0.1 shard_map.85.own_ref
  15.2 1.6 %collective-permute-start.5 = (f32[8,128]{1,0:T(8,128)S(1)}, f32[8,128]{1,0:T(8,128)S(1)}, u32[]{:S(2)}, u32[]{:S(2)}) collective-permute-start(f32[8,128]{1,0:T(8,128)S(1)} %shard_map.85.own_ref), channel_id=1, source_target_pairs={{0,1},{1,0},{2,3},{3,2},{4,5},{5,4},{6,7},{7,6},{8,9},{9,8},{10,11... | collective-permute-start | bytes 12296 | tf_op jit(solution)/shard_map/ppermute | solution.py:330
  16.8 0.0 copy-done.6
  16.8 0.0 copy-start.2
  16.8 4.0 %collective-permute-done.6.refs_5_ = bf16[128,384]{1,0:T(8,128)(2,1)S(1)} collective-permute-done((bf16[128,384]{1,0:T(8,128)(2,1)S(1)}, bf16[128,384]{1,0:T(8,128)(2,1)S(1)}, u32[]{:S(2)}, u32[]{:S(2)}) %collective-permute-start.6) | collective-permute-done | bytes 98336 | tf_op jit(solution)/shard_map/ppermute | solution.py:254
  20.8 0.5 %collective-permute-start.7 = (bf16[128,384]{1,0:T(8,128)(2,1)S(1)}, bf16[128,384]{1,0:T(8,128)(2,1)S(1)}, u32[]{:S(2)}, u32[]{:S(2)}) collective-permute-start(bf16[128,384]{1,0:T(8,128)(2,1)S(1)} %collective-permute-done.6.refs_5_), channel_id=1, source_target_pairs={{0,4},{2,6},{4,0},{6,2},{8,12},{10,14},{12,8},{14,10},{16,20},{18,... | collective-permute-start | bytes 294920 | tf_op jit(solution)/shard_map/ppermute | solution.py:254
  21.3 0.0 collective-permute-done.5.other_ref
  21.3 4.1 %collective-permute-done.7.refs_7_ = bf16[128,384]{1,0:T(8,128)(2,1)S(1)} collective-permute-done((bf16[128,384]{1,0:T(8,128)(2,1)S(1)}, bf16[128,384]{1,0:T(8,128)(2,1)S(1)}, u32[]{:S(2)}, u32[]{:S(2)}) %collective-permute-start.7) | collective-permute-done | bytes 98336 | tf_op jit(solution)/shard_map/ppermute | solution.py:254
  25.4 0.0 copy-done.2
  25.4 0.0 copy-start.7
  25.4 0.0 copy-start
  25.4 0.2 shard_map.87.refs_2_
  25.6 0.1 collective-permute-start.8
  25.7 0.4 %copy-done.7 = f32[384]{0:T(512)S(1)} copy-done((f32[384]{0:T(512)S(1)}, f32[384]{0:T(512)}, u32[]{:S(2)}) %copy-start.7) | copy-done | bytes 1560
  26.1 0.2 copy-done
  26.3 1.7 %shard_map.88 = (bf16[256,384]{1,0:T(8,128)(2,1)S(1)}, f32[256,384]{1,0:T(8,128)S(1)}, f32[256,768]{1,0:T(8,128)S(1)}) custom-call(f32[1,384]{1,0:T(1,128)S(1)} %reshape.6.gain_ref, f32[8,128]{1,0:T(8,128)S(1)} %shard_map.86.factors_ref, bf16[144,384]{1,0:T(8,128)(2,1)S(1)} %copy-done, bf16[144,384]{1,0:T(8,128)(2,1)S(1)} %collective-permute-done.1.refs_0_.refs_1_.raw_ref, ...), custom_call_target="tpu_custom_call" | custom-call | tf_op jit(solution)/shard_map/pallas_call | solution.py:357
  28.1 0.0 collective-permute-done.8.refs_0_
  28.1 0.0 copy-start.3
  28.1 0.0 copy-start.4
  28.1 1.0 %shard_map.90 = bf16[144,384]{1,0:T(8,128)(2,1)S(1)} custom-call(bf16[256,384]{1,0:T(8,128)(2,1)S(1)} %get-tuple-element.22.query_ref, bf16[144,384]{1,0:T(8,128)(2,1)S(1)} %collective-permute-done.1.refs_0_.refs_1_.raw_ref, bf16[1024,384]{1,0:T(8,128)(2,1)S(1)} %collective-permute-done.8.refs_0_, f32[256,384]{1,0:T(8,128)S(1)} %get-tuple-element.23.refs_1_, ...), custom_call_target="tpu_custom_call" | custom-call | tf_op jit(solution)/shard_map/pallas_call | solution.py:370
  29.1 0.1 collective-permute-start.9
  29.2 0.0 copy-done.3
  29.2 0.0 copy-done.4
  29.2 0.6 %shard_map.91.gate_ref = f32[16,384]{1,0:T(8,128)S(1)} custom-call(s32[2]{0:T(128)S(1)} %copy-done.4, f32[50,384]{1,0:T(8,128)S(1)} %copy-done.3), custom_call_target="tpu_custom_call" | custom-call | tf_op jit(solution)/shard_map/pallas_call | solution.py:388
  29.8 1.0 %shard_map.89 = (f32[128,384]{1,0:T(8,128)S(1)}, f32[8,384]{1,0:T(8,128)S(1)}) custom-call(bf16[256,384]{1,0:T(8,128)(2,1)S(1)} %get-tuple-element.22.query_ref, bf16[144,384]{1,0:T(8,128)(2,1)S(1)} %copy-done, bf16[1024,384]{1,0:T(8,128)(2,1)S(1)} %collective-permute-done.8.refs_0_, f32[256,384]{1,0:T(8,128)S(1)} %get-tuple-element.23.refs_1_, ...), custom_call_target="tpu_custom_call" | custom-call | tf_op jit(solution)/shard_map/pallas_call | solution.py:370
  30.7 3.4 %collective-permute-done.9.packet_ref = bf16[144,384]{1,0:T(8,128)(2,1)S(1)} collective-permute-done((bf16[144,384]{1,0:T(8,128)(2,1)S(1)}, bf16[144,384]{1,0:T(8,128)(2,1)S(1)}, u32[]{:S(2)}, u32[]{:S(2)}) %collective-permute-start.9) | collective-permute-done | bytes 110624 | tf_op jit(solution)/shard_map/ppermute | solution.py:254
  34.1 0.8 %shard_map.92 = bf16[128,384]{1,0:T(8,128)(2,1)} custom-call(f32[128,384]{1,0:T(8,128)S(1)} %get-tuple-element.25.own_ref, f32[8,384]{1,0:T(8,128)S(1)} %get-tuple-element.26.logs_ref, bf16[144,384]{1,0:T(8,128)(2,1)S(1)} %collective-permute-done.9.packet_ref, f32[16,384]{1,0:T(8,128)S(1)} %shard_map.91.gate_ref), custom_call_target="tpu_custom_call" | custom-call | tf_op jit(solution)/shard_map/pallas_call | solution.py:397
  (3 shorter events, 0.0 us)
Async XLA Ops:
  0.0 9.6 %collective-permute-start = (bf16[128,384]{1,0:T(8,128)(2,1)}, bf16[128,384]{1,0:T(8,128)(2,1)S(1)}, u32[]{:S(2)}, u32[]{:S(2)}) collective-permute-start(bf16[128,384]{1,0:T(8,128)(2,1)} %key_hbm.1), channel_id=1, source_target_pairs={{0,16},{2,18},{4,20},{6,22},{8,24},{10,26},{12,28},{14,30},{16,0},... | collective-permute-start | bytes 294920 | tf_op jit(solution)/shard_map/ppermute | solution.py:254
  4.0 10.0 %collective-permute-start.2 = (bf16[128,384]{1,0:T(8,128)(2,1)}, bf16[128,384]{1,0:T(8,128)(2,1)S(1)}, u32[]{:S(2)}, u32[]{:S(2)}) collective-permute-start(bf16[128,384]{1,0:T(8,128)(2,1)} %key_hbm.1), channel_id=1, source_target_pairs={{0,4},{2,6},{4,0},{6,2},{8,12},{10,14},{12,8},{14,10},{16,20},{18,... | collective-permute-start | bytes 294920 | tf_op jit(solution)/shard_map/ppermute | solution.py:254
  7.4 3.7 %copy-start.5 = (f32[8,128]{1,0:T(8,128)S(1)}, f32[8,128]{1,0:T(8,128)}, u32[]{:S(2)}) copy-start(f32[8,128]{1,0:T(8,128)} %get-tuple-element.16.before_ref) | copy-start | bytes 12292
  7.4 6.6 %collective-permute-start.1 = (bf16[144,384]{1,0:T(8,128)(2,1)}, bf16[144,384]{1,0:T(8,128)(2,1)S(1)}, u32[]{:S(2)}, u32[]{:S(2)}) collective-permute-start(bf16[144,384]{1,0:T(8,128)(2,1)} %get-tuple-element.18.refs_0_.raw_ref), channel_id=1, source_target_pairs={{0,8},{2,10},{4,12},{6,14},{8,0},{10,2},{12,4},{14,6},{16,24},{18,... | collective-permute-start | bytes 331784 | tf_op jit(solution)/shard_map/ppermute | solution.py:254
  9.1 5.0 %collective-permute-start.3 = (bf16[128,384]{1,0:T(8,128)(2,1)}, bf16[128,384]{1,0:T(8,128)(2,1)S(1)}, u32[]{:S(2)}, u32[]{:S(2)}) collective-permute-start(bf16[128,384]{1,0:T(8,128)(2,1)} %get-tuple-element.17.value_ref.refs_4_), channel_id=1, source_target_pairs={{0,4},{2,6},{4,0},{6,2},{8,12},{10,14},{12,8},{14,10},{16,20},{18,... | collective-permute-start | bytes 294920 | tf_op jit(solution)/shard_map/ppermute | solution.py:254
  9.6 5.5 %collective-permute-start.4 = (bf16[128,384]{1,0:T(8,128)(2,1)S(1)}, bf16[128,384]{1,0:T(8,128)(2,1)S(1)}, u32[]{:S(2)}, u32[]{:S(2)}) collective-permute-start(bf16[128,384]{1,0:T(8,128)(2,1)S(1)} %collective-permute-done.refs_0_.refs_1_), channel_id=1, source_target_pairs={{0,4},{2,6},{4,0},{6,2},{8,12},{10,14},{12,8},{14,10},{16,20},{18,... | collective-permute-start | bytes 294920 | tf_op jit(solution)/shard_map/ppermute | solution.py:254
  11.1 2.9 %copy-start.1 = (bf16[128,384]{1,0:T(8,128)(2,1)S(1)}, bf16[128,384]{1,0:T(8,128)(2,1)}, u32[]{:S(2)}) copy-start(bf16[128,384]{1,0:T(8,128)(2,1)} %get-tuple-element.17.value_ref.refs_4_) | copy-start | bytes 294916
  14.2 6.6 %collective-permute-start.6 = (bf16[128,384]{1,0:T(8,128)(2,1)S(1)}, bf16[128,384]{1,0:T(8,128)(2,1)S(1)}, u32[]{:S(2)}, u32[]{:S(2)}) collective-permute-start(bf16[128,384]{1,0:T(8,128)(2,1)S(1)} %get-tuple-element.21), channel_id=1, source_target_pairs={{0,16},{2,18},{4,20},{6,22},{8,24},{10,26},{12,28},{14,30},{16,0},... | collective-permute-start | bytes 294920 | tf_op jit(solution)/shard_map/ppermute | solution.py:254
  15.1 1.7 %copy-start.6 = (f32[384]{0:T(512)S(1)}, f32[384]{0:T(512)}, u32[]{:S(2)}) copy-start(f32[384]{0:T(512)} %param.12) | copy-start | bytes 4612
  15.2 6.1 %collective-permute-start.5 = (f32[8,128]{1,0:T(8,128)S(1)}, f32[8,128]{1,0:T(8,128)S(1)}, u32[]{:S(2)}, u32[]{:S(2)}) collective-permute-start(f32[8,128]{1,0:T(8,128)S(1)} %shard_map.85.own_ref), channel_id=1, source_target_pairs={{0,1},{1,0},{2,3},{3,2},{4,5},{5,4},{6,7},{7,6},{8,9},{9,8},{10,11... | collective-permute-start | bytes 12296 | tf_op jit(solution)/shard_map/ppermute | solution.py:330
  16.8 8.6 %copy-start.2 = (bf16[128,384]{1,0:T(8,128)(2,1)S(1)}, bf16[128,384]{1,0:T(8,128)(2,1)}, u32[]{:S(2)}) copy-start(bf16[128,384]{1,0:T(8,128)(2,1)} %get-tuple-element.20.refs_0_) | copy-start | bytes 294916
  20.8 4.6 %collective-permute-start.7 = (bf16[128,384]{1,0:T(8,128)(2,1)S(1)}, bf16[128,384]{1,0:T(8,128)(2,1)S(1)}, u32[]{:S(2)}, u32[]{:S(2)}) collective-permute-start(bf16[128,384]{1,0:T(8,128)(2,1)S(1)} %collective-permute-done.6.refs_5_), channel_id=1, source_target_pairs={{0,4},{2,6},{4,0},{6,2},{8,12},{10,14},{12,8},{14,10},{16,20},{18,... | collective-permute-start | bytes 294920 | tf_op jit(solution)/shard_map/ppermute | solution.py:254
  25.4 0.7 %copy-start.7 = (f32[384]{0:T(512)S(1)}, f32[384]{0:T(512)}, u32[]{:S(2)}) copy-start(f32[384]{0:T(512)} %param.11) | copy-start | bytes 4612
  25.4 0.9 %copy-start = (bf16[144,384]{1,0:T(8,128)(2,1)S(1)}, bf16[144,384]{1,0:T(8,128)(2,1)}, u32[]{:S(2)}) copy-start(bf16[144,384]{1,0:T(8,128)(2,1)} %get-tuple-element.18.refs_0_.raw_ref) | copy-start | bytes 331780
  25.6 2.5 %collective-permute-start.8 = (bf16[1024,384]{1,0:T(8,128)(2,1)S(1)}, bf16[1024,384]{1,0:T(8,128)(2,1)S(1)}, u32[]{:S(2)}, u32[]{:S(2)}) collective-permute-start(bf16[1024,384]{1,0:T(8,128)(2,1)S(1)} %shard_map.87.refs_2_), channel_id=1, source_target_pairs={{0,2},{2,0},{4,6},{6,4},{8,10},{10,8},{12,14},{14,12},{16,18},{18,... | collective-permute-start | bytes 2359304 | tf_op jit(solution)/shard_map/ppermute | solution.py:254
  28.1 1.1 %copy-start.3 = (f32[50,384]{1,0:T(8,128)S(1)}, f32[50,384]{1,0:T(8,128)}, u32[]{:S(2)}) copy-start(f32[50,384]{1,0:T(8,128)} %table_ref.1) | copy-start | bytes 230404
  28.1 1.1 %copy-start.4 = (s32[2]{0:T(128)S(1)}, s32[2]{0:T(128)}, u32[]{:S(2)}) copy-start(s32[2]{0:T(128)} %step_ref.1) | copy-start | bytes 28
  29.1 5.0 %collective-permute-start.9 = (bf16[144,384]{1,0:T(8,128)(2,1)S(1)}, bf16[144,384]{1,0:T(8,128)(2,1)S(1)}, u32[]{:S(2)}, u32[]{:S(2)}) collective-permute-start(bf16[144,384]{1,0:T(8,128)(2,1)S(1)} %shard_map.90), channel_id=1, source_target_pairs={{0,8},{2,10},{4,12},{6,14},{8,0},{10,2},{12,4},{14,6},{16,24},{18,... | collective-permute-start | bytes 331784 | tf_op jit(solution)/shard_map/ppermute | solution.py:254

commit v9 on v4

v9 whole, which is shorter than its diff:
```python
import functools

import jax
import jax.numpy as jnp
from jax import lax
from jax.experimental import pallas as pl
from jax.experimental.pallas import tpu as pltpu
from jax.sharding import PartitionSpec as P

HD = 128
BLK = 64
FRAME_TOK = 1560
EPSILON = 1e-06
LOG2E = 1.4426950408889634
SCALE = HD ** (-0.5) * LOG2E
MASKED = -1e30
EXTRA = 16
AHEAD = 4 * 10**9
QUERY_MASKS = (0, 2, 4, 6)
ANY = pl.BlockSpec(memory_space=pl.ANY)
VMEM = pl.BlockSpec(memory_space=pltpu.VMEM)
SMEM = pl.BlockSpec(memory_space=pltpu.SMEM)


def spread(row):
    return jnp.broadcast_to(row, (row.shape[1], row.shape[1])).T


def squares(source_ref):
    wide = source_ref[...].astype(jnp.float32)
    square = wide * wide
    part = square[:, :HD]
    for low in range(HD, square.shape[1], HD):
        part = part + square[:, low : low + HD]
    return jnp.sum(part.T, axis=0, keepdims=True)


def sums_kernel(query_hbm, key_hbm, out_ref, query_ref, key_ref, sems):
    copies = [
        pltpu.make_async_copy(query_hbm, query_ref, sems.at[0]),
        pltpu.make_async_copy(key_hbm, key_ref, sems.at[1]),
    ]
    for copy in copies:
        copy.start()
    for place, ref in enumerate((query_ref, key_ref)):
        copies[place].wait()
        out_ref[place : place + 1, :] = squares(ref)


def normed(source_ref, factor, gain_ref):
    parts = []
    for low in range(0, source_ref.shape[1], HD):
        wide = source_ref[:, low : low + HD].astype(jnp.float32)
        parts.append((wide * factor * gain_ref[:, low : low + HD]).astype(jnp.bfloat16))
    return jnp.concatenate(parts, axis=1)


def norm_kernel(
    full_width,
    query_ref,
    key_ref,
    value_ref,
    query_gain_ref,
    key_gain_ref,
    far_ref,
    own_ref,
    other_ref,
    query_out,
    key_out,
    pack_out,
):
    rows, width = query_ref.shape
    factors = lax.rsqrt((own_ref[...] + other_ref[...]) / full_width + EPSILON)
    key = normed(key_ref, spread(factors[1:2, :]), key_gain_ref)
    key_out[...] = key
    pack_out[:rows, :] = key
    pack_out[rows:, :] = value_ref[...]
    query_out[:rows, :] = normed(query_ref, spread(factors[0:1, :]), query_gain_ref)
    far = far_ref[...].astype(jnp.float32)
    far = jnp.concatenate([far, jnp.full((1, HD - far.shape[1]), -1.0)], axis=1)
    query_out[rows:, :HD] = jnp.broadcast_to(far, (EXTRA, HD)).astype(jnp.bfloat16)
    query_out[rows:, HD:] = jnp.zeros((EXTRA, width - HD), jnp.bfloat16)


def pack_kernel(*refs):
    *sources, out_ref = refs
    rows = sources[0].shape[0]
    for place, source_ref in enumerate(sources):
        out_ref[place * rows : (place + 1) * rows, :] = source_ref[...]


def key_bias(query_ref, query_mask, key_masks):
    me = lax.axis_index("tm")
    lane = lax.broadcasted_iota(jnp.int32, (1, HD), 1)
    half = (lane >= BLK).astype(jnp.float32)
    far = query_ref[HD:, :HD].astype(jnp.float32)[:1]
    parts = []
    for key_mask in key_masks:
        query_id, key_id = me ^ query_mask, me ^ key_mask
        choice = jnp.sum(jnp.where(lane == key_id, far, 0.0), axis=1, keepdims=True)
        taken = (choice == half) | (jnp.abs(query_id - key_id) <= 1)
        parts.append(jnp.where(taken, 0.0, MASKED))
    return jnp.concatenate(parts, axis=1)


def absorb(queries, packs, biases, olds, low):
    rows, high = HD, low + HD
    halves = [pack.shape[0] // 2 for pack in packs]
    keys = [pack[:half, low:high] for pack, half in zip(packs, halves)]
    values = [pack[half:, low:high] for pack, half in zip(packs, halves)]
    scores = lax.dot_general(
        jnp.concatenate([query[:rows, low:high] for query in queries], axis=0),
        jnp.concatenate(keys, axis=0),
        (((1,), (1,)), ((), ())),
        preferred_element_type=jnp.float32,
    )
    tops, totals, rounded = [], [], []
    for place, bias in enumerate(biases):
        logits = scores[place * rows : (place + 1) * rows] * SCALE + bias
        top = jnp.broadcast_to(jnp.max(logits, axis=1, keepdims=True), (rows, HD))
        if olds is not None:
            top = jnp.maximum(top, olds[place][0])
        weights = [
            jnp.exp2(logits[:, left : left + HD] - top)
            for left in range(0, logits.shape[1], HD)
        ]
        total = jnp.sum(functools.reduce(jnp.add, weights), axis=1, keepdims=True)
        tops.append(top)
        totals.append(jnp.broadcast_to(total, (rows, HD)))
        rounded.append(
            jnp.concatenate([weight.astype(jnp.bfloat16) for weight in weights], axis=1)
        )
    added = jnp.dot(
        jnp.concatenate(rounded, axis=0),
        jnp.concatenate(values, axis=0),
        preferred_element_type=jnp.float32,
    )
    results = []
    for place in range(len(biases)):
        context = added[place * rows : (place + 1) * rows]
        total = totals[place]
        if olds is not None:
            fade = jnp.exp2(olds[place][0] - tops[place])
            total = total + olds[place][1] * fade
            context = context + olds[place][2] * fade
        results.append((tops[place], total, context))
    return results


def held_state(context_ref, stats_ref, place, low):
    part, wide = slice(place * HD, (place + 1) * HD), 2 * low
    return (
        stats_ref[part, wide : wide + HD],
        stats_ref[part, wide + HD : wide + 2 * HD],
        context_ref[part, low : low + HD],
    )


def step_kernel(key_masks, resumed, *refs):
    count = len(QUERY_MASKS)
    queries, refs = refs[:count], refs[count:]
    held = len(refs) - 2 - 2 * resumed
    packs, olds, (context_out, stats_out) = refs[:held], refs[held:-2], refs[-2:]
    biases = [key_bias(ref, mask, key_masks) for ref, mask in zip(queries, QUERY_MASKS)]
    for low in range(0, context_out.shape[1], HD):
        state = None
        if resumed:
            state = [held_state(*olds, place, low) for place in range(count)]
        for place, result in enumerate(absorb(queries, packs, biases, state, low)):
            part, wide = slice(place * HD, (place + 1) * HD), 2 * low
            top, total, context = result
            context_out[part, low : low + HD] = context
            stats_out[part, wide : wide + HD] = top
            stats_out[part, wide + HD : wide + 2 * HD] = total


def last_kernel(place, key_masks, query_ref, pack_ref, context_ref, stats_ref, *outs):
    rows, width = HD, context_ref.shape[1]
    heads = width // HD
    bias = key_bias(query_ref, QUERY_MASKS[place], key_masks)
    lane = lax.broadcasted_iota(jnp.int32, (1, HD), 1)
    logs = jnp.zeros((rows, HD), jnp.float32)
    for head in range(heads):
        low, high = head * HD, (head + 1) * HD
        old = held_state(context_ref, stats_ref, place, low)
        ((top, total, context),) = absorb([query_ref], [pack_ref], [bias], [old], low)
        outs[0][:rows, low:high] = (context * (1.0 / total)).astype(outs[0].dtype)
        logs = jnp.where(lane == head, top + jnp.log2(total), logs)
    lines = logs.T
    sub = lax.broadcasted_iota(jnp.int32, (EXTRA, HD), 0)
    for head in range(heads):
        low, high = head * HD, (head + 1) * HD
        value = lines[head : head + 1, :]
        if place == 0:
            outs[1][:, low:high] = jnp.broadcast_to(value, (8, HD))
        else:
            first = value.astype(jnp.bfloat16).astype(jnp.float32)
            second = (value - first).astype(jnp.bfloat16).astype(jnp.float32)
            third = value - first - second
            outs[0][rows:, low:high] = jnp.where(
                sub == 0, first, jnp.where(sub == 1, second, third)
            ).astype(jnp.bfloat16)


def gate_kernel(step_ref, table_ref, out_ref):
    rows = out_ref.shape[0] // 2
    start = lax.axis_index("tm") * HD
    first = step_ref[start // FRAME_TOK]
    last = step_ref[(start + HD - 1) // FRAME_TOK]
    out_ref[:rows, :] = jnp.broadcast_to(table_ref[pl.ds(first, 1), :], (rows, out_ref.shape[1]))
    out_ref[rows:, :] = jnp.broadcast_to(table_ref[pl.ds(last, 1), :], (rows, out_ref.shape[1]))


def merge_kernel(own_ref, logs_ref, *refs):
    *packets, gate_ref, out_ref = refs
    rows, width = own_ref.shape
    logs = [logs_ref[:1, :]]
    for packet in packets:
        pieces = packet[rows:, :].astype(jnp.float32)
        logs.append(pieces[0:1] + pieces[1:2] + pieces[2:3])
    top = functools.reduce(jnp.maximum, logs)
    shares = [jnp.exp2(log - top) for log in logs]
    scale = 1.0 / sum(shares)
    shares = [share * scale for share in shares]
    start = lax.axis_index("tm") * rows
    first_rows = (start // FRAME_TOK + 1) * FRAME_TOK - start
    row_ids = lax.broadcasted_iota(jnp.int32, (rows, 1), 0)
    for low in range(0, width, HD):
        high = low + HD
        context = own_ref[:, low:high] * spread(shares[0][:, low:high])
        for packet, share in zip(packets, shares[1:]):
            context += packet[:rows, low:high].astype(jnp.float32) * spread(share[:, low:high])
        gate = jnp.where(
            row_ids < first_rows, gate_ref[0:1, low:high], gate_ref[8:9, low:high]
        )
        out_ref[:, low:high] = (context * gate).astype(jnp.bfloat16)


def exchange(array, mask):
    count = lax.axis_size("tm")
    return lax.ppermute(array, "tm", [(i, i ^ mask) for i in range(count)])


def gathered(array, bits):
    held = {0: array}
    for bit in bits:
        for mask in list(held):
            held[mask ^ bit] = exchange(held[mask], bit)
    return held


def cost(flops):
    return pl.CostEstimate(flops=flops, bytes_accessed=0, transcendentals=0)


def local(
    query_proj, key_proj, value_proj, query_gain, key_gain, gate_table, frame_step, far_blocks
):
    rows, width = query_proj.shape
    count = lax.axis_size("tm")
    splits = lax.axis_size("head")
    params = pltpu.CompilerParams(vmem_limit_bytes=(8 + count // 2) * 2**20)
    far_bits = [1 << place for place in range(3, count.bit_length() - 1)]

    sums = pl.pallas_call(
        sums_kernel,
        out_shape=jax.ShapeDtypeStruct((2, rows), jnp.float32),
        in_specs=[ANY, ANY],
        out_specs=VMEM,
        scratch_shapes=[
            pltpu.VMEM((rows, width), jnp.bfloat16),
            pltpu.VMEM((rows, width), jnp.bfloat16),
            pltpu.SemaphoreType.DMA((2,)),
        ],
    )(query_proj, key_proj)
    if splits == 2:
        others = lax.ppermute(sums, "head", [(0, 1), (1, 0)])
    else:
        sums = lax.psum(sums, "head")
        others = jnp.zeros_like(sums)

    query_packet, key_norm, near_pack = pl.pallas_call(
        functools.partial(norm_kernel, width * splits),
        out_shape=(
            jax.ShapeDtypeStruct((rows + EXTRA, width), jnp.bfloat16),
            jax.ShapeDtypeStruct((rows, width), jnp.bfloat16),
            jax.ShapeDtypeStruct((2 * rows, width), jnp.bfloat16),
        ),
        in_specs=[VMEM] * 8,
        out_specs=[VMEM] * 3,
        compiler_params=params,
    )(
        query_proj,
        key_proj,
        value_proj,
        query_gain.reshape(1, width),
        key_gain.reshape(1, width),
        far_blocks,
        sums,
        others,
    )
    values = gathered(value_proj, far_bits)
    keys = gathered(key_norm, far_bits)
    queries = [query_packet] + [exchange(query_packet, mask) for mask in QUERY_MASKS[1:]]
    far = [mask for mask in keys if mask]
    far_pack = pl.pallas_call(
        pack_kernel,
        out_shape=jax.ShapeDtypeStruct((2 * len(far) * rows, width), jnp.bfloat16),
        in_specs=[VMEM] * (2 * len(far)),
        out_specs=VMEM,
        compiler_params=params,
        cost_estimate=cost(AHEAD),
    )(*[keys[mask] for mask in far], *[values[mask] for mask in far])

    def step(masks, packs, *old):
        stacked = len(QUERY_MASKS) * rows
        return pl.pallas_call(
            functools.partial(step_kernel, masks, bool(old)),
            out_shape=[
                jax.ShapeDtypeStruct((stacked, width), jnp.float32),
                jax.ShapeDtypeStruct((stacked, 2 * width), jnp.float32),
            ],
            in_specs=[VMEM] * (len(QUERY_MASKS) + len(packs) + len(old)),
            out_specs=[VMEM] * 2,
            compiler_params=params,
            cost_estimate=cost(0 if old else 2 * AHEAD),
        )(*queries, *packs, *old)

    state = step([0, 1], [near_pack, exchange(near_pack, 1)])
    last_pack = exchange(far_pack, 1)
    state = step(far, [far_pack], *state)

    def last(place, out_shape):
        return pl.pallas_call(
            functools.partial(last_kernel, place, [mask ^ 1 for mask in far]),
            out_shape=out_shape,
            in_specs=[VMEM] * 4,
            out_specs=[VMEM] * len(out_shape),
            compiler_params=params,
        )(queries[place], last_pack, *state)

    packets = {}
    for place in (3, 1, 2):
        (packet,) = last(place, [jax.ShapeDtypeStruct((rows + EXTRA, width), jnp.bfloat16)])
        packets[place] = exchange(packet, QUERY_MASKS[place])
    own, own_logs = last(
        0,
        [
            jax.ShapeDtypeStruct((rows, width), jnp.float32),
            jax.ShapeDtypeStruct((8, width), jnp.float32),
        ],
    )
    gates = pl.pallas_call(
        gate_kernel,
        out_shape=jax.ShapeDtypeStruct((16, width), jnp.float32),
        in_specs=[SMEM, VMEM],
        out_specs=VMEM,
        compiler_params=params,
    )(frame_step, gate_table)
    return pl.pallas_call(
        merge_kernel,
        out_shape=jax.ShapeDtypeStruct((rows, width), jnp.bfloat16),
        in_specs=[VMEM] * 6,
        out_specs=VMEM,
        compiler_params=params,
    )(own, own_logs, packets[1], packets[2], packets[3], gates)


def solution(mesh):
    return jax.shard_map(
        local,
        mesh=mesh,
        in_specs=(
            P("tm", "head"),
            P("tm", "head"),
            P("tm", "head"),
            P("head"),
            P("head"),
            P(None, "head"),
            P(),
            P("tm", None),
        ),
        out_specs=P("tm", "head"),
        check_vma=False,
    )
```

time: 33.5 us -> 35.9 us (1.072)
  local copies, waits for them, and re-layouts: 0.77 us -> 5.38 us
  starting transfers between devices: 16.9 us -> 13.8 us
  Pallas kernels: 7.16 us -> 8.49 us
  waiting for transfers between devices: 8.41 us -> 7.86 us
    ppermute x10, starting transfers between devices: 15.3 us -> 10.8 us  [exchange(): return lax.ppermute(array, 'tm', [(i, i ^ mask) for i in range(count)])]
    unnamed x18 -> x14, local copies, waits for them, and re-layouts: 0.76 us -> 4.02 us
    ppermute x1, waiting for transfers between devices: 1.56 us -> 0.01 us  [local(): others = lax.ppermute(sums, 'head', [(0, 1), (1, 0)])]
    ppermute x1, starting transfers between devices: 1.58 us -> 3.03 us  [local(): others = lax.ppermute(sums, 'head', [(0, 1), (1, 0)])]
    reshape x2, local copies, waits for them, and re-layouts: 0.01 us -> 1.37 us  [the longest x1 0.68 us: local(): query_gain.reshape(1, width)]
    pallas_call x6 -> x9, Pallas kernels: 5.77 us -> 6.96 us  [the longest x4 3.49 us: last(): pl.pallas_call(functools.partial(last_kernel, place, [mask ^ 1 for mask i...]
    ppermute x10, waiting for transfers between devices: 6.85 us -> 7.86 us  [exchange(): return lax.ppermute(array, 'tm', [(i, i ^ mask) for i in range(count)])]
  transfers between devices with their start and end apart: 11 -> 11, of which waited for: 4 -> 5; matrix products, arithmetic and copies ran while one was open for 0% -> 4% of each run, Pallas kernels for 16% -> 14%
where the time goes in v9:
time: 35.9 us; the launch traced here: 35.6 us
  starting transfers between devices  13.8 us (38%)
  Pallas kernels  8.49 us (24%)
  waiting for transfers between devices  7.86 us (22%)
  local copies, waits for them, and re-layouts  5.38 us (15%)
    ppermute x10, starting transfers between devices, exchange(): return lax.ppermute(array, 'tm', [(i, i ^ mask) for i in range(count)])  10.8 us
    ppermute x10, waiting for transfers between devices, exchange(): return lax.ppermute(array, 'tm', [(i, i ^ mask) for i in range(count)])  7.86 us
    unnamed x14, local copies, waits for them, and re-layouts  4.02 us
    pallas_call x4, Pallas kernels, last(): pl.pallas_call(functools.partial(last_kernel, place, [mask ^ 1 for mask i...  3.49 us
    ppermute x1, starting transfers between devices, local(): others = lax.ppermute(sums, 'head', [(0, 1), (1, 0)])  3.03 us
    pallas_call x1, Pallas kernels, local(): pl.pallas_call(sums_kernel, out_shape=jax.ShapeDtypeStruct((2, rows), jnp...  1.69 us
    pallas_call x2, Pallas kernels, step(): pl.pallas_call(functools.partial(step_kernel, masks, bool(old)), out_shap...  1.63 us
    pallas_call x1, Pallas kernels, local(): pl.pallas_call(merge_kernel, out_shape=jax.ShapeDtypeStruct((rows, width)...  0.96 us
  transfers between devices with their start and end apart: 11, of which 5 were waited for; matrix products, arithmetic and copies ran while one was open for 4% of the time, Pallas kernels for 14%

profile of v9, /device:TPU:0, one launch (start us, length us, event | category | flops | bytes accessed | tf_op | source)
XLA Modules:
  0.0 35.6 jit_solution(1286883678295696048)
XLA Ops:
  0.0 1.7 %shard_map.82.own_ref = f32[2,128]{1,0:T(2,128)} custom-call(bf16[128,384]{1,0:T(8,128)(2,1)} %query_ref.1, bf16[128,384]{1,0:T(8,128)(2,1)} %key_ref.1), custom_call_target="tpu_custom_call" | custom-call | tf_op jit(solution)/shard_map/pallas_call | solution.py:265
  1.7 3.0 %collective-permute-start = (f32[2,128]{1,0:T(2,128)}, f32[2,128]{1,0:T(2,128)S(1)}, u32[]{:S(2)}, u32[]{:S(2)}) collective-permute-start(f32[2,128]{1,0:T(2,128)} %shard_map.82.own_ref), channel_id=1, source_target_pairs={{0,1},{1,0},{2,3},{3,2},{4,5},{5,4},{6,7},{7,6},{8,9},{9,8},{10,11... | collective-permute-start | bytes 3080 | tf_op jit(solution)/shard_map/ppermute | solution.py:277
  4.7 2.6 %collective-permute-start.2 = (bf16[128,384]{1,0:T(8,128)(2,1)}, bf16[128,384]{1,0:T(8,128)(2,1)S(1)}, u32[]{:S(2)}, u32[]{:S(2)}) collective-permute-start(bf16[128,384]{1,0:T(8,128)(2,1)} %value_ref.1), channel_id=1, source_target_pairs={{0,16},{2,18},{4,20},{6,22},{8,24},{10,26},{12,28},{14,30},{16,0},... | collective-permute-start | bytes 294920 | tf_op jit(solution)/shard_map/ppermute | solution.py:241
  7.3 0.7 %reshape.6.query_gain_ref = f32[1,384]{1,0:T(1,128)S(1)} reshape(f32[384]{0:T(512)} %param.11) | data formatting | bytes 3072 | tf_op jit(solution)/shard_map/reshape | solution.py:296
  8.0 0.7 %reshape.7.key_gain_ref = f32[1,384]{1,0:T(1,128)S(1)} reshape(f32[384]{0:T(512)} %param.12) | data formatting | bytes 3072 | tf_op jit(solution)/shard_map/reshape | solution.py:297
  8.7 0.0 collective-permute-done.other_ref
  8.7 0.0 copy-start
  8.7 0.9 %copy-done = bf16[128,384]{1,0:T(8,128)(2,1)S(1)} copy-done((bf16[128,384]{1,0:T(8,128)(2,1)S(1)}, bf16[128,384]{1,0:T(8,128)(2,1)}, u32[]{:S(2)}) %copy-start) | copy-done | bytes 98328
  9.6 0.0 copy-start.1
  9.6 0.9 %copy-done.1 = bf16[128,384]{1,0:T(8,128)(2,1)S(1)} copy-done((bf16[128,384]{1,0:T(8,128)(2,1)S(1)}, bf16[128,384]{1,0:T(8,128)(2,1)}, u32[]{:S(2)}) %copy-start.1) | copy-done | bytes 98328
  10.5 0.0 copy-start.2
  10.5 0.9 %copy-done.2 = bf16[128,384]{1,0:T(8,128)(2,1)S(1)} copy-done((bf16[128,384]{1,0:T(8,128)(2,1)S(1)}, bf16[128,384]{1,0:T(8,128)(2,1)}, u32[]{:S(2)}) %copy-start.2) | copy-done | bytes 98328
  11.4 0.0 copy-start.4
  11.4 0.7 %copy-done.4 = f32[2,128]{1,0:T(2,128)S(1)} copy-done((f32[2,128]{1,0:T(2,128)S(1)}, f32[2,128]{1,0:T(2,128)}, u32[]{:S(2)}) %copy-start.4) | copy-done | bytes 1048
  12.1 0.0 copy-start.5
  12.1 0.7 %copy-done.5 = s32[1,16]{1,0:T(1,128)S(1)} copy-done((s32[1,16]{1,0:T(1,128)S(1)}, s32[1,16]{1,0:T(1,128)}, u32[]{:S(2)}) %copy-start.5) | copy-done | bytes 88
  12.7 0.1 shard_map.83
  12.8 1.0 %collective-permute-start.1 = (bf16[128,384]{1,0:T(8,128)(2,1)S(1)}, bf16[128,384]{1,0:T(8,128)(2,1)S(1)}, u32[]{:S(2)}, u32[]{:S(2)}) collective-permute-start(bf16[128,384]{1,0:T(8,128)(2,1)S(1)} %get-tuple-element.15), channel_id=1, source_target_pairs={{0,16},{2,18},{4,20},{6,22},{8,24},{10,26},{12,28},{14,30},{16,0},... | collective-permute-start | bytes 294920 | tf_op jit(solution)/shard_map/ppermute | solution.py:241
  13.8 1.5 %collective-permute-start.4 = (bf16[144,384]{1,0:T(8,128)(2,1)S(1)}, bf16[144,384]{1,0:T(8,128)(2,1)S(1)}, u32[]{:S(2)}, u32[]{:S(2)}) collective-permute-start(bf16[144,384]{1,0:T(8,128)(2,1)S(1)} %get-tuple-element.14.refs_0_.query_ref), channel_id=1, source_target_pairs={{0,4},{2,6},{4,0},{6,2},{8,12},{10,14},{12,8},{14,10},{16,20},{18,... | collective-permute-start | bytes 331784 | tf_op jit(solution)/shard_map/ppermute | solution.py:241
  15.3 1.6 %collective-permute-start.5 = (bf16[144,384]{1,0:T(8,128)(2,1)S(1)}, bf16[144,384]{1,0:T(8,128)(2,1)S(1)}, u32[]{:S(2)}, u32[]{:S(2)}) collective-permute-start(bf16[144,384]{1,0:T(8,128)(2,1)S(1)} %get-tuple-element.14.refs_0_.query_ref), channel_id=1, source_target_pairs={{0,8},{2,10},{4,12},{6,14},{8,0},{10,2},{12,4},{14,6},{16,24},{18,... | collective-permute-start | bytes 331784 | tf_op jit(solution)/shard_map/ppermute | solution.py:241
  16.9 0.4 %collective-permute-start.6 = (bf16[144,384]{1,0:T(8,128)(2,1)S(1)}, bf16[144,384]{1,0:T(8,128)(2,1)S(1)}, u32[]{:S(2)}, u32[]{:S(2)}) collective-permute-start(bf16[144,384]{1,0:T(8,128)(2,1)S(1)} %get-tuple-element.14.refs_0_.query_ref), channel_id=1, source_target_pairs={{0,12},{2,14},{4,8},{6,10},{8,4},{10,6},{12,0},{14,2},{16,28},{18,... | collective-permute-start | bytes 331784 | tf_op jit(solution)/shard_map/ppermute | solution.py:241
  17.3 0.0 collective-permute-done.2.refs_1_
  17.3 0.0 collective-permute-start.7
  17.3 2.0 %collective-permute-done.1.refs_0_ = bf16[128,384]{1,0:T(8,128)(2,1)S(1)} collective-permute-done((bf16[128,384]{1,0:T(8,128)(2,1)S(1)}, bf16[128,384]{1,0:T(8,128)(2,1)S(1)}, u32[]{:S(2)}, u32[]{:S(2)}) %collective-permute-start.1) | collective-permute-done | bytes 98336 | tf_op jit(solution)/shard_map/ppermute | solution.py:241
  19.3 0.1 collective-permute-start.3
  19.4 0.0 collective-permute-done.4.refs_1_.query_ref
  19.4 1.9 %collective-permute-done.5.refs_2_.query_ref = bf16[144,384]{1,0:T(8,128)(2,1)S(1)} collective-permute-done((bf16[144,384]{1,0:T(8,128)(2,1)S(1)}, bf16[144,384]{1,0:T(8,128)(2,1)S(1)}, u32[]{:S(2)}, u32[]{:S(2)}) %collective-permute-start.5) | collective-permute-done | bytes 110624 | tf_op jit(solution)/shard_map/ppermute | solution.py:241
  21.3 1.5 %collective-permute-done.6.refs_3_.query_ref = bf16[144,384]{1,0:T(8,128)(2,1)S(1)} collective-permute-done((bf16[144,384]{1,0:T(8,128)(2,1)S(1)}, bf16[144,384]{1,0:T(8,128)(2,1)S(1)}, u32[]{:S(2)}, u32[]{:S(2)}) %collective-permute-start.6) | collective-permute-done | bytes 110624 | tf_op jit(solution)/shard_map/ppermute | solution.py:241
  22.9 0.0 collective-permute-done.7.refs_5_
  22.9 0.8 %shard_map.85 = (f32[512,384]{1,0:T(8,128)S(1)}, f32[512,768]{1,0:T(8,128)S(1)}) custom-call(bf16[144,384]{1,0:T(8,128)(2,1)S(1)} %get-tuple-element.14.refs_0_.query_ref, bf16[144,384]{1,0:T(8,128)(2,1)S(1)} %collective-permute-done.4.refs_1_.query_ref, bf16[144,384]{1,0:T(8,128)(2,1)S(1)} %collective-permute-done.5.refs_2_.query_ref, ...), custom_call_target="tpu_custom_call" | custom-call | flops 8000000000 | tf_op jit(solution)/shard_map/pallas_call | solution.py:317
  23.7 0.8 %shard_map.86 = (f32[512,384]{1,0:T(8,128)S(1)}, f32[512,768]{1,0:T(8,128)S(1)}) custom-call(bf16[144,384]{1,0:T(8,128)(2,1)S(1)} %get-tuple-element.14.refs_0_.query_ref, bf16[144,384]{1,0:T(8,128)(2,1)S(1)} %collective-permute-done.4.refs_1_.query_ref, bf16[144,384]{1,0:T(8,128)(2,1)S(1)} %collective-permute-done.5.refs_2_.query_ref, ...), custom_call_target="tpu_custom_call" | custom-call | tf_op jit(solution)/shard_map/pallas_call | solution.py:317
  24.5 0.0 collective-permute-done.3.pack_ref
  24.5 0.9 %shard_map.90 = bf16[144,384]{1,0:T(8,128)(2,1)S(1)} custom-call(bf16[144,384]{1,0:T(8,128)(2,1)S(1)} %collective-permute-done.6.refs_3_.query_ref, bf16[256,384]{1,0:T(8,128)(2,1)S(1)} %collective-permute-done.3.pack_ref, f32[512,384]{1,0:T(8,128)S(1)} %get-tuple-element.19.context_ref, f32[512,768]{1,0:T(8,128)S(1)} %get-tuple-element.20.stats_ref), custom_call_target="tpu_custom_call" | custom-call | tf_op jit(solution)/shard_map/pallas_call | solution.py:334
  25.4 1.2 %collective-permute-start.10 = (bf16[144,384]{1,0:T(8,128)(2,1)S(1)}, bf16[144,384]{1,0:T(8,128)(2,1)S(1)}, u32[]{:S(2)}, u32[]{:S(2)}) collective-permute-start(bf16[144,384]{1,0:T(8,128)(2,1)S(1)} %shard_map.90), channel_id=1, source_target_pairs={{0,12},{2,14},{4,8},{6,10},{8,4},{10,6},{12,0},{14,2},{16,28},{18,... | collective-permute-start | bytes 331784 | tf_op jit(solution)/shard_map/ppermute | solution.py:241
  26.6 0.9 %shard_map.89 = bf16[144,384]{1,0:T(8,128)(2,1)S(1)} custom-call(bf16[144,384]{1,0:T(8,128)(2,1)S(1)} %collective-permute-done.5.refs_2_.query_ref, bf16[256,384]{1,0:T(8,128)(2,1)S(1)} %collective-permute-done.3.pack_ref, f32[512,384]{1,0:T(8,128)S(1)} %get-tuple-element.19.context_ref, f32[512,768]{1,0:T(8,128)S(1)} %get-tuple-element.20.stats_ref), custom_call_target="tpu_custom_call" | custom-call | tf_op jit(solution)/shard_map/pallas_call | solution.py:334
  27.5 0.0 copy-start.3
  27.5 0.0 copy-start.6
  27.5 1.5 %collective-permute-start.9 = (bf16[144,384]{1,0:T(8,128)(2,1)S(1)}, bf16[144,384]{1,0:T(8,128)(2,1)S(1)}, u32[]{:S(2)}, u32[]{:S(2)}) collective-permute-start(bf16[144,384]{1,0:T(8,128)(2,1)S(1)} %shard_map.89), channel_id=1, source_target_pairs={{0,8},{2,10},{4,12},{6,14},{8,0},{10,2},{12,4},{14,6},{16,24},{18,... | collective-permute-start | bytes 331784 | tf_op jit(solution)/shard_map/ppermute | solution.py:241
  29.0 0.9 %shard_map.88 = bf16[144,384]{1,0:T(8,128)(2,1)S(1)} custom-call(bf16[144,384]{1,0:T(8,128)(2,1)S(1)} %collective-permute-done.4.refs_1_.query_ref, bf16[256,384]{1,0:T(8,128)(2,1)S(1)} %collective-permute-done.3.pack_ref, f32[512,384]{1,0:T(8,128)S(1)} %get-tuple-element.19.context_ref, f32[512,768]{1,0:T(8,128)S(1)} %get-tuple-element.20.stats_ref), custom_call_target="tpu_custom_call" | custom-call | tf_op jit(solution)/shard_map/pallas_call | solution.py:334
  29.9 1.0 %collective-permute-start.8 = (bf16[144,384]{1,0:T(8,128)(2,1)S(1)}, bf16[144,384]{1,0:T(8,128)(2,1)S(1)}, u32[]{:S(2)}, u32[]{:S(2)}) collective-permute-start(bf16[144,384]{1,0:T(8,128)(2,1)S(1)} %shard_map.88), channel_id=1, source_target_pairs={{0,4},{2,6},{4,0},{6,2},{8,12},{10,14},{12,8},{14,10},{16,20},{18,... | collective-permute-start | bytes 331784 | tf_op jit(solution)/shard_map/ppermute | solution.py:241
  30.8 0.0 copy-done.3
  30.8 0.0 copy-done.6
  30.8 0.6 %shard_map.91.refs_3_ = f32[16,384]{1,0:T(8,128)S(1)} custom-call(s32[2]{0:T(128)S(1)} %copy-done.6, f32[50,384]{1,0:T(8,128)S(1)} %copy-done.3), custom_call_target="tpu_custom_call" | custom-call | tf_op jit(solution)/shard_map/pallas_call | solution.py:353
  31.4 0.9 %shard_map.87 = (f32[128,384]{1,0:T(8,128)S(1)}, f32[8,384]{1,0:T(8,128)S(1)}) custom-call(bf16[144,384]{1,0:T(8,128)(2,1)S(1)} %get-tuple-element.14.refs_0_.query_ref, bf16[256,384]{1,0:T(8,128)(2,1)S(1)} %collective-permute-done.3.pack_ref, f32[512,384]{1,0:T(8,128)S(1)} %get-tuple-element.19.context_ref, f32[512,768]{1,0:T(8,128)S(1)} %get-tuple-element.20.stats_ref), custom_call_target="tpu_custom_call" | custom-call | tf_op jit(solution)/shard_map/pallas_call | solution.py:334
  32.3 0.0 collective-permute-done.10.refs_2_
  32.3 0.1 collective-permute-done.9.refs_1_
  32.3 2.3 %collective-permute-done.8.refs_0_ = bf16[144,384]{1,0:T(8,128)(2,1)S(1)} collective-permute-done((bf16[144,384]{1,0:T(8,128)(2,1)S(1)}, bf16[144,384]{1,0:T(8,128)(2,1)S(1)}, u32[]{:S(2)}, u32[]{:S(2)}) %collective-permute-start.8) | collective-permute-done | bytes 110624 | tf_op jit(solution)/shard_map/ppermute | solution.py:241
  34.7 1.0 %shard_map.92 = bf16[128,384]{1,0:T(8,128)(2,1)} custom-call(f32[128,384]{1,0:T(8,128)S(1)} %get-tuple-element.21.own_ref, f32[8,384]{1,0:T(8,128)S(1)} %get-tuple-element.22.logs_ref, bf16[144,384]{1,0:T(8,128)(2,1)S(1)} %collective-permute-done.8.refs_0_, bf16[144,384]{1,0:T(8,128)(2,1)S(1)} %collective-permute-done.9.refs_1_, ...), custom_call_target="tpu_custom_call" | custom-call | tf_op jit(solution)/shard_map/pallas_call | solution.py:360
  (1 shorter events, 0.0 us)
Async XLA Ops:
  1.7 7.0 %collective-permute-start = (f32[2,128]{1,0:T(2,128)}, f32[2,128]{1,0:T(2,128)S(1)}, u32[]{:S(2)}, u32[]{:S(2)}) collective-permute-start(f32[2,128]{1,0:T(2,128)} %shard_map.82.own_ref), channel_id=1, source_target_pairs={{0,1},{1,0},{2,3},{3,2},{4,5},{5,4},{6,7},{7,6},{8,9},{9,8},{10,11... | collective-permute-start | bytes 3080 | tf_op jit(solution)/shard_map/ppermute | solution.py:277
  4.7 12.6 %collective-permute-start.2 = (bf16[128,384]{1,0:T(8,128)(2,1)}, bf16[128,384]{1,0:T(8,128)(2,1)S(1)}, u32[]{:S(2)}, u32[]{:S(2)}) collective-permute-start(bf16[128,384]{1,0:T(8,128)(2,1)} %value_ref.1), channel_id=1, source_target_pairs={{0,16},{2,18},{4,20},{6,22},{8,24},{10,26},{12,28},{14,30},{16,0},... | collective-permute-start | bytes 294920 | tf_op jit(solution)/shard_map/ppermute | solution.py:241
  8.7 0.9 %copy-start = (bf16[128,384]{1,0:T(8,128)(2,1)S(1)}, bf16[128,384]{1,0:T(8,128)(2,1)}, u32[]{:S(2)}) copy-start(bf16[128,384]{1,0:T(8,128)(2,1)} %query_ref.1) | copy-start | bytes 294916
  9.6 0.9 %copy-start.1 = (bf16[128,384]{1,0:T(8,128)(2,1)S(1)}, bf16[128,384]{1,0:T(8,128)(2,1)}, u32[]{:S(2)}) copy-start(bf16[128,384]{1,0:T(8,128)(2,1)} %key_ref.1) | copy-start | bytes 294916
  10.5 0.9 %copy-start.2 = (bf16[128,384]{1,0:T(8,128)(2,1)S(1)}, bf16[128,384]{1,0:T(8,128)(2,1)}, u32[]{:S(2)}) copy-start(bf16[128,384]{1,0:T(8,128)(2,1)} %value_ref.1) | copy-start | bytes 294916
  11.4 0.7 %copy-start.4 = (f32[2,128]{1,0:T(2,128)S(1)}, f32[2,128]{1,0:T(2,128)}, u32[]{:S(2)}) copy-start(f32[2,128]{1,0:T(2,128)} %shard_map.82.own_ref) | copy-start | bytes 3076
  12.1 0.7 %copy-start.5 = (s32[1,16]{1,0:T(1,128)S(1)}, s32[1,16]{1,0:T(1,128)}, u32[]{:S(2)}) copy-start(s32[1,16]{1,0:T(1,128)} %far_ref.1) | copy-start | bytes 196
  12.8 6.4 %collective-permute-start.1 = (bf16[128,384]{1,0:T(8,128)(2,1)S(1)}, bf16[128,384]{1,0:T(8,128)(2,1)S(1)}, u32[]{:S(2)}, u32[]{:S(2)}) collective-permute-start(bf16[128,384]{1,0:T(8,128)(2,1)S(1)} %get-tuple-element.15), channel_id=1, source_target_pairs={{0,16},{2,18},{4,20},{6,22},{8,24},{10,26},{12,28},{14,30},{16,0},... | collective-permute-start | bytes 294920 | tf_op jit(solution)/shard_map/ppermute | solution.py:241
  13.8 5.6 %collective-permute-start.4 = (bf16[144,384]{1,0:T(8,128)(2,1)S(1)}, bf16[144,384]{1,0:T(8,128)(2,1)S(1)}, u32[]{:S(2)}, u32[]{:S(2)}) collective-permute-start(bf16[144,384]{1,0:T(8,128)(2,1)S(1)} %get-tuple-element.14.refs_0_.query_ref), channel_id=1, source_target_pairs={{0,4},{2,6},{4,0},{6,2},{8,12},{10,14},{12,8},{14,10},{16,20},{18,... | collective-permute-start | bytes 331784 | tf_op jit(solution)/shard_map/ppermute | solution.py:241
  15.3 6.0 %collective-permute-start.5 = (bf16[144,384]{1,0:T(8,128)(2,1)S(1)}, bf16[144,384]{1,0:T(8,128)(2,1)S(1)}, u32[]{:S(2)}, u32[]{:S(2)}) collective-permute-start(bf16[144,384]{1,0:T(8,128)(2,1)S(1)} %get-tuple-element.14.refs_0_.query_ref), channel_id=1, source_target_pairs={{0,8},{2,10},{4,12},{6,14},{8,0},{10,2},{12,4},{14,6},{16,24},{18,... | collective-permute-start | bytes 331784 | tf_op jit(solution)/shard_map/ppermute | solution.py:241
  16.9 6.0 %collective-permute-start.6 = (bf16[144,384]{1,0:T(8,128)(2,1)S(1)}, bf16[144,384]{1,0:T(8,128)(2,1)S(1)}, u32[]{:S(2)}, u32[]{:S(2)}) collective-permute-start(bf16[144,384]{1,0:T(8,128)(2,1)S(1)} %get-tuple-element.14.refs_0_.query_ref), channel_id=1, source_target_pairs={{0,12},{2,14},{4,8},{6,10},{8,4},{10,6},{12,0},{14,2},{16,28},{18,... | collective-permute-start | bytes 331784 | tf_op jit(solution)/shard_map/ppermute | solution.py:241
  17.3 5.6 %collective-permute-start.7 = (bf16[256,384]{1,0:T(8,128)(2,1)S(1)}, bf16[256,384]{1,0:T(8,128)(2,1)S(1)}, u32[]{:S(2)}, u32[]{:S(2)}) collective-permute-start(bf16[256,384]{1,0:T(8,128)(2,1)S(1)} %get-tuple-element.16.refs_4_), channel_id=1, source_target_pairs={{0,2},{2,0},{4,6},{6,4},{8,10},{10,8},{12,14},{14,12},{16,18},{18,... | collective-permute-start | bytes 589832 | tf_op jit(solution)/shard_map/ppermute | solution.py:241
  19.3 5.2 %collective-permute-start.3 = (bf16[256,384]{1,0:T(8,128)(2,1)S(1)}, bf16[256,384]{1,0:T(8,128)(2,1)S(1)}, u32[]{:S(2)}, u32[]{:S(2)}) collective-permute-start(bf16[256,384]{1,0:T(8,128)(2,1)S(1)} %shard_map.84.refs_4_), channel_id=1, source_target_pairs={{0,2},{2,0},{4,6},{6,4},{8,10},{10,8},{12,14},{14,12},{16,18},{18,... | collective-permute-start | bytes 589832 | tf_op jit(solution)/shard_map/ppermute | solution.py:241
  25.4 6.9 %collective-permute-start.10 = (bf16[144,384]{1,0:T(8,128)(2,1)S(1)}, bf16[144,384]{1,0:T(8,128)(2,1)S(1)}, u32[]{:S(2)}, u32[]{:S(2)}) collective-permute-start(bf16[144,384]{1,0:T(8,128)(2,1)S(1)} %shard_map.90), channel_id=1, source_target_pairs={{0,12},{2,14},{4,8},{6,10},{8,4},{10,6},{12,0},{14,2},{16,28},{18,... | collective-permute-start | bytes 331784 | tf_op jit(solution)/shard_map/ppermute | solution.py:241
  27.5 3.3 %copy-start.3 = (f32[50,384]{1,0:T(8,128)S(1)}, f32[50,384]{1,0:T(8,128)}, u32[]{:S(2)}) copy-start(f32[50,384]{1,0:T(8,128)} %table_ref.1) | copy-start | bytes 230404
  27.5 3.3 %copy-start.6 = (s32[2]{0:T(128)S(1)}, s32[2]{0:T(128)}, u32[]{:S(2)}) copy-start(s32[2]{0:T(128)} %step_ref.1) | copy-start | bytes 28
  27.5 4.8 %collective-permute-start.9 = (bf16[144,384]{1,0:T(8,128)(2,1)S(1)}, bf16[144,384]{1,0:T(8,128)(2,1)S(1)}, u32[]{:S(2)}, u32[]{:S(2)}) collective-permute-start(bf16[144,384]{1,0:T(8,128)(2,1)S(1)} %shard_map.89), channel_id=1, source_target_pairs={{0,8},{2,10},{4,12},{6,14},{8,0},{10,2},{12,4},{14,6},{16,24},{18,... | collective-permute-start | bytes 331784 | tf_op jit(solution)/shard_map/ppermute | solution.py:241
  29.9 4.8 %collective-permute-start.8 = (bf16[144,384]{1,0:T(8,128)(2,1)S(1)}, bf16[144,384]{1,0:T(8,128)(2,1)S(1)}, u32[]{:S(2)}, u32[]{:S(2)}) collective-permute-start(bf16[144,384]{1,0:T(8,128)(2,1)S(1)} %shard_map.88), channel_id=1, source_target_pairs={{0,4},{2,6},{4,0},{6,2},{8,12},{10,14},{12,8},{14,10},{16,20},{18,... | collective-permute-start | bytes 331784 | tf_op jit(solution)/shard_map/ppermute | solution.py:241

commit v10 on v6

v10 whole, which is shorter than its diff:
```python
import functools

import jax
import jax.numpy as jnp
from jax import lax
from jax.experimental import pallas as pl
from jax.experimental.pallas import tpu as pltpu
from jax.sharding import PartitionSpec as P

HD = 128
BLK = 64
FRAME_TOK = 1560
EPSILON = 1e-06
LOG2E = 1.4426950408889634
SCALE = HD ** (-0.5) * LOG2E
MASKED = -1e30
EXTRA = 16
ANY = pl.BlockSpec(memory_space=pl.ANY)
VMEM = pl.BlockSpec(memory_space=pltpu.VMEM)
SMEM = pl.BlockSpec(memory_space=pltpu.SMEM)


def spread(row):
    return jnp.broadcast_to(row, (row.shape[1], row.shape[1])).T


def squares(source_ref):
    wide = source_ref[:HD, :].astype(jnp.float32)
    square = wide * wide
    part = square[:, :HD]
    for low in range(HD, square.shape[1], HD):
        part = part + square[:, low : low + HD]
    return jnp.sum(part.T, axis=0, keepdims=True)


def own_kernel(
    query_hbm,
    key_hbm,
    value_hbm,
    far_hbm,
    query_out,
    key_out,
    value_out,
    sums_out,
    query_ref,
    far_ref,
    sems,
):
    rows, width = query_ref.shape
    copies = [
        pltpu.make_async_copy(query_hbm, query_ref, sems.at[0]),
        pltpu.make_async_copy(key_hbm, key_out, sems.at[1]),
        pltpu.make_async_copy(far_hbm, far_ref, sems.at[2]),
        pltpu.make_async_copy(value_hbm, value_out, sems.at[3]),
    ]
    for copy in copies:
        copy.start()
    query_out[rows:, HD:] = jnp.zeros((EXTRA, width - HD), jnp.bfloat16)
    sums_out[...] = jnp.zeros_like(sums_out)
    copies[0].wait()
    query_out[:rows, :] = query_ref[...]
    sums_out[0:1, :] = squares(query_ref)
    copies[1].wait()
    sums_out[1:2, :] = squares(key_out)
    copies[2].wait()
    far = far_ref[...].astype(jnp.float32)
    far = jnp.concatenate([far, jnp.full((1, HD - far.shape[1]), -1.0)], axis=1)
    query_out[rows:, :HD] = jnp.broadcast_to(far, (EXTRA, HD)).astype(jnp.bfloat16)
    copies[3].wait()


def sums_kernel(lines, before_ref, *refs):
    *sources, out_ref = refs
    out_ref[...] = before_ref[...]
    for line, source_ref in zip(lines, sources):
        out_ref[line : line + 1, :] = squares(source_ref)


def factor_of(line, full_width):
    return spread(lax.rsqrt(line / full_width + EPSILON))


def normed(source_ref, factor, gain_ref):
    parts = []
    for low in range(0, source_ref.shape[1], HD):
        wide = source_ref[:HD, low : low + HD].astype(jnp.float32)
        parts.append((wide * factor * gain_ref[:, low : low + HD]).astype(jnp.bfloat16))
    return jnp.concatenate(parts, axis=1)


def query_kernel(full_width, key_masks, gain_ref, own_ref, other_ref, *refs):
    queries, (query_out, bias_out) = refs[:2], refs[2:]
    me = lax.axis_index("tm")
    query_mask = lax.axis_size("tm") // 4
    lane = lax.broadcasted_iota(jnp.int32, (1, HD), 1)
    half = (lane >= BLK).astype(jnp.float32)
    for place, query_ref in enumerate(queries):
        line = 2 * place
        total = own_ref[line : line + 1, :] + other_ref[line : line + 1, :]
        query_out[place * HD : (place + 1) * HD, :] = normed(
            query_ref, factor_of(total, full_width), gain_ref
        )
        far = query_ref[HD:, :HD].astype(jnp.float32)[:1]
        query_id = me ^ (place * query_mask)
        for block, key_mask in enumerate(key_masks):
            key_id = me ^ key_mask
            choice = jnp.sum(jnp.where(lane == key_id, far, 0.0), axis=1, keepdims=True)
            taken = (choice == half) | (jnp.abs(query_id - key_id) <= 1)
            bias_out[8 * place : 8 * place + 8, block * HD : (block + 1) * HD] = (
                jnp.broadcast_to(jnp.where(taken, 0.0, MASKED), (8, HD))
            )


def pack_kernel(full_width, near, held, gain_ref, own_ref, other_ref, cross_ref, *refs):
    keys, values, pack_out = refs[:held], refs[held : 2 * held], refs[2 * held]
    for place, key_ref in enumerate(keys):
        line = 1 + place + (place > 0)
        if place < near:
            total = own_ref[line : line + 1, :] + other_ref[line : line + 1, :]
        else:
            total = squares(key_ref) + cross_ref[3:4, :]
        pack_out[place * HD : (place + 1) * HD, :] = normed(
            key_ref, factor_of(total, full_width), gain_ref
        )
    for place, value_ref in enumerate(values, start=held):
        pack_out[place * HD : (place + 1) * HD, :] = value_ref[...]


def absorb(query, pack_ref, biases, olds, low):
    high, half = low + HD, pack_ref.shape[0] // 2
    scores = lax.dot_general(
        query,
        pack_ref[:half, low:high],
        (((1,), (1,)), ((), ())),
        preferred_element_type=jnp.float32,
    )
    tops, totals, rounded = [], [], []
    for place, bias in enumerate(biases):
        logits = scores[place * HD : (place + 1) * HD] * SCALE + bias
        top = jnp.broadcast_to(jnp.max(logits, axis=1, keepdims=True), (HD, HD))
        if olds is not None:
            top = jnp.maximum(top, olds[place][0])
        weights = [
            jnp.exp2(logits[:, left : left + HD] - top)
            for left in range(0, logits.shape[1], HD)
        ]
        total = jnp.sum(functools.reduce(jnp.add, weights), axis=1, keepdims=True)
        tops.append(top)
        totals.append(jnp.broadcast_to(total, (HD, HD)))
        rounded.append(
            jnp.concatenate([weight.astype(jnp.bfloat16) for weight in weights], axis=1)
        )
    added = jnp.dot(
        jnp.concatenate(rounded, axis=0),
        pack_ref[half:, low:high],
        preferred_element_type=jnp.float32,
    )
    results = []
    for place in range(len(biases)):
        context = added[place * HD : (place + 1) * HD]
        total = totals[place]
        if olds is not None:
            fade = jnp.exp2(olds[place][0] - tops[place])
            total = total + olds[place][1] * fade
            context = context + olds[place][2] * fade
        results.append((tops[place], total, context))
    return results


def own_attention(query_ref, bias_ref, pack_ref, context_out, stats_out):
    keys = pack_ref.shape[0] // 2
    biases = [bias_ref[8 * place : 8 * place + 1, :keys] for place in range(2)]
    for low in range(0, query_ref.shape[1], HD):
        results = absorb(query_ref[:, low : low + HD], pack_ref, biases, None, low)
        for place, (top, total, context) in enumerate(results):
            part, wide = slice(place * HD, (place + 1) * HD), 2 * low
            context_out[part, low : low + HD] = context
            stats_out[part, wide : wide + HD] = top
            stats_out[part, wide + HD : wide + 2 * HD] = total


def last_attention(place, query_ref, bias_ref, pack_ref, context_ref, stats_ref, *outs):
    width, keys = query_ref.shape[1], pack_ref.shape[0] // 2
    part = slice(place * HD, (place + 1) * HD)
    bias = bias_ref[8 * place : 8 * place + 1, keys:]
    lane = lax.broadcasted_iota(jnp.int32, (1, HD), 1)
    columns = jnp.zeros((HD, HD), jnp.float32)
    for low in range(0, width, HD):
        wide = 2 * low
        old = (
            stats_ref[part, wide : wide + HD],
            stats_ref[part, wide + HD : wide + 2 * HD],
            context_ref[part, low : low + HD],
        )
        ((top, total, context),) = absorb(
            query_ref[part, low : low + HD], pack_ref, [bias], [old], low
        )
        outs[0][:HD, low : low + HD] = context.astype(outs[0].dtype)
        line = wide // HD
        columns = jnp.where(lane == line, top, jnp.where(lane == line + 1, total, columns))
    lines = columns.T
    sub = lax.broadcasted_iota(jnp.int32, (EXTRA, HD), 0)
    for low in range(0, width, HD):
        line = 2 * low // HD
        pair = (lines[line : line + 1, :], lines[line + 1 : line + 2, :])
        if place == 0:
            for row, value in enumerate(pair):
                outs[1][8 * row : 8 * row + 8, low : low + HD] = jnp.broadcast_to(value, (8, HD))
        else:
            piece_rows = jnp.zeros((EXTRA, HD), jnp.float32)
            for row, value in enumerate(pair):
                first = value.astype(jnp.bfloat16).astype(jnp.float32)
                second = (value - first).astype(jnp.bfloat16).astype(jnp.float32)
                for piece, part_value in enumerate((first, second, value - first - second)):
                    piece_rows = jnp.where(sub == 3 * row + piece, part_value, piece_rows)
            outs[0][HD:, low : low + HD] = piece_rows.astype(jnp.bfloat16)


def gate_kernel(step_ref, table_ref, out_ref):
    rows = out_ref.shape[0] // 2
    start = lax.axis_index("tm") * HD
    first = step_ref[start // FRAME_TOK]
    last = step_ref[(start + HD - 1) // FRAME_TOK]
    out_ref[:rows, :] = jnp.broadcast_to(table_ref[pl.ds(first, 1), :], (rows, out_ref.shape[1]))
    out_ref[rows:, :] = jnp.broadcast_to(table_ref[pl.ds(last, 1), :], (rows, out_ref.shape[1]))


def merge_kernel(own_ref, lines_ref, packet_ref, gate_ref, out_ref):
    rows, width = own_ref.shape
    pieces = packet_ref[rows:, :].astype(jnp.float32)
    own_top, own_total = lines_ref[0:1, :], lines_ref[8:9, :]
    other_top = pieces[0:1] + pieces[1:2] + pieces[2:3]
    other_total = pieces[3:4] + pieces[4:5] + pieces[5:6]
    top = jnp.maximum(own_top, other_top)
    own_share, other_share = jnp.exp2(own_top - top), jnp.exp2(other_top - top)
    scale = 1.0 / (own_total * own_share + other_total * other_share)
    own_share, other_share = own_share * scale, other_share * scale
    start = lax.axis_index("tm") * rows
    first_rows = (start // FRAME_TOK + 1) * FRAME_TOK - start
    row_ids = lax.broadcasted_iota(jnp.int32, (rows, 1), 0)
    for low in range(0, width, HD):
        high = low + HD
        context = own_ref[:, low:high] * spread(own_share[:, low:high])
        other = packet_ref[:rows, low:high].astype(jnp.float32)
        context += other * spread(other_share[:, low:high])
        gate = jnp.where(
            row_ids < first_rows, gate_ref[0:1, low:high], gate_ref[8:9, low:high]
        )
        out_ref[:, low:high] = (context * gate).astype(jnp.bfloat16)


def exchange(array, mask):
    count = lax.axis_size("tm")
    return lax.ppermute(array, "tm", [(i, i ^ mask) for i in range(count)])


def gathered(array, bits):
    held = {0: array}
    for bit in bits:
        for mask in list(held):
            held[mask ^ bit] = exchange(held[mask], bit)
    return held


def local(
    query_proj, key_proj, value_proj, query_gain, key_gain, gate_table, frame_step, far_blocks
):
    rows, width = query_proj.shape
    count = lax.axis_size("tm")
    splits = lax.axis_size("head")
    full_width = width * splits
    params = pltpu.CompilerParams(vmem_limit_bytes=(8 + count // 2) * 2**20)
    query_mask = count // 4
    bits = [1 << place for place in range(1, count.bit_length() - 1)]
    bits = [bit for bit in bits[::-1] if bit != query_mask]
    query_gain = query_gain.reshape(1, width)
    key_gain = key_gain.reshape(1, width)

    lines = 2 + 2 ** len(bits)
    lines += -lines % 8
    query_packet, own_key, own_value, own_sums = pl.pallas_call(
        own_kernel,
        out_shape=[
            jax.ShapeDtypeStruct((rows + EXTRA, width), jnp.bfloat16),
            jax.ShapeDtypeStruct((rows, width), jnp.bfloat16),
            jax.ShapeDtypeStruct((rows, width), jnp.bfloat16),
            jax.ShapeDtypeStruct((lines, rows), jnp.float32),
        ],
        in_specs=[ANY] * 4,
        out_specs=[VMEM] * 4,
        scratch_shapes=[
            pltpu.VMEM((rows, width), jnp.bfloat16),
            pltpu.VMEM(far_blocks.shape, jnp.int32),
            pltpu.SemaphoreType.DMA((4,)),
        ],
    )(query_proj, key_proj, value_proj, far_blocks)
    keys = gathered(key_proj, bits)
    keys[0] = own_key
    values = gathered(own_value, bits)
    queries = [query_packet, exchange(query_packet, query_mask)]
    masks = sorted(keys, key=lambda mask: (mask.bit_count(), -mask))
    near = 1 + len(bits)

    def summed(sums, sources, held):
        return pl.pallas_call(
            functools.partial(sums_kernel, held),
            out_shape=jax.ShapeDtypeStruct(own_sums.shape, jnp.float32),
            in_specs=[VMEM] * (1 + len(sources)),
            out_specs=VMEM,
            compiler_params=params,
        )(sums, *sources)

    sources = [queries[1]] + [keys[mask] for mask in masks[1:near]]
    sums = summed(own_sums, sources, range(2, near + 2))
    if splits == 2:
        others = lax.ppermute(sums, "head", [(0, 1), (1, 0)])
        pairs = []
        for i in range(2 * count):
            pairs.append((i, ((i // 2) ^ bits[1]) * 2 + (i % 2 ^ 1)))
        crossed = lax.ppermute(sums, ("tm", "head"), pairs)
    else:
        sources = [keys[mask] for mask in masks[near:]]
        sums = summed(sums, sources, range(near + 2, len(masks) + 2))
        sums = lax.psum(sums, "head")
        others = crossed = jnp.zeros_like(sums)

    all_masks = masks + [mask ^ 1 for mask in masks]
    query_norm, biases = pl.pallas_call(
        functools.partial(query_kernel, width * splits, all_masks),
        out_shape=[
            jax.ShapeDtypeStruct((2 * rows, width), jnp.bfloat16),
            jax.ShapeDtypeStruct((16, len(all_masks) * HD), jnp.float32),
        ],
        in_specs=[VMEM] * 5,
        out_specs=[VMEM] * 2,
        compiler_params=params,
    )(query_gain, sums, others, *queries)

    pack = pl.pallas_call(
        functools.partial(
            pack_kernel, width * splits, near if splits == 2 else len(masks), len(masks)
        ),
        out_shape=jax.ShapeDtypeStruct((2 * len(masks) * rows, width), jnp.bfloat16),
        in_specs=[VMEM] * (4 + 2 * len(masks)),
        out_specs=VMEM,
        compiler_params=params,
    )(
        key_gain,
        sums,
        others,
        crossed,
        *[keys[mask] for mask in masks],
        *[values[mask] for mask in masks],
    )
    other_pack = exchange(pack, 1)

    state = pl.pallas_call(
        own_attention,
        out_shape=[
            jax.ShapeDtypeStruct((2 * rows, width), jnp.float32),
            jax.ShapeDtypeStruct((2 * rows, 2 * width), jnp.float32),
        ],
        in_specs=[VMEM] * 3,
        out_specs=[VMEM] * 2,
        compiler_params=params,
    )(query_norm, biases, pack)

    def last(place, out_shape):
        return pl.pallas_call(
            functools.partial(last_attention, place),
            out_shape=out_shape,
            in_specs=[VMEM] * 5,
            out_specs=[VMEM] * len(out_shape),
            compiler_params=params,
        )(query_norm, biases, other_pack, *state)

    (packet,) = last(1, [jax.ShapeDtypeStruct((rows + EXTRA, width), jnp.bfloat16)])
    own, own_lines = last(
        0,
        [
            jax.ShapeDtypeStruct((rows, width), jnp.float32),
            jax.ShapeDtypeStruct((16, width), jnp.float32),
        ],
    )
    gates = pl.pallas_call(
        gate_kernel,
        out_shape=jax.ShapeDtypeStruct((16, width), jnp.float32),
        in_specs=[SMEM, VMEM],
        out_specs=VMEM,
        compiler_params=params,
    )(frame_step, gate_table)
    packet = exchange(packet, query_mask)

    return pl.pallas_call(
        merge_kernel,
        out_shape=jax.ShapeDtypeStruct((rows, width), jnp.bfloat16),
        in_specs=[VMEM] * 4,
        out_specs=VMEM,
        compiler_params=params,
    )(own, own_lines, packet, gates)


def solution(mesh):
    return jax.shard_map(
        local,
        mesh=mesh,
        in_specs=(
            P("tm", "head"),
            P("tm", "head"),
            P("tm", "head"),
            P("head"),
            P("head"),
            P(None, "head"),
            P(),
            P("tm", None),
        ),
        out_specs=P("tm", "head"),
        check_vma=False,
    )
```

time: 29.4 us -> 30.6 us (1.041)
  waiting for transfers between devices: 6.17 us -> 8.54 us
  Pallas kernels: 7.39 us -> 6.79 us
  starting transfers between devices: 14.9 us -> 14.4 us
    ppermute x0 -> x1, waiting for transfers between devices: none -> 2.42 us  [local(): crossed = lax.ppermute(sums, ('tm', 'head'), pairs)]
    ppermute x9, starting transfers between devices: 13.3 us -> 12.3 us  [exchange(): return lax.ppermute(array, 'tm', [(i, i ^ mask) for i in range(count)])]
    ppermute x9, waiting for transfers between devices: 5.25 us -> 4.56 us  [exchange(): return lax.ppermute(array, 'tm', [(i, i ^ mask) for i in range(count)])]
    ppermute x1, waiting for transfers between devices: 0.92 us -> 1.56 us  [local(): others = lax.ppermute(sums, 'head', [(0, 1), (1, 0)])]
    pallas_call x6, Pallas kernels: 4.13 us -> 3.5 us  [the longest x2 1.91 us: last(): pl.pallas_call(functools.partial(last_attention, place), out_shape=out_sh...]
    ppermute x0 -> x1, starting transfers between devices: none -> 0.51 us  [local(): crossed = lax.ppermute(sums, ('tm', 'head'), pairs)]
  transfers between devices with their start and end apart: 10 -> 11, of which waited for: 6 -> 5; matrix products, arithmetic and copies ran while one was open for 0% -> 0% of each run, Pallas kernels for 19% -> 16%
where the time goes in v10:
time: 30.6 us; the launch traced here: 30.5 us
  starting transfers between devices  14.4 us (47%)
  waiting for transfers between devices  8.54 us (28%)
  Pallas kernels  6.79 us (22%)
  local copies, waits for them, and re-layouts  0.61 us (2%)
    ppermute x9, starting transfers between devices, exchange(): return lax.ppermute(array, 'tm', [(i, i ^ mask) for i in range(count)])  12.3 us
    ppermute x9, waiting for transfers between devices, exchange(): return lax.ppermute(array, 'tm', [(i, i ^ mask) for i in range(count)])  4.56 us
    ppermute x1, waiting for transfers between devices, local(): crossed = lax.ppermute(sums, ('tm', 'head'), pairs)  2.42 us
    pallas_call x2, Pallas kernels, last(): pl.pallas_call(functools.partial(last_attention, place), out_shape=out_sh...  1.91 us
    pallas_call x1, Pallas kernels, local(): pl.pallas_call(own_kernel, out_shape=[jax.ShapeDtypeStruct((rows + EXTRA,...  1.88 us
    ppermute x1, starting transfers between devices, local(): others = lax.ppermute(sums, 'head', [(0, 1), (1, 0)])  1.58 us
    ppermute x1, waiting for transfers between devices, local(): others = lax.ppermute(sums, 'head', [(0, 1), (1, 0)])  1.56 us
    pallas_call x1, Pallas kernels, local(): pl.pallas_call(own_attention, out_shape=[jax.ShapeDtypeStruct((2 * rows,...  1.06 us
  transfers between devices with their start and end apart: 11, of which 5 were waited for; matrix products, arithmetic and copies ran while one was open for 0% of the time, Pallas kernels for 16%

profile of v10, /device:TPU:0, one launch (start us, length us, event | category | flops | bytes accessed | tf_op | source)
XLA Modules:
  0.0 30.5 jit_solution(3549656379134925840)
XLA Ops:
  0.0 0.0 copy-start.6
  0.0 4.0 %collective-permute-start.1 = (bf16[128,384]{1,0:T(8,128)(2,1)}, bf16[128,384]{1,0:T(8,128)(2,1)S(1)}, u32[]{:S(2)}, u32[]{:S(2)}) collective-permute-start(bf16[128,384]{1,0:T(8,128)(2,1)} %key_hbm.1), channel_id=1, source_target_pairs={{0,16},{2,18},{4,20},{6,22},{8,24},{10,26},{12,28},{14,30},{16,0},... | collective-permute-start | bytes 294920 | tf_op jit(solution)/shard_map/ppermute | solution.py:254
  4.0 1.9 %shard_map.82 = (bf16[144,384]{1,0:T(8,128)(2,1)}, bf16[128,384]{1,0:T(8,128)(2,1)}, bf16[128,384]{1,0:T(8,128)(2,1)}, f32[8,128]{1,0:T(8,128)}) custom-call(bf16[128,384]{1,0:T(8,128)(2,1)} %query_hbm.1, bf16[128,384]{1,0:T(8,128)(2,1)} %key_hbm.1, bf16[128,384]{1,0:T(8,128)(2,1)} %value_hbm.1, s32[1,16]{1,0:T(1,128)} %far_hbm.1), custom_call_target="tpu_custom_call" | custom-call | tf_op jit(solution)/shard_map/pallas_call | solution.py:281
  5.9 0.0 copy-start.4
  5.9 0.1 collective-permute-start.6
  6.0 1.9 %collective-permute-start = (bf16[144,384]{1,0:T(8,128)(2,1)}, bf16[144,384]{1,0:T(8,128)(2,1)S(1)}, u32[]{:S(2)}, u32[]{:S(2)}) collective-permute-start(bf16[144,384]{1,0:T(8,128)(2,1)} %get-tuple-element.16.refs_0_), channel_id=1, source_target_pairs={{0,8},{2,10},{4,12},{6,14},{8,0},{10,2},{12,4},{14,6},{16,24},{18,... | collective-permute-start | bytes 331784 | tf_op jit(solution)/shard_map/ppermute | solution.py:254
  7.9 0.0 copy-done.6
  7.9 1.5 %collective-permute-start.2 = (bf16[128,384]{1,0:T(8,128)(2,1)S(1)}, bf16[128,384]{1,0:T(8,128)(2,1)S(1)}, u32[]{:S(2)}, u32[]{:S(2)}) collective-permute-start(bf16[128,384]{1,0:T(8,128)(2,1)S(1)} %copy-done.6), channel_id=1, source_target_pairs={{0,4},{2,6},{4,0},{6,2},{8,12},{10,14},{12,8},{14,10},{16,20},{18,... | collective-permute-start | bytes 294920 | tf_op jit(solution)/shard_map/ppermute | solution.py:254
  9.4 0.5 %collective-permute-start.7 = (bf16[128,384]{1,0:T(8,128)(2,1)}, bf16[128,384]{1,0:T(8,128)(2,1)S(1)}, u32[]{:S(2)}, u32[]{:S(2)}) collective-permute-start(bf16[128,384]{1,0:T(8,128)(2,1)} %get-tuple-element.20.refs_4_), channel_id=1, source_target_pairs={{0,4},{2,6},{4,0},{6,2},{8,12},{10,14},{12,8},{14,10},{16,20},{18,... | collective-permute-start | bytes 294920 | tf_op jit(solution)/shard_map/ppermute | solution.py:254
  9.9 0.0 collective-permute-done.1.refs_1_
  9.9 1.5 %collective-permute-start.5 = (bf16[128,384]{1,0:T(8,128)(2,1)S(1)}, bf16[128,384]{1,0:T(8,128)(2,1)S(1)}, u32[]{:S(2)}, u32[]{:S(2)}) collective-permute-start(bf16[128,384]{1,0:T(8,128)(2,1)S(1)} %collective-permute-done.1.refs_1_), channel_id=1, source_target_pairs={{0,4},{2,6},{4,0},{6,2},{8,12},{10,14},{12,8},{14,10},{16,20},{18,... | collective-permute-start | bytes 294920 | tf_op jit(solution)/shard_map/ppermute | solution.py:254
  11.4 1.7 %collective-permute-done.6.refs_5_ = bf16[128,384]{1,0:T(8,128)(2,1)S(1)} collective-permute-done((bf16[128,384]{1,0:T(8,128)(2,1)}, bf16[128,384]{1,0:T(8,128)(2,1)S(1)}, u32[]{:S(2)}, u32[]{:S(2)}) %collective-permute-start.6) | collective-permute-done | bytes 98336 | tf_op jit(solution)/shard_map/ppermute | solution.py:254
  13.1 1.5 %collective-permute-start.8 = (bf16[128,384]{1,0:T(8,128)(2,1)S(1)}, bf16[128,384]{1,0:T(8,128)(2,1)S(1)}, u32[]{:S(2)}, u32[]{:S(2)}) collective-permute-start(bf16[128,384]{1,0:T(8,128)(2,1)S(1)} %collective-permute-done.6.refs_5_), channel_id=1, source_target_pairs={{0,4},{2,6},{4,0},{6,2},{8,12},{10,14},{12,8},{14,10},{16,20},{18,... | collective-permute-start | bytes 294920 | tf_op jit(solution)/shard_map/ppermute | solution.py:254
  14.6 0.0 collective-permute-done.2.refs_2_
  14.6 0.0 collective-permute-done.refs_0_.refs_1_
  14.6 0.0 copy-done.4
  14.6 0.0 copy-start.7
  14.6 0.0 copy-start.1
  14.6 0.0 copy-start.2
  14.6 0.1 shard_map.83.own_ref
  14.8 1.6 %collective-permute-start.3 = (f32[8,128]{1,0:T(8,128)S(1)}, f32[8,128]{1,0:T(8,128)S(1)}, u32[]{:S(2)}, u32[]{:S(2)}) collective-permute-start(f32[8,128]{1,0:T(8,128)S(1)} %shard_map.83.own_ref), channel_id=1, source_target_pairs={{0,1},{1,0},{2,3},{3,2},{4,5},{5,4},{6,7},{7,6},{8,9},{9,8},{10,11... | collective-permute-start | bytes 12296 | tf_op jit(solution)/shard_map/ppermute | solution.py:316
  16.4 0.5 %collective-permute-start.4 = (f32[8,128]{1,0:T(8,128)S(1)}, f32[8,128]{1,0:T(8,128)S(1)}, u32[]{:S(2)}, u32[]{:S(2)}) collective-permute-start(f32[8,128]{1,0:T(8,128)S(1)} %shard_map.83.own_ref), channel_id=1, source_target_pairs={{0,5},{1,4},{2,7},{3,6},{4,1},{5,0},{6,3},{7,2},{8,13},{9,12},{10,... | collective-permute-start | bytes 12296 | tf_op jit(solution)/shard_map/ppermute | solution.py:320
  16.9 0.0 copy-done.7
  16.9 0.0 collective-permute-done.7.refs_6_
  16.9 1.6 %collective-permute-done.3.other_ref = f32[8,128]{1,0:T(8,128)S(1)} collective-permute-done((f32[8,128]{1,0:T(8,128)S(1)}, f32[8,128]{1,0:T(8,128)S(1)}, u32[]{:S(2)}, u32[]{:S(2)}) %collective-permute-start.3) | collective-permute-done | bytes 4128 | tf_op jit(solution)/shard_map/ppermute | solution.py:316
  18.4 2.4 %collective-permute-done.4.cross_ref = f32[8,128]{1,0:T(8,128)S(1)} collective-permute-done((f32[8,128]{1,0:T(8,128)S(1)}, f32[8,128]{1,0:T(8,128)S(1)}, u32[]{:S(2)}, u32[]{:S(2)}) %collective-permute-start.4) | collective-permute-done | bytes 4128 | tf_op jit(solution)/shard_map/ppermute | solution.py:320
  20.9 0.0 collective-permute-done.5.refs_3_
  20.9 0.0 collective-permute-done.8.refs_7_
  20.9 0.0 copy-done.1
  20.9 0.0 copy-done.2
  20.9 0.0 copy-start.8
  20.9 0.0 copy-start
  20.9 0.2 shard_map.85.pack_ref
  21.1 0.1 collective-permute-start.9
  21.2 0.3 %copy-done.8 = f32[384]{0:T(512)S(1)} copy-done((f32[384]{0:T(512)S(1)}, f32[384]{0:T(512)}, u32[]{:S(2)}) %copy-start.8) | copy-done | bytes 1560
  21.6 0.2 copy-done
  21.8 0.2 shard_map.84
  22.0 1.1 %shard_map.86 = (f32[256,384]{1,0:T(8,128)S(1)}, f32[256,768]{1,0:T(8,128)S(1)}) custom-call(bf16[256,384]{1,0:T(8,128)(2,1)S(1)} %get-tuple-element.17.query_ref, f32[16,1024]{1,0:T(8,128)S(1)} %get-tuple-element.18.bias_ref, bf16[1024,384]{1,0:T(8,128)(2,1)S(1)} %shard_map.85.pack_ref), custom_call_target="tpu_custom_call" | custom-call | tf_op jit(solution)/shard_map/pallas_call | solution.py:357
  23.0 0.5 %collective-permute-done.9.pack_ref = bf16[1024,384]{1,0:T(8,128)(2,1)S(1)} collective-permute-done((bf16[1024,384]{1,0:T(8,128)(2,1)S(1)}, bf16[1024,384]{1,0:T(8,128)(2,1)S(1)}, u32[]{:S(2)}, u32[]{:S(2)}) %collective-permute-start.9) | collective-permute-done | bytes 786464 | tf_op jit(solution)/shard_map/ppermute | solution.py:254
  23.5 0.0 copy-start.3
  23.5 1.0 %shard_map.88 = bf16[144,384]{1,0:T(8,128)(2,1)S(1)} custom-call(bf16[256,384]{1,0:T(8,128)(2,1)S(1)} %get-tuple-element.17.query_ref, f32[16,1024]{1,0:T(8,128)S(1)} %get-tuple-element.18.bias_ref, bf16[1024,384]{1,0:T(8,128)(2,1)S(1)} %collective-permute-done.9.pack_ref, f32[256,384]{1,0:T(8,128)S(1)} %get-tuple-element.21.context_ref, ...), custom_call_target="tpu_custom_call" | custom-call | tf_op jit(solution)/shard_map/pallas_call | solution.py:369
  24.5 1.2 %collective-permute-start.10 = (bf16[144,384]{1,0:T(8,128)(2,1)S(1)}, bf16[144,384]{1,0:T(8,128)(2,1)S(1)}, u32[]{:S(2)}, u32[]{:S(2)}) collective-permute-start(bf16[144,384]{1,0:T(8,128)(2,1)S(1)} %shard_map.88), channel_id=1, source_target_pairs={{0,8},{2,10},{4,12},{6,14},{8,0},{10,2},{12,4},{14,6},{16,24},{18,... | collective-permute-start | bytes 331784 | tf_op jit(solution)/shard_map/ppermute | solution.py:254
  25.7 0.0 copy-done.3
  25.7 0.0 copy-done.5
  25.7 0.6 %shard_map.89.gate_ref = f32[16,384]{1,0:T(8,128)S(1)} custom-call(s32[2]{0:T(128)S(1)} %copy-done.5, f32[50,384]{1,0:T(8,128)S(1)} %copy-done.3), custom_call_target="tpu_custom_call" | custom-call | tf_op jit(solution)/shard_map/pallas_call | solution.py:385
  26.3 0.9 %shard_map.87 = (f32[128,384]{1,0:T(8,128)S(1)}, f32[16,384]{1,0:T(8,128)S(1)}) custom-call(bf16[256,384]{1,0:T(8,128)(2,1)S(1)} %get-tuple-element.17.query_ref, f32[16,1024]{1,0:T(8,128)S(1)} %get-tuple-element.18.bias_ref, bf16[1024,384]{1,0:T(8,128)(2,1)S(1)} %collective-permute-done.9.pack_ref, f32[256,384]{1,0:T(8,128)S(1)} %get-tuple-element.21.context_ref, ...), custom_call_target="tpu_custom_call" | custom-call | tf_op jit(solution)/shard_map/pallas_call | solution.py:369
  27.2 2.4 %collective-permute-done.10.packet_ref = bf16[144,384]{1,0:T(8,128)(2,1)S(1)} collective-permute-done((bf16[144,384]{1,0:T(8,128)(2,1)S(1)}, bf16[144,384]{1,0:T(8,128)(2,1)S(1)}, u32[]{:S(2)}, u32[]{:S(2)}) %collective-permute-start.10) | collective-permute-done | bytes 110624 | tf_op jit(solution)/shard_map/ppermute | solution.py:254
  29.6 0.8 %shard_map.90 = bf16[128,384]{1,0:T(8,128)(2,1)} custom-call(f32[128,384]{1,0:T(8,128)S(1)} %get-tuple-element.23.own_ref, f32[16,384]{1,0:T(8,128)S(1)} %get-tuple-element.24.lines_ref, bf16[144,384]{1,0:T(8,128)(2,1)S(1)} %collective-permute-done.10.packet_ref, f32[16,384]{1,0:T(8,128)S(1)} %shard_map.89.gate_ref), custom_call_target="tpu_custom_call" | custom-call | tf_op jit(solution)/shard_map/pallas_call | solution.py:394
  (3 shorter events, 0.0 us)
Async XLA Ops:
  0.0 7.9 %copy-start.6 = (bf16[128,384]{1,0:T(8,128)(2,1)S(1)}, bf16[128,384]{1,0:T(8,128)(2,1)}, u32[]{:S(2)}) copy-start(bf16[128,384]{1,0:T(8,128)(2,1)} %key_hbm.1) | copy-start | bytes 294916
  0.0 9.9 %collective-permute-start.1 = (bf16[128,384]{1,0:T(8,128)(2,1)}, bf16[128,384]{1,0:T(8,128)(2,1)S(1)}, u32[]{:S(2)}, u32[]{:S(2)}) collective-permute-start(bf16[128,384]{1,0:T(8,128)(2,1)} %key_hbm.1), channel_id=1, source_target_pairs={{0,16},{2,18},{4,20},{6,22},{8,24},{10,26},{12,28},{14,30},{16,0},... | collective-permute-start | bytes 294920 | tf_op jit(solution)/shard_map/ppermute | solution.py:254
  5.9 8.7 %copy-start.4 = (f32[8,128]{1,0:T(8,128)S(1)}, f32[8,128]{1,0:T(8,128)}, u32[]{:S(2)}) copy-start(f32[8,128]{1,0:T(8,128)} %get-tuple-element.15.before_ref) | copy-start | bytes 12292
  5.9 7.2 %collective-permute-start.6 = (bf16[128,384]{1,0:T(8,128)(2,1)}, bf16[128,384]{1,0:T(8,128)(2,1)S(1)}, u32[]{:S(2)}, u32[]{:S(2)}) collective-permute-start(bf16[128,384]{1,0:T(8,128)(2,1)} %get-tuple-element.20.refs_4_), channel_id=1, source_target_pairs={{0,16},{2,18},{4,20},{6,22},{8,24},{10,26},{12,28},{14,30},{16,0},... | collective-permute-start | bytes 294920 | tf_op jit(solution)/shard_map/ppermute | solution.py:254
  6.0 8.6 %collective-permute-start = (bf16[144,384]{1,0:T(8,128)(2,1)}, bf16[144,384]{1,0:T(8,128)(2,1)S(1)}, u32[]{:S(2)}, u32[]{:S(2)}) collective-permute-start(bf16[144,384]{1,0:T(8,128)(2,1)} %get-tuple-element.16.refs_0_), channel_id=1, source_target_pairs={{0,8},{2,10},{4,12},{6,14},{8,0},{10,2},{12,4},{14,6},{16,24},{18,... | collective-permute-start | bytes 331784 | tf_op jit(solution)/shard_map/ppermute | solution.py:254
  7.9 6.7 %collective-permute-start.2 = (bf16[128,384]{1,0:T(8,128)(2,1)S(1)}, bf16[128,384]{1,0:T(8,128)(2,1)S(1)}, u32[]{:S(2)}, u32[]{:S(2)}) collective-permute-start(bf16[128,384]{1,0:T(8,128)(2,1)S(1)} %copy-done.6), channel_id=1, source_target_pairs={{0,4},{2,6},{4,0},{6,2},{8,12},{10,14},{12,8},{14,10},{16,20},{18,... | collective-permute-start | bytes 294920 | tf_op jit(solution)/shard_map/ppermute | solution.py:254
  9.4 7.5 %collective-permute-start.7 = (bf16[128,384]{1,0:T(8,128)(2,1)}, bf16[128,384]{1,0:T(8,128)(2,1)S(1)}, u32[]{:S(2)}, u32[]{:S(2)}) collective-permute-start(bf16[128,384]{1,0:T(8,128)(2,1)} %get-tuple-element.20.refs_4_), channel_id=1, source_target_pairs={{0,4},{2,6},{4,0},{6,2},{8,12},{10,14},{12,8},{14,10},{16,20},{18,... | collective-permute-start | bytes 294920 | tf_op jit(solution)/shard_map/ppermute | solution.py:254
  9.9 10.9 %collective-permute-start.5 = (bf16[128,384]{1,0:T(8,128)(2,1)S(1)}, bf16[128,384]{1,0:T(8,128)(2,1)S(1)}, u32[]{:S(2)}, u32[]{:S(2)}) collective-permute-start(bf16[128,384]{1,0:T(8,128)(2,1)S(1)} %collective-permute-done.1.refs_1_), channel_id=1, source_target_pairs={{0,4},{2,6},{4,0},{6,2},{8,12},{10,14},{12,8},{14,10},{16,20},{18,... | collective-permute-start | bytes 294920 | tf_op jit(solution)/shard_map/ppermute | solution.py:254
  13.1 7.8 %collective-permute-start.8 = (bf16[128,384]{1,0:T(8,128)(2,1)S(1)}, bf16[128,384]{1,0:T(8,128)(2,1)S(1)}, u32[]{:S(2)}, u32[]{:S(2)}) collective-permute-start(bf16[128,384]{1,0:T(8,128)(2,1)S(1)} %collective-permute-done.6.refs_5_), channel_id=1, source_target_pairs={{0,4},{2,6},{4,0},{6,2},{8,12},{10,14},{12,8},{14,10},{16,20},{18,... | collective-permute-start | bytes 294920 | tf_op jit(solution)/shard_map/ppermute | solution.py:254
  14.6 2.3 %copy-start.7 = (f32[384]{0:T(512)S(1)}, f32[384]{0:T(512)}, u32[]{:S(2)}) copy-start(f32[384]{0:T(512)} %param.12) | copy-start | bytes 4612
  14.6 6.3 %copy-start.1 = (bf16[128,384]{1,0:T(8,128)(2,1)S(1)}, bf16[128,384]{1,0:T(8,128)(2,1)}, u32[]{:S(2)}) copy-start(bf16[128,384]{1,0:T(8,128)(2,1)} %get-tuple-element.19.refs_0_) | copy-start | bytes 294916
  14.6 6.3 %copy-start.2 = (bf16[128,384]{1,0:T(8,128)(2,1)S(1)}, bf16[128,384]{1,0:T(8,128)(2,1)}, u32[]{:S(2)}) copy-start(bf16[128,384]{1,0:T(8,128)(2,1)} %get-tuple-element.20.refs_4_) | copy-start | bytes 294916
  14.8 3.7 %collective-permute-start.3 = (f32[8,128]{1,0:T(8,128)S(1)}, f32[8,128]{1,0:T(8,128)S(1)}, u32[]{:S(2)}, u32[]{:S(2)}) collective-permute-start(f32[8,128]{1,0:T(8,128)S(1)} %shard_map.83.own_ref), channel_id=1, source_target_pairs={{0,1},{1,0},{2,3},{3,2},{4,5},{5,4},{6,7},{7,6},{8,9},{9,8},{10,11... | collective-permute-start | bytes 12296 | tf_op jit(solution)/shard_map/ppermute | solution.py:316
  16.4 4.5 %collective-permute-start.4 = (f32[8,128]{1,0:T(8,128)S(1)}, f32[8,128]{1,0:T(8,128)S(1)}, u32[]{:S(2)}, u32[]{:S(2)}) collective-permute-start(f32[8,128]{1,0:T(8,128)S(1)} %shard_map.83.own_ref), channel_id=1, source_target_pairs={{0,5},{1,4},{2,7},{3,6},{4,1},{5,0},{6,3},{7,2},{8,13},{9,12},{10,... | collective-permute-start | bytes 12296 | tf_op jit(solution)/shard_map/ppermute | solution.py:320
  20.9 0.7 %copy-start.8 = (f32[384]{0:T(512)S(1)}, f32[384]{0:T(512)}, u32[]{:S(2)}) copy-start(f32[384]{0:T(512)} %param.11) | copy-start | bytes 4612
  20.9 0.9 %copy-start = (bf16[144,384]{1,0:T(8,128)(2,1)S(1)}, bf16[144,384]{1,0:T(8,128)(2,1)}, u32[]{:S(2)}) copy-start(bf16[144,384]{1,0:T(8,128)(2,1)} %get-tuple-element.16.refs_0_) | copy-start | bytes 331780
  21.1 2.4 %collective-permute-start.9 = (bf16[1024,384]{1,0:T(8,128)(2,1)S(1)}, bf16[1024,384]{1,0:T(8,128)(2,1)S(1)}, u32[]{:S(2)}, u32[]{:S(2)}) collective-permute-start(bf16[1024,384]{1,0:T(8,128)(2,1)S(1)} %shard_map.85.pack_ref), channel_id=1, source_target_pairs={{0,2},{2,0},{4,6},{6,4},{8,10},{10,8},{12,14},{14,12},{16,18},{18,... | collective-permute-start | bytes 2359304 | tf_op jit(solution)/shard_map/ppermute | solution.py:254
  23.5 2.2 %copy-start.3 = (f32[50,384]{1,0:T(8,128)S(1)}, f32[50,384]{1,0:T(8,128)}, u32[]{:S(2)}) copy-start(f32[50,384]{1,0:T(8,128)} %table_ref.1) | copy-start | bytes 230404
  23.5 2.2 %copy-start.5 = (s32[2]{0:T(128)S(1)}, s32[2]{0:T(128)}, u32[]{:S(2)}) copy-start(s32[2]{0:T(128)} %step_ref.1) | copy-start | bytes 28
  24.5 5.2 %collective-permute-start.10 = (bf16[144,384]{1,0:T(8,128)(2,1)S(1)}, bf16[144,384]{1,0:T(8,128)(2,1)S(1)}, u32[]{:S(2)}, u32[]{:S(2)}) collective-permute-start(bf16[144,384]{1,0:T(8,128)(2,1)S(1)} %shard_map.88), channel_id=1, source_target_pairs={{0,8},{2,10},{4,12},{6,14},{8,0},{10,2},{12,4},{14,6},{16,24},{18,... | collective-permute-start | bytes 331784 | tf_op jit(solution)/shard_map/ppermute | solution.py:254

commit v11 on v10

--- a/solution.py
+++ b/solution.py
@@ -91,7 +91,8 @@
 def query_kernel(full_width, key_masks, gain_ref, own_ref, other_ref, *refs):
     queries, (query_out, bias_out) = refs[:2], refs[2:]
     me = lax.axis_index("tm")
-    query_mask = lax.axis_size("tm") // 4
+    count = lax.axis_size("tm")
+    query_mask = count // 2 + count // 4
     lane = lax.broadcasted_iota(jnp.int32, (1, HD), 1)
     half = (lane >= BLK).astype(jnp.float32)
     for place, query_ref in enumerate(queries):
@@ -270,9 +271,8 @@
     splits = lax.axis_size("head")
     full_width = width * splits
     params = pltpu.CompilerParams(vmem_limit_bytes=(8 + count // 2) * 2**20)
-    query_mask = count // 4
-    bits = [1 << place for place in range(1, count.bit_length() - 1)]
-    bits = [bit for bit in bits[::-1] if bit != query_mask]
+    query_mask = count // 2 + count // 4
+    bits = [1 << place for place in range(1, count.bit_length() - 2)][::-1]
     query_gain = query_gain.reshape(1, width)
     key_gain = key_gain.reshape(1, width)
 
@@ -296,7 +296,7 @@
     )(query_proj, key_proj, value_proj, far_blocks)
     keys = gathered(key_proj, bits)
     keys[0] = own_key
-    values = gathered(own_value, bits)
+    values = gathered(own_value, bits[::-1])
     queries = [query_packet, exchange(query_packet, query_mask)]
     masks = sorted(keys, key=lambda mask: (mask.bit_count(), -mask))
     near = 1 + len(bits)

time: 30.6 us -> 32.4 us (1.059)
  starting transfers between devices: 14.4 us -> 15.6 us
  waiting for transfers between devices: 8.54 us -> 9.15 us
    ppermute x9, starting transfers between devices: 12.3 us -> 13.7 us  [exchange(): return lax.ppermute(array, 'tm', [(i, i ^ mask) for i in range(count)])]
    ppermute x9, waiting for transfers between devices: 4.56 us -> 4.93 us  [exchange(): return lax.ppermute(array, 'tm', [(i, i ^ mask) for i in range(count)])]
  transfers between devices with their start and end apart: 11 -> 11, of which waited for: 5 -> 6; matrix products, arithmetic and copies ran while one was open for 0% -> 0% of each run, Pallas kernels for 16% -> 15%
where the time goes in v11:
time: 32.4 us; the launch traced here: 32.3 us
  starting transfers between devices  15.6 us (48%)
  waiting for transfers between devices  9.15 us (28%)
  Pallas kernels  6.79 us (21%)
  local copies, waits for them, and re-layouts  0.61 us (2%)
    ppermute x9, starting transfers between devices, exchange(): return lax.ppermute(array, 'tm', [(i, i ^ mask) for i in range(count)])  13.7 us
    ppermute x9, waiting for transfers between devices, exchange(): return lax.ppermute(array, 'tm', [(i, i ^ mask) for i in range(count)])  4.93 us
    ppermute x1, waiting for transfers between devices, local(): crossed = lax.ppermute(sums, ('tm', 'head'), pairs)  2.42 us
    pallas_call x2, Pallas kernels, last(): pl.pallas_call(functools.partial(last_attention, place), out_shape=out_sh...  1.91 us
    pallas_call x1, Pallas kernels, local(): pl.pallas_call(own_kernel, out_shape=[jax.ShapeDtypeStruct((rows + EXTRA,...  1.88 us
    ppermute x1, waiting for transfers between devices, local(): others = lax.ppermute(sums, 'head', [(0, 1), (1, 0)])  1.8 us
    ppermute x1, starting transfers between devices, local(): others = lax.ppermute(sums, 'head', [(0, 1), (1, 0)])  1.58 us
    pallas_call x1, Pallas kernels, local(): pl.pallas_call(own_attention, out_shape=[jax.ShapeDtypeStruct((2 * rows,...  1.06 us
  transfers between devices with their start and end apart: 11, of which 6 were waited for; matrix products, arithmetic and copies ran while one was open for 0% of the time, Pallas kernels for 15%

profile of v11, /device:TPU:0, one launch (start us, length us, event | category | flops | bytes accessed | tf_op | source)
XLA Modules:
  0.0 32.3 jit_solution(10289810164531075214)
XLA Ops:
  0.0 0.0 copy-start.6
  0.0 3.0 %collective-permute-start.1 = (bf16[128,384]{1,0:T(8,128)(2,1)}, bf16[128,384]{1,0:T(8,128)(2,1)S(1)}, u32[]{:S(2)}, u32[]{:S(2)}) collective-permute-start(bf16[128,384]{1,0:T(8,128)(2,1)} %key_hbm.1), channel_id=1, source_target_pairs={{0,8},{2,10},{4,12},{6,14},{8,0},{10,2},{12,4},{14,6},{16,24},{18,... | collective-permute-start | bytes 294920 | tf_op jit(solution)/shard_map/ppermute | solution.py:255
  3.0 1.9 %shard_map.82 = (bf16[144,384]{1,0:T(8,128)(2,1)}, bf16[128,384]{1,0:T(8,128)(2,1)}, bf16[128,384]{1,0:T(8,128)(2,1)}, f32[8,128]{1,0:T(8,128)}) custom-call(bf16[128,384]{1,0:T(8,128)(2,1)} %query_hbm.1, bf16[128,384]{1,0:T(8,128)(2,1)} %key_hbm.1, bf16[128,384]{1,0:T(8,128)(2,1)} %value_hbm.1, s32[1,16]{1,0:T(1,128)} %far_hbm.1), custom_call_target="tpu_custom_call" | custom-call | tf_op jit(solution)/shard_map/pallas_call | solution.py:281
  4.9 0.0 copy-start.4
  4.9 1.6 %collective-permute-start.7 = (bf16[128,384]{1,0:T(8,128)(2,1)}, bf16[128,384]{1,0:T(8,128)(2,1)S(1)}, u32[]{:S(2)}, u32[]{:S(2)}) collective-permute-start(bf16[128,384]{1,0:T(8,128)(2,1)} %get-tuple-element.20.refs_4_), channel_id=1, source_target_pairs={{0,4},{2,6},{4,0},{6,2},{8,12},{10,14},{12,8},{14,10},{16,20},{18,... | collective-permute-start | bytes 294920 | tf_op jit(solution)/shard_map/ppermute | solution.py:255
  6.5 2.5 %collective-permute-start = (bf16[144,384]{1,0:T(8,128)(2,1)}, bf16[144,384]{1,0:T(8,128)(2,1)S(1)}, u32[]{:S(2)}, u32[]{:S(2)}) collective-permute-start(bf16[144,384]{1,0:T(8,128)(2,1)} %get-tuple-element.16.refs_0_), channel_id=1, source_target_pairs={{0,24},{2,26},{4,28},{6,30},{8,16},{10,18},{12,20},{14,22},{16,8},... | collective-permute-start | bytes 331784 | tf_op jit(solution)/shard_map/ppermute | solution.py:255
  9.0 0.0 copy-done.6
  9.0 0.5 %collective-permute-start.2 = (bf16[128,384]{1,0:T(8,128)(2,1)S(1)}, bf16[128,384]{1,0:T(8,128)(2,1)S(1)}, u32[]{:S(2)}, u32[]{:S(2)}) collective-permute-start(bf16[128,384]{1,0:T(8,128)(2,1)S(1)} %copy-done.6), channel_id=1, source_target_pairs={{0,4},{2,6},{4,0},{6,2},{8,12},{10,14},{12,8},{14,10},{16,20},{18,... | collective-permute-start | bytes 294920 | tf_op jit(solution)/shard_map/ppermute | solution.py:255
  9.5 0.7 %collective-permute-start.6 = (bf16[128,384]{1,0:T(8,128)(2,1)}, bf16[128,384]{1,0:T(8,128)(2,1)S(1)}, u32[]{:S(2)}, u32[]{:S(2)}) collective-permute-start(bf16[128,384]{1,0:T(8,128)(2,1)} %get-tuple-element.20.refs_4_), channel_id=1, source_target_pairs={{0,8},{2,10},{4,12},{6,14},{8,0},{10,2},{12,4},{14,6},{16,24},{18,... | collective-permute-start | bytes 294920 | tf_op jit(solution)/shard_map/ppermute | solution.py:255
  10.2 0.0 collective-permute-done.1.refs_1_
  10.2 1.5 %collective-permute-start.5 = (bf16[128,384]{1,0:T(8,128)(2,1)S(1)}, bf16[128,384]{1,0:T(8,128)(2,1)S(1)}, u32[]{:S(2)}, u32[]{:S(2)}) collective-permute-start(bf16[128,384]{1,0:T(8,128)(2,1)S(1)} %collective-permute-done.1.refs_1_), channel_id=1, source_target_pairs={{0,4},{2,6},{4,0},{6,2},{8,12},{10,14},{12,8},{14,10},{16,20},{18,... | collective-permute-start | bytes 294920 | tf_op jit(solution)/shard_map/ppermute | solution.py:255
  11.7 0.0 collective-permute-done.7.refs_6_
  11.7 1.3 %collective-permute-start.8 = (bf16[128,384]{1,0:T(8,128)(2,1)S(1)}, bf16[128,384]{1,0:T(8,128)(2,1)S(1)}, u32[]{:S(2)}, u32[]{:S(2)}) collective-permute-start(bf16[128,384]{1,0:T(8,128)(2,1)S(1)} %collective-permute-done.7.refs_6_), channel_id=1, source_target_pairs={{0,8},{2,10},{4,12},{6,14},{8,0},{10,2},{12,4},{14,6},{16,24},{18,... | collective-permute-start | bytes 294920 | tf_op jit(solution)/shard_map/ppermute | solution.py:255
  13.0 0.7 %collective-permute-done.2.refs_2_ = bf16[128,384]{1,0:T(8,128)(2,1)S(1)} collective-permute-done((bf16[128,384]{1,0:T(8,128)(2,1)S(1)}, bf16[128,384]{1,0:T(8,128)(2,1)S(1)}, u32[]{:S(2)}, u32[]{:S(2)}) %collective-permute-start.2) | collective-permute-done | bytes 98336 | tf_op jit(solution)/shard_map/ppermute | solution.py:255
  13.7 0.8 %collective-permute-done.refs_0_.refs_1_ = bf16[144,384]{1,0:T(8,128)(2,1)S(1)} collective-permute-done((bf16[144,384]{1,0:T(8,128)(2,1)}, bf16[144,384]{1,0:T(8,128)(2,1)S(1)}, u32[]{:S(2)}, u32[]{:S(2)}) %collective-permute-start) | collective-permute-done | bytes 110624 | tf_op jit(solution)/shard_map/ppermute | solution.py:255
  14.5 0.0 copy-done.4
  14.5 0.0 copy-start.7
  14.5 0.0 copy-start.1
  14.5 0.0 copy-start.2
  14.5 0.1 shard_map.83.own_ref
  14.6 1.6 %collective-permute-start.3 = (f32[8,128]{1,0:T(8,128)S(1)}, f32[8,128]{1,0:T(8,128)S(1)}, u32[]{:S(2)}, u32[]{:S(2)}) collective-permute-start(f32[8,128]{1,0:T(8,128)S(1)} %shard_map.83.own_ref), channel_id=1, source_target_pairs={{0,1},{1,0},{2,3},{3,2},{4,5},{5,4},{6,7},{7,6},{8,9},{9,8},{10,11... | collective-permute-start | bytes 12296 | tf_op jit(solution)/shard_map/ppermute | solution.py:316
  16.2 0.3 collective-permute-start.4
  16.5 0.0 copy-done.7
  16.5 0.0 collective-permute-done.6.refs_5_
  16.5 1.8 %collective-permute-done.3.other_ref = f32[8,128]{1,0:T(8,128)S(1)} collective-permute-done((f32[8,128]{1,0:T(8,128)S(1)}, f32[8,128]{1,0:T(8,128)S(1)}, u32[]{:S(2)}, u32[]{:S(2)}) %collective-permute-start.3) | collective-permute-done | bytes 4128 | tf_op jit(solution)/shard_map/ppermute | solution.py:316
  18.3 2.4 %collective-permute-done.4.cross_ref = f32[8,128]{1,0:T(8,128)S(1)} collective-permute-done((f32[8,128]{1,0:T(8,128)S(1)}, f32[8,128]{1,0:T(8,128)S(1)}, u32[]{:S(2)}, u32[]{:S(2)}) %collective-permute-start.4) | collective-permute-done | bytes 4128 | tf_op jit(solution)/shard_map/ppermute | solution.py:320
  20.7 0.0 collective-permute-done.5.refs_3_
  20.7 0.0 collective-permute-done.8.refs_7_
  20.7 0.0 copy-done.1
  20.7 0.0 copy-done.2
  20.8 0.0 copy-start.8
  20.8 0.0 copy-start
  20.8 0.2 shard_map.85.pack_ref
  21.0 0.1 collective-permute-start.9
  21.1 0.3 %copy-done.8 = f32[384]{0:T(512)S(1)} copy-done((f32[384]{0:T(512)S(1)}, f32[384]{0:T(512)}, u32[]{:S(2)}) %copy-start.8) | copy-done | bytes 1560
  21.4 0.2 copy-done
  21.7 0.2 shard_map.84
  21.8 1.1 %shard_map.86 = (f32[256,384]{1,0:T(8,128)S(1)}, f32[256,768]{1,0:T(8,128)S(1)}) custom-call(bf16[256,384]{1,0:T(8,128)(2,1)S(1)} %get-tuple-element.17.query_ref, f32[16,1024]{1,0:T(8,128)S(1)} %get-tuple-element.18.bias_ref, bf16[1024,384]{1,0:T(8,128)(2,1)S(1)} %shard_map.85.pack_ref), custom_call_target="tpu_custom_call" | custom-call | tf_op jit(solution)/shard_map/pallas_call | solution.py:357
  22.9 0.5 %collective-permute-done.9.pack_ref = bf16[1024,384]{1,0:T(8,128)(2,1)S(1)} collective-permute-done((bf16[1024,384]{1,0:T(8,128)(2,1)S(1)}, bf16[1024,384]{1,0:T(8,128)(2,1)S(1)}, u32[]{:S(2)}, u32[]{:S(2)}) %collective-permute-start.9) | collective-permute-done | bytes 786464 | tf_op jit(solution)/shard_map/ppermute | solution.py:255
  23.4 0.0 copy-start.3
  23.4 1.0 %shard_map.88 = bf16[144,384]{1,0:T(8,128)(2,1)S(1)} custom-call(bf16[256,384]{1,0:T(8,128)(2,1)S(1)} %get-tuple-element.17.query_ref, f32[16,1024]{1,0:T(8,128)S(1)} %get-tuple-element.18.bias_ref, bf16[1024,384]{1,0:T(8,128)(2,1)S(1)} %collective-permute-done.9.pack_ref, f32[256,384]{1,0:T(8,128)S(1)} %get-tuple-element.21.context_ref, ...), custom_call_target="tpu_custom_call" | custom-call | tf_op jit(solution)/shard_map/pallas_call | solution.py:369
  24.3 2.5 %collective-permute-start.10 = (bf16[144,384]{1,0:T(8,128)(2,1)S(1)}, bf16[144,384]{1,0:T(8,128)(2,1)S(1)}, u32[]{:S(2)}, u32[]{:S(2)}) collective-permute-start(bf16[144,384]{1,0:T(8,128)(2,1)S(1)} %shard_map.88), channel_id=1, source_target_pairs={{0,24},{2,26},{4,28},{6,30},{8,16},{10,18},{12,20},{14,22},{16,8},... | collective-permute-start | bytes 331784 | tf_op jit(solution)/shard_map/ppermute | solution.py:255
  26.9 0.0 copy-done.3
  26.9 0.0 copy-done.5
  26.9 0.6 %shard_map.89.gate_ref = f32[16,384]{1,0:T(8,128)S(1)} custom-call(s32[2]{0:T(128)S(1)} %copy-done.5, f32[50,384]{1,0:T(8,128)S(1)} %copy-done.3), custom_call_target="tpu_custom_call" | custom-call | tf_op jit(solution)/shard_map/pallas_call | solution.py:385
  27.5 0.9 %shard_map.87 = (f32[128,384]{1,0:T(8,128)S(1)}, f32[16,384]{1,0:T(8,128)S(1)}) custom-call(bf16[256,384]{1,0:T(8,128)(2,1)S(1)} %get-tuple-element.17.query_ref, f32[16,1024]{1,0:T(8,128)S(1)} %get-tuple-element.18.bias_ref, bf16[1024,384]{1,0:T(8,128)(2,1)S(1)} %collective-permute-done.9.pack_ref, f32[256,384]{1,0:T(8,128)S(1)} %get-tuple-element.21.context_ref, ...), custom_call_target="tpu_custom_call" | custom-call | tf_op jit(solution)/shard_map/pallas_call | solution.py:369
  28.4 3.0 %collective-permute-done.10.packet_ref = bf16[144,384]{1,0:T(8,128)(2,1)S(1)} collective-permute-done((bf16[144,384]{1,0:T(8,128)(2,1)S(1)}, bf16[144,384]{1,0:T(8,128)(2,1)S(1)}, u32[]{:S(2)}, u32[]{:S(2)}) %collective-permute-start.10) | collective-permute-done | bytes 110624 | tf_op jit(solution)/shard_map/ppermute | solution.py:255
  31.4 0.8 %shard_map.90 = bf16[128,384]{1,0:T(8,128)(2,1)} custom-call(f32[128,384]{1,0:T(8,128)S(1)} %get-tuple-element.23.own_ref, f32[16,384]{1,0:T(8,128)S(1)} %get-tuple-element.24.lines_ref, bf16[144,384]{1,0:T(8,128)(2,1)S(1)} %collective-permute-done.10.packet_ref, f32[16,384]{1,0:T(8,128)S(1)} %shard_map.89.gate_ref), custom_call_target="tpu_custom_call" | custom-call | tf_op jit(solution)/shard_map/pallas_call | solution.py:394
  (3 shorter events, 0.0 us)
Async XLA Ops:
  0.0 9.0 %copy-start.6 = (bf16[128,384]{1,0:T(8,128)(2,1)S(1)}, bf16[128,384]{1,0:T(8,128)(2,1)}, u32[]{:S(2)}) copy-start(bf16[128,384]{1,0:T(8,128)(2,1)} %key_hbm.1) | copy-start | bytes 294916
  0.0 10.2 %collective-permute-start.1 = (bf16[128,384]{1,0:T(8,128)(2,1)}, bf16[128,384]{1,0:T(8,128)(2,1)S(1)}, u32[]{:S(2)}, u32[]{:S(2)}) collective-permute-start(bf16[128,384]{1,0:T(8,128)(2,1)} %key_hbm.1), channel_id=1, source_target_pairs={{0,8},{2,10},{4,12},{6,14},{8,0},{10,2},{12,4},{14,6},{16,24},{18,... | collective-permute-start | bytes 294920 | tf_op jit(solution)/shard_map/ppermute | solution.py:255
  4.9 9.6 %copy-start.4 = (f32[8,128]{1,0:T(8,128)S(1)}, f32[8,128]{1,0:T(8,128)}, u32[]{:S(2)}) copy-start(f32[8,128]{1,0:T(8,128)} %get-tuple-element.15.before_ref) | copy-start | bytes 12292
  4.9 6.7 %collective-permute-start.7 = (bf16[128,384]{1,0:T(8,128)(2,1)}, bf16[128,384]{1,0:T(8,128)(2,1)S(1)}, u32[]{:S(2)}, u32[]{:S(2)}) collective-permute-start(bf16[128,384]{1,0:T(8,128)(2,1)} %get-tuple-element.20.refs_4_), channel_id=1, source_target_pairs={{0,4},{2,6},{4,0},{6,2},{8,12},{10,14},{12,8},{14,10},{16,20},{18,... | collective-permute-start | bytes 294920 | tf_op jit(solution)/shard_map/ppermute | solution.py:255
  6.5 8.0 %collective-permute-start = (bf16[144,384]{1,0:T(8,128)(2,1)}, bf16[144,384]{1,0:T(8,128)(2,1)S(1)}, u32[]{:S(2)}, u32[]{:S(2)}) collective-permute-start(bf16[144,384]{1,0:T(8,128)(2,1)} %get-tuple-element.16.refs_0_), channel_id=1, source_target_pairs={{0,24},{2,26},{4,28},{6,30},{8,16},{10,18},{12,20},{14,22},{16,8},... | collective-permute-start | bytes 331784 | tf_op jit(solution)/shard_map/ppermute | solution.py:255
  9.0 4.7 %collective-permute-start.2 = (bf16[128,384]{1,0:T(8,128)(2,1)S(1)}, bf16[128,384]{1,0:T(8,128)(2,1)S(1)}, u32[]{:S(2)}, u32[]{:S(2)}) collective-permute-start(bf16[128,384]{1,0:T(8,128)(2,1)S(1)} %copy-done.6), channel_id=1, source_target_pairs={{0,4},{2,6},{4,0},{6,2},{8,12},{10,14},{12,8},{14,10},{16,20},{18,... | collective-permute-start | bytes 294920 | tf_op jit(solution)/shard_map/ppermute | solution.py:255
  9.5 7.0 %collective-permute-start.6 = (bf16[128,384]{1,0:T(8,128)(2,1)}, bf16[128,384]{1,0:T(8,128)(2,1)S(1)}, u32[]{:S(2)}, u32[]{:S(2)}) collective-permute-start(bf16[128,384]{1,0:T(8,128)(2,1)} %get-tuple-element.20.refs_4_), channel_id=1, source_target_pairs={{0,8},{2,10},{4,12},{6,14},{8,0},{10,2},{12,4},{14,6},{16,24},{18,... | collective-permute-start | bytes 294920 | tf_op jit(solution)/shard_map/ppermute | solution.py:255
  10.2 10.6 %collective-permute-start.5 = (bf16[128,384]{1,0:T(8,128)(2,1)S(1)}, bf16[128,384]{1,0:T(8,128)(2,1)S(1)}, u32[]{:S(2)}, u32[]{:S(2)}) collective-permute-start(bf16[128,384]{1,0:T(8,128)(2,1)S(1)} %collective-permute-done.1.refs_1_), channel_id=1, source_target_pairs={{0,4},{2,6},{4,0},{6,2},{8,12},{10,14},{12,8},{14,10},{16,20},{18,... | collective-permute-start | bytes 294920 | tf_op jit(solution)/shard_map/ppermute | solution.py:255
  11.7 9.1 %collective-permute-start.8 = (bf16[128,384]{1,0:T(8,128)(2,1)S(1)}, bf16[128,384]{1,0:T(8,128)(2,1)S(1)}, u32[]{:S(2)}, u32[]{:S(2)}) collective-permute-start(bf16[128,384]{1,0:T(8,128)(2,1)S(1)} %collective-permute-done.7.refs_6_), channel_id=1, source_target_pairs={{0,8},{2,10},{4,12},{6,14},{8,0},{10,2},{12,4},{14,6},{16,24},{18,... | collective-permute-start | bytes 294920 | tf_op jit(solution)/shard_map/ppermute | solution.py:255
  14.5 2.0 %copy-start.7 = (f32[384]{0:T(512)S(1)}, f32[384]{0:T(512)}, u32[]{:S(2)}) copy-start(f32[384]{0:T(512)} %param.12) | copy-start | bytes 4612
  14.5 6.3 %copy-start.1 = (bf16[128,384]{1,0:T(8,128)(2,1)S(1)}, bf16[128,384]{1,0:T(8,128)(2,1)}, u32[]{:S(2)}) copy-start(bf16[128,384]{1,0:T(8,128)(2,1)} %get-tuple-element.19.refs_0_) | copy-start | bytes 294916
  14.5 6.3 %copy-start.2 = (bf16[128,384]{1,0:T(8,128)(2,1)S(1)}, bf16[128,384]{1,0:T(8,128)(2,1)}, u32[]{:S(2)}) copy-start(bf16[128,384]{1,0:T(8,128)(2,1)} %get-tuple-element.20.refs_4_) | copy-start | bytes 294916
  14.6 3.7 %collective-permute-start.3 = (f32[8,128]{1,0:T(8,128)S(1)}, f32[8,128]{1,0:T(8,128)S(1)}, u32[]{:S(2)}, u32[]{:S(2)}) collective-permute-start(f32[8,128]{1,0:T(8,128)S(1)} %shard_map.83.own_ref), channel_id=1, source_target_pairs={{0,1},{1,0},{2,3},{3,2},{4,5},{5,4},{6,7},{7,6},{8,9},{9,8},{10,11... | collective-permute-start | bytes 12296 | tf_op jit(solution)/shard_map/ppermute | solution.py:316
  16.2 4.5 %collective-permute-start.4 = (f32[8,128]{1,0:T(8,128)S(1)}, f32[8,128]{1,0:T(8,128)S(1)}, u32[]{:S(2)}, u32[]{:S(2)}) collective-permute-start(f32[8,128]{1,0:T(8,128)S(1)} %shard_map.83.own_ref), channel_id=1, source_target_pairs={{0,5},{1,4},{2,7},{3,6},{4,1},{5,0},{6,3},{7,2},{8,13},{9,12},{10,... | collective-permute-start | bytes 12296 | tf_op jit(solution)/shard_map/ppermute | solution.py:320
  20.8 0.7 %copy-start.8 = (f32[384]{0:T(512)S(1)}, f32[384]{0:T(512)}, u32[]{:S(2)}) copy-start(f32[384]{0:T(512)} %param.11) | copy-start | bytes 4612
  20.8 0.9 %copy-start = (bf16[144,384]{1,0:T(8,128)(2,1)S(1)}, bf16[144,384]{1,0:T(8,128)(2,1)}, u32[]{:S(2)}) copy-start(bf16[144,384]{1,0:T(8,128)(2,1)} %get-tuple-element.16.refs_0_) | copy-start | bytes 331780
  21.0 2.4 %collective-permute-start.9 = (bf16[1024,384]{1,0:T(8,128)(2,1)S(1)}, bf16[1024,384]{1,0:T(8,128)(2,1)S(1)}, u32[]{:S(2)}, u32[]{:S(2)}) collective-permute-start(bf16[1024,384]{1,0:T(8,128)(2,1)S(1)} %shard_map.85.pack_ref), channel_id=1, source_target_pairs={{0,2},{2,0},{4,6},{6,4},{8,10},{10,8},{12,14},{14,12},{16,18},{18,... | collective-permute-start | bytes 2359304 | tf_op jit(solution)/shard_map/ppermute | solution.py:255
  23.4 3.5 %copy-start.3 = (f32[50,384]{1,0:T(8,128)S(1)}, f32[50,384]{1,0:T(8,128)}, u32[]{:S(2)}) copy-start(f32[50,384]{1,0:T(8,128)} %table_ref.1) | copy-start | bytes 230404
  23.4 3.5 %copy-start.5 = (s32[2]{0:T(128)S(1)}, s32[2]{0:T(128)}, u32[]{:S(2)}) copy-start(s32[2]{0:T(128)} %step_ref.1) | copy-start | bytes 28
  24.3 7.1 %collective-permute-start.10 = (bf16[144,384]{1,0:T(8,128)(2,1)S(1)}, bf16[144,384]{1,0:T(8,128)(2,1)S(1)}, u32[]{:S(2)}, u32[]{:S(2)}) collective-permute-start(bf16[144,384]{1,0:T(8,128)(2,1)S(1)} %shard_map.88), channel_id=1, source_target_pairs={{0,24},{2,26},{4,28},{6,30},{8,16},{10,18},{12,20},{14,22},{16,8},... | collective-permute-start | bytes 331784 | tf_op jit(solution)/shard_map/ppermute | solution.py:255

commit v12 on v11

--- a/solution.py
+++ b/solution.py
@@ -34,39 +34,29 @@
 
 
 def own_kernel(
-    query_hbm,
-    key_hbm,
-    value_hbm,
-    far_hbm,
-    query_out,
-    key_out,
-    value_out,
-    sums_out,
-    query_ref,
-    far_ref,
-    sems,
+    query_hbm, key_hbm, value_hbm, far_hbm, query_out, pair_out, sums_out, query_ref, far_ref, sems
 ):
     rows, width = query_ref.shape
     copies = [
-        pltpu.make_async_copy(query_hbm, query_ref, sems.at[0]),
-        pltpu.make_async_copy(key_hbm, key_out, sems.at[1]),
-        pltpu.make_async_copy(far_hbm, far_ref, sems.at[2]),
-        pltpu.make_async_copy(value_hbm, value_out, sems.at[3]),
+        pltpu.make_async_copy(key_hbm, pair_out.at[:rows, :], sems.at[0]),
+        pltpu.make_async_copy(value_hbm, pair_out.at[rows:, :], sems.at[1]),
+        pltpu.make_async_copy(query_hbm, query_ref, sems.at[2]),
+        pltpu.make_async_copy(far_hbm, far_ref, sems.at[3]),
     ]
     for copy in copies:
         copy.start()
     query_out[rows:, HD:] = jnp.zeros((EXTRA, width - HD), jnp.bfloat16)
     sums_out[...] = jnp.zeros_like(sums_out)
     copies[0].wait()
+    sums_out[1:2, :] = squares(pair_out)
+    copies[2].wait()
     query_out[:rows, :] = query_ref[...]
     sums_out[0:1, :] = squares(query_ref)
-    copies[1].wait()
-    sums_out[1:2, :] = squares(key_out)
-    copies[2].wait()
+    copies[3].wait()
     far = far_ref[...].astype(jnp.float32)
     far = jnp.concatenate([far, jnp.full((1, HD - far.shape[1]), -1.0)], axis=1)
     query_out[rows:, :HD] = jnp.broadcast_to(far, (EXTRA, HD)).astype(jnp.bfloat16)
-    copies[3].wait()
+    copies[1].wait()
 
 
 def sums_kernel(lines, before_ref, *refs):
@@ -112,19 +102,19 @@
             )
 
 
-def pack_kernel(full_width, near, held, gain_ref, own_ref, other_ref, cross_ref, *refs):
-    keys, values, pack_out = refs[:held], refs[held : 2 * held], refs[2 * held]
-    for place, key_ref in enumerate(keys):
+def pack_kernel(full_width, near, gain_ref, own_ref, other_ref, cross_ref, *refs):
+    *pairs, pack_out = refs
+    held = len(pairs)
+    for place, pair_ref in enumerate(pairs):
         line = 1 + place + (place > 0)
         if place < near:
             total = own_ref[line : line + 1, :] + other_ref[line : line + 1, :]
         else:
-            total = squares(key_ref) + cross_ref[3:4, :]
+            total = squares(pair_ref) + cross_ref[3:4, :]
         pack_out[place * HD : (place + 1) * HD, :] = normed(
-            key_ref, factor_of(total, full_width), gain_ref
-        )
-    for place, value_ref in enumerate(values, start=held):
-        pack_out[place * HD : (place + 1) * HD, :] = value_ref[...]
+            pair_ref, factor_of(total, full_width), gain_ref
+        )
+        pack_out[(held + place) * HD : (held + place + 1) * HD, :] = pair_ref[HD:, :]
 
 
 def absorb(query, pack_ref, biases, olds, low):
@@ -263,6 +253,10 @@
     return held
 
 
+def cost(flops):
+    return pl.CostEstimate(flops=flops, bytes_accessed=0, transcendentals=0)
+
+
 def local(
     query_proj, key_proj, value_proj, query_gain, key_gain, gate_table, frame_step, far_blocks
 ):
@@ -278,27 +272,24 @@
 
     lines = 2 + 2 ** len(bits)
     lines += -lines % 8
-    query_packet, own_key, own_value, own_sums = pl.pallas_call(
+    query_packet, own_pair, own_sums = pl.pallas_call(
         own_kernel,
         out_shape=[
             jax.ShapeDtypeStruct((rows + EXTRA, width), jnp.bfloat16),
-            jax.ShapeDtypeStruct((rows, width), jnp.bfloat16),
-            jax.ShapeDtypeStruct((rows, width), jnp.bfloat16),
+            jax.ShapeDtypeStruct((2 * rows, width), jnp.bfloat16),
             jax.ShapeDtypeStruct((lines, rows), jnp.float32),
         ],
         in_specs=[ANY] * 4,
-        out_specs=[VMEM] * 4,
+        out_specs=[VMEM] * 3,
         scratch_shapes=[
             pltpu.VMEM((rows, width), jnp.bfloat16),
             pltpu.VMEM(far_blocks.shape, jnp.int32),
             pltpu.SemaphoreType.DMA((4,)),
         ],
     )(query_proj, key_proj, value_proj, far_blocks)
-    keys = gathered(key_proj, bits)
-    keys[0] = own_key
-    values = gathered(own_value, bits[::-1])
+    blocks = gathered(own_pair, bits)
     queries = [query_packet, exchange(query_packet, query_mask)]
-    masks = sorted(keys, key=lambda mask: (mask.bit_count(), -mask))
+    masks = sorted(blocks, key=lambda mask: (mask.bit_count(), -mask))
     near = 1 + len(bits)
 
     def summed(sums, sources, held):
@@ -308,9 +299,10 @@
             in_specs=[VMEM] * (1 + len(sources)),
             out_specs=VMEM,
             compiler_params=params,
+            cost_estimate=cost(4 * 10**9),
         )(sums, *sources)
 
-    sources = [queries[1]] + [keys[mask] for mask in masks[1:near]]
+    sources = [queries[1]] + [blocks[mask] for mask in masks[1:near]]
     sums = summed(own_sums, sources, range(2, near + 2))
     if splits == 2:
         others = lax.ppermute(sums, "head", [(0, 1), (1, 0)])
@@ -319,7 +311,7 @@
             pairs.append((i, ((i // 2) ^ bits[1]) * 2 + (i % 2 ^ 1)))
         crossed = lax.ppermute(sums, ("tm", "head"), pairs)
     else:
-        sources = [keys[mask] for mask in masks[near:]]
+        sources = [blocks[mask] for mask in masks[near:]]
         sums = summed(sums, sources, range(near + 2, len(masks) + 2))
         sums = lax.psum(sums, "head")
         others = crossed = jnp.zeros_like(sums)
@@ -337,11 +329,9 @@
     )(query_gain, sums, others, *queries)
 
     pack = pl.pallas_call(
-        functools.partial(
-            pack_kernel, width * splits, near if splits == 2 else len(masks), len(masks)
-        ),
+        functools.partial(pack_kernel, width * splits, near if splits == 2 else len(masks)),
         out_shape=jax.ShapeDtypeStruct((2 * len(masks) * rows, width), jnp.bfloat16),
-        in_specs=[VMEM] * (4 + 2 * len(masks)),
+        in_specs=[VMEM] * (4 + len(masks)),
         out_specs=VMEM,
         compiler_params=params,
     )(
@@ -349,8 +339,7 @@
         sums,
         others,
         crossed,
-        *[keys[mask] for mask in masks],
-        *[values[mask] for mask in masks],
+        *[blocks[mask] for mask in masks],
     )
     other_pack = exchange(pack, 1)
 

time: 32.4 us -> 32.5 us (level)
  waiting for transfers between devices: 9.15 us -> 10.3 us
  local copies, waits for them, and re-layouts: 0.61 us -> 0.03 us
  starting transfers between devices: 15.6 us -> 15.2 us
    ppermute x9 -> x6, waiting for transfers between devices: 4.93 us -> 7.2 us  [exchange(): return lax.ppermute(array, 'tm', [(i, i ^ mask) for i in range(count)])]
    ppermute x9 -> x6, starting transfers between devices: 13.7 us -> 12.2 us  [exchange(): return lax.ppermute(array, 'tm', [(i, i ^ mask) for i in range(count)])]
    ppermute x1, waiting for transfers between devices: 1.8 us -> 0.64 us  [local(): others = lax.ppermute(sums, 'head', [(0, 1), (1, 0)])]
    ppermute x1, starting transfers between devices: 0.28 us -> 1.43 us  [local(): crossed = lax.ppermute(sums, ('tm', 'head'), pairs)]
    unnamed x18 -> x14, local copies, waits for them, and re-layouts: 0.6 us -> 0.03 us
  transfers between devices with their start and end apart: 11 -> 8, of which waited for: 6 -> 6; matrix products, arithmetic and copies ran while one was open for 0% -> 0% of each run, Pallas kernels for 15% -> 9%
where the time goes in v12:
time: 32.5 us; the launch traced here: 32.4 us
  starting transfers between devices  15.2 us (47%)
  waiting for transfers between devices  10.3 us (32%)
  Pallas kernels  6.79 us (21%)
    ppermute x6, starting transfers between devices, exchange(): return lax.ppermute(array, 'tm', [(i, i ^ mask) for i in range(count)])  12.2 us
    ppermute x6, waiting for transfers between devices, exchange(): return lax.ppermute(array, 'tm', [(i, i ^ mask) for i in range(count)])  7.2 us
    ppermute x1, waiting for transfers between devices, local(): crossed = lax.ppermute(sums, ('tm', 'head'), pairs)  2.42 us
    pallas_call x2, Pallas kernels, last(): pl.pallas_call(functools.partial(last_attention, place), out_shape=out_sh...  1.91 us
    pallas_call x1, Pallas kernels, local(): pl.pallas_call(own_kernel, out_shape=[jax.ShapeDtypeStruct((rows + EXTRA,...  1.88 us
    ppermute x1, starting transfers between devices, local(): others = lax.ppermute(sums, 'head', [(0, 1), (1, 0)])  1.58 us
    ppermute x1, starting transfers between devices, local(): crossed = lax.ppermute(sums, ('tm', 'head'), pairs)  1.43 us
    pallas_call x1, Pallas kernels, local(): pl.pallas_call(own_attention, out_shape=[jax.ShapeDtypeStruct((2 * rows,...  1.06 us
  transfers between devices with their start and end apart: 8, of which 6 were waited for; matrix products, arithmetic and copies ran while one was open for 0% of the time, Pallas kernels for 9%

profile of v12, /device:TPU:0, one launch (start us, length us, event | category | flops | bytes accessed | tf_op | source)
XLA Modules:
  0.0 32.4 jit_solution(4619206737544892207)
XLA Ops:
  0.0 1.9 %shard_map.82 = (bf16[144,384]{1,0:T(8,128)(2,1)}, bf16[256,384]{1,0:T(8,128)(2,1)}, f32[8,128]{1,0:T(8,128)}) custom-call(bf16[128,384]{1,0:T(8,128)(2,1)} %query_hbm.1, bf16[128,384]{1,0:T(8,128)(2,1)} %key_hbm.1, bf16[128,384]{1,0:T(8,128)(2,1)} %value_hbm.1, s32[1,16]{1,0:T(1,128)} %far_hbm.1), custom_call_target="tpu_custom_call" | custom-call | tf_op jit(solution)/shard_map/pallas_call | solution.py:275
  1.9 0.0 copy-start.4
  1.9 3.1 %collective-permute-start.1 = (bf16[256,384]{1,0:T(8,128)(2,1)}, bf16[256,384]{1,0:T(8,128)(2,1)S(1)}, u32[]{:S(2)}, u32[]{:S(2)}) collective-permute-start(bf16[256,384]{1,0:T(8,128)(2,1)} %get-tuple-element.16.refs_0_), channel_id=1, source_target_pairs={{0,8},{2,10},{4,12},{6,14},{8,0},{10,2},{12,4},{14,6},{16,24},{18,... | collective-permute-start | bytes 589832 | tf_op jit(solution)/shard_map/ppermute | solution.py:245
  5.0 1.5 %collective-permute-start.2 = (bf16[256,384]{1,0:T(8,128)(2,1)}, bf16[256,384]{1,0:T(8,128)(2,1)S(1)}, u32[]{:S(2)}, u32[]{:S(2)}) collective-permute-start(bf16[256,384]{1,0:T(8,128)(2,1)} %get-tuple-element.16.refs_0_), channel_id=1, source_target_pairs={{0,4},{2,6},{4,0},{6,2},{8,12},{10,14},{12,8},{14,10},{16,20},{18,... | collective-permute-start | bytes 589832 | tf_op jit(solution)/shard_map/ppermute | solution.py:245
  6.5 2.5 %collective-permute-start = (bf16[144,384]{1,0:T(8,128)(2,1)}, bf16[144,384]{1,0:T(8,128)(2,1)S(1)}, u32[]{:S(2)}, u32[]{:S(2)}) collective-permute-start(bf16[144,384]{1,0:T(8,128)(2,1)} %get-tuple-element.15.refs_0_), channel_id=1, source_target_pairs={{0,24},{2,26},{4,28},{6,30},{8,16},{10,18},{12,20},{14,22},{16,8},... | collective-permute-start | bytes 331784 | tf_op jit(solution)/shard_map/ppermute | solution.py:245
  9.0 1.2 %collective-permute-done.1.refs_1_ = bf16[256,384]{1,0:T(8,128)(2,1)S(1)} collective-permute-done((bf16[256,384]{1,0:T(8,128)(2,1)}, bf16[256,384]{1,0:T(8,128)(2,1)S(1)}, u32[]{:S(2)}, u32[]{:S(2)}) %collective-permute-start.1) | collective-permute-done | bytes 196640 | tf_op jit(solution)/shard_map/ppermute | solution.py:245
  10.2 1.9 %collective-permute-start.5 = (bf16[256,384]{1,0:T(8,128)(2,1)S(1)}, bf16[256,384]{1,0:T(8,128)(2,1)S(1)}, u32[]{:S(2)}, u32[]{:S(2)}) collective-permute-start(bf16[256,384]{1,0:T(8,128)(2,1)S(1)} %collective-permute-done.1.refs_1_), channel_id=1, source_target_pairs={{0,4},{2,6},{4,0},{6,2},{8,12},{10,14},{12,8},{14,10},{16,20},{18,... | collective-permute-start | bytes 589832 | tf_op jit(solution)/shard_map/ppermute | solution.py:245
  12.1 2.6 %collective-permute-done.refs_0_.refs_1_ = bf16[144,384]{1,0:T(8,128)(2,1)S(1)} collective-permute-done((bf16[144,384]{1,0:T(8,128)(2,1)}, bf16[144,384]{1,0:T(8,128)(2,1)S(1)}, u32[]{:S(2)}, u32[]{:S(2)}) %collective-permute-start) | collective-permute-done | bytes 110624 | tf_op jit(solution)/shard_map/ppermute | solution.py:245
  14.7 0.0 collective-permute-done.2.refs_2_
  14.7 0.0 copy-done.4
  14.7 0.0 copy-start.5
  14.7 0.0 copy-start
  14.7 0.1 shard_map.83.own_ref
  14.8 1.6 %collective-permute-start.3 = (f32[8,128]{1,0:T(8,128)S(1)}, f32[8,128]{1,0:T(8,128)S(1)}, u32[]{:S(2)}, u32[]{:S(2)}) collective-permute-start(f32[8,128]{1,0:T(8,128)S(1)} %shard_map.83.own_ref), channel_id=1, source_target_pairs={{0,1},{1,0},{2,3},{3,2},{4,5},{5,4},{6,7},{7,6},{8,9},{9,8},{10,11... | collective-permute-start | bytes 12296 | tf_op jit(solution)/shard_map/ppermute | solution.py:308
  16.4 1.4 %collective-permute-start.4 = (f32[8,128]{1,0:T(8,128)S(1)}, f32[8,128]{1,0:T(8,128)S(1)}, u32[]{:S(2)}, u32[]{:S(2)}) collective-permute-start(f32[8,128]{1,0:T(8,128)S(1)} %shard_map.83.own_ref), channel_id=1, source_target_pairs={{0,5},{1,4},{2,7},{3,6},{4,1},{5,0},{6,3},{7,2},{8,13},{9,12},{10,... | collective-permute-start | bytes 12296 | tf_op jit(solution)/shard_map/ppermute | solution.py:312
  17.8 0.0 copy-done.5
  17.8 0.0 copy-start.6
  17.8 0.0 copy-start.1
  17.9 0.6 %collective-permute-done.3.other_ref = f32[8,128]{1,0:T(8,128)S(1)} collective-permute-done((f32[8,128]{1,0:T(8,128)S(1)}, f32[8,128]{1,0:T(8,128)S(1)}, u32[]{:S(2)}, u32[]{:S(2)}) %collective-permute-start.3) | collective-permute-done | bytes 4128 | tf_op jit(solution)/shard_map/ppermute | solution.py:308
  18.5 2.4 %collective-permute-done.4.cross_ref = f32[8,128]{1,0:T(8,128)S(1)} collective-permute-done((f32[8,128]{1,0:T(8,128)S(1)}, f32[8,128]{1,0:T(8,128)S(1)}, u32[]{:S(2)}, u32[]{:S(2)}) %collective-permute-start.4) | collective-permute-done | bytes 4128 | tf_op jit(solution)/shard_map/ppermute | solution.py:312
  20.9 0.0 collective-permute-done.5.refs_3_
  20.9 0.0 copy-done
  20.9 0.2 shard_map.85.pack_ref
  21.2 0.1 collective-permute-start.6
  21.2 0.0 copy-done.6
  21.3 0.0 copy-done.1
  21.3 0.2 shard_map.84
  21.4 1.1 %shard_map.86 = (f32[256,384]{1,0:T(8,128)S(1)}, f32[256,768]{1,0:T(8,128)S(1)}) custom-call(bf16[256,384]{1,0:T(8,128)(2,1)S(1)} %get-tuple-element.17.query_ref, f32[16,1024]{1,0:T(8,128)S(1)} %get-tuple-element.18.bias_ref, bf16[1024,384]{1,0:T(8,128)(2,1)S(1)} %shard_map.85.pack_ref), custom_call_target="tpu_custom_call" | custom-call | tf_op jit(solution)/shard_map/pallas_call | solution.py:346
  22.5 1.0 %collective-permute-done.6.pack_ref = bf16[1024,384]{1,0:T(8,128)(2,1)S(1)} collective-permute-done((bf16[1024,384]{1,0:T(8,128)(2,1)S(1)}, bf16[1024,384]{1,0:T(8,128)(2,1)S(1)}, u32[]{:S(2)}, u32[]{:S(2)}) %collective-permute-start.6) | collective-permute-done | bytes 786464 | tf_op jit(solution)/shard_map/ppermute | solution.py:245
  23.5 0.0 copy-start.2
  23.5 0.0 copy-start.3
  23.5 1.0 %shard_map.88 = bf16[144,384]{1,0:T(8,128)(2,1)S(1)} custom-call(bf16[256,384]{1,0:T(8,128)(2,1)S(1)} %get-tuple-element.17.query_ref, f32[16,1024]{1,0:T(8,128)S(1)} %get-tuple-element.18.bias_ref, bf16[1024,384]{1,0:T(8,128)(2,1)S(1)} %collective-permute-done.6.pack_ref, f32[256,384]{1,0:T(8,128)S(1)} %get-tuple-element.19.context_ref, ...), custom_call_target="tpu_custom_call" | custom-call | tf_op jit(solution)/shard_map/pallas_call | solution.py:358
  24.5 3.1 %collective-permute-start.7 = (bf16[144,384]{1,0:T(8,128)(2,1)S(1)}, bf16[144,384]{1,0:T(8,128)(2,1)S(1)}, u32[]{:S(2)}, u32[]{:S(2)}) collective-permute-start(bf16[144,384]{1,0:T(8,128)(2,1)S(1)} %shard_map.88), channel_id=1, source_target_pairs={{0,24},{2,26},{4,28},{6,30},{8,16},{10,18},{12,20},{14,22},{16,8},... | collective-permute-start | bytes 331784 | tf_op jit(solution)/shard_map/ppermute | solution.py:245
  27.6 0.0 copy-done.2
  27.6 0.0 copy-done.3
  27.6 0.6 %shard_map.89.gate_ref = f32[16,384]{1,0:T(8,128)S(1)} custom-call(s32[2]{0:T(128)S(1)} %copy-done.3, f32[50,384]{1,0:T(8,128)S(1)} %copy-done.2), custom_call_target="tpu_custom_call" | custom-call | tf_op jit(solution)/shard_map/pallas_call | solution.py:374
  28.2 0.9 %shard_map.87 = (f32[128,384]{1,0:T(8,128)S(1)}, f32[16,384]{1,0:T(8,128)S(1)}) custom-call(bf16[256,384]{1,0:T(8,128)(2,1)S(1)} %get-tuple-element.17.query_ref, f32[16,1024]{1,0:T(8,128)S(1)} %get-tuple-element.18.bias_ref, bf16[1024,384]{1,0:T(8,128)(2,1)S(1)} %collective-permute-done.6.pack_ref, f32[256,384]{1,0:T(8,128)S(1)} %get-tuple-element.19.context_ref, ...), custom_call_target="tpu_custom_call" | custom-call | tf_op jit(solution)/shard_map/pallas_call | solution.py:358
  29.2 2.4 %collective-permute-done.7.packet_ref = bf16[144,384]{1,0:T(8,128)(2,1)S(1)} collective-permute-done((bf16[144,384]{1,0:T(8,128)(2,1)S(1)}, bf16[144,384]{1,0:T(8,128)(2,1)S(1)}, u32[]{:S(2)}, u32[]{:S(2)}) %collective-permute-start.7) | collective-permute-done | bytes 110624 | tf_op jit(solution)/shard_map/ppermute | solution.py:245
  31.5 0.8 %shard_map.90 = bf16[128,384]{1,0:T(8,128)(2,1)} custom-call(f32[128,384]{1,0:T(8,128)S(1)} %get-tuple-element.21.own_ref, f32[16,384]{1,0:T(8,128)S(1)} %get-tuple-element.22.lines_ref, bf16[144,384]{1,0:T(8,128)(2,1)S(1)} %collective-permute-done.7.packet_ref, f32[16,384]{1,0:T(8,128)S(1)} %shard_map.89.gate_ref), custom_call_target="tpu_custom_call" | custom-call | tf_op jit(solution)/shard_map/pallas_call | solution.py:383
  (2 shorter events, 0.0 us)
Async XLA Ops:
  1.9 12.8 %copy-start.4 = (f32[8,128]{1,0:T(8,128)S(1)}, f32[8,128]{1,0:T(8,128)}, u32[]{:S(2)}) copy-start(f32[8,128]{1,0:T(8,128)} %get-tuple-element.14.before_ref) | copy-start | bytes 12292
  1.9 8.3 %collective-permute-start.1 = (bf16[256,384]{1,0:T(8,128)(2,1)}, bf16[256,384]{1,0:T(8,128)(2,1)S(1)}, u32[]{:S(2)}, u32[]{:S(2)}) collective-permute-start(bf16[256,384]{1,0:T(8,128)(2,1)} %get-tuple-element.16.refs_0_), channel_id=1, source_target_pairs={{0,8},{2,10},{4,12},{6,14},{8,0},{10,2},{12,4},{14,6},{16,24},{18,... | collective-permute-start | bytes 589832 | tf_op jit(solution)/shard_map/ppermute | solution.py:245
  5.0 9.7 %collective-permute-start.2 = (bf16[256,384]{1,0:T(8,128)(2,1)}, bf16[256,384]{1,0:T(8,128)(2,1)S(1)}, u32[]{:S(2)}, u32[]{:S(2)}) collective-permute-start(bf16[256,384]{1,0:T(8,128)(2,1)} %get-tuple-element.16.refs_0_), channel_id=1, source_target_pairs={{0,4},{2,6},{4,0},{6,2},{8,12},{10,14},{12,8},{14,10},{16,20},{18,... | collective-permute-start | bytes 589832 | tf_op jit(solution)/shard_map/ppermute | solution.py:245
  6.5 8.2 %collective-permute-start = (bf16[144,384]{1,0:T(8,128)(2,1)}, bf16[144,384]{1,0:T(8,128)(2,1)S(1)}, u32[]{:S(2)}, u32[]{:S(2)}) collective-permute-start(bf16[144,384]{1,0:T(8,128)(2,1)} %get-tuple-element.15.refs_0_), channel_id=1, source_target_pairs={{0,24},{2,26},{4,28},{6,30},{8,16},{10,18},{12,20},{14,22},{16,8},... | collective-permute-start | bytes 331784 | tf_op jit(solution)/shard_map/ppermute | solution.py:245
  10.2 10.7 %collective-permute-start.5 = (bf16[256,384]{1,0:T(8,128)(2,1)S(1)}, bf16[256,384]{1,0:T(8,128)(2,1)S(1)}, u32[]{:S(2)}, u32[]{:S(2)}) collective-permute-start(bf16[256,384]{1,0:T(8,128)(2,1)S(1)} %collective-permute-done.1.refs_1_), channel_id=1, source_target_pairs={{0,4},{2,6},{4,0},{6,2},{8,12},{10,14},{12,8},{14,10},{16,20},{18,... | collective-permute-start | bytes 589832 | tf_op jit(solution)/shard_map/ppermute | solution.py:245
  14.7 3.2 %copy-start.5 = (f32[384]{0:T(512)S(1)}, f32[384]{0:T(512)}, u32[]{:S(2)}) copy-start(f32[384]{0:T(512)} %param.12) | copy-start | bytes 4612
  14.7 6.2 %copy-start = (bf16[256,384]{1,0:T(8,128)(2,1)S(1)}, bf16[256,384]{1,0:T(8,128)(2,1)}, u32[]{:S(2)}) copy-start(bf16[256,384]{1,0:T(8,128)(2,1)} %get-tuple-element.16.refs_0_) | copy-start | bytes 589828
  14.8 3.7 %collective-permute-start.3 = (f32[8,128]{1,0:T(8,128)S(1)}, f32[8,128]{1,0:T(8,128)S(1)}, u32[]{:S(2)}, u32[]{:S(2)}) collective-permute-start(f32[8,128]{1,0:T(8,128)S(1)} %shard_map.83.own_ref), channel_id=1, source_target_pairs={{0,1},{1,0},{2,3},{3,2},{4,5},{5,4},{6,7},{7,6},{8,9},{9,8},{10,11... | collective-permute-start | bytes 12296 | tf_op jit(solution)/shard_map/ppermute | solution.py:308
  16.4 4.5 %collective-permute-start.4 = (f32[8,128]{1,0:T(8,128)S(1)}, f32[8,128]{1,0:T(8,128)S(1)}, u32[]{:S(2)}, u32[]{:S(2)}) collective-permute-start(f32[8,128]{1,0:T(8,128)S(1)} %shard_map.83.own_ref), channel_id=1, source_target_pairs={{0,5},{1,4},{2,7},{3,6},{4,1},{5,0},{6,3},{7,2},{8,13},{9,12},{10,... | collective-permute-start | bytes 12296 | tf_op jit(solution)/shard_map/ppermute | solution.py:312
  17.8 3.4 %copy-start.6 = (f32[384]{0:T(512)S(1)}, f32[384]{0:T(512)}, u32[]{:S(2)}) copy-start(f32[384]{0:T(512)} %param.11) | copy-start | bytes 4612
  17.8 3.4 %copy-start.1 = (bf16[144,384]{1,0:T(8,128)(2,1)S(1)}, bf16[144,384]{1,0:T(8,128)(2,1)}, u32[]{:S(2)}) copy-start(bf16[144,384]{1,0:T(8,128)(2,1)} %get-tuple-element.15.refs_0_) | copy-start | bytes 331780
  21.2 2.4 %collective-permute-start.6 = (bf16[1024,384]{1,0:T(8,128)(2,1)S(1)}, bf16[1024,384]{1,0:T(8,128)(2,1)S(1)}, u32[]{:S(2)}, u32[]{:S(2)}) collective-permute-start(bf16[1024,384]{1,0:T(8,128)(2,1)S(1)} %shard_map.85.pack_ref), channel_id=1, source_target_pairs={{0,2},{2,0},{4,6},{6,4},{8,10},{10,8},{12,14},{14,12},{16,18},{18,... | collective-permute-start | bytes 2359304 | tf_op jit(solution)/shard_map/ppermute | solution.py:245
  23.5 4.1 %copy-start.2 = (f32[50,384]{1,0:T(8,128)S(1)}, f32[50,384]{1,0:T(8,128)}, u32[]{:S(2)}) copy-start(f32[50,384]{1,0:T(8,128)} %table_ref.1) | copy-start | bytes 230404
  23.5 4.1 %copy-start.3 = (s32[2]{0:T(128)S(1)}, s32[2]{0:T(128)}, u32[]{:S(2)}) copy-start(s32[2]{0:T(128)} %step_ref.1) | copy-start | bytes 28
  24.5 7.1 %collective-permute-start.7 = (bf16[144,384]{1,0:T(8,128)(2,1)S(1)}, bf16[144,384]{1,0:T(8,128)(2,1)S(1)}, u32[]{:S(2)}, u32[]{:S(2)}) collective-permute-start(bf16[144,384]{1,0:T(8,128)(2,1)S(1)} %shard_map.88), channel_id=1, source_target_pairs={{0,24},{2,26},{4,28},{6,30},{8,16},{10,18},{12,20},{14,22},{16,8},... | collective-permute-start | bytes 331784 | tf_op jit(solution)/shard_map/ppermute | solution.py:245

commit v13 on v12

--- a/solution.py
+++ b/solution.py
@@ -15,6 +15,7 @@
 SCALE = HD ** (-0.5) * LOG2E
 MASKED = -1e30
 EXTRA = 16
+AHEAD = 4 * 10**9
 ANY = pl.BlockSpec(memory_space=pl.ANY)
 VMEM = pl.BlockSpec(memory_space=pltpu.VMEM)
 SMEM = pl.BlockSpec(memory_space=pltpu.SMEM)
@@ -81,8 +82,7 @@
 def query_kernel(full_width, key_masks, gain_ref, own_ref, other_ref, *refs):
     queries, (query_out, bias_out) = refs[:2], refs[2:]
     me = lax.axis_index("tm")
-    count = lax.axis_size("tm")
-    query_mask = count // 2 + count // 4
+    query_mask = lax.axis_size("tm") // 4
     lane = lax.broadcasted_iota(jnp.int32, (1, HD), 1)
     half = (lane >= BLK).astype(jnp.float32)
     for place, query_ref in enumerate(queries):
@@ -102,98 +102,138 @@
             )
 
 
-def pack_kernel(full_width, near, gain_ref, own_ref, other_ref, cross_ref, *refs):
+def early_kernel(full_width, gain_ref, own_ref, other_ref, key_ref, value_ref, *refs):
     *pairs, pack_out = refs
-    held = len(pairs)
-    for place, pair_ref in enumerate(pairs):
+    held = 1 + len(pairs)
+    sources = [(pairs[0], pairs[0]), (key_ref, value_ref)] + [(pair, pair) for pair in pairs[1:]]
+    for place, (key, value) in enumerate(sources):
         line = 1 + place + (place > 0)
-        if place < near:
+        total = own_ref[line : line + 1, :] + other_ref[line : line + 1, :]
+        pack_out[place * HD : (place + 1) * HD, :] = normed(
+            key, factor_of(total, full_width), gain_ref
+        )
+        low = 0 if value is value_ref else HD
+        pack_out[(held + place) * HD : (held + place + 1) * HD, :] = value[low : low + HD, :]
+
+
+def late_kernel(full_width, lines, gain_ref, own_ref, other_ref, cross_ref, *refs):
+    *pairs, _, pack_out = refs
+    held = len(pairs) // 2
+    for place, (key, value) in enumerate(zip(pairs[:held], pairs[held:])):
+        if lines is None:
+            total = squares(key) + cross_ref[3:4, :]
+        else:
+            line = lines[place]
             total = own_ref[line : line + 1, :] + other_ref[line : line + 1, :]
-        else:
-            total = squares(pair_ref) + cross_ref[3:4, :]
         pack_out[place * HD : (place + 1) * HD, :] = normed(
-            pair_ref, factor_of(total, full_width), gain_ref
-        )
-        pack_out[(held + place) * HD : (held + place + 1) * HD, :] = pair_ref[HD:, :]
-
-
-def absorb(query, pack_ref, biases, olds, low):
-    high, half = low + HD, pack_ref.shape[0] // 2
-    scores = lax.dot_general(
-        query,
-        pack_ref[:half, low:high],
-        (((1,), (1,)), ((), ())),
-        preferred_element_type=jnp.float32,
+            key, factor_of(total, full_width), gain_ref
+        )
+        pack_out[(held + place) * HD : (held + place + 1) * HD, :] = value[...]
+
+
+def absorb(queries, pack_ref, biases, olds):
+    half = pack_ref.shape[0] // 2
+    heads, count = len(queries), len(biases)
+    scores = []
+    for head, query in enumerate(queries):
+        scores.append(
+            lax.dot_general(
+                query,
+                pack_ref[:half, head * HD : (head + 1) * HD],
+                (((1,), (1,)), ((), ())),
+                preferred_element_type=jnp.float32,
+            )
+        )
+    spots = [(head, place) for head in range(heads) for place in range(count)]
+    logits, tops, weights, totals = {}, {}, {}, {}
+    for head, place in spots:
+        part = scores[head][place * HD : (place + 1) * HD]
+        logits[head, place] = part * SCALE + biases[place]
+    for spot in spots:
+        top = jnp.broadcast_to(jnp.max(logits[spot], axis=1, keepdims=True), (HD, HD))
+        tops[spot] = top if olds is None else jnp.maximum(top, olds[spot][0])
+    for spot in spots:
+        weights[spot] = [
+            jnp.exp2(logits[spot][:, left : left + HD] - tops[spot])
+            for left in range(0, half, HD)
+        ]
+    added = []
+    for head in range(heads):
+        rounded = [
+            jnp.concatenate([w.astype(jnp.bfloat16) for w in weights[head, place]], axis=1)
+            for place in range(count)
+        ]
+        added.append(
+            jnp.dot(
+                jnp.concatenate(rounded, axis=0),
+                pack_ref[half:, head * HD : (head + 1) * HD],
+                preferred_element_type=jnp.float32,
+            )
+        )
+    for spot in spots:
+        total = jnp.sum(functools.reduce(jnp.add, weights[spot]), axis=1, keepdims=True)
+        totals[spot] = jnp.broadcast_to(total, (HD, HD))
+    results = {}
+    for head, place in spots:
+        spot = (head, place)
+        context, total = added[head][place * HD : (place + 1) * HD], totals[spot]
+        if olds is not None:
+            fade = jnp.exp2(olds[spot][0] - tops[spot])
+            total = total + olds[spot][1] * fade
+            context = context + olds[spot][2] * fade
+        results[spot] = (tops[spot], total, context)
+    return results
+
+
+def held_state(context_ref, stats_ref, head, place):
+    part, low, wide = slice(place * HD, (place + 1) * HD), head * HD, 2 * head * HD
+    return (
+        stats_ref[part, wide : wide + HD],
+        stats_ref[part, wide + HD : wide + 2 * HD],
+        context_ref[part, low : low + HD],
     )
-    tops, totals, rounded = [], [], []
-    for place, bias in enumerate(biases):
-        logits = scores[place * HD : (place + 1) * HD] * SCALE + bias
-        top = jnp.broadcast_to(jnp.max(logits, axis=1, keepdims=True), (HD, HD))
-        if olds is not None:
-            top = jnp.maximum(top, olds[place][0])
-        weights = [
-            jnp.exp2(logits[:, left : left + HD] - top)
-            for left in range(0, logits.shape[1], HD)
-        ]
-        total = jnp.sum(functools.reduce(jnp.add, weights), axis=1, keepdims=True)
-        tops.append(top)
-        totals.append(jnp.broadcast_to(total, (HD, HD)))
-        rounded.append(
-            jnp.concatenate([weight.astype(jnp.bfloat16) for weight in weights], axis=1)
-        )
-    added = jnp.dot(
-        jnp.concatenate(rounded, axis=0),
-        pack_ref[half:, low:high],
-        preferred_element_type=jnp.float32,
-    )
-    results = []
-    for place in range(len(biases)):
-        context = added[place * HD : (place + 1) * HD]
-        total = totals[place]
-        if olds is not None:
-            fade = jnp.exp2(olds[place][0] - tops[place])
-            total = total + olds[place][1] * fade
-            context = context + olds[place][2] * fade
-        results.append((tops[place], total, context))
-    return results
-
-
-def own_attention(query_ref, bias_ref, pack_ref, context_out, stats_out):
-    keys = pack_ref.shape[0] // 2
-    biases = [bias_ref[8 * place : 8 * place + 1, :keys] for place in range(2)]
-    for low in range(0, query_ref.shape[1], HD):
-        results = absorb(query_ref[:, low : low + HD], pack_ref, biases, None, low)
-        for place, (top, total, context) in enumerate(results):
-            part, wide = slice(place * HD, (place + 1) * HD), 2 * low
-            context_out[part, low : low + HD] = context
-            stats_out[part, wide : wide + HD] = top
-            stats_out[part, wide + HD : wide + 2 * HD] = total
+
+
+def step_kernel(first, query_ref, bias_ref, pack_ref, *refs):
+    olds, (context_out, stats_out) = refs[:-2], refs[-2:]
+    heads, keys = query_ref.shape[1] // HD, pack_ref.shape[0] // 2
+    left = first * HD
+    biases = [bias_ref[8 * place : 8 * place + 1, left : left + keys] for place in range(2)]
+    state = None
+    if olds:
+        state = {
+            (head, place): held_state(*olds, head, place)
+            for head in range(heads)
+            for place in range(2)
+        }
+    queries = [query_ref[:, head * HD : (head + 1) * HD] for head in range(heads)]
+    for (head, place), result in absorb(queries, pack_ref, biases, state).items():
+        part, low, wide = slice(place * HD, (place + 1) * HD), head * HD, 2 * head * HD
+        top, total, context = result
+        context_out[part, low : low + HD] = context
+        stats_out[part, wide : wide + HD] = top
+        stats_out[part, wide + HD : wide + 2 * HD] = total
 
 
 def last_attention(place, query_ref, bias_ref, pack_ref, context_ref, stats_ref, *outs):
-    width, keys = query_ref.shape[1], pack_ref.shape[0] // 2
+    heads, keys = query_ref.shape[1] // HD, pack_ref.shape[0] // 2
     part = slice(place * HD, (place + 1) * HD)
-    bias = bias_ref[8 * place : 8 * place + 1, keys:]
+    bias = bias_ref[8 * place : 8 * place + 1, bias_ref.shape[1] - keys :]
     lane = lax.broadcasted_iota(jnp.int32, (1, HD), 1)
+    state = {(h, 0): held_state(context_ref, stats_ref, h, place) for h in range(heads)}
+    queries = [query_ref[part, head * HD : (head + 1) * HD] for head in range(heads)]
+    results = absorb(queries, pack_ref, [bias], state)
     columns = jnp.zeros((HD, HD), jnp.float32)
-    for low in range(0, width, HD):
-        wide = 2 * low
-        old = (
-            stats_ref[part, wide : wide + HD],
-            stats_ref[part, wide + HD : wide + 2 * HD],
-            context_ref[part, low : low + HD],
-        )
-        ((top, total, context),) = absorb(
-            query_ref[part, low : low + HD], pack_ref, [bias], [old], low
-        )
-        outs[0][:HD, low : low + HD] = context.astype(outs[0].dtype)
-        line = wide // HD
+    for head in range(heads):
+        top, total, context = results[head, 0]
+        outs[0][:HD, head * HD : (head + 1) * HD] = context.astype(outs[0].dtype)
+        line = 2 * head
         columns = jnp.where(lane == line, top, jnp.where(lane == line + 1, total, columns))
     lines = columns.T
     sub = lax.broadcasted_iota(jnp.int32, (EXTRA, HD), 0)
-    for low in range(0, width, HD):
-        line = 2 * low // HD
-        pair = (lines[line : line + 1, :], lines[line + 1 : line + 2, :])
+    for head in range(heads):
+        low = head * HD
+        pair = (lines[2 * head : 2 * head + 1, :], lines[2 * head + 1 : 2 * head + 2, :])
         if place == 0:
             for row, value in enumerate(pair):
                 outs[1][8 * row : 8 * row + 8, low : low + HD] = jnp.broadcast_to(value, (8, HD))
@@ -265,8 +305,9 @@
     splits = lax.axis_size("head")
     full_width = width * splits
     params = pltpu.CompilerParams(vmem_limit_bytes=(8 + count // 2) * 2**20)
-    query_mask = count // 2 + count // 4
-    bits = [1 << place for place in range(1, count.bit_length() - 2)][::-1]
+    query_mask = count // 4
+    bits = [1 << place for place in range(1, count.bit_length() - 1)]
+    bits = [bit for bit in bits[::-1] if bit != query_mask]
     query_gain = query_gain.reshape(1, width)
     key_gain = key_gain.reshape(1, width)
 
@@ -287,36 +328,42 @@
             pltpu.SemaphoreType.DMA((4,)),
         ],
     )(query_proj, key_proj, value_proj, far_blocks)
-    blocks = gathered(own_pair, bits)
+    far = bits[0]
+    far_key, far_value = exchange(key_proj, far), exchange(value_proj, far)
+    pairs = gathered(own_pair, bits[1:])
+    late_keys, late_values = gathered(far_key, bits[1:]), gathered(far_value, bits[1:])
     queries = [query_packet, exchange(query_packet, query_mask)]
-    masks = sorted(blocks, key=lambda mask: (mask.bit_count(), -mask))
-    near = 1 + len(bits)
-
-    def summed(sums, sources, held):
+    early = [0, far] + sorted(mask for mask in pairs if mask)
+    late = sorted(mask ^ far for mask in late_keys if mask)
+    late_lines = range(2 + len(early), 2 + len(early) + len(late))
+
+    def summed(sums, sources, held, flops=0):
         return pl.pallas_call(
             functools.partial(sums_kernel, held),
             out_shape=jax.ShapeDtypeStruct(own_sums.shape, jnp.float32),
             in_specs=[VMEM] * (1 + len(sources)),
             out_specs=VMEM,
             compiler_params=params,
-            cost_estimate=cost(4 * 10**9),
+            cost_estimate=cost(flops),
         )(sums, *sources)
 
-    sources = [queries[1]] + [blocks[mask] for mask in masks[1:near]]
-    sums = summed(own_sums, sources, range(2, near + 2))
+    sums = summed(own_sums, [far_key], [3], 2 * AHEAD)
+    sources = [queries[1]] + [pairs[mask] for mask in early[2:]]
+    sums = summed(sums, sources, [2, *range(4, 3 + len(sources))])
     if splits == 2:
         others = lax.ppermute(sums, "head", [(0, 1), (1, 0)])
-        pairs = []
+        flips = []
         for i in range(2 * count):
-            pairs.append((i, ((i // 2) ^ bits[1]) * 2 + (i % 2 ^ 1)))
-        crossed = lax.ppermute(sums, ("tm", "head"), pairs)
+            flips.append((i, ((i // 2) ^ bits[1]) * 2 + (i % 2 ^ 1)))
+        crossed = lax.ppermute(sums, ("tm", "head"), flips)
+        late_lines = None
     else:
-        sources = [blocks[mask] for mask in masks[near:]]
-        sums = summed(sums, sources, range(near + 2, len(masks) + 2))
+        sums = summed(sums, [late_keys[mask ^ far] for mask in late], late_lines)
         sums = lax.psum(sums, "head")
         others = crossed = jnp.zeros_like(sums)
 
-    all_masks = masks + [mask ^ 1 for mask in masks]
+    early_masks = early + [mask ^ 1 for mask in early]
+    all_masks = early_masks + late + [mask ^ 1 for mask in late]
     query_norm, biases = pl.pallas_call(
         functools.partial(query_kernel, width * splits, all_masks),
         out_shape=[
@@ -328,31 +375,47 @@
         compiler_params=params,
     )(query_gain, sums, others, *queries)
 
-    pack = pl.pallas_call(
-        functools.partial(pack_kernel, width * splits, near if splits == 2 else len(masks)),
-        out_shape=jax.ShapeDtypeStruct((2 * len(masks) * rows, width), jnp.bfloat16),
-        in_specs=[VMEM] * (4 + len(masks)),
-        out_specs=VMEM,
-        compiler_params=params,
-    )(
-        key_gain,
-        sums,
-        others,
-        crossed,
-        *[blocks[mask] for mask in masks],
+    def packed(kernel, masks, operands, flops):
+        return pl.pallas_call(
+            kernel,
+            out_shape=jax.ShapeDtypeStruct((2 * len(masks) * rows, width), jnp.bfloat16),
+            in_specs=[VMEM] * (1 + len(operands)),
+            out_specs=VMEM,
+            compiler_params=params,
+            cost_estimate=cost(flops),
+        )(key_gain, *operands)
+
+    early_pack = packed(
+        functools.partial(early_kernel, width * splits),
+        early,
+        [sums, others, far_key, far_value, own_pair] + [pairs[mask] for mask in early[2:]],
+        AHEAD,
     )
-    other_pack = exchange(pack, 1)
-
-    state = pl.pallas_call(
-        own_attention,
-        out_shape=[
-            jax.ShapeDtypeStruct((2 * rows, width), jnp.float32),
-            jax.ShapeDtypeStruct((2 * rows, 2 * width), jnp.float32),
-        ],
-        in_specs=[VMEM] * 3,
-        out_specs=[VMEM] * 2,
-        compiler_params=params,
-    )(query_norm, biases, pack)
+    def step(first, pack, *state):
+        return pl.pallas_call(
+            functools.partial(step_kernel, first),
+            out_shape=[
+                jax.ShapeDtypeStruct((2 * rows, width), jnp.float32),
+                jax.ShapeDtypeStruct((2 * rows, 2 * width), jnp.float32),
+            ],
+            in_specs=[VMEM] * (3 + len(state)),
+            out_specs=[VMEM] * 2,
+            compiler_params=params,
+        )(query_norm, biases, pack, *state)
+
+    state = step(0, early_pack)
+    late_pack = packed(
+        functools.partial(late_kernel, width * splits, late_lines),
+        late,
+        [sums, others, crossed]
+        + [late_keys[mask ^ far] for mask in late]
+        + [late_values[mask ^ far] for mask in late]
+        + [state[1]],
+        3 * AHEAD,
+    )
+    state = step(len(early), exchange(early_pack, 1), *state)
+    state = step(2 * len(early), late_pack, *state)
+    last_pack = exchange(late_pack, 1)
 
     def last(place, out_shape):
         return pl.pallas_call(
@@ -361,7 +424,7 @@
             in_specs=[VMEM] * 5,
             out_specs=[VMEM] * len(out_shape),
             compiler_params=params,
-        )(query_norm, biases, other_pack, *state)
+        )(query_norm, biases, last_pack, *state)
 
     (packet,) = last(1, [jax.ShapeDtypeStruct((rows + EXTRA, width), jnp.bfloat16)])
     own, own_lines = last(

time: 32.5 us -> 31.5 us (0.969)
  starting transfers between devices: 15.2 us -> 12.6 us
  waiting for transfers between devices: 10.3 us -> 11.6 us
  local copies, waits for them, and re-layouts: 0.03 us -> 0.39 us
    ppermute x6 -> x9, waiting for transfers between devices: 7.2 us -> 10.9 us  [exchange(): return lax.ppermute(array, 'tm', [(i, i ^ mask) for i in range(count)])]
    ppermute x6 -> x9, starting transfers between devices: 12.2 us -> 9.81 us  [exchange(): return lax.ppermute(array, 'tm', [(i, i ^ mask) for i in range(count)])]
    ppermute x1, waiting for transfers between devices: 2.42 us -> 0.69 us  [local(): crossed = lax.ppermute(sums, ('tm', 'head'), flips)]
    pallas_call x2, Pallas kernels: 1.91 us -> 0.88 us  [last(): pl.pallas_call(functools.partial(last_attention, place), out_shape=out_sh...]
    pallas_call x2 -> x5, Pallas kernels: 1.29 us -> 2.06 us  [the longest x3 1.68 us: step(): pl.pallas_call(functools.partial(step_kernel, first), out_shape=[jax.Shap...]
    ppermute x1, waiting for transfers between devices: 0.64 us -> 0.01 us  [local(): others = lax.ppermute(sums, 'head', [(0, 1), (1, 0)])]
    unnamed x14, local copies, waits for them, and re-layouts: 0.03 us -> 0.39 us
  transfers between devices with their start and end apart: 8 -> 11, of which waited for: 6 -> 7; matrix products, arithmetic and copies ran while one was open for 0% -> 0% of each run, Pallas kernels for 9% -> 17%
where the time goes in v13:
time: 31.5 us; the launch traced here: 31.4 us
  starting transfers between devices  12.6 us (40%)
  waiting for transfers between devices  11.6 us (37%)
  Pallas kernels  6.61 us (21%)
  local copies, waits for them, and re-layouts  0.39 us (1%)
    ppermute x9, waiting for transfers between devices, exchange(): return lax.ppermute(array, 'tm', [(i, i ^ mask) for i in range(count)])  10.9 us
    ppermute x9, starting transfers between devices, exchange(): return lax.ppermute(array, 'tm', [(i, i ^ mask) for i in range(count)])  9.81 us
    pallas_call x1, Pallas kernels, local(): pl.pallas_call(own_kernel, out_shape=[jax.ShapeDtypeStruct((rows + EXTRA,...  1.88 us
    pallas_call x3, Pallas kernels, step(): pl.pallas_call(functools.partial(step_kernel, first), out_shape=[jax.Shap...  1.68 us
    ppermute x1, starting transfers between devices, local(): others = lax.ppermute(sums, 'head', [(0, 1), (1, 0)])  1.64 us
    ppermute x1, starting transfers between devices, local(): crossed = lax.ppermute(sums, ('tm', 'head'), flips)  1.18 us
    pallas_call x2, Pallas kernels, last(): pl.pallas_call(functools.partial(last_attention, place), out_shape=out_sh...  0.88 us
    pallas_call x1, Pallas kernels, local(): pl.pallas_call(merge_kernel, out_shape=jax.ShapeDtypeStruct((rows, width)...  0.85 us
  transfers between devices with their start and end apart: 11, of which 7 were waited for; matrix products, arithmetic and copies ran while one was open for 0% of the time, Pallas kernels for 17%

profile of v13, /device:TPU:0, one launch (start us, length us, event | category | flops | bytes accessed | tf_op | source)
XLA Modules:
  0.0 31.4 jit_solution(9190752217455522638)
XLA Ops:
  0.0 4.0 %collective-permute-start = (bf16[128,384]{1,0:T(8,128)(2,1)}, bf16[128,384]{1,0:T(8,128)(2,1)S(1)}, u32[]{:S(2)}, u32[]{:S(2)}) collective-permute-start(bf16[128,384]{1,0:T(8,128)(2,1)} %key_hbm.1), channel_id=1, source_target_pairs={{0,16},{2,18},{4,20},{6,22},{8,24},{10,26},{12,28},{14,30},{16,0},... | collective-permute-start | bytes 294920 | tf_op jit(solution)/shard_map/ppermute | solution.py:285
  4.0 0.0 collective-permute-start.6
  4.1 1.9 %shard_map.82 = (bf16[144,384]{1,0:T(8,128)(2,1)}, bf16[256,384]{1,0:T(8,128)(2,1)}, f32[8,128]{1,0:T(8,128)}) custom-call(bf16[128,384]{1,0:T(8,128)(2,1)} %query_hbm.1, bf16[128,384]{1,0:T(8,128)(2,1)} %key_hbm.1, bf16[128,384]{1,0:T(8,128)(2,1)} %value_hbm.1, s32[1,16]{1,0:T(1,128)} %far_hbm.1), custom_call_target="tpu_custom_call" | custom-call | tf_op jit(solution)/shard_map/pallas_call | solution.py:316
  6.0 0.0 copy-start.4
  6.0 1.9 %collective-permute-start.2 = (bf16[256,384]{1,0:T(8,128)(2,1)}, bf16[256,384]{1,0:T(8,128)(2,1)S(1)}, u32[]{:S(2)}, u32[]{:S(2)}) collective-permute-start(bf16[256,384]{1,0:T(8,128)(2,1)} %get-tuple-element.20.refs_0_), channel_id=1, source_target_pairs={{0,4},{2,6},{4,0},{6,2},{8,12},{10,14},{12,8},{14,10},{16,20},{18,... | collective-permute-start | bytes 589832 | tf_op jit(solution)/shard_map/ppermute | solution.py:285
  7.8 1.6 %collective-permute-start.1 = (bf16[144,384]{1,0:T(8,128)(2,1)}, bf16[144,384]{1,0:T(8,128)(2,1)S(1)}, u32[]{:S(2)}, u32[]{:S(2)}) collective-permute-start(bf16[144,384]{1,0:T(8,128)(2,1)} %get-tuple-element.19.refs_0_), channel_id=1, source_target_pairs={{0,8},{2,10},{4,12},{6,14},{8,0},{10,2},{12,4},{14,6},{16,24},{18,... | collective-permute-start | bytes 331784 | tf_op jit(solution)/shard_map/ppermute | solution.py:285
  9.4 2.8 %collective-permute-done.refs_0_.key_ref = bf16[128,384]{1,0:T(8,128)(2,1)S(1)} collective-permute-done((bf16[128,384]{1,0:T(8,128)(2,1)}, bf16[128,384]{1,0:T(8,128)(2,1)S(1)}, u32[]{:S(2)}, u32[]{:S(2)}) %collective-permute-start) | collective-permute-done | bytes 98336 | tf_op jit(solution)/shard_map/ppermute | solution.py:285
  12.2 0.0 copy-done.4
  12.2 0.1 shard_map.83.before_ref
  12.3 0.0 copy-start.5
  12.3 0.0 copy-start.3
  12.3 2.4 %collective-permute-done.1.refs_0_.refs_1_ = bf16[144,384]{1,0:T(8,128)(2,1)S(1)} collective-permute-done((bf16[144,384]{1,0:T(8,128)(2,1)}, bf16[144,384]{1,0:T(8,128)(2,1)S(1)}, u32[]{:S(2)}, u32[]{:S(2)}) %collective-permute-start.1) | collective-permute-done | bytes 110624 | tf_op jit(solution)/shard_map/ppermute | solution.py:285
  14.7 0.0 collective-permute-done.2.refs_1_
  14.7 0.1 shard_map.84.own_ref
  14.8 0.0 copy-start.6
  14.8 1.6 %collective-permute-start.3 = (f32[8,128]{1,0:T(8,128)S(1)}, f32[8,128]{1,0:T(8,128)S(1)}, u32[]{:S(2)}, u32[]{:S(2)}) collective-permute-start(f32[8,128]{1,0:T(8,128)S(1)} %shard_map.84.own_ref), channel_id=1, source_target_pairs={{0,1},{1,0},{2,3},{3,2},{4,5},{5,4},{6,7},{7,6},{8,9},{9,8},{10,11... | collective-permute-start | bytes 12296 | tf_op jit(solution)/shard_map/ppermute | solution.py:354
  16.4 0.0 copy-done.5
  16.5 0.0 copy-done.6
  16.5 0.0 copy-start
  16.5 1.3 %collective-permute-start.5 = (bf16[128,384]{1,0:T(8,128)(2,1)S(1)}, bf16[128,384]{1,0:T(8,128)(2,1)S(1)}, u32[]{:S(2)}, u32[]{:S(2)}) collective-permute-start(bf16[128,384]{1,0:T(8,128)(2,1)S(1)} %collective-permute-done.refs_0_.key_ref), channel_id=1, source_target_pairs={{0,4},{2,6},{4,0},{6,2},{8,12},{10,14},{12,8},{14,10},{16,20},{18,... | collective-permute-start | bytes 294920 | tf_op jit(solution)/shard_map/ppermute | solution.py:285
  17.8 0.0 collective-permute-done.6.value_ref
  17.8 0.8 %collective-permute-start.7 = (bf16[128,384]{1,0:T(8,128)(2,1)S(1)}, bf16[128,384]{1,0:T(8,128)(2,1)S(1)}, u32[]{:S(2)}, u32[]{:S(2)}) collective-permute-start(bf16[128,384]{1,0:T(8,128)(2,1)S(1)} %collective-permute-done.6.value_ref), channel_id=1, source_target_pairs={{0,4},{2,6},{4,0},{6,2},{8,12},{10,14},{12,8},{14,10},{16,20},{18,... | collective-permute-start | bytes 294920 | tf_op jit(solution)/shard_map/ppermute | solution.py:285
  18.6 1.2 %collective-permute-start.4 = (f32[8,128]{1,0:T(8,128)S(1)}, f32[8,128]{1,0:T(8,128)S(1)}, u32[]{:S(2)}, u32[]{:S(2)}) collective-permute-start(f32[8,128]{1,0:T(8,128)S(1)} %shard_map.84.own_ref), channel_id=1, source_target_pairs={{0,5},{1,4},{2,7},{3,6},{4,1},{5,0},{6,3},{7,2},{8,13},{9,12},{10,... | collective-permute-start | bytes 12296 | tf_op jit(solution)/shard_map/ppermute | solution.py:358
  19.8 0.0 collective-permute-done.3.other_ref
  19.8 0.0 copy-done.3
  19.8 0.2 shard_map.86.pack_ref
  19.9 0.1 collective-permute-start.9
  20.0 0.0 copy-done
  20.0 0.2 shard_map.85
  20.2 0.6 %shard_map.87 = (f32[256,384]{1,0:T(8,128)S(1)}, f32[256,768]{1,0:T(8,128)S(1)}) custom-call(bf16[256,384]{1,0:T(8,128)(2,1)S(1)} %get-tuple-element.21.query_ref, f32[16,1024]{1,0:T(8,128)S(1)} %get-tuple-element.22.bias_ref, bf16[768,384]{1,0:T(8,128)(2,1)S(1)} %shard_map.86.pack_ref), custom_call_target="tpu_custom_call" | custom-call | tf_op jit(solution)/shard_map/pallas_call | solution.py:395
  20.8 0.4 %collective-permute-done.5.refs_0_ = bf16[128,384]{1,0:T(8,128)(2,1)S(1)} collective-permute-done((bf16[128,384]{1,0:T(8,128)(2,1)S(1)}, bf16[128,384]{1,0:T(8,128)(2,1)S(1)}, u32[]{:S(2)}, u32[]{:S(2)}) %collective-permute-start.5) | collective-permute-done | bytes 98336 | tf_op jit(solution)/shard_map/ppermute | solution.py:285
  21.2 1.2 %collective-permute-done.7.refs_1_ = bf16[128,384]{1,0:T(8,128)(2,1)S(1)} collective-permute-done((bf16[128,384]{1,0:T(8,128)(2,1)S(1)}, bf16[128,384]{1,0:T(8,128)(2,1)S(1)}, u32[]{:S(2)}, u32[]{:S(2)}) %collective-permute-start.7) | collective-permute-done | bytes 98336 | tf_op jit(solution)/shard_map/ppermute | solution.py:285
  22.4 0.7 %collective-permute-done.4.cross_ref = f32[8,128]{1,0:T(8,128)S(1)} collective-permute-done((f32[8,128]{1,0:T(8,128)S(1)}, f32[8,128]{1,0:T(8,128)S(1)}, u32[]{:S(2)}, u32[]{:S(2)}) %collective-permute-start.4) | collective-permute-done | bytes 4128 | tf_op jit(solution)/shard_map/ppermute | solution.py:358
  23.1 0.2 shard_map.88.pack_ref
  23.3 0.1 collective-permute-start.8
  23.4 0.0 collective-permute-done.9.pack_ref
  23.4 0.6 %shard_map.89 = (f32[256,384]{1,0:T(8,128)S(1)}, f32[256,768]{1,0:T(8,128)S(1)}) custom-call(bf16[256,384]{1,0:T(8,128)(2,1)S(1)} %get-tuple-element.21.query_ref, f32[16,1024]{1,0:T(8,128)S(1)} %get-tuple-element.22.bias_ref, bf16[768,384]{1,0:T(8,128)(2,1)S(1)} %collective-permute-done.9.pack_ref, f32[256,384]{1,0:T(8,128)S(1)} %get-tuple-element.24.refs_0_, ...), custom_call_target="tpu_custom_call" | custom-call | tf_op jit(solution)/shard_map/pallas_call | solution.py:395
  24.0 0.5 %shard_map.90 = (f32[256,384]{1,0:T(8,128)S(1)}, f32[256,768]{1,0:T(8,128)S(1)}) custom-call(bf16[256,384]{1,0:T(8,128)(2,1)S(1)} %get-tuple-element.21.query_ref, f32[16,1024]{1,0:T(8,128)S(1)} %get-tuple-element.22.bias_ref, bf16[256,384]{1,0:T(8,128)(2,1)S(1)} %shard_map.88.pack_ref, f32[256,384]{1,0:T(8,128)S(1)} %get-tuple-element.25.refs_0_, ...), custom_call_target="tpu_custom_call" | custom-call | tf_op jit(solution)/shard_map/pallas_call | solution.py:395
  24.5 0.3 collective-permute-done.8.pack_ref
  24.8 0.0 copy-start.1
  24.8 0.4 %shard_map.92 = bf16[144,384]{1,0:T(8,128)(2,1)S(1)} custom-call(bf16[256,384]{1,0:T(8,128)(2,1)S(1)} %get-tuple-element.21.query_ref, f32[16,1024]{1,0:T(8,128)S(1)} %get-tuple-element.22.bias_ref, bf16[256,384]{1,0:T(8,128)(2,1)S(1)} %collective-permute-done.8.pack_ref, f32[256,384]{1,0:T(8,128)S(1)} %get-tuple-element.27.context_ref, ...), custom_call_target="tpu_custom_call" | custom-call | tf_op jit(solution)/shard_map/pallas_call | solution.py:421
  25.3 0.1 collective-permute-start.10
  25.3 0.4 %copy-done.1 = f32[50,384]{1,0:T(8,128)S(1)} copy-done((f32[50,384]{1,0:T(8,128)S(1)}, f32[50,384]{1,0:T(8,128)}, u32[]{:S(2)}) %copy-start.1) | copy-done | bytes 76824
  25.7 0.0 copy-done.2
  25.7 0.6 %shard_map.93.gate_ref = f32[16,384]{1,0:T(8,128)S(1)} custom-call(s32[2]{0:T(128)S(1)} %copy-done.2, f32[50,384]{1,0:T(8,128)S(1)} %copy-done.1), custom_call_target="tpu_custom_call" | custom-call | tf_op jit(solution)/shard_map/pallas_call | solution.py:437
  26.3 0.4 %shard_map.91 = (f32[128,384]{1,0:T(8,128)S(1)}, f32[16,384]{1,0:T(8,128)S(1)}) custom-call(bf16[256,384]{1,0:T(8,128)(2,1)S(1)} %get-tuple-element.21.query_ref, f32[16,1024]{1,0:T(8,128)S(1)} %get-tuple-element.22.bias_ref, bf16[256,384]{1,0:T(8,128)(2,1)S(1)} %collective-permute-done.8.pack_ref, f32[256,384]{1,0:T(8,128)S(1)} %get-tuple-element.27.context_ref, ...), custom_call_target="tpu_custom_call" | custom-call | tf_op jit(solution)/shard_map/pallas_call | solution.py:421
  26.7 3.8 %collective-permute-done.10.packet_ref = bf16[144,384]{1,0:T(8,128)(2,1)S(1)} collective-permute-done((bf16[144,384]{1,0:T(8,128)(2,1)S(1)}, bf16[144,384]{1,0:T(8,128)(2,1)S(1)}, u32[]{:S(2)}, u32[]{:S(2)}) %collective-permute-start.10) | collective-permute-done | bytes 110624 | tf_op jit(solution)/shard_map/ppermute | solution.py:285
  30.5 0.8 %shard_map.94 = bf16[128,384]{1,0:T(8,128)(2,1)} custom-call(f32[128,384]{1,0:T(8,128)S(1)} %get-tuple-element.29.own_ref, f32[16,384]{1,0:T(8,128)S(1)} %get-tuple-element.30.lines_ref, bf16[144,384]{1,0:T(8,128)(2,1)S(1)} %collective-permute-done.10.packet_ref, f32[16,384]{1,0:T(8,128)S(1)} %shard_map.93.gate_ref), custom_call_target="tpu_custom_call" | custom-call | tf_op jit(solution)/shard_map/pallas_call | solution.py:446
  (3 shorter events, 0.0 us)
Async XLA Ops:
  0.0 12.2 %collective-permute-start = (bf16[128,384]{1,0:T(8,128)(2,1)}, bf16[128,384]{1,0:T(8,128)(2,1)S(1)}, u32[]{:S(2)}, u32[]{:S(2)}) collective-permute-start(bf16[128,384]{1,0:T(8,128)(2,1)} %key_hbm.1), channel_id=1, source_target_pairs={{0,16},{2,18},{4,20},{6,22},{8,24},{10,26},{12,28},{14,30},{16,0},... | collective-permute-start | bytes 294920 | tf_op jit(solution)/shard_map/ppermute | solution.py:285
  4.0 13.7 %collective-permute-start.6 = (bf16[128,384]{1,0:T(8,128)(2,1)}, bf16[128,384]{1,0:T(8,128)(2,1)S(1)}, u32[]{:S(2)}, u32[]{:S(2)}) collective-permute-start(bf16[128,384]{1,0:T(8,128)(2,1)} %value_hbm.1), channel_id=1, source_target_pairs={{0,16},{2,18},{4,20},{6,22},{8,24},{10,26},{12,28},{14,30},{16,0},... | collective-permute-start | bytes 294920 | tf_op jit(solution)/shard_map/ppermute | solution.py:285
  6.0 6.2 %copy-start.4 = (f32[8,128]{1,0:T(8,128)S(1)}, f32[8,128]{1,0:T(8,128)}, u32[]{:S(2)}) copy-start(f32[8,128]{1,0:T(8,128)} %get-tuple-element.18.before_ref) | copy-start | bytes 12292
  6.0 8.7 %collective-permute-start.2 = (bf16[256,384]{1,0:T(8,128)(2,1)}, bf16[256,384]{1,0:T(8,128)(2,1)S(1)}, u32[]{:S(2)}, u32[]{:S(2)}) collective-permute-start(bf16[256,384]{1,0:T(8,128)(2,1)} %get-tuple-element.20.refs_0_), channel_id=1, source_target_pairs={{0,4},{2,6},{4,0},{6,2},{8,12},{10,14},{12,8},{14,10},{16,20},{18,... | collective-permute-start | bytes 589832 | tf_op jit(solution)/shard_map/ppermute | solution.py:285
  7.8 6.8 %collective-permute-start.1 = (bf16[144,384]{1,0:T(8,128)(2,1)}, bf16[144,384]{1,0:T(8,128)(2,1)S(1)}, u32[]{:S(2)}, u32[]{:S(2)}) collective-permute-start(bf16[144,384]{1,0:T(8,128)(2,1)} %get-tuple-element.19.refs_0_), channel_id=1, source_target_pairs={{0,8},{2,10},{4,12},{6,14},{8,0},{10,2},{12,4},{14,6},{16,24},{18,... | collective-permute-start | bytes 331784 | tf_op jit(solution)/shard_map/ppermute | solution.py:285
  12.3 4.2 %copy-start.5 = (f32[384]{0:T(512)S(1)}, f32[384]{0:T(512)}, u32[]{:S(2)}) copy-start(f32[384]{0:T(512)} %param.12) | copy-start | bytes 4612
  12.3 7.5 %copy-start.3 = (bf16[256,384]{1,0:T(8,128)(2,1)S(1)}, bf16[256,384]{1,0:T(8,128)(2,1)}, u32[]{:S(2)}) copy-start(bf16[256,384]{1,0:T(8,128)(2,1)} %get-tuple-element.20.refs_0_) | copy-start | bytes 589828
  14.8 1.7 %copy-start.6 = (f32[384]{0:T(512)S(1)}, f32[384]{0:T(512)}, u32[]{:S(2)}) copy-start(f32[384]{0:T(512)} %param.11) | copy-start | bytes 4612
  14.8 4.9 %collective-permute-start.3 = (f32[8,128]{1,0:T(8,128)S(1)}, f32[8,128]{1,0:T(8,128)S(1)}, u32[]{:S(2)}, u32[]{:S(2)}) collective-permute-start(f32[8,128]{1,0:T(8,128)S(1)} %shard_map.84.own_ref), channel_id=1, source_target_pairs={{0,1},{1,0},{2,3},{3,2},{4,5},{5,4},{6,7},{7,6},{8,9},{9,8},{10,11... | collective-permute-start | bytes 12296 | tf_op jit(solution)/shard_map/ppermute | solution.py:354
  16.5 3.5 %copy-start = (bf16[144,384]{1,0:T(8,128)(2,1)S(1)}, bf16[144,384]{1,0:T(8,128)(2,1)}, u32[]{:S(2)}) copy-start(bf16[144,384]{1,0:T(8,128)(2,1)} %get-tuple-element.19.refs_0_) | copy-start | bytes 331780
  16.5 4.7 %collective-permute-start.5 = (bf16[128,384]{1,0:T(8,128)(2,1)S(1)}, bf16[128,384]{1,0:T(8,128)(2,1)S(1)}, u32[]{:S(2)}, u32[]{:S(2)}) collective-permute-start(bf16[128,384]{1,0:T(8,128)(2,1)S(1)} %collective-permute-done.refs_0_.key_ref), channel_id=1, source_target_pairs={{0,4},{2,6},{4,0},{6,2},{8,12},{10,14},{12,8},{14,10},{16,20},{18,... | collective-permute-start | bytes 294920 | tf_op jit(solution)/shard_map/ppermute | solution.py:285
  17.8 4.6 %collective-permute-start.7 = (bf16[128,384]{1,0:T(8,128)(2,1)S(1)}, bf16[128,384]{1,0:T(8,128)(2,1)S(1)}, u32[]{:S(2)}, u32[]{:S(2)}) collective-permute-start(bf16[128,384]{1,0:T(8,128)(2,1)S(1)} %collective-permute-done.6.value_ref), channel_id=1, source_target_pairs={{0,4},{2,6},{4,0},{6,2},{8,12},{10,14},{12,8},{14,10},{16,20},{18,... | collective-permute-start | bytes 294920 | tf_op jit(solution)/shard_map/ppermute | solution.py:285
  18.6 4.5 %collective-permute-start.4 = (f32[8,128]{1,0:T(8,128)S(1)}, f32[8,128]{1,0:T(8,128)S(1)}, u32[]{:S(2)}, u32[]{:S(2)}) collective-permute-start(f32[8,128]{1,0:T(8,128)S(1)} %shard_map.84.own_ref), channel_id=1, source_target_pairs={{0,5},{1,4},{2,7},{3,6},{4,1},{5,0},{6,3},{7,2},{8,13},{9,12},{10,... | collective-permute-start | bytes 12296 | tf_op jit(solution)/shard_map/ppermute | solution.py:358
  19.9 3.5 %collective-permute-start.9 = (bf16[768,384]{1,0:T(8,128)(2,1)S(1)}, bf16[768,384]{1,0:T(8,128)(2,1)S(1)}, u32[]{:S(2)}, u32[]{:S(2)}) collective-permute-start(bf16[768,384]{1,0:T(8,128)(2,1)S(1)} %shard_map.86.pack_ref), channel_id=1, source_target_pairs={{0,2},{2,0},{4,6},{6,4},{8,10},{10,8},{12,14},{14,12},{16,18},{18,... | collective-permute-start | bytes 1769480 | tf_op jit(solution)/shard_map/ppermute | solution.py:285
  23.3 1.5 %collective-permute-start.8 = (bf16[256,384]{1,0:T(8,128)(2,1)S(1)}, bf16[256,384]{1,0:T(8,128)(2,1)S(1)}, u32[]{:S(2)}, u32[]{:S(2)}) collective-permute-start(bf16[256,384]{1,0:T(8,128)(2,1)S(1)} %shard_map.88.pack_ref), channel_id=1, source_target_pairs={{0,2},{2,0},{4,6},{6,4},{8,10},{10,8},{12,14},{14,12},{16,18},{18,... | collective-permute-start | bytes 589832 | tf_op jit(solution)/shard_map/ppermute | solution.py:285
  24.8 0.9 %copy-start.1 = (f32[50,384]{1,0:T(8,128)S(1)}, f32[50,384]{1,0:T(8,128)}, u32[]{:S(2)}) copy-start(f32[50,384]{1,0:T(8,128)} %table_ref.1) | copy-start | bytes 230404
  24.8 0.9 %copy-start.2 = (s32[2]{0:T(128)S(1)}, s32[2]{0:T(128)}, u32[]{:S(2)}) copy-start(s32[2]{0:T(128)} %step_ref.1) | copy-start | bytes 28
  25.3 5.2 %collective-permute-start.10 = (bf16[144,384]{1,0:T(8,128)(2,1)S(1)}, bf16[144,384]{1,0:T(8,128)(2,1)S(1)}, u32[]{:S(2)}, u32[]{:S(2)}) collective-permute-start(bf16[144,384]{1,0:T(8,128)(2,1)S(1)} %shard_map.92), channel_id=1, source_target_pairs={{0,8},{2,10},{4,12},{6,14},{8,0},{10,2},{12,4},{14,6},{16,24},{18,... | collective-permute-start | bytes 331784 | tf_op jit(solution)/shard_map/ppermute | solution.py:285

commit v14 on v13

--- a/solution.py
+++ b/solution.py
@@ -34,29 +34,20 @@
     return jnp.sum(part.T, axis=0, keepdims=True)
 
 
-def own_kernel(
-    query_hbm, key_hbm, value_hbm, far_hbm, query_out, pair_out, sums_out, query_ref, far_ref, sems
-):
-    rows, width = query_ref.shape
+def own_kernel(query_hbm, key_hbm, value_hbm, pair_out, sums_out, query_ref, sems):
+    rows = query_ref.shape[0]
     copies = [
         pltpu.make_async_copy(key_hbm, pair_out.at[:rows, :], sems.at[0]),
         pltpu.make_async_copy(value_hbm, pair_out.at[rows:, :], sems.at[1]),
         pltpu.make_async_copy(query_hbm, query_ref, sems.at[2]),
-        pltpu.make_async_copy(far_hbm, far_ref, sems.at[3]),
     ]
     for copy in copies:
         copy.start()
-    query_out[rows:, HD:] = jnp.zeros((EXTRA, width - HD), jnp.bfloat16)
     sums_out[...] = jnp.zeros_like(sums_out)
     copies[0].wait()
     sums_out[1:2, :] = squares(pair_out)
     copies[2].wait()
-    query_out[:rows, :] = query_ref[...]
     sums_out[0:1, :] = squares(query_ref)
-    copies[3].wait()
-    far = far_ref[...].astype(jnp.float32)
-    far = jnp.concatenate([far, jnp.full((1, HD - far.shape[1]), -1.0)], axis=1)
-    query_out[rows:, :HD] = jnp.broadcast_to(far, (EXTRA, HD)).astype(jnp.bfloat16)
     copies[1].wait()
 
 
@@ -79,18 +70,21 @@
     return jnp.concatenate(parts, axis=1)
 
 
-def query_kernel(full_width, key_masks, gain_ref, own_ref, other_ref, *refs):
-    queries, (query_out, bias_out) = refs[:2], refs[2:]
+def query_kernel(full_width, query_ref, far_ref, gain_ref, own_ref, other_ref, out_ref):
+    total = own_ref[0:1, :] + other_ref[0:1, :]
+    out_ref[:HD, :] = normed(query_ref, factor_of(total, full_width), gain_ref)
+    far = far_ref[...].astype(jnp.float32)
+    far = jnp.concatenate([far, jnp.full((1, HD - far.shape[1]), -1.0)], axis=1)
+    out_ref[HD:, :HD] = jnp.broadcast_to(far, (EXTRA, HD)).astype(jnp.bfloat16)
+    out_ref[HD:, HD:] = jnp.zeros((EXTRA, out_ref.shape[1] - HD), jnp.bfloat16)
+
+
+def bias_kernel(key_masks, own_ref, remote_ref, bias_out):
     me = lax.axis_index("tm")
     query_mask = lax.axis_size("tm") // 4
     lane = lax.broadcasted_iota(jnp.int32, (1, HD), 1)
     half = (lane >= BLK).astype(jnp.float32)
-    for place, query_ref in enumerate(queries):
-        line = 2 * place
-        total = own_ref[line : line + 1, :] + other_ref[line : line + 1, :]
-        query_out[place * HD : (place + 1) * HD, :] = normed(
-            query_ref, factor_of(total, full_width), gain_ref
-        )
+    for place, query_ref in enumerate((own_ref, remote_ref)):
         far = query_ref[HD:, :HD].astype(jnp.float32)[:1]
         query_id = me ^ (place * query_mask)
         for block, key_mask in enumerate(key_masks):
@@ -194,9 +188,9 @@
     )
 
 
-def step_kernel(first, query_ref, bias_ref, pack_ref, *refs):
+def step_kernel(first, own_ref, remote_ref, bias_ref, pack_ref, *refs):
     olds, (context_out, stats_out) = refs[:-2], refs[-2:]
-    heads, keys = query_ref.shape[1] // HD, pack_ref.shape[0] // 2
+    heads, keys = own_ref.shape[1] // HD, pack_ref.shape[0] // 2
     left = first * HD
     biases = [bias_ref[8 * place : 8 * place + 1, left : left + keys] for place in range(2)]
     state = None
@@ -206,7 +200,10 @@
             for head in range(heads)
             for place in range(2)
         }
-    queries = [query_ref[:, head * HD : (head + 1) * HD] for head in range(heads)]
+    queries = [
+        jnp.concatenate([ref[:HD, head * HD : (head + 1) * HD] for ref in (own_ref, remote_ref)])
+        for head in range(heads)
+    ]
     for (head, place), result in absorb(queries, pack_ref, biases, state).items():
         part, low, wide = slice(place * HD, (place + 1) * HD), head * HD, 2 * head * HD
         top, total, context = result
@@ -221,7 +218,7 @@
     bias = bias_ref[8 * place : 8 * place + 1, bias_ref.shape[1] - keys :]
     lane = lax.broadcasted_iota(jnp.int32, (1, HD), 1)
     state = {(h, 0): held_state(context_ref, stats_ref, h, place) for h in range(heads)}
-    queries = [query_ref[part, head * HD : (head + 1) * HD] for head in range(heads)]
+    queries = [query_ref[:HD, head * HD : (head + 1) * HD] for head in range(heads)]
     results = absorb(queries, pack_ref, [bias], state)
     columns = jnp.zeros((HD, HD), jnp.float32)
     for head in range(heads):
@@ -313,26 +310,23 @@
 
     lines = 2 + 2 ** len(bits)
     lines += -lines % 8
-    query_packet, own_pair, own_sums = pl.pallas_call(
+    own_pair, own_sums = pl.pallas_call(
         own_kernel,
         out_shape=[
-            jax.ShapeDtypeStruct((rows + EXTRA, width), jnp.bfloat16),
             jax.ShapeDtypeStruct((2 * rows, width), jnp.bfloat16),
             jax.ShapeDtypeStruct((lines, rows), jnp.float32),
         ],
-        in_specs=[ANY] * 4,
-        out_specs=[VMEM] * 3,
+        in_specs=[ANY] * 3,
+        out_specs=[VMEM] * 2,
         scratch_shapes=[
             pltpu.VMEM((rows, width), jnp.bfloat16),
-            pltpu.VMEM(far_blocks.shape, jnp.int32),
-            pltpu.SemaphoreType.DMA((4,)),
+            pltpu.SemaphoreType.DMA((3,)),
         ],
-    )(query_proj, key_proj, value_proj, far_blocks)
+    )(query_proj, key_proj, value_proj)
     far = bits[0]
     far_key, far_value = exchange(key_proj, far), exchange(value_proj, far)
     pairs = gathered(own_pair, bits[1:])
     late_keys, late_values = gathered(far_key, bits[1:]), gathered(far_value, bits[1:])
-    queries = [query_packet, exchange(query_packet, query_mask)]
     early = [0, far] + sorted(mask for mask in pairs if mask)
     late = sorted(mask ^ far for mask in late_keys if mask)
     late_lines = range(2 + len(early), 2 + len(early) + len(late))
@@ -348,8 +342,8 @@
         )(sums, *sources)
 
     sums = summed(own_sums, [far_key], [3], 2 * AHEAD)
-    sources = [queries[1]] + [pairs[mask] for mask in early[2:]]
-    sums = summed(sums, sources, [2, *range(4, 3 + len(sources))])
+    sources = [pairs[mask] for mask in early[2:]]
+    sums = summed(sums, sources, range(4, 4 + len(sources)))
     if splits == 2:
         others = lax.ppermute(sums, "head", [(0, 1), (1, 0)])
         flips = []
@@ -364,16 +358,21 @@
 
     early_masks = early + [mask ^ 1 for mask in early]
     all_masks = early_masks + late + [mask ^ 1 for mask in late]
-    query_norm, biases = pl.pallas_call(
-        functools.partial(query_kernel, width * splits, all_masks),
-        out_shape=[
-            jax.ShapeDtypeStruct((2 * rows, width), jnp.bfloat16),
-            jax.ShapeDtypeStruct((16, len(all_masks) * HD), jnp.float32),
-        ],
+    query_packet = pl.pallas_call(
+        functools.partial(query_kernel, width * splits),
+        out_shape=jax.ShapeDtypeStruct((rows + EXTRA, width), jnp.bfloat16),
         in_specs=[VMEM] * 5,
-        out_specs=[VMEM] * 2,
+        out_specs=VMEM,
         compiler_params=params,
-    )(query_gain, sums, others, *queries)
+    )(query_proj, far_blocks, query_gain, sums, others)
+    queries = [query_packet, exchange(query_packet, query_mask)]
+    biases = pl.pallas_call(
+        functools.partial(bias_kernel, all_masks),
+        out_shape=jax.ShapeDtypeStruct((16, len(all_masks) * HD), jnp.float32),
+        in_specs=[VMEM] * 2,
+        out_specs=VMEM,
+        compiler_params=params,
+    )(*queries)
 
     def packed(kernel, masks, operands, flops):
         return pl.pallas_call(
@@ -398,10 +397,10 @@
                 jax.ShapeDtypeStruct((2 * rows, width), jnp.float32),
                 jax.ShapeDtypeStruct((2 * rows, 2 * width), jnp.float32),
             ],
-            in_specs=[VMEM] * (3 + len(state)),
+            in_specs=[VMEM] * (4 + len(state)),
             out_specs=[VMEM] * 2,
             compiler_params=params,
-        )(query_norm, biases, pack, *state)
+        )(*queries, biases, pack, *state)
 
     state = step(0, early_pack)
     late_pack = packed(
@@ -424,7 +423,7 @@
             in_specs=[VMEM] * 5,
             out_specs=[VMEM] * len(out_shape),
             compiler_params=params,
-        )(query_norm, biases, last_pack, *state)
+        )(queries[place], biases, last_pack, *state)
 
     (packet,) = last(1, [jax.ShapeDtypeStruct((rows + EXTRA, width), jnp.bfloat16)])
     own, own_lines = last(

time: 31.5 us -> 32.6 us (1.035)
  starting transfers between devices: 12.6 us -> 13.6 us
  local copies, waits for them, and re-layouts: 0.39 us -> 0.73 us
    ppermute x1, waiting for transfers between devices: 0.69 us -> 0.01 us  [local(): crossed = lax.ppermute(sums, ('tm', 'head'), flips)]
    ppermute x9, starting transfers between devices: 9.81 us -> 10.3 us  [exchange(): return lax.ppermute(array, 'tm', [(i, i ^ mask) for i in range(count)])]
    ppermute x9, waiting for transfers between devices: 10.9 us -> 11.3 us  [exchange(): return lax.ppermute(array, 'tm', [(i, i ^ mask) for i in range(count)])]
    unnamed x14 -> x16, local copies, waits for them, and re-layouts: 0.39 us -> 0.72 us
    pallas_call x2 -> x3, Pallas kernels: 2.03 us -> 2.02 us  [the longest x1 1.81 us: local(): pl.pallas_call(own_kernel, out_shape=[jax.ShapeDtypeStruct((2 * rows, wid...]
  transfers between devices with their start and end apart: 11 -> 11, of which waited for: 7 -> 4; matrix products, arithmetic and copies ran while one was open for 0% -> 0% of each run, Pallas kernels for 17% -> 16%
where the time goes in v14:
time: 32.6 us; the launch traced here: 32.4 us
  starting transfers between devices  13.6 us (42%)
  waiting for transfers between devices  11.3 us (35%)
  Pallas kernels  6.64 us (20%)
  local copies, waits for them, and re-layouts  0.73 us (2%)
    ppermute x9, waiting for transfers between devices, exchange(): return lax.ppermute(array, 'tm', [(i, i ^ mask) for i in range(count)])  11.3 us
    ppermute x9, starting transfers between devices, exchange(): return lax.ppermute(array, 'tm', [(i, i ^ mask) for i in range(count)])  10.3 us
    pallas_call x1, Pallas kernels, local(): pl.pallas_call(own_kernel, out_shape=[jax.ShapeDtypeStruct((2 * rows, wid...  1.81 us
    ppermute x1, starting transfers between devices, local(): others = lax.ppermute(sums, 'head', [(0, 1), (1, 0)])  1.8 us
    pallas_call x3, Pallas kernels, step(): pl.pallas_call(functools.partial(step_kernel, first), out_shape=[jax.Shap...  1.72 us
    ppermute x1, starting transfers between devices, local(): crossed = lax.ppermute(sums, ('tm', 'head'), flips)  1.45 us
    pallas_call x2, Pallas kernels, last(): pl.pallas_call(functools.partial(last_attention, place), out_shape=out_sh...  0.9 us
    pallas_call x1, Pallas kernels, local(): pl.pallas_call(merge_kernel, out_shape=jax.ShapeDtypeStruct((rows, width)...  0.85 us
  transfers between devices with their start and end apart: 11, of which 4 were waited for; matrix products, arithmetic and copies ran while one was open for 0% of the time, Pallas kernels for 16%

profile of v14, /device:TPU:0, one launch (start us, length us, event | category | flops | bytes accessed | tf_op | source)
XLA Modules:
  0.0 32.4 jit_solution(12699997132746011759)
XLA Ops:
  0.0 4.0 %collective-permute-start = (bf16[128,384]{1,0:T(8,128)(2,1)}, bf16[128,384]{1,0:T(8,128)(2,1)S(1)}, u32[]{:S(2)}, u32[]{:S(2)}) collective-permute-start(bf16[128,384]{1,0:T(8,128)(2,1)} %key_hbm.1), channel_id=1, source_target_pairs={{0,16},{2,18},{4,20},{6,22},{8,24},{10,26},{12,28},{14,30},{16,0},... | collective-permute-start | bytes 294920 | tf_op jit(solution)/shard_map/ppermute | solution.py:282
  4.0 0.0 collective-permute-start.6
  4.1 1.8 %shard_map.82 = (bf16[256,384]{1,0:T(8,128)(2,1)}, f32[8,128]{1,0:T(8,128)}) custom-call(bf16[128,384]{1,0:T(8,128)(2,1)} %query_ref.1, bf16[128,384]{1,0:T(8,128)(2,1)} %key_hbm.1, bf16[128,384]{1,0:T(8,128)(2,1)} %value_hbm.1), custom_call_target="tpu_custom_call" | custom-call | tf_op jit(solution)/shard_map/pallas_call | solution.py:313
  5.9 1.9 %collective-permute-start.1 = (bf16[256,384]{1,0:T(8,128)(2,1)}, bf16[256,384]{1,0:T(8,128)(2,1)S(1)}, u32[]{:S(2)}, u32[]{:S(2)}) collective-permute-start(bf16[256,384]{1,0:T(8,128)(2,1)} %get-tuple-element.16.refs_0_), channel_id=1, source_target_pairs={{0,4},{2,6},{4,0},{6,2},{8,12},{10,14},{12,8},{14,10},{16,20},{18,... | collective-permute-start | bytes 589832 | tf_op jit(solution)/shard_map/ppermute | solution.py:282
  7.8 4.3 %collective-permute-done.refs_0_.key_ref = bf16[128,384]{1,0:T(8,128)(2,1)S(1)} collective-permute-done((bf16[128,384]{1,0:T(8,128)(2,1)}, bf16[128,384]{1,0:T(8,128)(2,1)S(1)}, u32[]{:S(2)}, u32[]{:S(2)}) %collective-permute-start) | collective-permute-done | bytes 98336 | tf_op jit(solution)/shard_map/ppermute | solution.py:282
  12.1 0.0 copy-start.5
  12.1 0.7 %copy-done.5 = f32[8,128]{1,0:T(8,128)S(1)} copy-done((f32[8,128]{1,0:T(8,128)S(1)}, f32[8,128]{1,0:T(8,128)}, u32[]{:S(2)}) %copy-start.5) | copy-done | bytes 4120
  12.8 0.1 shard_map.83.before_ref
  12.9 0.0 copy-start.6
  12.9 0.0 copy-start
  12.9 0.0 collective-permute-done.1.refs_0_.refs_1_
  12.9 0.1 shard_map.84.own_ref
  13.0 0.0 copy-start.7
  13.0 1.8 %collective-permute-start.2 = (f32[8,128]{1,0:T(8,128)S(1)}, f32[8,128]{1,0:T(8,128)S(1)}, u32[]{:S(2)}, u32[]{:S(2)}) collective-permute-start(f32[8,128]{1,0:T(8,128)S(1)} %shard_map.84.own_ref), channel_id=1, source_target_pairs={{0,1},{1,0},{2,3},{3,2},{4,5},{5,4},{6,7},{7,6},{8,9},{9,8},{10,11... | collective-permute-start | bytes 12296 | tf_op jit(solution)/shard_map/ppermute | solution.py:348
  14.8 0.0 copy-done.6
  14.8 0.0 copy-done.7
  14.9 1.6 %collective-permute-start.5 = (bf16[128,384]{1,0:T(8,128)(2,1)S(1)}, bf16[128,384]{1,0:T(8,128)(2,1)S(1)}, u32[]{:S(2)}, u32[]{:S(2)}) collective-permute-start(bf16[128,384]{1,0:T(8,128)(2,1)S(1)} %collective-permute-done.refs_0_.key_ref), channel_id=1, source_target_pairs={{0,4},{2,6},{4,0},{6,2},{8,12},{10,14},{12,8},{14,10},{16,20},{18,... | collective-permute-start | bytes 294920 | tf_op jit(solution)/shard_map/ppermute | solution.py:282
  16.4 0.0 collective-permute-done.6.value_ref
  16.4 0.5 %collective-permute-start.7 = (bf16[128,384]{1,0:T(8,128)(2,1)S(1)}, bf16[128,384]{1,0:T(8,128)(2,1)S(1)}, u32[]{:S(2)}, u32[]{:S(2)}) collective-permute-start(bf16[128,384]{1,0:T(8,128)(2,1)S(1)} %collective-permute-done.6.value_ref), channel_id=1, source_target_pairs={{0,4},{2,6},{4,0},{6,2},{8,12},{10,14},{12,8},{14,10},{16,20},{18,... | collective-permute-start | bytes 294920 | tf_op jit(solution)/shard_map/ppermute | solution.py:282
  17.0 1.5 %collective-permute-start.4 = (f32[8,128]{1,0:T(8,128)S(1)}, f32[8,128]{1,0:T(8,128)S(1)}, u32[]{:S(2)}, u32[]{:S(2)}) collective-permute-start(f32[8,128]{1,0:T(8,128)S(1)} %shard_map.84.own_ref), channel_id=1, source_target_pairs={{0,5},{1,4},{2,7},{3,6},{4,1},{5,0},{6,3},{7,2},{8,13},{9,12},{10,... | collective-permute-start | bytes 12296 | tf_op jit(solution)/shard_map/ppermute | solution.py:352
  18.4 0.0 collective-permute-done.2.other_ref
  18.4 0.0 copy-done
  18.4 0.0 copy-done.2
  18.4 0.1 shard_map.85.own_ref.query_ref
  18.5 1.1 %collective-permute-start.3 = (bf16[144,384]{1,0:T(8,128)(2,1)S(1)}, bf16[144,384]{1,0:T(8,128)(2,1)S(1)}, u32[]{:S(2)}, u32[]{:S(2)}) collective-permute-start(bf16[144,384]{1,0:T(8,128)(2,1)S(1)} %shard_map.85.own_ref.query_ref), channel_id=1, source_target_pairs={{0,8},{2,10},{4,12},{6,14},{8,0},{10,2},{12,4},{14,6},{16,24},{18,... | collective-permute-start | bytes 331784 | tf_op jit(solution)/shard_map/ppermute | solution.py:282
  19.6 0.0 copy-done.4
  19.6 0.2 shard_map.87.pack_ref
  19.8 0.1 collective-permute-start.9
  19.9 3.5 %collective-permute-done.3.remote_ref.query_ref = bf16[144,384]{1,0:T(8,128)(2,1)S(1)} collective-permute-done((bf16[144,384]{1,0:T(8,128)(2,1)S(1)}, bf16[144,384]{1,0:T(8,128)(2,1)S(1)}, u32[]{:S(2)}, u32[]{:S(2)}) %collective-permute-start.3) | collective-permute-done | bytes 110624 | tf_op jit(solution)/shard_map/ppermute | solution.py:282
  23.4 0.1 shard_map.86.bias_ref
  23.5 0.6 %shard_map.88 = (f32[256,384]{1,0:T(8,128)S(1)}, f32[256,768]{1,0:T(8,128)S(1)}) custom-call(bf16[144,384]{1,0:T(8,128)(2,1)S(1)} %shard_map.85.own_ref.query_ref, bf16[144,384]{1,0:T(8,128)(2,1)S(1)} %collective-permute-done.3.remote_ref.query_ref, f32[16,1024]{1,0:T(8,128)S(1)} %shard_map.86.bias_ref, bf16[768,384]{1,0:T(8,128)(2,1)S(1)} %shard_map.87.pack_ref), custom_call_target="tpu_custom_call" | custom-call | tf_op jit(solution)/shard_map/pallas_call | solution.py:394
  24.0 0.0 collective-permute-done.5.refs_0_
  24.1 0.0 collective-permute-done.7.refs_1_
  24.1 0.0 collective-permute-done.4.cross_ref
  24.1 0.2 shard_map.89.pack_ref
  24.3 0.1 collective-permute-start.8
  24.4 0.0 collective-permute-done.9.pack_ref
  24.4 0.7 %shard_map.90 = (f32[256,384]{1,0:T(8,128)S(1)}, f32[256,768]{1,0:T(8,128)S(1)}) custom-call(bf16[144,384]{1,0:T(8,128)(2,1)S(1)} %shard_map.85.own_ref.query_ref, bf16[144,384]{1,0:T(8,128)(2,1)S(1)} %collective-permute-done.3.remote_ref.query_ref, f32[16,1024]{1,0:T(8,128)S(1)} %shard_map.86.bias_ref, ...), custom_call_target="tpu_custom_call" | custom-call | tf_op jit(solution)/shard_map/pallas_call | solution.py:394
  25.1 0.5 %shard_map.91 = (f32[256,384]{1,0:T(8,128)S(1)}, f32[256,768]{1,0:T(8,128)S(1)}) custom-call(bf16[144,384]{1,0:T(8,128)(2,1)S(1)} %shard_map.85.own_ref.query_ref, bf16[144,384]{1,0:T(8,128)(2,1)S(1)} %collective-permute-done.3.remote_ref.query_ref, f32[16,1024]{1,0:T(8,128)S(1)} %shard_map.86.bias_ref, bf16[256,384]{1,0:T(8,128)(2,1)S(1)} %shard_map.89.pack_ref, ...), custom_call_target="tpu_custom_call" | custom-call | tf_op jit(solution)/shard_map/pallas_call | solution.py:394
  25.5 0.3 collective-permute-done.8.pack_ref
  25.8 0.5 %shard_map.93 = bf16[144,384]{1,0:T(8,128)(2,1)S(1)} custom-call(bf16[144,384]{1,0:T(8,128)(2,1)S(1)} %collective-permute-done.3.remote_ref.query_ref, f32[16,1024]{1,0:T(8,128)S(1)} %shard_map.86.bias_ref, bf16[256,384]{1,0:T(8,128)(2,1)S(1)} %collective-permute-done.8.pack_ref, f32[256,384]{1,0:T(8,128)S(1)} %get-tuple-element.21.context_ref, ...), custom_call_target="tpu_custom_call" | custom-call | tf_op jit(solution)/shard_map/pallas_call | solution.py:420
  26.3 1.1 %collective-permute-start.10 = (bf16[144,384]{1,0:T(8,128)(2,1)S(1)}, bf16[144,384]{1,0:T(8,128)(2,1)S(1)}, u32[]{:S(2)}, u32[]{:S(2)}) collective-permute-start(bf16[144,384]{1,0:T(8,128)(2,1)S(1)} %shard_map.93), channel_id=1, source_target_pairs={{0,8},{2,10},{4,12},{6,14},{8,0},{10,2},{12,4},{14,6},{16,24},{18,... | collective-permute-start | bytes 331784 | tf_op jit(solution)/shard_map/ppermute | solution.py:282
  27.3 0.0 copy-done.1
  27.3 0.0 copy-done.3
  27.4 0.6 %shard_map.94.gate_ref = f32[16,384]{1,0:T(8,128)S(1)} custom-call(s32[2]{0:T(128)S(1)} %copy-done.3, f32[50,384]{1,0:T(8,128)S(1)} %copy-done.1), custom_call_target="tpu_custom_call" | custom-call | tf_op jit(solution)/shard_map/pallas_call | solution.py:436
  27.9 0.4 %shard_map.92 = (f32[128,384]{1,0:T(8,128)S(1)}, f32[16,384]{1,0:T(8,128)S(1)}) custom-call(bf16[144,384]{1,0:T(8,128)(2,1)S(1)} %shard_map.85.own_ref.query_ref, f32[16,1024]{1,0:T(8,128)S(1)} %shard_map.86.bias_ref, bf16[256,384]{1,0:T(8,128)(2,1)S(1)} %collective-permute-done.8.pack_ref, f32[256,384]{1,0:T(8,128)S(1)} %get-tuple-element.21.context_ref, ...), custom_call_target="tpu_custom_call" | custom-call | tf_op jit(solution)/shard_map/pallas_call | solution.py:420
  28.4 3.2 %collective-permute-done.10.packet_ref = bf16[144,384]{1,0:T(8,128)(2,1)S(1)} collective-permute-done((bf16[144,384]{1,0:T(8,128)(2,1)S(1)}, bf16[144,384]{1,0:T(8,128)(2,1)S(1)}, u32[]{:S(2)}, u32[]{:S(2)}) %collective-permute-start.10) | collective-permute-done | bytes 110624 | tf_op jit(solution)/shard_map/ppermute | solution.py:282
  31.6 0.8 %shard_map.95 = bf16[128,384]{1,0:T(8,128)(2,1)} custom-call(f32[128,384]{1,0:T(8,128)S(1)} %get-tuple-element.23.own_ref, f32[16,384]{1,0:T(8,128)S(1)} %get-tuple-element.24.lines_ref, bf16[144,384]{1,0:T(8,128)(2,1)S(1)} %collective-permute-done.10.packet_ref, f32[16,384]{1,0:T(8,128)S(1)} %shard_map.94.gate_ref), custom_call_target="tpu_custom_call" | custom-call | tf_op jit(solution)/shard_map/pallas_call | solution.py:445
  (6 shorter events, 0.0 us)
Async XLA Ops:
  0.0 12.1 %collective-permute-start = (bf16[128,384]{1,0:T(8,128)(2,1)}, bf16[128,384]{1,0:T(8,128)(2,1)S(1)}, u32[]{:S(2)}, u32[]{:S(2)}) collective-permute-start(bf16[128,384]{1,0:T(8,128)(2,1)} %key_hbm.1), channel_id=1, source_target_pairs={{0,16},{2,18},{4,20},{6,22},{8,24},{10,26},{12,28},{14,30},{16,0},... | collective-permute-start | bytes 294920 | tf_op jit(solution)/shard_map/ppermute | solution.py:282
  4.0 12.4 %collective-permute-start.6 = (bf16[128,384]{1,0:T(8,128)(2,1)}, bf16[128,384]{1,0:T(8,128)(2,1)S(1)}, u32[]{:S(2)}, u32[]{:S(2)}) collective-permute-start(bf16[128,384]{1,0:T(8,128)(2,1)} %value_hbm.1), channel_id=1, source_target_pairs={{0,16},{2,18},{4,20},{6,22},{8,24},{10,26},{12,28},{14,30},{16,0},... | collective-permute-start | bytes 294920 | tf_op jit(solution)/shard_map/ppermute | solution.py:282
  5.9 7.0 %collective-permute-start.1 = (bf16[256,384]{1,0:T(8,128)(2,1)}, bf16[256,384]{1,0:T(8,128)(2,1)S(1)}, u32[]{:S(2)}, u32[]{:S(2)}) collective-permute-start(bf16[256,384]{1,0:T(8,128)(2,1)} %get-tuple-element.16.refs_0_), channel_id=1, source_target_pairs={{0,4},{2,6},{4,0},{6,2},{8,12},{10,14},{12,8},{14,10},{16,20},{18,... | collective-permute-start | bytes 589832 | tf_op jit(solution)/shard_map/ppermute | solution.py:282
  12.1 0.7 %copy-start.5 = (f32[8,128]{1,0:T(8,128)S(1)}, f32[8,128]{1,0:T(8,128)}, u32[]{:S(2)}) copy-start(f32[8,128]{1,0:T(8,128)} %get-tuple-element.15.before_ref) | copy-start | bytes 12292
  12.8 6.9 %copy-start.4 = (bf16[256,384]{1,0:T(8,128)(2,1)S(1)}, bf16[256,384]{1,0:T(8,128)(2,1)}, u32[]{:S(2)}) copy-start(bf16[256,384]{1,0:T(8,128)(2,1)} %get-tuple-element.16.refs_0_) | copy-start | bytes 589828
  12.9 2.0 %copy-start.6 = (f32[384]{0:T(512)S(1)}, f32[384]{0:T(512)}, u32[]{:S(2)}) copy-start(f32[384]{0:T(512)} %param.11) | copy-start | bytes 4612
  12.9 5.5 %copy-start = (bf16[128,384]{1,0:T(8,128)(2,1)S(1)}, bf16[128,384]{1,0:T(8,128)(2,1)}, u32[]{:S(2)}) copy-start(bf16[128,384]{1,0:T(8,128)(2,1)} %query_ref.1) | copy-start | bytes 294916
  13.0 1.8 %copy-start.7 = (f32[384]{0:T(512)S(1)}, f32[384]{0:T(512)}, u32[]{:S(2)}) copy-start(f32[384]{0:T(512)} %param.12) | copy-start | bytes 4612
  13.0 5.4 %collective-permute-start.2 = (f32[8,128]{1,0:T(8,128)S(1)}, f32[8,128]{1,0:T(8,128)S(1)}, u32[]{:S(2)}, u32[]{:S(2)}) collective-permute-start(f32[8,128]{1,0:T(8,128)S(1)} %shard_map.84.own_ref), channel_id=1, source_target_pairs={{0,1},{1,0},{2,3},{3,2},{4,5},{5,4},{6,7},{7,6},{8,9},{9,8},{10,11... | collective-permute-start | bytes 12296 | tf_op jit(solution)/shard_map/ppermute | solution.py:348
  14.8 3.6 %copy-start.2 = (s32[1,16]{1,0:T(1,128)S(1)}, s32[1,16]{1,0:T(1,128)}, u32[]{:S(2)}) copy-start(s32[1,16]{1,0:T(1,128)} %far_ref.1) | copy-start | bytes 196
  14.9 9.2 %collective-permute-start.5 = (bf16[128,384]{1,0:T(8,128)(2,1)S(1)}, bf16[128,384]{1,0:T(8,128)(2,1)S(1)}, u32[]{:S(2)}, u32[]{:S(2)}) collective-permute-start(bf16[128,384]{1,0:T(8,128)(2,1)S(1)} %collective-permute-done.refs_0_.key_ref), channel_id=1, source_target_pairs={{0,4},{2,6},{4,0},{6,2},{8,12},{10,14},{12,8},{14,10},{16,20},{18,... | collective-permute-start | bytes 294920 | tf_op jit(solution)/shard_map/ppermute | solution.py:282
  16.4 7.6 %collective-permute-start.7 = (bf16[128,384]{1,0:T(8,128)(2,1)S(1)}, bf16[128,384]{1,0:T(8,128)(2,1)S(1)}, u32[]{:S(2)}, u32[]{:S(2)}) collective-permute-start(bf16[128,384]{1,0:T(8,128)(2,1)S(1)} %collective-permute-done.6.value_ref), channel_id=1, source_target_pairs={{0,4},{2,6},{4,0},{6,2},{8,12},{10,14},{12,8},{14,10},{16,20},{18,... | collective-permute-start | bytes 294920 | tf_op jit(solution)/shard_map/ppermute | solution.py:282
  17.0 7.1 %collective-permute-start.4 = (f32[8,128]{1,0:T(8,128)S(1)}, f32[8,128]{1,0:T(8,128)S(1)}, u32[]{:S(2)}, u32[]{:S(2)}) collective-permute-start(f32[8,128]{1,0:T(8,128)S(1)} %shard_map.84.own_ref), channel_id=1, source_target_pairs={{0,5},{1,4},{2,7},{3,6},{4,1},{5,0},{6,3},{7,2},{8,13},{9,12},{10,... | collective-permute-start | bytes 12296 | tf_op jit(solution)/shard_map/ppermute | solution.py:352
  18.5 4.8 %collective-permute-start.3 = (bf16[144,384]{1,0:T(8,128)(2,1)S(1)}, bf16[144,384]{1,0:T(8,128)(2,1)S(1)}, u32[]{:S(2)}, u32[]{:S(2)}) collective-permute-start(bf16[144,384]{1,0:T(8,128)(2,1)S(1)} %shard_map.85.own_ref.query_ref), channel_id=1, source_target_pairs={{0,8},{2,10},{4,12},{6,14},{8,0},{10,2},{12,4},{14,6},{16,24},{18,... | collective-permute-start | bytes 331784 | tf_op jit(solution)/shard_map/ppermute | solution.py:282
  19.8 4.6 %collective-permute-start.9 = (bf16[768,384]{1,0:T(8,128)(2,1)S(1)}, bf16[768,384]{1,0:T(8,128)(2,1)S(1)}, u32[]{:S(2)}, u32[]{:S(2)}) collective-permute-start(bf16[768,384]{1,0:T(8,128)(2,1)S(1)} %shard_map.87.pack_ref), channel_id=1, source_target_pairs={{0,2},{2,0},{4,6},{6,4},{8,10},{10,8},{12,14},{14,12},{16,18},{18,... | collective-permute-start | bytes 1769480 | tf_op jit(solution)/shard_map/ppermute | solution.py:282
  24.3 1.5 %collective-permute-start.8 = (bf16[256,384]{1,0:T(8,128)(2,1)S(1)}, bf16[256,384]{1,0:T(8,128)(2,1)S(1)}, u32[]{:S(2)}, u32[]{:S(2)}) collective-permute-start(bf16[256,384]{1,0:T(8,128)(2,1)S(1)} %shard_map.89.pack_ref), channel_id=1, source_target_pairs={{0,2},{2,0},{4,6},{6,4},{8,10},{10,8},{12,14},{14,12},{16,18},{18,... | collective-permute-start | bytes 589832 | tf_op jit(solution)/shard_map/ppermute | solution.py:282
  25.8 1.5 %copy-start.1 = (f32[50,384]{1,0:T(8,128)S(1)}, f32[50,384]{1,0:T(8,128)}, u32[]{:S(2)}) copy-start(f32[50,384]{1,0:T(8,128)} %table_ref.1) | copy-start | bytes 230404
  25.8 1.5 %copy-start.3 = (s32[2]{0:T(128)S(1)}, s32[2]{0:T(128)}, u32[]{:S(2)}) copy-start(s32[2]{0:T(128)} %step_ref.1) | copy-start | bytes 28
  26.3 5.3 %collective-permute-start.10 = (bf16[144,384]{1,0:T(8,128)(2,1)S(1)}, bf16[144,384]{1,0:T(8,128)(2,1)S(1)}, u32[]{:S(2)}, u32[]{:S(2)}) collective-permute-start(bf16[144,384]{1,0:T(8,128)(2,1)S(1)} %shard_map.93), channel_id=1, source_target_pairs={{0,8},{2,10},{4,12},{6,14},{8,0},{10,2},{12,4},{14,6},{16,24},{18,... | collective-permute-start | bytes 331784 | tf_op jit(solution)/shard_map/ppermute | solution.py:282

commit v15 on v13

--- a/solution.py
+++ b/solution.py
@@ -15,7 +15,7 @@
 SCALE = HD ** (-0.5) * LOG2E
 MASKED = -1e30
 EXTRA = 16
-AHEAD = 4 * 10**9
+UNIT = 10**9
 ANY = pl.BlockSpec(memory_space=pl.ANY)
 VMEM = pl.BlockSpec(memory_space=pltpu.VMEM)
 SMEM = pl.BlockSpec(memory_space=pltpu.SMEM)
@@ -60,11 +60,17 @@
     copies[1].wait()
 
 
-def sums_kernel(lines, before_ref, *refs):
+def relay_kernel(own_ref, cross_ref, out_ref):
+    out_ref[...] = jnp.zeros_like(out_ref)
+    out_ref[0:1, :] = own_ref[1:2, :]
+    out_ref[1:2, :] = cross_ref[1:2, :]
+
+
+def squares_kernel(*refs):
     *sources, out_ref = refs
-    out_ref[...] = before_ref[...]
-    for line, source_ref in zip(lines, sources):
-        out_ref[line : line + 1, :] = squares(source_ref)
+    out_ref[...] = jnp.zeros_like(out_ref)
+    for place, source_ref in enumerate(sources):
+        out_ref[place : place + 1, :] = squares(source_ref)
 
 
 def factor_of(line, full_width):
@@ -79,15 +85,14 @@
     return jnp.concatenate(parts, axis=1)
 
 
-def query_kernel(full_width, key_masks, gain_ref, own_ref, other_ref, *refs):
-    queries, (query_out, bias_out) = refs[:2], refs[2:]
+def query_kernel(full_width, key_masks, rows, gain_ref, *refs):
+    queries, others, (query_out, bias_out) = refs[:2], refs[2:4], refs[4:]
     me = lax.axis_index("tm")
     query_mask = lax.axis_size("tm") // 4
     lane = lax.broadcasted_iota(jnp.int32, (1, HD), 1)
     half = (lane >= BLK).astype(jnp.float32)
     for place, query_ref in enumerate(queries):
-        line = 2 * place
-        total = own_ref[line : line + 1, :] + other_ref[line : line + 1, :]
+        total = squares(query_ref) + others[place][rows[place] : rows[place] + 1, :]
         query_out[place * HD : (place + 1) * HD, :] = normed(
             query_ref, factor_of(total, full_width), gain_ref
         )
@@ -102,33 +107,16 @@
             )
 
 
-def early_kernel(full_width, gain_ref, own_ref, other_ref, key_ref, value_ref, *refs):
-    *pairs, pack_out = refs
-    held = 1 + len(pairs)
-    sources = [(pairs[0], pairs[0]), (key_ref, value_ref)] + [(pair, pair) for pair in pairs[1:]]
-    for place, (key, value) in enumerate(sources):
-        line = 1 + place + (place > 0)
-        total = own_ref[line : line + 1, :] + other_ref[line : line + 1, :]
+def pack_kernel(full_width, held, rows, gain_ref, *refs):
+    keys, values, others = refs[:held], refs[held : 2 * held], refs[2 * held : 3 * held]
+    pack_out = refs[-1]
+    for place, (key, value) in enumerate(zip(keys, values)):
+        total = squares(key) + others[place][rows[place] : rows[place] + 1, :]
         pack_out[place * HD : (place + 1) * HD, :] = normed(
             key, factor_of(total, full_width), gain_ref
         )
-        low = 0 if value is value_ref else HD
+        low = value.shape[0] - HD
         pack_out[(held + place) * HD : (held + place + 1) * HD, :] = value[low : low + HD, :]
-
-
-def late_kernel(full_width, lines, gain_ref, own_ref, other_ref, cross_ref, *refs):
-    *pairs, _, pack_out = refs
-    held = len(pairs) // 2
-    for place, (key, value) in enumerate(zip(pairs[:held], pairs[held:])):
-        if lines is None:
-            total = squares(key) + cross_ref[3:4, :]
-        else:
-            line = lines[place]
-            total = own_ref[line : line + 1, :] + other_ref[line : line + 1, :]
-        pack_out[place * HD : (place + 1) * HD, :] = normed(
-            key, factor_of(total, full_width), gain_ref
-        )
-        pack_out[(held + place) * HD : (held + place + 1) * HD, :] = value[...]
 
 
 def absorb(queries, pack_ref, biases, olds):
@@ -311,14 +299,12 @@
     query_gain = query_gain.reshape(1, width)
     key_gain = key_gain.reshape(1, width)
 
-    lines = 2 + 2 ** len(bits)
-    lines += -lines % 8
     query_packet, own_pair, own_sums = pl.pallas_call(
         own_kernel,
         out_shape=[
             jax.ShapeDtypeStruct((rows + EXTRA, width), jnp.bfloat16),
             jax.ShapeDtypeStruct((2 * rows, width), jnp.bfloat16),
-            jax.ShapeDtypeStruct((lines, rows), jnp.float32),
+            jax.ShapeDtypeStruct((8, rows), jnp.float32),
         ],
         in_specs=[ANY] * 4,
         out_specs=[VMEM] * 3,
@@ -335,37 +321,49 @@
     queries = [query_packet, exchange(query_packet, query_mask)]
     early = [0, far] + sorted(mask for mask in pairs if mask)
     late = sorted(mask ^ far for mask in late_keys if mask)
-    late_lines = range(2 + len(early), 2 + len(early) + len(late))
-
-    def summed(sums, sources, held, flops=0):
-        return pl.pallas_call(
-            functools.partial(sums_kernel, held),
-            out_shape=jax.ShapeDtypeStruct(own_sums.shape, jnp.float32),
-            in_specs=[VMEM] * (1 + len(sources)),
+    if splits == 2:
+        flipped = [query_mask, bits[1]]
+        others = lax.ppermute(own_sums, "head", [(0, 1), (1, 0)])
+        across = []
+        for mask in flipped:
+            flips = []
+            for i in range(2 * count):
+                flips.append((i, ((i // 2) ^ mask) * 2 + (i % 2 ^ 1)))
+            across.append(lax.ppermute(own_sums, ("tm", "head"), flips))
+        relay = pl.pallas_call(
+            relay_kernel,
+            out_shape=jax.ShapeDtypeStruct((8, rows), jnp.float32),
+            in_specs=[VMEM] * 2,
             out_specs=VMEM,
             compiler_params=params,
-            cost_estimate=cost(flops),
-        )(sums, *sources)
-
-    sums = summed(own_sums, [far_key], [3], 2 * AHEAD)
-    sources = [queries[1]] + [pairs[mask] for mask in early[2:]]
-    sums = summed(sums, sources, [2, *range(4, 3 + len(sources))])
-    if splits == 2:
-        others = lax.ppermute(sums, "head", [(0, 1), (1, 0)])
-        flips = []
-        for i in range(2 * count):
-            flips.append((i, ((i // 2) ^ bits[1]) * 2 + (i % 2 ^ 1)))
-        crossed = lax.ppermute(sums, ("tm", "head"), flips)
-        late_lines = None
+            cost_estimate=cost(UNIT),
+        )(others, across[1])
+        relayed = exchange(relay, far)
+        query_others = [(others, 0), (across[0], 0)]
+        early_others = [(others, 1), (relayed, 0), (across[1], 1)]
+        late_others = [(relayed, 1)]
     else:
-        sums = summed(sums, [late_keys[mask ^ far] for mask in late], late_lines)
-        sums = lax.psum(sums, "head")
-        others = crossed = jnp.zeros_like(sums)
+        sources = queries + [far_key] + [pairs[mask] for mask in early if mask != far]
+        sources += [late_keys[mask ^ far] for mask in late]
+        lines = len(sources) + -len(sources) % 8
+        own_rows = pl.pallas_call(
+            squares_kernel,
+            out_shape=jax.ShapeDtypeStruct((lines, rows), jnp.float32),
+            in_specs=[VMEM] * len(sources),
+            out_specs=VMEM,
+            compiler_params=params,
+        )(*sources)
+        rest = lax.psum(own_rows, "head") - own_rows
+        query_others = [(rest, 0), (rest, 1)]
+        early_others = [(rest, 3), (rest, 2)] + [(rest, 4 + i) for i in range(len(early) - 2)]
+        late_others = [(rest, 2 + len(early) + i) for i in range(len(late))]
 
     early_masks = early + [mask ^ 1 for mask in early]
     all_masks = early_masks + late + [mask ^ 1 for mask in late]
     query_norm, biases = pl.pallas_call(
-        functools.partial(query_kernel, width * splits, all_masks),
+        functools.partial(
+            query_kernel, width * splits, all_masks, [row for _, row in query_others]
+        ),
         out_shape=[
             jax.ShapeDtypeStruct((2 * rows, width), jnp.bfloat16),
             jax.ShapeDtypeStruct((16, len(all_masks) * HD), jnp.float32),
@@ -373,24 +371,36 @@
         in_specs=[VMEM] * 5,
         out_specs=[VMEM] * 2,
         compiler_params=params,
-    )(query_gain, sums, others, *queries)
-
-    def packed(kernel, masks, operands, flops):
+    )(query_gain, *queries, *[rest for rest, _ in query_others])
+
+    def packed(keys, values, other_rows, flops, *after):
+        held = len(keys)
         return pl.pallas_call(
-            kernel,
-            out_shape=jax.ShapeDtypeStruct((2 * len(masks) * rows, width), jnp.bfloat16),
-            in_specs=[VMEM] * (1 + len(operands)),
+            functools.partial(pack_kernel, width * splits, held, [row for _, row in other_rows]),
+            out_shape=jax.ShapeDtypeStruct((2 * held * rows, width), jnp.bfloat16),
+            in_specs=[VMEM] * (1 + 3 * held + len(after)),
             out_specs=VMEM,
             compiler_params=params,
             cost_estimate=cost(flops),
-        )(key_gain, *operands)
-
+        )(key_gain, *keys, *values, *[rest for rest, _ in other_rows], *after)
+
+    far_rows = pl.pallas_call(
+        squares_kernel,
+        out_shape=jax.ShapeDtypeStruct((8, rows), jnp.float32),
+        in_specs=[VMEM],
+        out_specs=VMEM,
+        compiler_params=params,
+        cost_estimate=cost(8 * UNIT),
+    )(far_key)
+    near = [pairs[mask] for mask in early if mask != far]
     early_pack = packed(
-        functools.partial(early_kernel, width * splits),
-        early,
-        [sums, others, far_key, far_value, own_pair] + [pairs[mask] for mask in early[2:]],
-        AHEAD,
+        [near[0], far_key, *near[1:]],
+        [near[0], far_value, *near[1:]],
+        early_others,
+        4 * UNIT,
+        far_rows,
     )
+
     def step(first, pack, *state):
         return pl.pallas_call(
             functools.partial(step_kernel, first),
@@ -405,13 +415,11 @@
 
     state = step(0, early_pack)
     late_pack = packed(
-        functools.partial(late_kernel, width * splits, late_lines),
-        late,
-        [sums, others, crossed]
-        + [late_keys[mask ^ far] for mask in late]
-        + [late_values[mask ^ far] for mask in late]
-        + [state[1]],
-        3 * AHEAD,
+        [late_keys[mask ^ far] for mask in late],
+        [late_values[mask ^ far] for mask in late],
+        late_others,
+        12 * UNIT,
+        state[1],
     )
     state = step(len(early), exchange(early_pack, 1), *state)
     state = step(2 * len(early), late_pack, *state)

time: 31.5 us -> 30.5 us (0.968)
  waiting for transfers between devices: 11.6 us -> 6.03 us
  starting transfers between devices: 12.6 us -> 17.4 us
  local copies, waits for them, and re-layouts: 0.39 us -> 0.03 us
    ppermute x9 -> x10, waiting for transfers between devices: 10.9 us -> 6.02 us  [exchange(): return lax.ppermute(array, 'tm', [(i, i ^ mask) for i in range(count)])]
    ppermute x2 -> x3, starting transfers between devices: 2.82 us -> 5.55 us  [the longest x2 3.97 us: local(): across.append(lax.ppermute(own_sums, ('tm', 'head'), flips))]
    ppermute x9 -> x10, starting transfers between devices: 9.81 us -> 11.8 us  [exchange(): return lax.ppermute(array, 'tm', [(i, i ^ mask) for i in range(count)])]
    ppermute x2 -> x3, waiting for transfers between devices: 0.69 us -> 0.01 us  [the longest x2 0.01 us: local(): across.append(lax.ppermute(own_sums, ('tm', 'head'), flips))]
    unnamed x14, local copies, waits for them, and re-layouts: 0.39 us -> 0.03 us
  transfers between devices with their start and end apart: 11 -> 13, of which waited for: 7 -> 6; matrix products, arithmetic and copies ran while one was open for 0% -> 0% of each run, Pallas kernels for 17% -> 18%
where the time goes in v15:
time: 30.5 us; the launch traced here: 30.3 us
  starting transfers between devices  17.4 us (57%)
  Pallas kernels  6.76 us (22%)
  waiting for transfers between devices  6.03 us (20%)
    ppermute x10, starting transfers between devices, exchange(): return lax.ppermute(array, 'tm', [(i, i ^ mask) for i in range(count)])  11.8 us
    ppermute x10, waiting for transfers between devices, exchange(): return lax.ppermute(array, 'tm', [(i, i ^ mask) for i in range(count)])  6.02 us
    ppermute x2, starting transfers between devices, local(): across.append(lax.ppermute(own_sums, ('tm', 'head'), flips))  3.97 us
    pallas_call x1, Pallas kernels, local(): pl.pallas_call(own_kernel, out_shape=[jax.ShapeDtypeStruct((rows + EXTRA,...  1.91 us
    pallas_call x3, Pallas kernels, step(): pl.pallas_call(functools.partial(step_kernel, first), out_shape=[jax.Shap...  1.68 us
    ppermute x1, starting transfers between devices, local(): others = lax.ppermute(own_sums, 'head', [(0, 1), (1, 0)])  1.58 us
    pallas_call x2, Pallas kernels, last(): pl.pallas_call(functools.partial(last_attention, place), out_shape=out_sh...  0.88 us
    pallas_call x1, Pallas kernels, local(): pl.pallas_call(merge_kernel, out_shape=jax.ShapeDtypeStruct((rows, width)...  0.85 us
  transfers between devices with their start and end apart: 13, of which 6 were waited for; matrix products, arithmetic and copies ran while one was open for 0% of the time, Pallas kernels for 18%

profile of v15, /device:TPU:0, one launch (start us, length us, event | category | flops | bytes accessed | tf_op | source)
XLA Modules:
  0.0 30.3 jit_solution(15716903218182248293)
XLA Ops:
  0.0 0.0 copy-start.4
  0.0 4.0 %collective-permute-start.3 = (bf16[128,384]{1,0:T(8,128)(2,1)}, bf16[128,384]{1,0:T(8,128)(2,1)S(1)}, u32[]{:S(2)}, u32[]{:S(2)}) collective-permute-start(bf16[128,384]{1,0:T(8,128)(2,1)} %key_hbm.1), channel_id=1, source_target_pairs={{0,16},{2,18},{4,20},{6,22},{8,24},{10,26},{12,28},{14,30},{16,0},... | collective-permute-start | bytes 294920 | tf_op jit(solution)/shard_map/ppermute | solution.py:273
  4.0 1.9 %shard_map.82 = (bf16[144,384]{1,0:T(8,128)(2,1)}, bf16[256,384]{1,0:T(8,128)(2,1)}, f32[8,128]{1,0:T(8,128)}) custom-call(bf16[128,384]{1,0:T(8,128)(2,1)} %query_hbm.1, bf16[128,384]{1,0:T(8,128)(2,1)} %key_hbm.1, bf16[128,384]{1,0:T(8,128)(2,1)} %value_hbm.1, s32[1,16]{1,0:T(1,128)} %far_hbm.1), custom_call_target="tpu_custom_call" | custom-call | tf_op jit(solution)/shard_map/pallas_call | solution.py:302
  6.0 0.0 copy-start.6
  6.0 1.6 %collective-permute-start.1 = (f32[8,128]{1,0:T(8,128)}, f32[8,128]{1,0:T(8,128)S(1)}, u32[]{:S(2)}, u32[]{:S(2)}) collective-permute-start(f32[8,128]{1,0:T(8,128)} %get-tuple-element.19), channel_id=1, source_target_pairs={{0,1},{1,0},{2,3},{3,2},{4,5},{5,4},{6,7},{7,6},{8,9},{9,8},{10,11... | collective-permute-start | bytes 12296 | tf_op jit(solution)/shard_map/ppermute | solution.py:326
  7.6 1.4 %collective-permute-start.7 = (f32[8,128]{1,0:T(8,128)}, f32[8,128]{1,0:T(8,128)S(1)}, u32[]{:S(2)}, u32[]{:S(2)}) collective-permute-start(f32[8,128]{1,0:T(8,128)} %get-tuple-element.19), channel_id=1, source_target_pairs={{0,5},{1,4},{2,7},{3,6},{4,1},{5,0},{6,3},{7,2},{8,13},{9,12},{10,... | collective-permute-start | bytes 12296 | tf_op jit(solution)/shard_map/ppermute | solution.py:332
  9.0 0.0 copy-done.4
  9.0 0.3 %collective-permute-start.5 = (bf16[128,384]{1,0:T(8,128)(2,1)S(1)}, bf16[128,384]{1,0:T(8,128)(2,1)S(1)}, u32[]{:S(2)}, u32[]{:S(2)}) collective-permute-start(bf16[128,384]{1,0:T(8,128)(2,1)S(1)} %copy-done.4), channel_id=1, source_target_pairs={{0,16},{2,18},{4,20},{6,22},{8,24},{10,26},{12,28},{14,30},{16,0},... | collective-permute-start | bytes 294920 | tf_op jit(solution)/shard_map/ppermute | solution.py:273
  9.3 2.5 %collective-permute-start.2 = (f32[8,128]{1,0:T(8,128)}, f32[8,128]{1,0:T(8,128)S(1)}, u32[]{:S(2)}, u32[]{:S(2)}) collective-permute-start(f32[8,128]{1,0:T(8,128)} %get-tuple-element.19), channel_id=1, source_target_pairs={{0,9},{1,8},{2,11},{3,10},{4,13},{5,12},{6,15},{7,14},{8,1},{9,0},... | collective-permute-start | bytes 12296 | tf_op jit(solution)/shard_map/ppermute | solution.py:332
  11.9 0.0 copy-done.5
  11.9 0.0 copy-done.6
  11.9 0.0 collective-permute-done.1.refs_2_.own_ref.refs_6_
  11.9 0.6 %collective-permute-start.9 = (bf16[256,384]{1,0:T(8,128)(2,1)}, bf16[256,384]{1,0:T(8,128)(2,1)S(1)}, u32[]{:S(2)}, u32[]{:S(2)}) collective-permute-start(bf16[256,384]{1,0:T(8,128)(2,1)} %get-tuple-element.22.refs_0_.refs_3_), channel_id=1, source_target_pairs={{0,4},{2,6},{4,0},{6,2},{8,12},{10,14},{12,8},{14,10},{16,20},{18,... | collective-permute-start | bytes 589832 | tf_op jit(solution)/shard_map/ppermute | solution.py:273
  12.5 0.0 collective-permute-done.7.cross_ref.refs_8_
  12.5 1.4 %collective-permute-start = (bf16[144,384]{1,0:T(8,128)(2,1)}, bf16[144,384]{1,0:T(8,128)(2,1)S(1)}, u32[]{:S(2)}, u32[]{:S(2)}) collective-permute-start(bf16[144,384]{1,0:T(8,128)(2,1)} %get-tuple-element.18.refs_0_), channel_id=1, source_target_pairs={{0,8},{2,10},{4,12},{6,14},{8,0},{10,2},{12,4},{14,6},{16,24},{18,... | collective-permute-start | bytes 331784 | tf_op jit(solution)/shard_map/ppermute | solution.py:273
  13.9 0.0 collective-permute-done.3.refs_0_.refs_1_
  13.9 1.7 %collective-permute-start.8 = (f32[8,128]{1,0:T(8,128)S(1)}, f32[8,128]{1,0:T(8,128)S(1)}, u32[]{:S(2)}, u32[]{:S(2)}) collective-permute-start(f32[8,128]{1,0:T(8,128)S(1)} %shard_map.84), channel_id=1, source_target_pairs={{0,16},{2,18},{4,20},{6,22},{8,24},{10,26},{12,28},{14,30},{16,0},... | collective-permute-start | bytes 12296 | tf_op jit(solution)/shard_map/ppermute | solution.py:273
  15.6 0.1 shard_map.85.refs_9_
  15.7 0.0 copy-start.3
  15.7 0.0 collective-permute-done.2.refs_3_
  15.7 1.6 %collective-permute-start.4 = (bf16[128,384]{1,0:T(8,128)(2,1)S(1)}, bf16[128,384]{1,0:T(8,128)(2,1)S(1)}, u32[]{:S(2)}, u32[]{:S(2)}) collective-permute-start(bf16[128,384]{1,0:T(8,128)(2,1)S(1)} %collective-permute-done.3.refs_0_.refs_1_), channel_id=1, source_target_pairs={{0,4},{2,6},{4,0},{6,2},{8,12},{10,14},{12,8},{14,10},{16,20},{18,... | collective-permute-start | bytes 294920 | tf_op jit(solution)/shard_map/ppermute | solution.py:273
  17.3 0.0 collective-permute-done.5.refs_4_
  17.3 0.5 %collective-permute-start.6 = (bf16[128,384]{1,0:T(8,128)(2,1)S(1)}, bf16[128,384]{1,0:T(8,128)(2,1)S(1)}, u32[]{:S(2)}, u32[]{:S(2)}) collective-permute-start(bf16[128,384]{1,0:T(8,128)(2,1)S(1)} %collective-permute-done.5.refs_4_), channel_id=1, source_target_pairs={{0,4},{2,6},{4,0},{6,2},{8,12},{10,14},{12,8},{14,10},{16,20},{18,... | collective-permute-start | bytes 294920 | tf_op jit(solution)/shard_map/ppermute | solution.py:273
  17.8 0.0 collective-permute-done.refs_1_
  17.8 0.0 copy-done
  17.8 0.3 shard_map.83
  18.1 0.4 %collective-permute-done.8.refs_7_.refs_2_ = f32[8,128]{1,0:T(8,128)S(1)} collective-permute-done((f32[8,128]{1,0:T(8,128)S(1)}, f32[8,128]{1,0:T(8,128)S(1)}, u32[]{:S(2)}, u32[]{:S(2)}) %collective-permute-start.8) | collective-permute-done | bytes 4128 | tf_op jit(solution)/shard_map/ppermute | solution.py:273
  18.5 1.2 %collective-permute-done.9.refs_2_.refs_5_ = bf16[256,384]{1,0:T(8,128)(2,1)S(1)} collective-permute-done((bf16[256,384]{1,0:T(8,128)(2,1)}, bf16[256,384]{1,0:T(8,128)(2,1)S(1)}, u32[]{:S(2)}, u32[]{:S(2)}) %collective-permute-start.9) | collective-permute-done | bytes 196640 | tf_op jit(solution)/shard_map/ppermute | solution.py:273
  19.7 0.0 copy-done.3
  19.7 0.3 shard_map.86.pack_ref
  20.0 0.1 collective-permute-start.11
  20.0 0.6 %shard_map.87 = (f32[256,384]{1,0:T(8,128)S(1)}, f32[256,768]{1,0:T(8,128)S(1)}) custom-call(bf16[256,384]{1,0:T(8,128)(2,1)S(1)} %get-tuple-element.20.query_ref, f32[16,1024]{1,0:T(8,128)S(1)} %get-tuple-element.21.bias_ref, bf16[768,384]{1,0:T(8,128)(2,1)S(1)} %shard_map.86.pack_ref), custom_call_target="tpu_custom_call" | custom-call | tf_op jit(solution)/shard_map/pallas_call | solution.py:405
  20.6 0.4 %collective-permute-done.4.refs_0_ = bf16[128,384]{1,0:T(8,128)(2,1)S(1)} collective-permute-done((bf16[128,384]{1,0:T(8,128)(2,1)S(1)}, bf16[128,384]{1,0:T(8,128)(2,1)S(1)}, u32[]{:S(2)}, u32[]{:S(2)}) %collective-permute-start.4) | collective-permute-done | bytes 98336 | tf_op jit(solution)/shard_map/ppermute | solution.py:273
  21.0 1.1 %collective-permute-done.6.refs_1_ = bf16[128,384]{1,0:T(8,128)(2,1)S(1)} collective-permute-done((bf16[128,384]{1,0:T(8,128)(2,1)S(1)}, bf16[128,384]{1,0:T(8,128)(2,1)S(1)}, u32[]{:S(2)}, u32[]{:S(2)}) %collective-permute-start.6) | collective-permute-done | bytes 98336 | tf_op jit(solution)/shard_map/ppermute | solution.py:273
  22.0 0.2 shard_map.88.pack_ref
  22.3 0.1 collective-permute-start.10
  22.4 0.0 collective-permute-done.11.pack_ref
  22.4 0.6 %shard_map.89 = (f32[256,384]{1,0:T(8,128)S(1)}, f32[256,768]{1,0:T(8,128)S(1)}) custom-call(bf16[256,384]{1,0:T(8,128)(2,1)S(1)} %get-tuple-element.20.query_ref, f32[16,1024]{1,0:T(8,128)S(1)} %get-tuple-element.21.bias_ref, bf16[768,384]{1,0:T(8,128)(2,1)S(1)} %collective-permute-done.11.pack_ref, f32[256,384]{1,0:T(8,128)S(1)} %get-tuple-element.24.refs_0_, ...), custom_call_target="tpu_custom_call" | custom-call | tf_op jit(solution)/shard_map/pallas_call | solution.py:405
  23.0 0.5 %shard_map.90 = (f32[256,384]{1,0:T(8,128)S(1)}, f32[256,768]{1,0:T(8,128)S(1)}) custom-call(bf16[256,384]{1,0:T(8,128)(2,1)S(1)} %get-tuple-element.20.query_ref, f32[16,1024]{1,0:T(8,128)S(1)} %get-tuple-element.21.bias_ref, bf16[256,384]{1,0:T(8,128)(2,1)S(1)} %shard_map.88.pack_ref, f32[256,384]{1,0:T(8,128)S(1)} %get-tuple-element.25.refs_0_, ...), custom_call_target="tpu_custom_call" | custom-call | tf_op jit(solution)/shard_map/pallas_call | solution.py:405
  23.5 0.3 collective-permute-done.10.pack_ref
  23.8 0.4 %shard_map.92 = bf16[144,384]{1,0:T(8,128)(2,1)S(1)} custom-call(bf16[256,384]{1,0:T(8,128)(2,1)S(1)} %get-tuple-element.20.query_ref, f32[16,1024]{1,0:T(8,128)S(1)} %get-tuple-element.21.bias_ref, bf16[256,384]{1,0:T(8,128)(2,1)S(1)} %collective-permute-done.10.pack_ref, f32[256,384]{1,0:T(8,128)S(1)} %get-tuple-element.27.context_ref, ...), custom_call_target="tpu_custom_call" | custom-call | tf_op jit(solution)/shard_map/pallas_call | solution.py:429
  24.2 1.5 %collective-permute-start.12 = (bf16[144,384]{1,0:T(8,128)(2,1)S(1)}, bf16[144,384]{1,0:T(8,128)(2,1)S(1)}, u32[]{:S(2)}, u32[]{:S(2)}) collective-permute-start(bf16[144,384]{1,0:T(8,128)(2,1)S(1)} %shard_map.92), channel_id=1, source_target_pairs={{0,8},{2,10},{4,12},{6,14},{8,0},{10,2},{12,4},{14,6},{16,24},{18,... | collective-permute-start | bytes 331784 | tf_op jit(solution)/shard_map/ppermute | solution.py:273
  25.7 0.0 copy-done.1
  25.7 0.0 copy-done.2
  25.7 0.6 %shard_map.93.gate_ref = f32[16,384]{1,0:T(8,128)S(1)} custom-call(s32[2]{0:T(128)S(1)} %copy-done.2, f32[50,384]{1,0:T(8,128)S(1)} %copy-done.1), custom_call_target="tpu_custom_call" | custom-call | tf_op jit(solution)/shard_map/pallas_call | solution.py:445
  26.3 0.4 %shard_map.91 = (f32[128,384]{1,0:T(8,128)S(1)}, f32[16,384]{1,0:T(8,128)S(1)}) custom-call(bf16[256,384]{1,0:T(8,128)(2,1)S(1)} %get-tuple-element.20.query_ref, f32[16,1024]{1,0:T(8,128)S(1)} %get-tuple-element.21.bias_ref, bf16[256,384]{1,0:T(8,128)(2,1)S(1)} %collective-permute-done.10.pack_ref, f32[256,384]{1,0:T(8,128)S(1)} %get-tuple-element.27.context_ref, ...), custom_call_target="tpu_custom_call" | custom-call | tf_op jit(solution)/shard_map/pallas_call | solution.py:429
  26.8 2.7 %collective-permute-done.12.packet_ref = bf16[144,384]{1,0:T(8,128)(2,1)S(1)} collective-permute-done((bf16[144,384]{1,0:T(8,128)(2,1)S(1)}, bf16[144,384]{1,0:T(8,128)(2,1)S(1)}, u32[]{:S(2)}, u32[]{:S(2)}) %collective-permute-start.12) | collective-permute-done | bytes 110624 | tf_op jit(solution)/shard_map/ppermute | solution.py:273
  29.5 0.8 %shard_map.94 = bf16[128,384]{1,0:T(8,128)(2,1)} custom-call(f32[128,384]{1,0:T(8,128)S(1)} %get-tuple-element.29.own_ref, f32[16,384]{1,0:T(8,128)S(1)} %get-tuple-element.30.lines_ref, bf16[144,384]{1,0:T(8,128)(2,1)S(1)} %collective-permute-done.12.packet_ref, f32[16,384]{1,0:T(8,128)S(1)} %shard_map.93.gate_ref), custom_call_target="tpu_custom_call" | custom-call | tf_op jit(solution)/shard_map/pallas_call | solution.py:454
  (7 shorter events, 0.0 us)
Async XLA Ops:
  0.0 9.0 %copy-start.4 = (bf16[128,384]{1,0:T(8,128)(2,1)S(1)}, bf16[128,384]{1,0:T(8,128)(2,1)}, u32[]{:S(2)}) copy-start(bf16[128,384]{1,0:T(8,128)(2,1)} %value_hbm.1) | copy-start | bytes 294916
  0.0 13.9 %collective-permute-start.3 = (bf16[128,384]{1,0:T(8,128)(2,1)}, bf16[128,384]{1,0:T(8,128)(2,1)S(1)}, u32[]{:S(2)}, u32[]{:S(2)}) collective-permute-start(bf16[128,384]{1,0:T(8,128)(2,1)} %key_hbm.1), channel_id=1, source_target_pairs={{0,16},{2,18},{4,20},{6,22},{8,24},{10,26},{12,28},{14,30},{16,0},... | collective-permute-start | bytes 294920 | tf_op jit(solution)/shard_map/ppermute | solution.py:273
  4.0 7.8 %copy-start.5 = (f32[384]{0:T(512)S(1)}, f32[384]{0:T(512)}, u32[]{:S(2)}) copy-start(f32[384]{0:T(512)} %param.12) | copy-start | bytes 4612
  6.0 5.9 %copy-start.6 = (f32[384]{0:T(512)S(1)}, f32[384]{0:T(512)}, u32[]{:S(2)}) copy-start(f32[384]{0:T(512)} %param.11) | copy-start | bytes 4612
  6.0 5.9 %collective-permute-start.1 = (f32[8,128]{1,0:T(8,128)}, f32[8,128]{1,0:T(8,128)S(1)}, u32[]{:S(2)}, u32[]{:S(2)}) collective-permute-start(f32[8,128]{1,0:T(8,128)} %get-tuple-element.19), channel_id=1, source_target_pairs={{0,1},{1,0},{2,3},{3,2},{4,5},{5,4},{6,7},{7,6},{8,9},{9,8},{10,11... | collective-permute-start | bytes 12296 | tf_op jit(solution)/shard_map/ppermute | solution.py:326
  7.6 4.9 %collective-permute-start.7 = (f32[8,128]{1,0:T(8,128)}, f32[8,128]{1,0:T(8,128)S(1)}, u32[]{:S(2)}, u32[]{:S(2)}) collective-permute-start(f32[8,128]{1,0:T(8,128)} %get-tuple-element.19), channel_id=1, source_target_pairs={{0,5},{1,4},{2,7},{3,6},{4,1},{5,0},{6,3},{7,2},{8,13},{9,12},{10,... | collective-permute-start | bytes 12296 | tf_op jit(solution)/shard_map/ppermute | solution.py:332
  9.0 8.3 %collective-permute-start.5 = (bf16[128,384]{1,0:T(8,128)(2,1)S(1)}, bf16[128,384]{1,0:T(8,128)(2,1)S(1)}, u32[]{:S(2)}, u32[]{:S(2)}) collective-permute-start(bf16[128,384]{1,0:T(8,128)(2,1)S(1)} %copy-done.4), channel_id=1, source_target_pairs={{0,16},{2,18},{4,20},{6,22},{8,24},{10,26},{12,28},{14,30},{16,0},... | collective-permute-start | bytes 294920 | tf_op jit(solution)/shard_map/ppermute | solution.py:273
  9.3 6.4 %collective-permute-start.2 = (f32[8,128]{1,0:T(8,128)}, f32[8,128]{1,0:T(8,128)S(1)}, u32[]{:S(2)}, u32[]{:S(2)}) collective-permute-start(f32[8,128]{1,0:T(8,128)} %get-tuple-element.19), channel_id=1, source_target_pairs={{0,9},{1,8},{2,11},{3,10},{4,13},{5,12},{6,15},{7,14},{8,1},{9,0},... | collective-permute-start | bytes 12296 | tf_op jit(solution)/shard_map/ppermute | solution.py:332
  11.9 7.8 %collective-permute-start.9 = (bf16[256,384]{1,0:T(8,128)(2,1)}, bf16[256,384]{1,0:T(8,128)(2,1)S(1)}, u32[]{:S(2)}, u32[]{:S(2)}) collective-permute-start(bf16[256,384]{1,0:T(8,128)(2,1)} %get-tuple-element.22.refs_0_.refs_3_), channel_id=1, source_target_pairs={{0,4},{2,6},{4,0},{6,2},{8,12},{10,14},{12,8},{14,10},{16,20},{18,... | collective-permute-start | bytes 589832 | tf_op jit(solution)/shard_map/ppermute | solution.py:273
  12.5 5.3 %collective-permute-start = (bf16[144,384]{1,0:T(8,128)(2,1)}, bf16[144,384]{1,0:T(8,128)(2,1)S(1)}, u32[]{:S(2)}, u32[]{:S(2)}) collective-permute-start(bf16[144,384]{1,0:T(8,128)(2,1)} %get-tuple-element.18.refs_0_), channel_id=1, source_target_pairs={{0,8},{2,10},{4,12},{6,14},{8,0},{10,2},{12,4},{14,6},{16,24},{18,... | collective-permute-start | bytes 331784 | tf_op jit(solution)/shard_map/ppermute | solution.py:273
  13.9 3.9 %copy-start = (bf16[144,384]{1,0:T(8,128)(2,1)S(1)}, bf16[144,384]{1,0:T(8,128)(2,1)}, u32[]{:S(2)}) copy-start(bf16[144,384]{1,0:T(8,128)(2,1)} %get-tuple-element.18.refs_0_) | copy-start | bytes 331780
  13.9 4.6 %collective-permute-start.8 = (f32[8,128]{1,0:T(8,128)S(1)}, f32[8,128]{1,0:T(8,128)S(1)}, u32[]{:S(2)}, u32[]{:S(2)}) collective-permute-start(f32[8,128]{1,0:T(8,128)S(1)} %shard_map.84), channel_id=1, source_target_pairs={{0,16},{2,18},{4,20},{6,22},{8,24},{10,26},{12,28},{14,30},{16,0},... | collective-permute-start | bytes 12296 | tf_op jit(solution)/shard_map/ppermute | solution.py:273
  15.7 4.0 %copy-start.3 = (bf16[256,384]{1,0:T(8,128)(2,1)S(1)}, bf16[256,384]{1,0:T(8,128)(2,1)}, u32[]{:S(2)}) copy-start(bf16[256,384]{1,0:T(8,128)(2,1)} %get-tuple-element.22.refs_0_.refs_3_) | copy-start | bytes 589828
  15.7 5.3 %collective-permute-start.4 = (bf16[128,384]{1,0:T(8,128)(2,1)S(1)}, bf16[128,384]{1,0:T(8,128)(2,1)S(1)}, u32[]{:S(2)}, u32[]{:S(2)}) collective-permute-start(bf16[128,384]{1,0:T(8,128)(2,1)S(1)} %collective-permute-done.3.refs_0_.refs_1_), channel_id=1, source_target_pairs={{0,4},{2,6},{4,0},{6,2},{8,12},{10,14},{12,8},{14,10},{16,20},{18,... | collective-permute-start | bytes 294920 | tf_op jit(solution)/shard_map/ppermute | solution.py:273
  17.3 4.8 %collective-permute-start.6 = (bf16[128,384]{1,0:T(8,128)(2,1)S(1)}, bf16[128,384]{1,0:T(8,128)(2,1)S(1)}, u32[]{:S(2)}, u32[]{:S(2)}) collective-permute-start(bf16[128,384]{1,0:T(8,128)(2,1)S(1)} %collective-permute-done.5.refs_4_), channel_id=1, source_target_pairs={{0,4},{2,6},{4,0},{6,2},{8,12},{10,14},{12,8},{14,10},{16,20},{18,... | collective-permute-start | bytes 294920 | tf_op jit(solution)/shard_map/ppermute | solution.py:273
  20.0 2.4 %collective-permute-start.11 = (bf16[768,384]{1,0:T(8,128)(2,1)S(1)}, bf16[768,384]{1,0:T(8,128)(2,1)S(1)}, u32[]{:S(2)}, u32[]{:S(2)}) collective-permute-start(bf16[768,384]{1,0:T(8,128)(2,1)S(1)} %shard_map.86.pack_ref), channel_id=1, source_target_pairs={{0,2},{2,0},{4,6},{6,4},{8,10},{10,8},{12,14},{14,12},{16,18},{18,... | collective-permute-start | bytes 1769480 | tf_op jit(solution)/shard_map/ppermute | solution.py:273
  22.3 1.5 %collective-permute-start.10 = (bf16[256,384]{1,0:T(8,128)(2,1)S(1)}, bf16[256,384]{1,0:T(8,128)(2,1)S(1)}, u32[]{:S(2)}, u32[]{:S(2)}) collective-permute-start(bf16[256,384]{1,0:T(8,128)(2,1)S(1)} %shard_map.88.pack_ref), channel_id=1, source_target_pairs={{0,2},{2,0},{4,6},{6,4},{8,10},{10,8},{12,14},{14,12},{16,18},{18,... | collective-permute-start | bytes 589832 | tf_op jit(solution)/shard_map/ppermute | solution.py:273
  23.8 2.0 %copy-start.1 = (f32[50,384]{1,0:T(8,128)S(1)}, f32[50,384]{1,0:T(8,128)}, u32[]{:S(2)}) copy-start(f32[50,384]{1,0:T(8,128)} %table_ref.1) | copy-start | bytes 230404
  23.8 2.0 %copy-start.2 = (s32[2]{0:T(128)S(1)}, s32[2]{0:T(128)}, u32[]{:S(2)}) copy-start(s32[2]{0:T(128)} %step_ref.1) | copy-start | bytes 28
  24.2 5.3 %collective-permute-start.12 = (bf16[144,384]{1,0:T(8,128)(2,1)S(1)}, bf16[144,384]{1,0:T(8,128)(2,1)S(1)}, u32[]{:S(2)}, u32[]{:S(2)}) collective-permute-start(bf16[144,384]{1,0:T(8,128)(2,1)S(1)} %shard_map.92), channel_id=1, source_target_pairs={{0,8},{2,10},{4,12},{6,14},{8,0},{10,2},{12,4},{14,6},{16,24},{18,... | collective-permute-start | bytes 331784 | tf_op jit(solution)/shard_map/ppermute | solution.py:273

commit v16 on v14

--- a/solution.py
+++ b/solution.py
@@ -15,7 +15,7 @@
 SCALE = HD ** (-0.5) * LOG2E
 MASKED = -1e30
 EXTRA = 16
-AHEAD = 4 * 10**9
+UNIT = 10**9
 ANY = pl.BlockSpec(memory_space=pl.ANY)
 VMEM = pl.BlockSpec(memory_space=pltpu.VMEM)
 SMEM = pl.BlockSpec(memory_space=pltpu.SMEM)
@@ -34,28 +34,10 @@
     return jnp.sum(part.T, axis=0, keepdims=True)
 
 
-def own_kernel(query_hbm, key_hbm, value_hbm, pair_out, sums_out, query_ref, sems):
-    rows = query_ref.shape[0]
-    copies = [
-        pltpu.make_async_copy(key_hbm, pair_out.at[:rows, :], sems.at[0]),
-        pltpu.make_async_copy(value_hbm, pair_out.at[rows:, :], sems.at[1]),
-        pltpu.make_async_copy(query_hbm, query_ref, sems.at[2]),
-    ]
-    for copy in copies:
-        copy.start()
-    sums_out[...] = jnp.zeros_like(sums_out)
-    copies[0].wait()
-    sums_out[1:2, :] = squares(pair_out)
-    copies[2].wait()
-    sums_out[0:1, :] = squares(query_ref)
-    copies[1].wait()
-
-
-def sums_kernel(lines, before_ref, *refs):
-    *sources, out_ref = refs
-    out_ref[...] = before_ref[...]
-    for line, source_ref in zip(lines, sources):
-        out_ref[line : line + 1, :] = squares(source_ref)
+def sums_kernel(query_ref, key_ref, out_ref):
+    out_ref[...] = jnp.zeros_like(out_ref)
+    out_ref[0:1, :] = squares(query_ref)
+    out_ref[1:2, :] = squares(key_ref)
 
 
 def factor_of(line, full_width):
@@ -70,13 +52,31 @@
     return jnp.concatenate(parts, axis=1)
 
 
-def query_kernel(full_width, query_ref, far_ref, gain_ref, own_ref, other_ref, out_ref):
+def key_kernel(full_width, key_ref, gain_ref, own_ref, other_ref, out_ref):
+    total = own_ref[1:2, :] + other_ref[1:2, :]
+    out_ref[...] = normed(key_ref, factor_of(total, full_width), gain_ref)
+
+
+def query_kernel(
+    full_width,
+    query_ref,
+    key_ref,
+    value_ref,
+    gain_ref,
+    far_ref,
+    own_ref,
+    other_ref,
+    query_out,
+    pair_out,
+):
+    pair_out[:HD, :] = key_ref[...]
+    pair_out[HD:, :] = value_ref[...]
     total = own_ref[0:1, :] + other_ref[0:1, :]
-    out_ref[:HD, :] = normed(query_ref, factor_of(total, full_width), gain_ref)
+    query_out[:HD, :] = normed(query_ref, factor_of(total, full_width), gain_ref)
     far = far_ref[...].astype(jnp.float32)
     far = jnp.concatenate([far, jnp.full((1, HD - far.shape[1]), -1.0)], axis=1)
-    out_ref[HD:, :HD] = jnp.broadcast_to(far, (EXTRA, HD)).astype(jnp.bfloat16)
-    out_ref[HD:, HD:] = jnp.zeros((EXTRA, out_ref.shape[1] - HD), jnp.bfloat16)
+    query_out[HD:, :HD] = jnp.broadcast_to(far, (EXTRA, HD)).astype(jnp.bfloat16)
+    query_out[HD:, HD:] = jnp.zeros((EXTRA, query_out.shape[1] - HD), jnp.bfloat16)
 
 
 def bias_kernel(key_masks, own_ref, remote_ref, bias_out):
@@ -96,33 +96,17 @@
             )
 
 
-def early_kernel(full_width, gain_ref, own_ref, other_ref, key_ref, value_ref, *refs):
-    *pairs, pack_out = refs
-    held = 1 + len(pairs)
-    sources = [(pairs[0], pairs[0]), (key_ref, value_ref)] + [(pair, pair) for pair in pairs[1:]]
-    for place, (key, value) in enumerate(sources):
-        line = 1 + place + (place > 0)
-        total = own_ref[line : line + 1, :] + other_ref[line : line + 1, :]
-        pack_out[place * HD : (place + 1) * HD, :] = normed(
-            key, factor_of(total, full_width), gain_ref
-        )
-        low = 0 if value is value_ref else HD
-        pack_out[(held + place) * HD : (held + place + 1) * HD, :] = value[low : low + HD, :]
-
-
-def late_kernel(full_width, lines, gain_ref, own_ref, other_ref, cross_ref, *refs):
-    *pairs, _, pack_out = refs
-    held = len(pairs) // 2
-    for place, (key, value) in enumerate(zip(pairs[:held], pairs[held:])):
-        if lines is None:
-            total = squares(key) + cross_ref[3:4, :]
-        else:
-            line = lines[place]
-            total = own_ref[line : line + 1, :] + other_ref[line : line + 1, :]
-        pack_out[place * HD : (place + 1) * HD, :] = normed(
-            key, factor_of(total, full_width), gain_ref
-        )
-        pack_out[(held + place) * HD : (held + place + 1) * HD, :] = value[...]
+def copy_kernel(source_ref, out_ref):
+    out_ref[...] = source_ref[...]
+
+
+def pack_kernel(held, *refs):
+    keys, values, pack_out = refs[:held], refs[held : 2 * held], refs[-1]
+    for place, key_ref in enumerate(keys):
+        pack_out[place * HD : (place + 1) * HD, :] = key_ref[:HD, :]
+    for place, value_ref in enumerate(values, start=held):
+        low = value_ref.shape[0] - HD
+        pack_out[place * HD : (place + 1) * HD, :] = value_ref[low:, :]
 
 
 def absorb(queries, pack_ref, biases, olds):
@@ -308,64 +292,53 @@
     query_gain = query_gain.reshape(1, width)
     key_gain = key_gain.reshape(1, width)
 
-    lines = 2 + 2 ** len(bits)
-    lines += -lines % 8
-    own_pair, own_sums = pl.pallas_call(
-        own_kernel,
+    far = bits[0]
+    far_value = exchange(value_proj, far)
+    sums = pl.pallas_call(
+        sums_kernel,
+        out_shape=jax.ShapeDtypeStruct((8, rows), jnp.float32),
+        in_specs=[VMEM] * 2,
+        out_specs=VMEM,
+        compiler_params=params,
+    )(query_proj, key_proj)
+    if splits == 2:
+        others = lax.ppermute(sums, "head", [(0, 1), (1, 0)])
+    else:
+        sums = lax.psum(sums, "head")
+        others = jnp.zeros_like(sums)
+    own_key = pl.pallas_call(
+        functools.partial(key_kernel, width * splits),
+        out_shape=jax.ShapeDtypeStruct((rows, width), jnp.bfloat16),
+        in_specs=[VMEM] * 4,
+        out_specs=VMEM,
+        compiler_params=params,
+    )(key_proj, key_gain, sums, others)
+    query_packet, own_pair = pl.pallas_call(
+        functools.partial(query_kernel, width * splits),
         out_shape=[
+            jax.ShapeDtypeStruct((rows + EXTRA, width), jnp.bfloat16),
             jax.ShapeDtypeStruct((2 * rows, width), jnp.bfloat16),
-            jax.ShapeDtypeStruct((lines, rows), jnp.float32),
         ],
-        in_specs=[ANY] * 3,
+        in_specs=[VMEM] * 7,
         out_specs=[VMEM] * 2,
-        scratch_shapes=[
-            pltpu.VMEM((rows, width), jnp.bfloat16),
-            pltpu.SemaphoreType.DMA((3,)),
-        ],
-    )(query_proj, key_proj, value_proj)
-    far = bits[0]
-    far_key, far_value = exchange(key_proj, far), exchange(value_proj, far)
+        compiler_params=params,
+    )(query_proj, own_key, value_proj, query_gain, far_blocks, sums, others)
+    far_key = exchange(own_key, far)
     pairs = gathered(own_pair, bits[1:])
+    queries = [query_packet, exchange(query_packet, query_mask)]
+    far_value = pl.pallas_call(
+        copy_kernel,
+        out_shape=jax.ShapeDtypeStruct((rows, width), jnp.bfloat16),
+        in_specs=[VMEM],
+        out_specs=VMEM,
+        compiler_params=params,
+        cost_estimate=cost(4 * UNIT),
+    )(far_value)
     late_keys, late_values = gathered(far_key, bits[1:]), gathered(far_value, bits[1:])
     early = [0, far] + sorted(mask for mask in pairs if mask)
     late = sorted(mask ^ far for mask in late_keys if mask)
-    late_lines = range(2 + len(early), 2 + len(early) + len(late))
-
-    def summed(sums, sources, held, flops=0):
-        return pl.pallas_call(
-            functools.partial(sums_kernel, held),
-            out_shape=jax.ShapeDtypeStruct(own_sums.shape, jnp.float32),
-            in_specs=[VMEM] * (1 + len(sources)),
-            out_specs=VMEM,
-            compiler_params=params,
-            cost_estimate=cost(flops),
-        )(sums, *sources)
-
-    sums = summed(own_sums, [far_key], [3], 2 * AHEAD)
-    sources = [pairs[mask] for mask in early[2:]]
-    sums = summed(sums, sources, range(4, 4 + len(sources)))
-    if splits == 2:
-        others = lax.ppermute(sums, "head", [(0, 1), (1, 0)])
-        flips = []
-        for i in range(2 * count):
-            flips.append((i, ((i // 2) ^ bits[1]) * 2 + (i % 2 ^ 1)))
-        crossed = lax.ppermute(sums, ("tm", "head"), flips)
-        late_lines = None
-    else:
-        sums = summed(sums, [late_keys[mask ^ far] for mask in late], late_lines)
-        sums = lax.psum(sums, "head")
-        others = crossed = jnp.zeros_like(sums)
-
     early_masks = early + [mask ^ 1 for mask in early]
     all_masks = early_masks + late + [mask ^ 1 for mask in late]
-    query_packet = pl.pallas_call(
-        functools.partial(query_kernel, width * splits),
-        out_shape=jax.ShapeDtypeStruct((rows + EXTRA, width), jnp.bfloat16),
-        in_specs=[VMEM] * 5,
-        out_specs=VMEM,
-        compiler_params=params,
-    )(query_proj, far_blocks, query_gain, sums, others)
-    queries = [query_packet, exchange(query_packet, query_mask)]
     biases = pl.pallas_call(
         functools.partial(bias_kernel, all_masks),
         out_shape=jax.ShapeDtypeStruct((16, len(all_masks) * HD), jnp.float32),
@@ -374,22 +347,20 @@
         compiler_params=params,
     )(*queries)
 
-    def packed(kernel, masks, operands, flops):
+    def packed(keys, values, flops, *after):
+        held = len(keys)
         return pl.pallas_call(
-            kernel,
-            out_shape=jax.ShapeDtypeStruct((2 * len(masks) * rows, width), jnp.bfloat16),
-            in_specs=[VMEM] * (1 + len(operands)),
+            functools.partial(pack_kernel, held),
+            out_shape=jax.ShapeDtypeStruct((2 * held * rows, width), jnp.bfloat16),
+            in_specs=[VMEM] * (2 * held + len(after)),
             out_specs=VMEM,
             compiler_params=params,
             cost_estimate=cost(flops),
-        )(key_gain, *operands)
-
-    early_pack = packed(
-        functools.partial(early_kernel, width * splits),
-        early,
-        [sums, others, far_key, far_value, own_pair] + [pairs[mask] for mask in early[2:]],
-        AHEAD,
-    )
+        )(*keys, *values, *after)
+
+    near = [pairs[mask] for mask in early if mask != far]
+    early_pack = packed([near[0], far_key, *near[1:]], [near[0], far_value, *near[1:]], 0)
+
     def step(first, pack, *state):
         return pl.pallas_call(
             functools.partial(step_kernel, first),
@@ -404,13 +375,10 @@
 
     state = step(0, early_pack)
     late_pack = packed(
-        functools.partial(late_kernel, width * splits, late_lines),
-        late,
-        [sums, others, crossed]
-        + [late_keys[mask ^ far] for mask in late]
-        + [late_values[mask ^ far] for mask in late]
-        + [state[1]],
-        3 * AHEAD,
+        [late_keys[mask ^ far] for mask in late],
+        [late_values[mask ^ far] for mask in late],
+        12 * UNIT,
+        state[1],
     )
     state = step(len(early), exchange(early_pack, 1), *state)
     state = step(2 * len(early), late_pack, *state)

time: 32.6 us -> 29.1 us (0.89)
  Pallas kernels: 6.64 us -> 4.54 us
  starting transfers between devices: 13.6 us -> 12.2 us
  waiting for transfers between devices: 11.3 us -> 10.2 us
  local copies, waits for them, and re-layouts: 0.73 us -> 1.82 us
    ppermute x9, waiting for transfers between devices: 11.3 us -> 8.15 us  [exchange(): return lax.ppermute(array, 'tm', [(i, i ^ mask) for i in range(count)])]
    pallas_call x5, Pallas kernels: 2.39 us -> 0.3 us  [the longest x1 0.11 us: local(): pl.pallas_call(functools.partial(key_kernel, width * splits), out_shape=j...]
    ppermute x1, waiting for transfers between devices: 0.01 us -> 2.05 us  [local(): others = lax.ppermute(sums, 'head', [(0, 1), (1, 0)])]
    ppermute x1 -> x0, starting transfers between devices: 1.45 us -> none  [local(): crossed = lax.ppermute(sums, ('tm', 'head'), flips)]
    unnamed x16 -> x18, local copies, waits for them, and re-layouts: 0.72 us -> 1.82 us
  transfers between devices with their start and end apart: 11 -> 10, of which waited for: 4 -> 7; matrix products, arithmetic and copies ran while one was open for 0% -> 0% of each run, Pallas kernels for 16% -> 11%
where the time goes in v16:
time: 29.1 us; the launch traced here: 28.9 us
  starting transfers between devices  12.2 us (42%)
  waiting for transfers between devices  10.2 us (35%)
  Pallas kernels  4.54 us (16%)
  local copies, waits for them, and re-layouts  1.82 us (6%)
    ppermute x9, starting transfers between devices, exchange(): return lax.ppermute(array, 'tm', [(i, i ^ mask) for i in range(count)])  10.6 us
    ppermute x9, waiting for transfers between devices, exchange(): return lax.ppermute(array, 'tm', [(i, i ^ mask) for i in range(count)])  8.15 us
    ppermute x1, waiting for transfers between devices, local(): others = lax.ppermute(sums, 'head', [(0, 1), (1, 0)])  2.05 us
    unnamed x18, local copies, waits for them, and re-layouts  1.82 us
    pallas_call x3, Pallas kernels, step(): pl.pallas_call(functools.partial(step_kernel, first), out_shape=[jax.Shap...  1.69 us
    ppermute x1, starting transfers between devices, local(): others = lax.ppermute(sums, 'head', [(0, 1), (1, 0)])  1.58 us
    pallas_call x2, Pallas kernels, last(): pl.pallas_call(functools.partial(last_attention, place), out_shape=out_sh...  0.9 us
    pallas_call x1, Pallas kernels, local(): pl.pallas_call(merge_kernel, out_shape=jax.ShapeDtypeStruct((rows, width)...  0.85 us
  transfers between devices with their start and end apart: 10, of which 7 were waited for; matrix products, arithmetic and copies ran while one was open for 0% of the time, Pallas kernels for 11%

profile of v16, /device:TPU:0, one launch (start us, length us, event | category | flops | bytes accessed | tf_op | source)
XLA Modules:
  0.0 28.9 jit_solution(13705597583340830496)
XLA Ops:
  0.0 4.0 %collective-permute-start.4 = (bf16[128,384]{1,0:T(8,128)(2,1)}, bf16[128,384]{1,0:T(8,128)(2,1)S(1)}, u32[]{:S(2)}, u32[]{:S(2)}) collective-permute-start(bf16[128,384]{1,0:T(8,128)(2,1)} %value_ref.1), channel_id=1, source_target_pairs={{0,16},{2,18},{4,20},{6,22},{8,24},{10,26},{12,28},{14,30},{16,0},... | collective-permute-start | bytes 294920 | tf_op jit(solution)/shard_map/ppermute | solution.py:266
  4.0 0.0 copy-start
  4.0 0.9 %copy-done = bf16[128,384]{1,0:T(8,128)(2,1)S(1)} copy-done((bf16[128,384]{1,0:T(8,128)(2,1)S(1)}, bf16[128,384]{1,0:T(8,128)(2,1)}, u32[]{:S(2)}) %copy-start) | copy-done | bytes 98328
  4.9 0.0 copy-start.2
  4.9 0.9 %copy-done.2 = bf16[128,384]{1,0:T(8,128)(2,1)S(1)} copy-done((bf16[128,384]{1,0:T(8,128)(2,1)S(1)}, bf16[128,384]{1,0:T(8,128)(2,1)}, u32[]{:S(2)}) %copy-start.2) | copy-done | bytes 98328
  5.8 0.0 copy-start.7
  5.8 0.0 copy-start.1
  5.8 0.1 shard_map.82.own_ref
  5.9 0.0 copy-start.8
  6.0 1.6 %collective-permute-start = (f32[8,128]{1,0:T(8,128)S(1)}, f32[8,128]{1,0:T(8,128)S(1)}, u32[]{:S(2)}, u32[]{:S(2)}) collective-permute-start(f32[8,128]{1,0:T(8,128)S(1)} %shard_map.82.own_ref), channel_id=1, source_target_pairs={{0,1},{1,0},{2,3},{3,2},{4,5},{5,4},{6,7},{7,6},{8,9},{9,8},{10,11... | collective-permute-start | bytes 12296 | tf_op jit(solution)/shard_map/ppermute | solution.py:305
  7.5 0.0 copy-done.7
  7.5 0.0 copy-done.8
  7.6 0.0 copy-start.3
  7.6 0.0 copy-start.5
  7.6 2.0 %collective-permute-done.other_ref = f32[8,128]{1,0:T(8,128)S(1)} collective-permute-done((f32[8,128]{1,0:T(8,128)S(1)}, f32[8,128]{1,0:T(8,128)S(1)}, u32[]{:S(2)}, u32[]{:S(2)}) %collective-permute-start) | collective-permute-done | bytes 4128 | tf_op jit(solution)/shard_map/ppermute | solution.py:305
  9.6 0.0 copy-done.1
  9.6 0.1 shard_map.83.key_ref
  9.8 0.1 collective-permute-start.2
  9.8 0.0 copy-done.3
  9.8 0.0 copy-done.5
  9.8 0.1 shard_map.84
  10.0 1.9 %collective-permute-start.1 = (bf16[144,384]{1,0:T(8,128)(2,1)S(1)}, bf16[144,384]{1,0:T(8,128)(2,1)S(1)}, u32[]{:S(2)}, u32[]{:S(2)}) collective-permute-start(bf16[144,384]{1,0:T(8,128)(2,1)S(1)} %get-tuple-element.15.own_ref.query_ref), channel_id=1, source_target_pairs={{0,8},{2,10},{4,12},{6,14},{8,0},{10,2},{12,4},{14,6},{16,24},{18,... | collective-permute-start | bytes 331784 | tf_op jit(solution)/shard_map/ppermute | solution.py:266
  11.9 1.5 %collective-permute-start.6 = (bf16[256,384]{1,0:T(8,128)(2,1)S(1)}, bf16[256,384]{1,0:T(8,128)(2,1)S(1)}, u32[]{:S(2)}, u32[]{:S(2)}) collective-permute-start(bf16[256,384]{1,0:T(8,128)(2,1)S(1)} %get-tuple-element.16.refs_0_.refs_3_), channel_id=1, source_target_pairs={{0,4},{2,6},{4,0},{6,2},{8,12},{10,14},{12,8},{14,10},{16,20},{18,... | collective-permute-start | bytes 589832 | tf_op jit(solution)/shard_map/ppermute | solution.py:266
  13.4 0.0 collective-permute-done.4.source_ref
  13.4 0.6 %collective-permute-start.5 = (bf16[128,384]{1,0:T(8,128)(2,1)S(1)}, bf16[128,384]{1,0:T(8,128)(2,1)S(1)}, u32[]{:S(2)}, u32[]{:S(2)}) collective-permute-start(bf16[128,384]{1,0:T(8,128)(2,1)S(1)} %shard_map.86.refs_4_), channel_id=1, source_target_pairs={{0,4},{2,6},{4,0},{6,2},{8,12},{10,14},{12,8},{14,10},{16,20},{18,... | collective-permute-start | bytes 294920 | tf_op jit(solution)/shard_map/ppermute | solution.py:266
  14.0 1.3 %collective-permute-done.2.refs_1_ = bf16[128,384]{1,0:T(8,128)(2,1)S(1)} collective-permute-done((bf16[128,384]{1,0:T(8,128)(2,1)S(1)}, bf16[128,384]{1,0:T(8,128)(2,1)S(1)}, u32[]{:S(2)}, u32[]{:S(2)}) %collective-permute-start.2) | collective-permute-done | bytes 98336 | tf_op jit(solution)/shard_map/ppermute | solution.py:266
  15.4 1.5 %collective-permute-start.3 = (bf16[128,384]{1,0:T(8,128)(2,1)S(1)}, bf16[128,384]{1,0:T(8,128)(2,1)S(1)}, u32[]{:S(2)}, u32[]{:S(2)}) collective-permute-start(bf16[128,384]{1,0:T(8,128)(2,1)S(1)} %collective-permute-done.2.refs_1_), channel_id=1, source_target_pairs={{0,4},{2,6},{4,0},{6,2},{8,12},{10,14},{12,8},{14,10},{16,20},{18,... | collective-permute-start | bytes 294920 | tf_op jit(solution)/shard_map/ppermute | solution.py:266
  16.9 0.0 collective-permute-done.1.remote_ref.query_ref
  16.9 0.1 shard_map.85.bias_ref
  17.0 1.6 %collective-permute-done.6.refs_2_.refs_5_ = bf16[256,384]{1,0:T(8,128)(2,1)S(1)} collective-permute-done((bf16[256,384]{1,0:T(8,128)(2,1)S(1)}, bf16[256,384]{1,0:T(8,128)(2,1)S(1)}, u32[]{:S(2)}, u32[]{:S(2)}) %collective-permute-start.6) | collective-permute-done | bytes 196640 | tf_op jit(solution)/shard_map/ppermute | solution.py:266
  18.6 0.1 shard_map.87.pack_ref
  18.7 0.1 collective-permute-start.8
  18.8 0.6 %shard_map.88 = (f32[256,384]{1,0:T(8,128)S(1)}, f32[256,768]{1,0:T(8,128)S(1)}) custom-call(bf16[144,384]{1,0:T(8,128)(2,1)S(1)} %get-tuple-element.15.own_ref.query_ref, bf16[144,384]{1,0:T(8,128)(2,1)S(1)} %collective-permute-done.1.remote_ref.query_ref, f32[16,1024]{1,0:T(8,128)S(1)} %shard_map.85.bias_ref, bf16[768,384]{1,0:T(8,128)(2,1)S(1)} %shard_map.87.pack_ref), custom_call_target="tpu_custom_call" | custom-call | tf_op jit(solution)/shard_map/pallas_call | solution.py:365
  19.3 0.4 %collective-permute-done.5.refs_1_ = bf16[128,384]{1,0:T(8,128)(2,1)S(1)} collective-permute-done((bf16[128,384]{1,0:T(8,128)(2,1)S(1)}, bf16[128,384]{1,0:T(8,128)(2,1)S(1)}, u32[]{:S(2)}, u32[]{:S(2)}) %collective-permute-start.5) | collective-permute-done | bytes 98336 | tf_op jit(solution)/shard_map/ppermute | solution.py:266
  19.7 1.1 %collective-permute-done.3.refs_0_ = bf16[128,384]{1,0:T(8,128)(2,1)S(1)} collective-permute-done((bf16[128,384]{1,0:T(8,128)(2,1)S(1)}, bf16[128,384]{1,0:T(8,128)(2,1)S(1)}, u32[]{:S(2)}, u32[]{:S(2)}) %collective-permute-start.3) | collective-permute-done | bytes 98336 | tf_op jit(solution)/shard_map/ppermute | solution.py:266
  20.8 0.1 collective-permute-start.7
  20.9 0.0 collective-permute-done.8.pack_ref
  20.9 0.6 %shard_map.90 = (f32[256,384]{1,0:T(8,128)S(1)}, f32[256,768]{1,0:T(8,128)S(1)}) custom-call(bf16[144,384]{1,0:T(8,128)(2,1)S(1)} %get-tuple-element.15.own_ref.query_ref, bf16[144,384]{1,0:T(8,128)(2,1)S(1)} %collective-permute-done.1.remote_ref.query_ref, f32[16,1024]{1,0:T(8,128)S(1)} %shard_map.85.bias_ref, ...), custom_call_target="tpu_custom_call" | custom-call | tf_op jit(solution)/shard_map/pallas_call | solution.py:365
  21.6 0.5 %shard_map.91 = (f32[256,384]{1,0:T(8,128)S(1)}, f32[256,768]{1,0:T(8,128)S(1)}) custom-call(bf16[144,384]{1,0:T(8,128)(2,1)S(1)} %get-tuple-element.15.own_ref.query_ref, bf16[144,384]{1,0:T(8,128)(2,1)S(1)} %collective-permute-done.1.remote_ref.query_ref, f32[16,1024]{1,0:T(8,128)S(1)} %shard_map.85.bias_ref, bf16[256,384]{1,0:T(8,128)(2,1)S(1)} %shard_map.89.pack_ref, ...), custom_call_target="tpu_custom_call" | custom-call | tf_op jit(solution)/shard_map/pallas_call | solution.py:365
  22.0 0.3 collective-permute-done.7.pack_ref
  22.3 0.5 %shard_map.93 = bf16[144,384]{1,0:T(8,128)(2,1)S(1)} custom-call(bf16[144,384]{1,0:T(8,128)(2,1)S(1)} %collective-permute-done.1.remote_ref.query_ref, f32[16,1024]{1,0:T(8,128)S(1)} %shard_map.85.bias_ref, bf16[256,384]{1,0:T(8,128)(2,1)S(1)} %collective-permute-done.7.pack_ref, f32[256,384]{1,0:T(8,128)S(1)} %get-tuple-element.21.context_ref, ...), custom_call_target="tpu_custom_call" | custom-call | tf_op jit(solution)/shard_map/pallas_call | solution.py:388
  22.8 0.8 %collective-permute-start.9 = (bf16[144,384]{1,0:T(8,128)(2,1)S(1)}, bf16[144,384]{1,0:T(8,128)(2,1)S(1)}, u32[]{:S(2)}, u32[]{:S(2)}) collective-permute-start(bf16[144,384]{1,0:T(8,128)(2,1)S(1)} %shard_map.93), channel_id=1, source_target_pairs={{0,8},{2,10},{4,12},{6,14},{8,0},{10,2},{12,4},{14,6},{16,24},{18,... | collective-permute-start | bytes 331784 | tf_op jit(solution)/shard_map/ppermute | solution.py:266
  23.6 0.0 copy-done.4
  23.6 0.0 copy-done.6
  23.6 0.6 %shard_map.94.gate_ref = f32[16,384]{1,0:T(8,128)S(1)} custom-call(s32[2]{0:T(128)S(1)} %copy-done.6, f32[50,384]{1,0:T(8,128)S(1)} %copy-done.4), custom_call_target="tpu_custom_call" | custom-call | tf_op jit(solution)/shard_map/pallas_call | solution.py:404
  24.2 0.4 %shard_map.92 = (f32[128,384]{1,0:T(8,128)S(1)}, f32[16,384]{1,0:T(8,128)S(1)}) custom-call(bf16[144,384]{1,0:T(8,128)(2,1)S(1)} %get-tuple-element.15.own_ref.query_ref, f32[16,1024]{1,0:T(8,128)S(1)} %shard_map.85.bias_ref, bf16[256,384]{1,0:T(8,128)(2,1)S(1)} %collective-permute-done.7.pack_ref, f32[256,384]{1,0:T(8,128)S(1)} %get-tuple-element.21.context_ref, ...), custom_call_target="tpu_custom_call" | custom-call | tf_op jit(solution)/shard_map/pallas_call | solution.py:388
  24.7 3.4 %collective-permute-done.9.packet_ref = bf16[144,384]{1,0:T(8,128)(2,1)S(1)} collective-permute-done((bf16[144,384]{1,0:T(8,128)(2,1)S(1)}, bf16[144,384]{1,0:T(8,128)(2,1)S(1)}, u32[]{:S(2)}, u32[]{:S(2)}) %collective-permute-start.9) | collective-permute-done | bytes 110624 | tf_op jit(solution)/shard_map/ppermute | solution.py:266
  28.1 0.8 %shard_map.95 = bf16[128,384]{1,0:T(8,128)(2,1)} custom-call(f32[128,384]{1,0:T(8,128)S(1)} %get-tuple-element.23.own_ref, f32[16,384]{1,0:T(8,128)S(1)} %get-tuple-element.24.lines_ref, bf16[144,384]{1,0:T(8,128)(2,1)S(1)} %collective-permute-done.9.packet_ref, f32[16,384]{1,0:T(8,128)S(1)} %shard_map.94.gate_ref), custom_call_target="tpu_custom_call" | custom-call | tf_op jit(solution)/shard_map/pallas_call | solution.py:413
  (6 shorter events, 0.0 us)
Async XLA Ops:
  0.0 13.4 %collective-permute-start.4 = (bf16[128,384]{1,0:T(8,128)(2,1)}, bf16[128,384]{1,0:T(8,128)(2,1)S(1)}, u32[]{:S(2)}, u32[]{:S(2)}) collective-permute-start(bf16[128,384]{1,0:T(8,128)(2,1)} %value_ref.1), channel_id=1, source_target_pairs={{0,16},{2,18},{4,20},{6,22},{8,24},{10,26},{12,28},{14,30},{16,0},... | collective-permute-start | bytes 294920 | tf_op jit(solution)/shard_map/ppermute | solution.py:266
  4.0 0.9 %copy-start = (bf16[128,384]{1,0:T(8,128)(2,1)S(1)}, bf16[128,384]{1,0:T(8,128)(2,1)}, u32[]{:S(2)}) copy-start(bf16[128,384]{1,0:T(8,128)(2,1)} %key_ref.3) | copy-start | bytes 294916
  4.9 0.9 %copy-start.2 = (bf16[128,384]{1,0:T(8,128)(2,1)S(1)}, bf16[128,384]{1,0:T(8,128)(2,1)}, u32[]{:S(2)}) copy-start(bf16[128,384]{1,0:T(8,128)(2,1)} %query_ref.3) | copy-start | bytes 294916
  5.8 1.7 %copy-start.7 = (f32[384]{0:T(512)S(1)}, f32[384]{0:T(512)}, u32[]{:S(2)}) copy-start(f32[384]{0:T(512)} %param.12) | copy-start | bytes 4612
  5.8 3.8 %copy-start.1 = (bf16[128,384]{1,0:T(8,128)(2,1)S(1)}, bf16[128,384]{1,0:T(8,128)(2,1)}, u32[]{:S(2)}) copy-start(bf16[128,384]{1,0:T(8,128)(2,1)} %key_ref.3) | copy-start | bytes 294916
  5.9 1.6 %copy-start.8 = (f32[384]{0:T(512)S(1)}, f32[384]{0:T(512)}, u32[]{:S(2)}) copy-start(f32[384]{0:T(512)} %param.11) | copy-start | bytes 4612
  6.0 3.7 %collective-permute-start = (f32[8,128]{1,0:T(8,128)S(1)}, f32[8,128]{1,0:T(8,128)S(1)}, u32[]{:S(2)}, u32[]{:S(2)}) collective-permute-start(f32[8,128]{1,0:T(8,128)S(1)} %shard_map.82.own_ref), channel_id=1, source_target_pairs={{0,1},{1,0},{2,3},{3,2},{4,5},{5,4},{6,7},{7,6},{8,9},{9,8},{10,11... | collective-permute-start | bytes 12296 | tf_op jit(solution)/shard_map/ppermute | solution.py:305
  7.6 2.3 %copy-start.3 = (bf16[128,384]{1,0:T(8,128)(2,1)S(1)}, bf16[128,384]{1,0:T(8,128)(2,1)}, u32[]{:S(2)}) copy-start(bf16[128,384]{1,0:T(8,128)(2,1)} %value_ref.1) | copy-start | bytes 294916
  7.6 2.3 %copy-start.5 = (s32[1,16]{1,0:T(1,128)S(1)}, s32[1,16]{1,0:T(1,128)}, u32[]{:S(2)}) copy-start(s32[1,16]{1,0:T(1,128)} %far_ref.1) | copy-start | bytes 196
  9.8 5.6 %collective-permute-start.2 = (bf16[128,384]{1,0:T(8,128)(2,1)S(1)}, bf16[128,384]{1,0:T(8,128)(2,1)S(1)}, u32[]{:S(2)}, u32[]{:S(2)}) collective-permute-start(bf16[128,384]{1,0:T(8,128)(2,1)S(1)} %shard_map.83.key_ref), channel_id=1, source_target_pairs={{0,16},{2,18},{4,20},{6,22},{8,24},{10,26},{12,28},{14,30},{16,0},... | collective-permute-start | bytes 294920 | tf_op jit(solution)/shard_map/ppermute | solution.py:266
  10.0 6.9 %collective-permute-start.1 = (bf16[144,384]{1,0:T(8,128)(2,1)S(1)}, bf16[144,384]{1,0:T(8,128)(2,1)S(1)}, u32[]{:S(2)}, u32[]{:S(2)}) collective-permute-start(bf16[144,384]{1,0:T(8,128)(2,1)S(1)} %get-tuple-element.15.own_ref.query_ref), channel_id=1, source_target_pairs={{0,8},{2,10},{4,12},{6,14},{8,0},{10,2},{12,4},{14,6},{16,24},{18,... | collective-permute-start | bytes 331784 | tf_op jit(solution)/shard_map/ppermute | solution.py:266
  11.9 6.7 %collective-permute-start.6 = (bf16[256,384]{1,0:T(8,128)(2,1)S(1)}, bf16[256,384]{1,0:T(8,128)(2,1)S(1)}, u32[]{:S(2)}, u32[]{:S(2)}) collective-permute-start(bf16[256,384]{1,0:T(8,128)(2,1)S(1)} %get-tuple-element.16.refs_0_.refs_3_), channel_id=1, source_target_pairs={{0,4},{2,6},{4,0},{6,2},{8,12},{10,14},{12,8},{14,10},{16,20},{18,... | collective-permute-start | bytes 589832 | tf_op jit(solution)/shard_map/ppermute | solution.py:266
  13.4 6.3 %collective-permute-start.5 = (bf16[128,384]{1,0:T(8,128)(2,1)S(1)}, bf16[128,384]{1,0:T(8,128)(2,1)S(1)}, u32[]{:S(2)}, u32[]{:S(2)}) collective-permute-start(bf16[128,384]{1,0:T(8,128)(2,1)S(1)} %shard_map.86.refs_4_), channel_id=1, source_target_pairs={{0,4},{2,6},{4,0},{6,2},{8,12},{10,14},{12,8},{14,10},{16,20},{18,... | collective-permute-start | bytes 294920 | tf_op jit(solution)/shard_map/ppermute | solution.py:266
  15.4 5.4 %collective-permute-start.3 = (bf16[128,384]{1,0:T(8,128)(2,1)S(1)}, bf16[128,384]{1,0:T(8,128)(2,1)S(1)}, u32[]{:S(2)}, u32[]{:S(2)}) collective-permute-start(bf16[128,384]{1,0:T(8,128)(2,1)S(1)} %collective-permute-done.2.refs_1_), channel_id=1, source_target_pairs={{0,4},{2,6},{4,0},{6,2},{8,12},{10,14},{12,8},{14,10},{16,20},{18,... | collective-permute-start | bytes 294920 | tf_op jit(solution)/shard_map/ppermute | solution.py:266
  18.7 2.2 %collective-permute-start.8 = (bf16[768,384]{1,0:T(8,128)(2,1)S(1)}, bf16[768,384]{1,0:T(8,128)(2,1)S(1)}, u32[]{:S(2)}, u32[]{:S(2)}) collective-permute-start(bf16[768,384]{1,0:T(8,128)(2,1)S(1)} %shard_map.87.pack_ref), channel_id=1, source_target_pairs={{0,2},{2,0},{4,6},{6,4},{8,10},{10,8},{12,14},{14,12},{16,18},{18,... | collective-permute-start | bytes 1769480 | tf_op jit(solution)/shard_map/ppermute | solution.py:266
  20.8 1.5 %collective-permute-start.7 = (bf16[256,384]{1,0:T(8,128)(2,1)S(1)}, bf16[256,384]{1,0:T(8,128)(2,1)S(1)}, u32[]{:S(2)}, u32[]{:S(2)}) collective-permute-start(bf16[256,384]{1,0:T(8,128)(2,1)S(1)} %shard_map.89.pack_ref), channel_id=1, source_target_pairs={{0,2},{2,0},{4,6},{6,4},{8,10},{10,8},{12,14},{14,12},{16,18},{18,... | collective-permute-start | bytes 589832 | tf_op jit(solution)/shard_map/ppermute | solution.py:266
  22.3 1.3 %copy-start.4 = (f32[50,384]{1,0:T(8,128)S(1)}, f32[50,384]{1,0:T(8,128)}, u32[]{:S(2)}) copy-start(f32[50,384]{1,0:T(8,128)} %table_ref.1) | copy-start | bytes 230404
  22.3 1.3 %copy-start.6 = (s32[2]{0:T(128)S(1)}, s32[2]{0:T(128)}, u32[]{:S(2)}) copy-start(s32[2]{0:T(128)} %step_ref.1) | copy-start | bytes 28
  22.8 5.3 %collective-permute-start.9 = (bf16[144,384]{1,0:T(8,128)(2,1)S(1)}, bf16[144,384]{1,0:T(8,128)(2,1)S(1)}, u32[]{:S(2)}, u32[]{:S(2)}) collective-permute-start(bf16[144,384]{1,0:T(8,128)(2,1)S(1)} %shard_map.93), channel_id=1, source_target_pairs={{0,8},{2,10},{4,12},{6,14},{8,0},{10,2},{12,4},{14,6},{16,24},{18,... | collective-permute-start | bytes 331784 | tf_op jit(solution)/shard_map/ppermute | solution.py:266

commit v17 on v16

--- a/solution.py
+++ b/solution.py
@@ -60,17 +60,12 @@
 def query_kernel(
     full_width,
     query_ref,
-    key_ref,
-    value_ref,
     gain_ref,
     far_ref,
     own_ref,
     other_ref,
     query_out,
-    pair_out,
 ):
-    pair_out[:HD, :] = key_ref[...]
-    pair_out[HD:, :] = value_ref[...]
     total = own_ref[0:1, :] + other_ref[0:1, :]
     query_out[:HD, :] = normed(query_ref, factor_of(total, full_width), gain_ref)
     far = far_ref[...].astype(jnp.float32)
@@ -101,12 +96,8 @@
 
 
 def pack_kernel(held, *refs):
-    keys, values, pack_out = refs[:held], refs[held : 2 * held], refs[-1]
-    for place, key_ref in enumerate(keys):
-        pack_out[place * HD : (place + 1) * HD, :] = key_ref[:HD, :]
-    for place, value_ref in enumerate(values, start=held):
-        low = value_ref.shape[0] - HD
-        pack_out[place * HD : (place + 1) * HD, :] = value_ref[low:, :]
+    for place, source_ref in enumerate(refs[: 2 * held]):
+        refs[-1][place * HD : (place + 1) * HD, :] = source_ref[...]
 
 
 def absorb(queries, pack_ref, biases, olds):
@@ -313,18 +304,16 @@
         out_specs=VMEM,
         compiler_params=params,
     )(key_proj, key_gain, sums, others)
-    query_packet, own_pair = pl.pallas_call(
+    near_values = gathered(value_proj, bits[1:])
+    near_keys = gathered(own_key, bits[1:])
+    query_packet = pl.pallas_call(
         functools.partial(query_kernel, width * splits),
-        out_shape=[
-            jax.ShapeDtypeStruct((rows + EXTRA, width), jnp.bfloat16),
-            jax.ShapeDtypeStruct((2 * rows, width), jnp.bfloat16),
-        ],
-        in_specs=[VMEM] * 7,
-        out_specs=[VMEM] * 2,
-        compiler_params=params,
-    )(query_proj, own_key, value_proj, query_gain, far_blocks, sums, others)
+        out_shape=jax.ShapeDtypeStruct((rows + EXTRA, width), jnp.bfloat16),
+        in_specs=[VMEM] * 5,
+        out_specs=VMEM,
+        compiler_params=params,
+    )(query_proj, query_gain, far_blocks, sums, others)
     far_key = exchange(own_key, far)
-    pairs = gathered(own_pair, bits[1:])
     queries = [query_packet, exchange(query_packet, query_mask)]
     far_value = pl.pallas_call(
         copy_kernel,
@@ -335,7 +324,7 @@
         cost_estimate=cost(4 * UNIT),
     )(far_value)
     late_keys, late_values = gathered(far_key, bits[1:]), gathered(far_value, bits[1:])
-    early = [0, far] + sorted(mask for mask in pairs if mask)
+    early = [0, far] + sorted(mask for mask in near_keys if mask)
     late = sorted(mask ^ far for mask in late_keys if mask)
     early_masks = early + [mask ^ 1 for mask in early]
     all_masks = early_masks + late + [mask ^ 1 for mask in late]
@@ -358,8 +347,10 @@
             cost_estimate=cost(flops),
         )(*keys, *values, *after)
 
-    near = [pairs[mask] for mask in early if mask != far]
-    early_pack = packed([near[0], far_key, *near[1:]], [near[0], far_value, *near[1:]], 0)
+    near_keys[far], near_values[far] = far_key, far_value
+    early_pack = packed(
+        [near_keys[mask] for mask in early], [near_values[mask] for mask in early], 0
+    )
 
     def step(first, pack, *state):
         return pl.pallas_call(

time: 29.1 us -> 28.6 us (0.983)
  waiting for transfers between devices: 10.2 us -> 6.78 us
  starting transfers between devices: 12.2 us -> 15.1 us
    ppermute x9 -> x10, starting transfers between devices: 10.6 us -> 13.5 us  [exchange(): return lax.ppermute(array, 'tm', [(i, i ^ mask) for i in range(count)])]
    ppermute x9 -> x10, waiting for transfers between devices: 8.15 us -> 6.21 us  [exchange(): return lax.ppermute(array, 'tm', [(i, i ^ mask) for i in range(count)])]
    ppermute x1, waiting for transfers between devices: 2.05 us -> 0.57 us  [local(): others = lax.ppermute(sums, 'head', [(0, 1), (1, 0)])]
  transfers between devices with their start and end apart: 10 -> 11, of which waited for: 7 -> 6; matrix products, arithmetic and copies ran while one was open for 0% -> 0% of each run, Pallas kernels for 11% -> 11%
where the time goes in v17:
time: 28.6 us; the launch traced here: 28.4 us
  starting transfers between devices  15.1 us (53%)
  waiting for transfers between devices  6.78 us (24%)
  Pallas kernels  4.54 us (16%)
  local copies, waits for them, and re-layouts  1.82 us (6%)
    ppermute x10, starting transfers between devices, exchange(): return lax.ppermute(array, 'tm', [(i, i ^ mask) for i in range(count)])  13.5 us
    ppermute x10, waiting for transfers between devices, exchange(): return lax.ppermute(array, 'tm', [(i, i ^ mask) for i in range(count)])  6.21 us
    unnamed x18, local copies, waits for them, and re-layouts  1.82 us
    pallas_call x3, Pallas kernels, step(): pl.pallas_call(functools.partial(step_kernel, first), out_shape=[jax.Shap...  1.7 us
    ppermute x1, starting transfers between devices, local(): others = lax.ppermute(sums, 'head', [(0, 1), (1, 0)])  1.58 us
    pallas_call x2, Pallas kernels, last(): pl.pallas_call(functools.partial(last_attention, place), out_shape=out_sh...  0.9 us
    pallas_call x1, Pallas kernels, local(): pl.pallas_call(merge_kernel, out_shape=jax.ShapeDtypeStruct((rows, width)...  0.85 us
  transfers between devices with their start and end apart: 11, of which 6 were waited for; matrix products, arithmetic and copies ran while one was open for 0% of the time, Pallas kernels for 11%

profile of v17, /device:TPU:0, one launch (start us, length us, event | category | flops | bytes accessed | tf_op | source)
XLA Modules:
  0.0 28.4 jit_solution(1362391776198800360)
XLA Ops:
  0.0 4.0 %collective-permute-start.4 = (bf16[128,384]{1,0:T(8,128)(2,1)}, bf16[128,384]{1,0:T(8,128)(2,1)S(1)}, u32[]{:S(2)}, u32[]{:S(2)}) collective-permute-start(bf16[128,384]{1,0:T(8,128)(2,1)} %refs_3_.1), channel_id=1, source_target_pairs={{0,16},{2,18},{4,20},{6,22},{8,24},{10,26},{12,28},{14,30},{16,0},... | collective-permute-start | bytes 294920 | tf_op jit(solution)/shard_map/ppermute | solution.py:257
  4.0 0.0 copy-start
  4.0 0.9 %copy-done = bf16[128,384]{1,0:T(8,128)(2,1)S(1)} copy-done((bf16[128,384]{1,0:T(8,128)(2,1)S(1)}, bf16[128,384]{1,0:T(8,128)(2,1)}, u32[]{:S(2)}) %copy-start) | copy-done | bytes 98328
  4.9 0.9 %copy-done.2 = bf16[128,384]{1,0:T(8,128)(2,1)S(1)} copy-done((bf16[128,384]{1,0:T(8,128)(2,1)S(1)}, bf16[128,384]{1,0:T(8,128)(2,1)}, u32[]{:S(2)}) %copy-start.2) | copy-done | bytes 98328
  5.8 0.0 copy-start.3
  5.8 0.0 copy-start.7
  5.8 0.1 shard_map.82.own_ref
  5.9 0.0 copy-start.8
  6.0 1.6 %collective-permute-start = (f32[8,128]{1,0:T(8,128)S(1)}, f32[8,128]{1,0:T(8,128)S(1)}, u32[]{:S(2)}, u32[]{:S(2)}) collective-permute-start(f32[8,128]{1,0:T(8,128)S(1)} %shard_map.82.own_ref), channel_id=1, source_target_pairs={{0,1},{1,0},{2,3},{3,2},{4,5},{5,4},{6,7},{7,6},{8,9},{9,8},{10,11... | collective-permute-start | bytes 12296 | tf_op jit(solution)/shard_map/ppermute | solution.py:296
  7.5 0.0 copy-done.3
  7.5 1.5 %collective-permute-start.7 = (bf16[128,384]{1,0:T(8,128)(2,1)S(1)}, bf16[128,384]{1,0:T(8,128)(2,1)S(1)}, u32[]{:S(2)}, u32[]{:S(2)}) collective-permute-start(bf16[128,384]{1,0:T(8,128)(2,1)S(1)} %copy-done.3), channel_id=1, source_target_pairs={{0,4},{2,6},{4,0},{6,2},{8,12},{10,14},{12,8},{14,10},{16,20},{18,... | collective-permute-start | bytes 294920 | tf_op jit(solution)/shard_map/ppermute | solution.py:257
  9.0 0.0 copy-done.7
  9.0 0.0 copy-done.8
  9.1 0.0 copy-start.5
  9.1 0.6 %collective-permute-done.other_ref = f32[8,128]{1,0:T(8,128)S(1)} collective-permute-done((f32[8,128]{1,0:T(8,128)S(1)}, f32[8,128]{1,0:T(8,128)S(1)}, u32[]{:S(2)}, u32[]{:S(2)}) %collective-permute-start) | collective-permute-done | bytes 4128 | tf_op jit(solution)/shard_map/ppermute | solution.py:296
  9.6 0.0 copy-done.1
  9.6 0.1 shard_map.85.refs_0_
  9.8 0.1 collective-permute-start.2
  9.8 1.8 %collective-permute-start.6 = (bf16[128,384]{1,0:T(8,128)(2,1)S(1)}, bf16[128,384]{1,0:T(8,128)(2,1)S(1)}, u32[]{:S(2)}, u32[]{:S(2)}) collective-permute-start(bf16[128,384]{1,0:T(8,128)(2,1)S(1)} %shard_map.85.refs_0_), channel_id=1, source_target_pairs={{0,4},{2,6},{4,0},{6,2},{8,12},{10,14},{12,8},{14,10},{16,20},{18,... | collective-permute-start | bytes 294920 | tf_op jit(solution)/shard_map/ppermute | solution.py:257
  11.6 0.0 copy-done.5
  11.6 0.1 shard_map.83.own_ref.query_ref
  11.8 1.6 %collective-permute-start.1 = (bf16[144,384]{1,0:T(8,128)(2,1)S(1)}, bf16[144,384]{1,0:T(8,128)(2,1)S(1)}, u32[]{:S(2)}, u32[]{:S(2)}) collective-permute-start(bf16[144,384]{1,0:T(8,128)(2,1)S(1)} %shard_map.83.own_ref.query_ref), channel_id=1, source_target_pairs={{0,8},{2,10},{4,12},{6,14},{8,0},{10,2},{12,4},{14,6},{16,24},{18,... | collective-permute-start | bytes 331784 | tf_op jit(solution)/shard_map/ppermute | solution.py:257
  13.4 0.0 collective-permute-done.4.source_ref
  13.4 0.6 %collective-permute-start.5 = (bf16[128,384]{1,0:T(8,128)(2,1)S(1)}, bf16[128,384]{1,0:T(8,128)(2,1)S(1)}, u32[]{:S(2)}, u32[]{:S(2)}) collective-permute-start(bf16[128,384]{1,0:T(8,128)(2,1)S(1)} %shard_map.86.refs_4_), channel_id=1, source_target_pairs={{0,4},{2,6},{4,0},{6,2},{8,12},{10,14},{12,8},{14,10},{16,20},{18,... | collective-permute-start | bytes 294920 | tf_op jit(solution)/shard_map/ppermute | solution.py:257
  14.0 1.3 %collective-permute-done.2.refs_1_ = bf16[128,384]{1,0:T(8,128)(2,1)S(1)} collective-permute-done((bf16[128,384]{1,0:T(8,128)(2,1)S(1)}, bf16[128,384]{1,0:T(8,128)(2,1)S(1)}, u32[]{:S(2)}, u32[]{:S(2)}) %collective-permute-start.2) | collective-permute-done | bytes 98336 | tf_op jit(solution)/shard_map/ppermute | solution.py:257
  15.3 1.6 %collective-permute-start.3 = (bf16[128,384]{1,0:T(8,128)(2,1)S(1)}, bf16[128,384]{1,0:T(8,128)(2,1)S(1)}, u32[]{:S(2)}, u32[]{:S(2)}) collective-permute-start(bf16[128,384]{1,0:T(8,128)(2,1)S(1)} %collective-permute-done.2.refs_1_), channel_id=1, source_target_pairs={{0,4},{2,6},{4,0},{6,2},{8,12},{10,14},{12,8},{14,10},{16,20},{18,... | collective-permute-start | bytes 294920 | tf_op jit(solution)/shard_map/ppermute | solution.py:257
  16.9 0.0 collective-permute-done.7.refs_5_
  16.9 0.0 collective-permute-done.6.refs_2_
  16.9 0.1 shard_map.87.pack_ref
  17.0 0.1 collective-permute-start.9
  17.1 0.0 collective-permute-done.1.remote_ref.query_ref
  17.1 0.1 shard_map.84.bias_ref
  17.2 0.6 %shard_map.88 = (f32[256,384]{1,0:T(8,128)S(1)}, f32[256,768]{1,0:T(8,128)S(1)}) custom-call(bf16[144,384]{1,0:T(8,128)(2,1)S(1)} %shard_map.83.own_ref.query_ref, bf16[144,384]{1,0:T(8,128)(2,1)S(1)} %collective-permute-done.1.remote_ref.query_ref, f32[16,1024]{1,0:T(8,128)S(1)} %shard_map.84.bias_ref, bf16[768,384]{1,0:T(8,128)(2,1)S(1)} %shard_map.87.pack_ref), custom_call_target="tpu_custom_call" | custom-call | tf_op jit(solution)/shard_map/pallas_call | solution.py:356
  17.8 1.0 %collective-permute-done.5.refs_1_ = bf16[128,384]{1,0:T(8,128)(2,1)S(1)} collective-permute-done((bf16[128,384]{1,0:T(8,128)(2,1)S(1)}, bf16[128,384]{1,0:T(8,128)(2,1)S(1)}, u32[]{:S(2)}, u32[]{:S(2)}) %collective-permute-start.5) | collective-permute-done | bytes 98336 | tf_op jit(solution)/shard_map/ppermute | solution.py:257
  18.7 1.2 %collective-permute-done.3.refs_0_ = bf16[128,384]{1,0:T(8,128)(2,1)S(1)} collective-permute-done((bf16[128,384]{1,0:T(8,128)(2,1)S(1)}, bf16[128,384]{1,0:T(8,128)(2,1)S(1)}, u32[]{:S(2)}, u32[]{:S(2)}) %collective-permute-start.3) | collective-permute-done | bytes 98336 | tf_op jit(solution)/shard_map/ppermute | solution.py:257
  20.0 0.1 collective-permute-start.8
  20.1 0.0 collective-permute-done.9.pack_ref
  20.1 0.6 %shard_map.90 = (f32[256,384]{1,0:T(8,128)S(1)}, f32[256,768]{1,0:T(8,128)S(1)}) custom-call(bf16[144,384]{1,0:T(8,128)(2,1)S(1)} %shard_map.83.own_ref.query_ref, bf16[144,384]{1,0:T(8,128)(2,1)S(1)} %collective-permute-done.1.remote_ref.query_ref, f32[16,1024]{1,0:T(8,128)S(1)} %shard_map.84.bias_ref, ...), custom_call_target="tpu_custom_call" | custom-call | tf_op jit(solution)/shard_map/pallas_call | solution.py:356
  20.7 0.5 %shard_map.91 = (f32[256,384]{1,0:T(8,128)S(1)}, f32[256,768]{1,0:T(8,128)S(1)}) custom-call(bf16[144,384]{1,0:T(8,128)(2,1)S(1)} %shard_map.83.own_ref.query_ref, bf16[144,384]{1,0:T(8,128)(2,1)S(1)} %collective-permute-done.1.remote_ref.query_ref, f32[16,1024]{1,0:T(8,128)S(1)} %shard_map.84.bias_ref, bf16[256,384]{1,0:T(8,128)(2,1)S(1)} %shard_map.89.pack_ref, ...), custom_call_target="tpu_custom_call" | custom-call | tf_op jit(solution)/shard_map/pallas_call | solution.py:356
  21.2 0.3 collective-permute-done.8.pack_ref
  21.5 0.5 %shard_map.93 = bf16[144,384]{1,0:T(8,128)(2,1)S(1)} custom-call(bf16[144,384]{1,0:T(8,128)(2,1)S(1)} %collective-permute-done.1.remote_ref.query_ref, f32[16,1024]{1,0:T(8,128)S(1)} %shard_map.84.bias_ref, bf16[256,384]{1,0:T(8,128)(2,1)S(1)} %collective-permute-done.8.pack_ref, f32[256,384]{1,0:T(8,128)S(1)} %get-tuple-element.17.context_ref, ...), custom_call_target="tpu_custom_call" | custom-call | tf_op jit(solution)/shard_map/pallas_call | solution.py:379
  22.0 2.1 %collective-permute-start.10 = (bf16[144,384]{1,0:T(8,128)(2,1)S(1)}, bf16[144,384]{1,0:T(8,128)(2,1)S(1)}, u32[]{:S(2)}, u32[]{:S(2)}) collective-permute-start(bf16[144,384]{1,0:T(8,128)(2,1)S(1)} %shard_map.93), channel_id=1, source_target_pairs={{0,8},{2,10},{4,12},{6,14},{8,0},{10,2},{12,4},{14,6},{16,24},{18,... | collective-permute-start | bytes 331784 | tf_op jit(solution)/shard_map/ppermute | solution.py:257
  24.1 0.0 copy-done.4
  24.1 0.0 copy-done.6
  24.1 0.6 %shard_map.94.gate_ref = f32[16,384]{1,0:T(8,128)S(1)} custom-call(s32[2]{0:T(128)S(1)} %copy-done.6, f32[50,384]{1,0:T(8,128)S(1)} %copy-done.4), custom_call_target="tpu_custom_call" | custom-call | tf_op jit(solution)/shard_map/pallas_call | solution.py:395
  24.7 0.4 %shard_map.92 = (f32[128,384]{1,0:T(8,128)S(1)}, f32[16,384]{1,0:T(8,128)S(1)}) custom-call(bf16[144,384]{1,0:T(8,128)(2,1)S(1)} %shard_map.83.own_ref.query_ref, f32[16,1024]{1,0:T(8,128)S(1)} %shard_map.84.bias_ref, bf16[256,384]{1,0:T(8,128)(2,1)S(1)} %collective-permute-done.8.pack_ref, f32[256,384]{1,0:T(8,128)S(1)} %get-tuple-element.17.context_ref, ...), custom_call_target="tpu_custom_call" | custom-call | tf_op jit(solution)/shard_map/pallas_call | solution.py:379
  25.1 2.4 %collective-permute-done.10.packet_ref = bf16[144,384]{1,0:T(8,128)(2,1)S(1)} collective-permute-done((bf16[144,384]{1,0:T(8,128)(2,1)S(1)}, bf16[144,384]{1,0:T(8,128)(2,1)S(1)}, u32[]{:S(2)}, u32[]{:S(2)}) %collective-permute-start.10) | collective-permute-done | bytes 110624 | tf_op jit(solution)/shard_map/ppermute | solution.py:257
  27.5 0.8 %shard_map.95 = bf16[128,384]{1,0:T(8,128)(2,1)} custom-call(f32[128,384]{1,0:T(8,128)S(1)} %get-tuple-element.19.own_ref, f32[16,384]{1,0:T(8,128)S(1)} %get-tuple-element.20.lines_ref, bf16[144,384]{1,0:T(8,128)(2,1)S(1)} %collective-permute-done.10.packet_ref, f32[16,384]{1,0:T(8,128)S(1)} %shard_map.94.gate_ref), custom_call_target="tpu_custom_call" | custom-call | tf_op jit(solution)/shard_map/pallas_call | solution.py:404
  (8 shorter events, 0.0 us)
Async XLA Ops:
  0.0 13.4 %collective-permute-start.4 = (bf16[128,384]{1,0:T(8,128)(2,1)}, bf16[128,384]{1,0:T(8,128)(2,1)S(1)}, u32[]{:S(2)}, u32[]{:S(2)}) collective-permute-start(bf16[128,384]{1,0:T(8,128)(2,1)} %refs_3_.1), channel_id=1, source_target_pairs={{0,16},{2,18},{4,20},{6,22},{8,24},{10,26},{12,28},{14,30},{16,0},... | collective-permute-start | bytes 294920 | tf_op jit(solution)/shard_map/ppermute | solution.py:257
  4.0 0.9 %copy-start = (bf16[128,384]{1,0:T(8,128)(2,1)S(1)}, bf16[128,384]{1,0:T(8,128)(2,1)}, u32[]{:S(2)}) copy-start(bf16[128,384]{1,0:T(8,128)(2,1)} %key_ref.3) | copy-start | bytes 294916
  4.9 0.9 %copy-start.2 = (bf16[128,384]{1,0:T(8,128)(2,1)S(1)}, bf16[128,384]{1,0:T(8,128)(2,1)}, u32[]{:S(2)}) copy-start(bf16[128,384]{1,0:T(8,128)(2,1)} %query_ref.3) | copy-start | bytes 294916
  5.8 1.7 %copy-start.3 = (bf16[128,384]{1,0:T(8,128)(2,1)S(1)}, bf16[128,384]{1,0:T(8,128)(2,1)}, u32[]{:S(2)}) copy-start(bf16[128,384]{1,0:T(8,128)(2,1)} %refs_3_.1) | copy-start | bytes 294916
  5.8 3.2 %copy-start.7 = (f32[384]{0:T(512)S(1)}, f32[384]{0:T(512)}, u32[]{:S(2)}) copy-start(f32[384]{0:T(512)} %param.11) | copy-start | bytes 4612
  5.8 3.8 %copy-start.1 = (bf16[128,384]{1,0:T(8,128)(2,1)S(1)}, bf16[128,384]{1,0:T(8,128)(2,1)}, u32[]{:S(2)}) copy-start(bf16[128,384]{1,0:T(8,128)(2,1)} %key_ref.3) | copy-start | bytes 294916
  5.9 3.1 %copy-start.8 = (f32[384]{0:T(512)S(1)}, f32[384]{0:T(512)}, u32[]{:S(2)}) copy-start(f32[384]{0:T(512)} %param.12) | copy-start | bytes 4612
  6.0 3.7 %collective-permute-start = (f32[8,128]{1,0:T(8,128)S(1)}, f32[8,128]{1,0:T(8,128)S(1)}, u32[]{:S(2)}, u32[]{:S(2)}) collective-permute-start(f32[8,128]{1,0:T(8,128)S(1)} %shard_map.82.own_ref), channel_id=1, source_target_pairs={{0,1},{1,0},{2,3},{3,2},{4,5},{5,4},{6,7},{7,6},{8,9},{9,8},{10,11... | collective-permute-start | bytes 12296 | tf_op jit(solution)/shard_map/ppermute | solution.py:296
  7.5 9.4 %collective-permute-start.7 = (bf16[128,384]{1,0:T(8,128)(2,1)S(1)}, bf16[128,384]{1,0:T(8,128)(2,1)S(1)}, u32[]{:S(2)}, u32[]{:S(2)}) collective-permute-start(bf16[128,384]{1,0:T(8,128)(2,1)S(1)} %copy-done.3), channel_id=1, source_target_pairs={{0,4},{2,6},{4,0},{6,2},{8,12},{10,14},{12,8},{14,10},{16,20},{18,... | collective-permute-start | bytes 294920 | tf_op jit(solution)/shard_map/ppermute | solution.py:257
  9.1 2.6 %copy-start.5 = (s32[1,16]{1,0:T(1,128)S(1)}, s32[1,16]{1,0:T(1,128)}, u32[]{:S(2)}) copy-start(s32[1,16]{1,0:T(1,128)} %far_ref.1) | copy-start | bytes 196
  9.8 5.6 %collective-permute-start.2 = (bf16[128,384]{1,0:T(8,128)(2,1)S(1)}, bf16[128,384]{1,0:T(8,128)(2,1)S(1)}, u32[]{:S(2)}, u32[]{:S(2)}) collective-permute-start(bf16[128,384]{1,0:T(8,128)(2,1)S(1)} %shard_map.85.refs_0_), channel_id=1, source_target_pairs={{0,16},{2,18},{4,20},{6,22},{8,24},{10,26},{12,28},{14,30},{16,0},... | collective-permute-start | bytes 294920 | tf_op jit(solution)/shard_map/ppermute | solution.py:257
  9.8 7.1 %collective-permute-start.6 = (bf16[128,384]{1,0:T(8,128)(2,1)S(1)}, bf16[128,384]{1,0:T(8,128)(2,1)S(1)}, u32[]{:S(2)}, u32[]{:S(2)}) collective-permute-start(bf16[128,384]{1,0:T(8,128)(2,1)S(1)} %shard_map.85.refs_0_), channel_id=1, source_target_pairs={{0,4},{2,6},{4,0},{6,2},{8,12},{10,14},{12,8},{14,10},{16,20},{18,... | collective-permute-start | bytes 294920 | tf_op jit(solution)/shard_map/ppermute | solution.py:257
  11.8 5.3 %collective-permute-start.1 = (bf16[144,384]{1,0:T(8,128)(2,1)S(1)}, bf16[144,384]{1,0:T(8,128)(2,1)S(1)}, u32[]{:S(2)}, u32[]{:S(2)}) collective-permute-start(bf16[144,384]{1,0:T(8,128)(2,1)S(1)} %shard_map.83.own_ref.query_ref), channel_id=1, source_target_pairs={{0,8},{2,10},{4,12},{6,14},{8,0},{10,2},{12,4},{14,6},{16,24},{18,... | collective-permute-start | bytes 331784 | tf_op jit(solution)/shard_map/ppermute | solution.py:257
  13.4 5.3 %collective-permute-start.5 = (bf16[128,384]{1,0:T(8,128)(2,1)S(1)}, bf16[128,384]{1,0:T(8,128)(2,1)S(1)}, u32[]{:S(2)}, u32[]{:S(2)}) collective-permute-start(bf16[128,384]{1,0:T(8,128)(2,1)S(1)} %shard_map.86.refs_4_), channel_id=1, source_target_pairs={{0,4},{2,6},{4,0},{6,2},{8,12},{10,14},{12,8},{14,10},{16,20},{18,... | collective-permute-start | bytes 294920 | tf_op jit(solution)/shard_map/ppermute | solution.py:257
  15.3 4.6 %collective-permute-start.3 = (bf16[128,384]{1,0:T(8,128)(2,1)S(1)}, bf16[128,384]{1,0:T(8,128)(2,1)S(1)}, u32[]{:S(2)}, u32[]{:S(2)}) collective-permute-start(bf16[128,384]{1,0:T(8,128)(2,1)S(1)} %collective-permute-done.2.refs_1_), channel_id=1, source_target_pairs={{0,4},{2,6},{4,0},{6,2},{8,12},{10,14},{12,8},{14,10},{16,20},{18,... | collective-permute-start | bytes 294920 | tf_op jit(solution)/shard_map/ppermute | solution.py:257
  17.0 3.1 %collective-permute-start.9 = (bf16[768,384]{1,0:T(8,128)(2,1)S(1)}, bf16[768,384]{1,0:T(8,128)(2,1)S(1)}, u32[]{:S(2)}, u32[]{:S(2)}) collective-permute-start(bf16[768,384]{1,0:T(8,128)(2,1)S(1)} %shard_map.87.pack_ref), channel_id=1, source_target_pairs={{0,2},{2,0},{4,6},{6,4},{8,10},{10,8},{12,14},{14,12},{16,18},{18,... | collective-permute-start | bytes 1769480 | tf_op jit(solution)/shard_map/ppermute | solution.py:257
  20.0 1.5 %collective-permute-start.8 = (bf16[256,384]{1,0:T(8,128)(2,1)S(1)}, bf16[256,384]{1,0:T(8,128)(2,1)S(1)}, u32[]{:S(2)}, u32[]{:S(2)}) collective-permute-start(bf16[256,384]{1,0:T(8,128)(2,1)S(1)} %shard_map.89.pack_ref), channel_id=1, source_target_pairs={{0,2},{2,0},{4,6},{6,4},{8,10},{10,8},{12,14},{14,12},{16,18},{18,... | collective-permute-start | bytes 589832 | tf_op jit(solution)/shard_map/ppermute | solution.py:257
  21.5 2.6 %copy-start.4 = (f32[50,384]{1,0:T(8,128)S(1)}, f32[50,384]{1,0:T(8,128)}, u32[]{:S(2)}) copy-start(f32[50,384]{1,0:T(8,128)} %table_ref.1) | copy-start | bytes 230404
  21.5 2.6 %copy-start.6 = (s32[2]{0:T(128)S(1)}, s32[2]{0:T(128)}, u32[]{:S(2)}) copy-start(s32[2]{0:T(128)} %step_ref.1) | copy-start | bytes 28
  22.0 5.6 %collective-permute-start.10 = (bf16[144,384]{1,0:T(8,128)(2,1)S(1)}, bf16[144,384]{1,0:T(8,128)(2,1)S(1)}, u32[]{:S(2)}, u32[]{:S(2)}) collective-permute-start(bf16[144,384]{1,0:T(8,128)(2,1)S(1)} %shard_map.93), channel_id=1, source_target_pairs={{0,8},{2,10},{4,12},{6,14},{8,0},{10,2},{12,4},{14,6},{16,24},{18,... | collective-permute-start | bytes 331784 | tf_op jit(solution)/shard_map/ppermute | solution.py:257

commit v18 on v17

--- a/solution.py
+++ b/solution.py
@@ -312,6 +312,7 @@
         in_specs=[VMEM] * 5,
         out_specs=VMEM,
         compiler_params=params,
+        cost_estimate=cost(4 * UNIT),
     )(query_proj, query_gain, far_blocks, sums, others)
     far_key = exchange(own_key, far)
     queries = [query_packet, exchange(query_packet, query_mask)]
@@ -349,7 +350,7 @@
 
     near_keys[far], near_values[far] = far_key, far_value
     early_pack = packed(
-        [near_keys[mask] for mask in early], [near_values[mask] for mask in early], 0
+        [near_keys[mask] for mask in early], [near_values[mask] for mask in early], 4 * UNIT
     )
 
     def step(first, pack, *state):

time: 28.6 us -> 29.5 us (1.031)
  starting transfers between devices: 15.1 us -> 16.3 us
  waiting for transfers between devices: 6.78 us -> 6.41 us
    ppermute x1, starting transfers between devices: 1.58 us -> 3.03 us  [local(): others = lax.ppermute(sums, 'head', [(0, 1), (1, 0)])]
    ppermute x1, waiting for transfers between devices: 0.57 us -> 0.01 us  [local(): others = lax.ppermute(sums, 'head', [(0, 1), (1, 0)])]
  transfers between devices with their start and end apart: 11 -> 11, of which waited for: 6 -> 4; matrix products, arithmetic and copies ran while one was open for 0% -> 0% of each run, Pallas kernels for 11% -> 11%
where the time goes in v18:
time: 29.5 us; the launch traced here: 29.3 us
  starting transfers between devices  16.3 us (55%)
  waiting for transfers between devices  6.41 us (22%)
  Pallas kernels  4.56 us (15%)
  local copies, waits for them, and re-layouts  1.82 us (6%)
    ppermute x10, starting transfers between devices, exchange(): return lax.ppermute(array, 'tm', [(i, i ^ mask) for i in range(count)])  13.3 us
    ppermute x10, waiting for transfers between devices, exchange(): return lax.ppermute(array, 'tm', [(i, i ^ mask) for i in range(count)])  6.41 us
    ppermute x1, starting transfers between devices, local(): others = lax.ppermute(sums, 'head', [(0, 1), (1, 0)])  3.03 us
    unnamed x18, local copies, waits for them, and re-layouts  1.82 us
    pallas_call x3, Pallas kernels, step(): pl.pallas_call(functools.partial(step_kernel, first), out_shape=[jax.Shap...  1.72 us
    pallas_call x2, Pallas kernels, last(): pl.pallas_call(functools.partial(last_attention, place), out_shape=out_sh...  0.9 us
    pallas_call x1, Pallas kernels, local(): pl.pallas_call(merge_kernel, out_shape=jax.ShapeDtypeStruct((rows, width)...  0.85 us
  transfers between devices with their start and end apart: 11, of which 4 were waited for; matrix products, arithmetic and copies ran while one was open for 0% of the time, Pallas kernels for 11%

profile of v18, /device:TPU:0, one launch (start us, length us, event | category | flops | bytes accessed | tf_op | source)
XLA Modules:
  0.0 29.3 jit_solution(9490023390987726094)
XLA Ops:
  0.0 0.0 copy-start
  0.0 0.9 %copy-done = bf16[128,384]{1,0:T(8,128)(2,1)S(1)} copy-done((bf16[128,384]{1,0:T(8,128)(2,1)S(1)}, bf16[128,384]{1,0:T(8,128)(2,1)}, u32[]{:S(2)}) %copy-start) | copy-done | bytes 98328
  0.9 0.0 copy-start.2
  0.9 0.9 %copy-done.2 = bf16[128,384]{1,0:T(8,128)(2,1)S(1)} copy-done((bf16[128,384]{1,0:T(8,128)(2,1)S(1)}, bf16[128,384]{1,0:T(8,128)(2,1)}, u32[]{:S(2)}) %copy-start.2) | copy-done | bytes 98328
  1.8 0.0 copy-start.5
  1.8 0.1 shard_map.82.own_ref
  1.9 0.0 copy-start.8
  1.9 3.0 %collective-permute-start = (f32[8,128]{1,0:T(8,128)S(1)}, f32[8,128]{1,0:T(8,128)S(1)}, u32[]{:S(2)}, u32[]{:S(2)}) collective-permute-start(f32[8,128]{1,0:T(8,128)S(1)} %shard_map.82.own_ref), channel_id=1, source_target_pairs={{0,1},{1,0},{2,3},{3,2},{4,5},{5,4},{6,7},{7,6},{8,9},{9,8},{10,11... | collective-permute-start | bytes 12296 | tf_op jit(solution)/shard_map/ppermute | solution.py:296
  5.0 0.0 copy-done.5
  5.0 2.6 %collective-permute-start.4 = (bf16[128,384]{1,0:T(8,128)(2,1)S(1)}, bf16[128,384]{1,0:T(8,128)(2,1)S(1)}, u32[]{:S(2)}, u32[]{:S(2)}) collective-permute-start(bf16[128,384]{1,0:T(8,128)(2,1)S(1)} %copy-done.5), channel_id=1, source_target_pairs={{0,16},{2,18},{4,20},{6,22},{8,24},{10,26},{12,28},{14,30},{16,0},... | collective-permute-start | bytes 294920 | tf_op jit(solution)/shard_map/ppermute | solution.py:257
  7.5 1.5 %collective-permute-start.7 = (bf16[128,384]{1,0:T(8,128)(2,1)S(1)}, bf16[128,384]{1,0:T(8,128)(2,1)S(1)}, u32[]{:S(2)}, u32[]{:S(2)}) collective-permute-start(bf16[128,384]{1,0:T(8,128)(2,1)S(1)} %copy-done.5), channel_id=1, source_target_pairs={{0,4},{2,6},{4,0},{6,2},{8,12},{10,14},{12,8},{14,10},{16,20},{18,... | collective-permute-start | bytes 294920 | tf_op jit(solution)/shard_map/ppermute | solution.py:257
  9.0 0.0 copy-done.7
  9.0 0.0 copy-done.8
  9.1 0.0 copy-start.6
  9.1 0.0 collective-permute-done.other_ref
  9.1 0.0 copy-done.1
  9.1 0.1 shard_map.85.refs_0_
  9.2 0.6 %collective-permute-start.2 = (bf16[128,384]{1,0:T(8,128)(2,1)S(1)}, bf16[128,384]{1,0:T(8,128)(2,1)S(1)}, u32[]{:S(2)}, u32[]{:S(2)}) collective-permute-start(bf16[128,384]{1,0:T(8,128)(2,1)S(1)} %shard_map.85.refs_0_), channel_id=1, source_target_pairs={{0,16},{2,18},{4,20},{6,22},{8,24},{10,26},{12,28},{14,30},{16,0},... | collective-permute-start | bytes 294920 | tf_op jit(solution)/shard_map/ppermute | solution.py:257
  9.8 1.5 %collective-permute-start.6 = (bf16[128,384]{1,0:T(8,128)(2,1)S(1)}, bf16[128,384]{1,0:T(8,128)(2,1)S(1)}, u32[]{:S(2)}, u32[]{:S(2)}) collective-permute-start(bf16[128,384]{1,0:T(8,128)(2,1)S(1)} %shard_map.85.refs_0_), channel_id=1, source_target_pairs={{0,4},{2,6},{4,0},{6,2},{8,12},{10,14},{12,8},{14,10},{16,20},{18,... | collective-permute-start | bytes 294920 | tf_op jit(solution)/shard_map/ppermute | solution.py:257
  11.3 0.0 copy-done.6
  11.3 0.1 shard_map.83.own_ref.query_ref
  11.4 1.6 %collective-permute-start.1 = (bf16[144,384]{1,0:T(8,128)(2,1)S(1)}, bf16[144,384]{1,0:T(8,128)(2,1)S(1)}, u32[]{:S(2)}, u32[]{:S(2)}) collective-permute-start(bf16[144,384]{1,0:T(8,128)(2,1)S(1)} %shard_map.83.own_ref.query_ref), channel_id=1, source_target_pairs={{0,8},{2,10},{4,12},{6,14},{8,0},{10,2},{12,4},{14,6},{16,24},{18,... | collective-permute-start | bytes 331784 | tf_op jit(solution)/shard_map/ppermute | solution.py:257
  13.1 0.0 collective-permute-done.4.source_ref
  13.1 2.8 %collective-permute-start.5 = (bf16[128,384]{1,0:T(8,128)(2,1)S(1)}, bf16[128,384]{1,0:T(8,128)(2,1)S(1)}, u32[]{:S(2)}, u32[]{:S(2)}) collective-permute-start(bf16[128,384]{1,0:T(8,128)(2,1)S(1)} %shard_map.86.refs_4_), channel_id=1, source_target_pairs={{0,4},{2,6},{4,0},{6,2},{8,12},{10,14},{12,8},{14,10},{16,20},{18,... | collective-permute-start | bytes 294920 | tf_op jit(solution)/shard_map/ppermute | solution.py:257
  15.9 0.7 %collective-permute-done.2.refs_1_ = bf16[128,384]{1,0:T(8,128)(2,1)S(1)} collective-permute-done((bf16[128,384]{1,0:T(8,128)(2,1)S(1)}, bf16[128,384]{1,0:T(8,128)(2,1)S(1)}, u32[]{:S(2)}, u32[]{:S(2)}) %collective-permute-start.2) | collective-permute-done | bytes 98336 | tf_op jit(solution)/shard_map/ppermute | solution.py:257
  16.5 1.4 %collective-permute-start.3 = (bf16[128,384]{1,0:T(8,128)(2,1)S(1)}, bf16[128,384]{1,0:T(8,128)(2,1)S(1)}, u32[]{:S(2)}, u32[]{:S(2)}) collective-permute-start(bf16[128,384]{1,0:T(8,128)(2,1)S(1)} %collective-permute-done.2.refs_1_), channel_id=1, source_target_pairs={{0,4},{2,6},{4,0},{6,2},{8,12},{10,14},{12,8},{14,10},{16,20},{18,... | collective-permute-start | bytes 294920 | tf_op jit(solution)/shard_map/ppermute | solution.py:257
  18.0 0.0 collective-permute-done.7.refs_5_
  18.0 0.0 collective-permute-done.6.refs_2_
  18.0 0.1 shard_map.87.pack_ref
  18.0 0.1 collective-permute-start.9
  18.1 0.0 collective-permute-done.1.remote_ref.query_ref
  18.1 0.1 shard_map.84.bias_ref
  18.2 0.6 %shard_map.88 = (f32[256,384]{1,0:T(8,128)S(1)}, f32[256,768]{1,0:T(8,128)S(1)}) custom-call(bf16[144,384]{1,0:T(8,128)(2,1)S(1)} %shard_map.83.own_ref.query_ref, bf16[144,384]{1,0:T(8,128)(2,1)S(1)} %collective-permute-done.1.remote_ref.query_ref, f32[16,1024]{1,0:T(8,128)S(1)} %shard_map.84.bias_ref, bf16[768,384]{1,0:T(8,128)(2,1)S(1)} %shard_map.87.pack_ref), custom_call_target="tpu_custom_call" | custom-call | tf_op jit(solution)/shard_map/pallas_call | solution.py:357
  18.8 0.0 collective-permute-done.5.refs_1_
  18.8 2.3 %collective-permute-done.3.refs_0_ = bf16[128,384]{1,0:T(8,128)(2,1)S(1)} collective-permute-done((bf16[128,384]{1,0:T(8,128)(2,1)S(1)}, bf16[128,384]{1,0:T(8,128)(2,1)S(1)}, u32[]{:S(2)}, u32[]{:S(2)}) %collective-permute-start.3) | collective-permute-done | bytes 98336 | tf_op jit(solution)/shard_map/ppermute | solution.py:257
  21.2 0.1 collective-permute-start.8
  21.3 0.0 collective-permute-done.9.pack_ref
  21.3 0.7 %shard_map.90 = (f32[256,384]{1,0:T(8,128)S(1)}, f32[256,768]{1,0:T(8,128)S(1)}) custom-call(bf16[144,384]{1,0:T(8,128)(2,1)S(1)} %shard_map.83.own_ref.query_ref, bf16[144,384]{1,0:T(8,128)(2,1)S(1)} %collective-permute-done.1.remote_ref.query_ref, f32[16,1024]{1,0:T(8,128)S(1)} %shard_map.84.bias_ref, ...), custom_call_target="tpu_custom_call" | custom-call | tf_op jit(solution)/shard_map/pallas_call | solution.py:357
  21.9 0.5 %shard_map.91 = (f32[256,384]{1,0:T(8,128)S(1)}, f32[256,768]{1,0:T(8,128)S(1)}) custom-call(bf16[144,384]{1,0:T(8,128)(2,1)S(1)} %shard_map.83.own_ref.query_ref, bf16[144,384]{1,0:T(8,128)(2,1)S(1)} %collective-permute-done.1.remote_ref.query_ref, f32[16,1024]{1,0:T(8,128)S(1)} %shard_map.84.bias_ref, bf16[256,384]{1,0:T(8,128)(2,1)S(1)} %shard_map.89.pack_ref, ...), custom_call_target="tpu_custom_call" | custom-call | tf_op jit(solution)/shard_map/pallas_call | solution.py:357
  22.4 0.3 collective-permute-done.8.pack_ref
  22.7 0.5 %shard_map.93 = bf16[144,384]{1,0:T(8,128)(2,1)S(1)} custom-call(bf16[144,384]{1,0:T(8,128)(2,1)S(1)} %collective-permute-done.1.remote_ref.query_ref, f32[16,1024]{1,0:T(8,128)S(1)} %shard_map.84.bias_ref, bf16[256,384]{1,0:T(8,128)(2,1)S(1)} %collective-permute-done.8.pack_ref, f32[256,384]{1,0:T(8,128)S(1)} %get-tuple-element.17.context_ref, ...), custom_call_target="tpu_custom_call" | custom-call | tf_op jit(solution)/shard_map/pallas_call | solution.py:380
  23.1 1.1 %collective-permute-start.10 = (bf16[144,384]{1,0:T(8,128)(2,1)S(1)}, bf16[144,384]{1,0:T(8,128)(2,1)S(1)}, u32[]{:S(2)}, u32[]{:S(2)}) collective-permute-start(bf16[144,384]{1,0:T(8,128)(2,1)S(1)} %shard_map.93), channel_id=1, source_target_pairs={{0,8},{2,10},{4,12},{6,14},{8,0},{10,2},{12,4},{14,6},{16,24},{18,... | collective-permute-start | bytes 331784 | tf_op jit(solution)/shard_map/ppermute | solution.py:257
  24.3 0.0 copy-done.3
  24.3 0.0 copy-done.4
  24.3 0.6 %shard_map.94.gate_ref = f32[16,384]{1,0:T(8,128)S(1)} custom-call(s32[2]{0:T(128)S(1)} %copy-done.4, f32[50,384]{1,0:T(8,128)S(1)} %copy-done.3), custom_call_target="tpu_custom_call" | custom-call | tf_op jit(solution)/shard_map/pallas_call | solution.py:396
  24.9 0.4 %shard_map.92 = (f32[128,384]{1,0:T(8,128)S(1)}, f32[16,384]{1,0:T(8,128)S(1)}) custom-call(bf16[144,384]{1,0:T(8,128)(2,1)S(1)} %shard_map.83.own_ref.query_ref, f32[16,1024]{1,0:T(8,128)S(1)} %shard_map.84.bias_ref, bf16[256,384]{1,0:T(8,128)(2,1)S(1)} %collective-permute-done.8.pack_ref, f32[256,384]{1,0:T(8,128)S(1)} %get-tuple-element.17.context_ref, ...), custom_call_target="tpu_custom_call" | custom-call | tf_op jit(solution)/shard_map/pallas_call | solution.py:380
  25.3 3.1 %collective-permute-done.10.packet_ref = bf16[144,384]{1,0:T(8,128)(2,1)S(1)} collective-permute-done((bf16[144,384]{1,0:T(8,128)(2,1)S(1)}, bf16[144,384]{1,0:T(8,128)(2,1)S(1)}, u32[]{:S(2)}, u32[]{:S(2)}) %collective-permute-start.10) | collective-permute-done | bytes 110624 | tf_op jit(solution)/shard_map/ppermute | solution.py:257
  28.4 0.8 %shard_map.95 = bf16[128,384]{1,0:T(8,128)(2,1)} custom-call(f32[128,384]{1,0:T(8,128)S(1)} %get-tuple-element.19.own_ref, f32[16,384]{1,0:T(8,128)S(1)} %get-tuple-element.20.lines_ref, bf16[144,384]{1,0:T(8,128)(2,1)S(1)} %collective-permute-done.10.packet_ref, f32[16,384]{1,0:T(8,128)S(1)} %shard_map.94.gate_ref), custom_call_target="tpu_custom_call" | custom-call | tf_op jit(solution)/shard_map/pallas_call | solution.py:405
  (8 shorter events, 0.0 us)
Async XLA Ops:
  0.0 0.9 %copy-start = (bf16[128,384]{1,0:T(8,128)(2,1)S(1)}, bf16[128,384]{1,0:T(8,128)(2,1)}, u32[]{:S(2)}) copy-start(bf16[128,384]{1,0:T(8,128)(2,1)} %key_ref.3) | copy-start | bytes 294916
  0.9 0.9 %copy-start.2 = (bf16[128,384]{1,0:T(8,128)(2,1)S(1)}, bf16[128,384]{1,0:T(8,128)(2,1)}, u32[]{:S(2)}) copy-start(bf16[128,384]{1,0:T(8,128)(2,1)} %query_ref.3) | copy-start | bytes 294916
  1.8 3.2 %copy-start.5 = (bf16[128,384]{1,0:T(8,128)(2,1)S(1)}, bf16[128,384]{1,0:T(8,128)(2,1)}, u32[]{:S(2)}) copy-start(bf16[128,384]{1,0:T(8,128)(2,1)} %refs_3_.1) | copy-start | bytes 294916
  1.8 7.2 %copy-start.7 = (f32[384]{0:T(512)S(1)}, f32[384]{0:T(512)}, u32[]{:S(2)}) copy-start(f32[384]{0:T(512)} %param.11) | copy-start | bytes 4612
  1.8 7.3 %copy-start.1 = (bf16[128,384]{1,0:T(8,128)(2,1)S(1)}, bf16[128,384]{1,0:T(8,128)(2,1)}, u32[]{:S(2)}) copy-start(bf16[128,384]{1,0:T(8,128)(2,1)} %key_ref.3) | copy-start | bytes 294916
  1.9 7.1 %copy-start.8 = (f32[384]{0:T(512)S(1)}, f32[384]{0:T(512)}, u32[]{:S(2)}) copy-start(f32[384]{0:T(512)} %param.12) | copy-start | bytes 4612
  1.9 7.1 %collective-permute-start = (f32[8,128]{1,0:T(8,128)S(1)}, f32[8,128]{1,0:T(8,128)S(1)}, u32[]{:S(2)}, u32[]{:S(2)}) collective-permute-start(f32[8,128]{1,0:T(8,128)S(1)} %shard_map.82.own_ref), channel_id=1, source_target_pairs={{0,1},{1,0},{2,3},{3,2},{4,5},{5,4},{6,7},{7,6},{8,9},{9,8},{10,11... | collective-permute-start | bytes 12296 | tf_op jit(solution)/shard_map/ppermute | solution.py:296
  5.0 8.1 %collective-permute-start.4 = (bf16[128,384]{1,0:T(8,128)(2,1)S(1)}, bf16[128,384]{1,0:T(8,128)(2,1)S(1)}, u32[]{:S(2)}, u32[]{:S(2)}) collective-permute-start(bf16[128,384]{1,0:T(8,128)(2,1)S(1)} %copy-done.5), channel_id=1, source_target_pairs={{0,16},{2,18},{4,20},{6,22},{8,24},{10,26},{12,28},{14,30},{16,0},... | collective-permute-start | bytes 294920 | tf_op jit(solution)/shard_map/ppermute | solution.py:257
  7.5 10.4 %collective-permute-start.7 = (bf16[128,384]{1,0:T(8,128)(2,1)S(1)}, bf16[128,384]{1,0:T(8,128)(2,1)S(1)}, u32[]{:S(2)}, u32[]{:S(2)}) collective-permute-start(bf16[128,384]{1,0:T(8,128)(2,1)S(1)} %copy-done.5), channel_id=1, source_target_pairs={{0,4},{2,6},{4,0},{6,2},{8,12},{10,14},{12,8},{14,10},{16,20},{18,... | collective-permute-start | bytes 294920 | tf_op jit(solution)/shard_map/ppermute | solution.py:257
  9.1 2.3 %copy-start.6 = (s32[1,16]{1,0:T(1,128)S(1)}, s32[1,16]{1,0:T(1,128)}, u32[]{:S(2)}) copy-start(s32[1,16]{1,0:T(1,128)} %far_ref.1) | copy-start | bytes 196
  9.2 7.3 %collective-permute-start.2 = (bf16[128,384]{1,0:T(8,128)(2,1)S(1)}, bf16[128,384]{1,0:T(8,128)(2,1)S(1)}, u32[]{:S(2)}, u32[]{:S(2)}) collective-permute-start(bf16[128,384]{1,0:T(8,128)(2,1)S(1)} %shard_map.85.refs_0_), channel_id=1, source_target_pairs={{0,16},{2,18},{4,20},{6,22},{8,24},{10,26},{12,28},{14,30},{16,0},... | collective-permute-start | bytes 294920 | tf_op jit(solution)/shard_map/ppermute | solution.py:257
  9.8 8.2 %collective-permute-start.6 = (bf16[128,384]{1,0:T(8,128)(2,1)S(1)}, bf16[128,384]{1,0:T(8,128)(2,1)S(1)}, u32[]{:S(2)}, u32[]{:S(2)}) collective-permute-start(bf16[128,384]{1,0:T(8,128)(2,1)S(1)} %shard_map.85.refs_0_), channel_id=1, source_target_pairs={{0,4},{2,6},{4,0},{6,2},{8,12},{10,14},{12,8},{14,10},{16,20},{18,... | collective-permute-start | bytes 294920 | tf_op jit(solution)/shard_map/ppermute | solution.py:257
  11.4 6.7 %collective-permute-start.1 = (bf16[144,384]{1,0:T(8,128)(2,1)S(1)}, bf16[144,384]{1,0:T(8,128)(2,1)S(1)}, u32[]{:S(2)}, u32[]{:S(2)}) collective-permute-start(bf16[144,384]{1,0:T(8,128)(2,1)S(1)} %shard_map.83.own_ref.query_ref), channel_id=1, source_target_pairs={{0,8},{2,10},{4,12},{6,14},{8,0},{10,2},{12,4},{14,6},{16,24},{18,... | collective-permute-start | bytes 331784 | tf_op jit(solution)/shard_map/ppermute | solution.py:257
  13.1 5.7 %collective-permute-start.5 = (bf16[128,384]{1,0:T(8,128)(2,1)S(1)}, bf16[128,384]{1,0:T(8,128)(2,1)S(1)}, u32[]{:S(2)}, u32[]{:S(2)}) collective-permute-start(bf16[128,384]{1,0:T(8,128)(2,1)S(1)} %shard_map.86.refs_4_), channel_id=1, source_target_pairs={{0,4},{2,6},{4,0},{6,2},{8,12},{10,14},{12,8},{14,10},{16,20},{18,... | collective-permute-start | bytes 294920 | tf_op jit(solution)/shard_map/ppermute | solution.py:257
  16.5 4.6 %collective-permute-start.3 = (bf16[128,384]{1,0:T(8,128)(2,1)S(1)}, bf16[128,384]{1,0:T(8,128)(2,1)S(1)}, u32[]{:S(2)}, u32[]{:S(2)}) collective-permute-start(bf16[128,384]{1,0:T(8,128)(2,1)S(1)} %collective-permute-done.2.refs_1_), channel_id=1, source_target_pairs={{0,4},{2,6},{4,0},{6,2},{8,12},{10,14},{12,8},{14,10},{16,20},{18,... | collective-permute-start | bytes 294920 | tf_op jit(solution)/shard_map/ppermute | solution.py:257
  18.0 3.2 %collective-permute-start.9 = (bf16[768,384]{1,0:T(8,128)(2,1)S(1)}, bf16[768,384]{1,0:T(8,128)(2,1)S(1)}, u32[]{:S(2)}, u32[]{:S(2)}) collective-permute-start(bf16[768,384]{1,0:T(8,128)(2,1)S(1)} %shard_map.87.pack_ref), channel_id=1, source_target_pairs={{0,2},{2,0},{4,6},{6,4},{8,10},{10,8},{12,14},{14,12},{16,18},{18,... | collective-permute-start | bytes 1769480 | tf_op jit(solution)/shard_map/ppermute | solution.py:257
  21.2 1.5 %collective-permute-start.8 = (bf16[256,384]{1,0:T(8,128)(2,1)S(1)}, bf16[256,384]{1,0:T(8,128)(2,1)S(1)}, u32[]{:S(2)}, u32[]{:S(2)}) collective-permute-start(bf16[256,384]{1,0:T(8,128)(2,1)S(1)} %shard_map.89.pack_ref), channel_id=1, source_target_pairs={{0,2},{2,0},{4,6},{6,4},{8,10},{10,8},{12,14},{14,12},{16,18},{18,... | collective-permute-start | bytes 589832 | tf_op jit(solution)/shard_map/ppermute | solution.py:257
  22.7 1.6 %copy-start.3 = (f32[50,384]{1,0:T(8,128)S(1)}, f32[50,384]{1,0:T(8,128)}, u32[]{:S(2)}) copy-start(f32[50,384]{1,0:T(8,128)} %table_ref.1) | copy-start | bytes 230404
  22.7 1.6 %copy-start.4 = (s32[2]{0:T(128)S(1)}, s32[2]{0:T(128)}, u32[]{:S(2)}) copy-start(s32[2]{0:T(128)} %step_ref.1) | copy-start | bytes 28
  23.1 5.3 %collective-permute-start.10 = (bf16[144,384]{1,0:T(8,128)(2,1)S(1)}, bf16[144,384]{1,0:T(8,128)(2,1)S(1)}, u32[]{:S(2)}, u32[]{:S(2)}) collective-permute-start(bf16[144,384]{1,0:T(8,128)(2,1)S(1)} %shard_map.93), channel_id=1, source_target_pairs={{0,8},{2,10},{4,12},{6,14},{8,0},{10,2},{12,4},{14,6},{16,24},{18,... | collective-permute-start | bytes 331784 | tf_op jit(solution)/shard_map/ppermute | solution.py:257

commit v19 on v17

--- a/solution.py
+++ b/solution.py
@@ -23,21 +23,6 @@
 
 def spread(row):
     return jnp.broadcast_to(row, (row.shape[1], row.shape[1])).T
-
-
-def squares(source_ref):
-    wide = source_ref[:HD, :].astype(jnp.float32)
-    square = wide * wide
-    part = square[:, :HD]
-    for low in range(HD, square.shape[1], HD):
-        part = part + square[:, low : low + HD]
-    return jnp.sum(part.T, axis=0, keepdims=True)
-
-
-def sums_kernel(query_ref, key_ref, out_ref):
-    out_ref[...] = jnp.zeros_like(out_ref)
-    out_ref[0:1, :] = squares(query_ref)
-    out_ref[1:2, :] = squares(key_ref)
 
 
 def factor_of(line, full_width):
@@ -285,13 +270,10 @@
 
     far = bits[0]
     far_value = exchange(value_proj, far)
-    sums = pl.pallas_call(
-        sums_kernel,
-        out_shape=jax.ShapeDtypeStruct((8, rows), jnp.float32),
-        in_specs=[VMEM] * 2,
-        out_specs=VMEM,
-        compiler_params=params,
-    )(query_proj, key_proj)
+    query_f, key_f = query_proj.astype(jnp.float32), key_proj.astype(jnp.float32)
+    sums = jnp.stack(
+        [jnp.sum(query_f * query_f, axis=-1), jnp.sum(key_f * key_f, axis=-1)], axis=0
+    )
     if splits == 2:
         others = lax.ppermute(sums, "head", [(0, 1), (1, 0)])
     else:

time: 28.6 us -> 27.7 us (0.969)
  local copies, waits for them, and re-layouts: 1.82 us -> 0.04 us
  other arithmetic: 0 us -> 1.11 us
    unnamed x18 -> x16, local copies, waits for them, and re-layouts: 1.82 us -> 0.04 us
    reduce_sum x0 -> x2, other arithmetic: none -> 1.1 us  [the longest x1 1 us: local(): jnp.sum(query_f * query_f, axis=-1)]
  transfers between devices with their start and end apart: 11 -> 11, of which waited for: 6 -> 6; matrix products, arithmetic and copies ran while one was open for 0% -> 4% of each run, Pallas kernels for 11% -> 11%
where the time goes in v19:
time: 27.7 us; the launch traced here: 27.6 us
  starting transfers between devices  15.1 us (55%)
  waiting for transfers between devices  6.75 us (24%)
  Pallas kernels  4.42 us (16%)
  other arithmetic  1.11 us (4%)
    ppermute x10, starting transfers between devices, exchange(): return lax.ppermute(array, 'tm', [(i, i ^ mask) for i in range(count)])  13.5 us
    ppermute x10, waiting for transfers between devices, exchange(): return lax.ppermute(array, 'tm', [(i, i ^ mask) for i in range(count)])  6.23 us
    pallas_call x3, Pallas kernels, step(): pl.pallas_call(functools.partial(step_kernel, first), out_shape=[jax.Shap...  1.69 us
    ppermute x1, starting transfers between devices, local(): others = lax.ppermute(sums, 'head', [(0, 1), (1, 0)])  1.58 us
    reduce_sum x1, other arithmetic, local(): jnp.sum(query_f * query_f, axis=-1)  1 us
    pallas_call x2, Pallas kernels, last(): pl.pallas_call(functools.partial(last_attention, place), out_shape=out_sh...  0.9 us
    pallas_call x1, Pallas kernels, local(): pl.pallas_call(merge_kernel, out_shape=jax.ShapeDtypeStruct((rows, width)...  0.85 us
    pallas_call x1, Pallas kernels, local(): pl.pallas_call(gate_kernel, out_shape=jax.ShapeDtypeStruct((16, width), j...  0.57 us
  transfers between devices with their start and end apart: 11, of which 6 were waited for; matrix products, arithmetic and copies ran while one was open for 4% of the time, Pallas kernels for 11%

profile of v19, /device:TPU:0, one launch (start us, length us, event | category | flops | bytes accessed | tf_op | source)
XLA Modules:
  0.0 27.6 jit_solution(16556566275873475060)
XLA Ops:
  0.0 0.0 copy-start
  0.0 4.0 %collective-permute-start.4 = (bf16[128,384]{1,0:T(8,128)(2,1)}, bf16[128,384]{1,0:T(8,128)(2,1)S(1)}, u32[]{:S(2)}, u32[]{:S(2)}) collective-permute-start(bf16[128,384]{1,0:T(8,128)(2,1)} %refs_3_.1), channel_id=1, source_target_pairs={{0,16},{2,18},{4,20},{6,22},{8,24},{10,26},{12,28},{14,30},{16,0},... | collective-permute-start | bytes 294920 | tf_op jit(solution)/shard_map/ppermute | solution.py:242
  4.0 1.0 %multiply_reduce_fusion.1 = f32[128]{0:T(128)S(1)} fusion(bf16[128,384]{1,0:T(8,128)(2,1)} %query_ref.1), kind=kLoop, calls=%fused_computation.1 | loop fusion | flops 147328 | bytes 98816 | tf_op jit(solution)/shard_map/reduce_sum | solution.py:275
  5.0 0.0 copy-done
  5.1 0.1 multiply_reduce_fusion
  5.2 0.0 copy-start.6
  5.2 0.0 copy-start.7
  5.2 1.6 %collective-permute-start = (f32[2,128]{1,0:T(2,128)S(1)}, f32[2,128]{1,0:T(2,128)S(1)}, u32[]{:S(2)}, u32[]{:S(2)}) collective-permute-start(f32[2,128]{1,0:T(2,128)S(1)} %pad_maximum_fusion.own_ref), channel_id=1, source_target_pairs={{0,1},{1,0},{2,3},{3,2},{4,5},{5,4},{6,7},{7,6},{8,9},{9,8},{10,11... | collective-permute-start | bytes 3080 | tf_op jit(solution)/shard_map/ppermute | solution.py:278
  6.8 0.0 copy-done.2
  6.8 1.5 %collective-permute-start.7 = (bf16[128,384]{1,0:T(8,128)(2,1)S(1)}, bf16[128,384]{1,0:T(8,128)(2,1)S(1)}, u32[]{:S(2)}, u32[]{:S(2)}) collective-permute-start(bf16[128,384]{1,0:T(8,128)(2,1)S(1)} %copy-done.2), channel_id=1, source_target_pairs={{0,4},{2,6},{4,0},{6,2},{8,12},{10,14},{12,8},{14,10},{16,20},{18,... | collective-permute-start | bytes 294920 | tf_op jit(solution)/shard_map/ppermute | solution.py:242
  8.3 0.0 copy-done.6
  8.3 0.0 copy-done.7
  8.3 0.0 copy-start.1
  8.3 0.0 copy-start.5
  8.3 0.5 %collective-permute-done.other_ref = f32[2,128]{1,0:T(2,128)S(1)} collective-permute-done((f32[2,128]{1,0:T(2,128)S(1)}, f32[2,128]{1,0:T(2,128)S(1)}, u32[]{:S(2)}, u32[]{:S(2)}) %collective-permute-start) | collective-permute-done | bytes 1056 | tf_op jit(solution)/shard_map/ppermute | solution.py:278
  8.8 0.1 shard_map.84.refs_0_
  9.0 0.1 collective-permute-start.2
  9.1 1.8 %collective-permute-start.6 = (bf16[128,384]{1,0:T(8,128)(2,1)S(1)}, bf16[128,384]{1,0:T(8,128)(2,1)S(1)}, u32[]{:S(2)}, u32[]{:S(2)}) collective-permute-start(bf16[128,384]{1,0:T(8,128)(2,1)S(1)} %shard_map.84.refs_0_), channel_id=1, source_target_pairs={{0,4},{2,6},{4,0},{6,2},{8,12},{10,14},{12,8},{14,10},{16,20},{18,... | collective-permute-start | bytes 294920 | tf_op jit(solution)/shard_map/ppermute | solution.py:242
  10.8 0.0 copy-done.1
  10.9 0.0 copy-done.5
  10.9 0.1 shard_map.82.own_ref.query_ref
  11.0 1.6 %collective-permute-start.1 = (bf16[144,384]{1,0:T(8,128)(2,1)S(1)}, bf16[144,384]{1,0:T(8,128)(2,1)S(1)}, u32[]{:S(2)}, u32[]{:S(2)}) collective-permute-start(bf16[144,384]{1,0:T(8,128)(2,1)S(1)} %shard_map.82.own_ref.query_ref), channel_id=1, source_target_pairs={{0,8},{2,10},{4,12},{6,14},{8,0},{10,2},{12,4},{14,6},{16,24},{18,... | collective-permute-start | bytes 331784 | tf_op jit(solution)/shard_map/ppermute | solution.py:242
  12.6 0.0 collective-permute-done.4.source_ref
  12.6 0.6 %collective-permute-start.5 = (bf16[128,384]{1,0:T(8,128)(2,1)S(1)}, bf16[128,384]{1,0:T(8,128)(2,1)S(1)}, u32[]{:S(2)}, u32[]{:S(2)}) collective-permute-start(bf16[128,384]{1,0:T(8,128)(2,1)S(1)} %shard_map.85.refs_4_), channel_id=1, source_target_pairs={{0,4},{2,6},{4,0},{6,2},{8,12},{10,14},{12,8},{14,10},{16,20},{18,... | collective-permute-start | bytes 294920 | tf_op jit(solution)/shard_map/ppermute | solution.py:242
  13.2 1.3 %collective-permute-done.2.refs_1_ = bf16[128,384]{1,0:T(8,128)(2,1)S(1)} collective-permute-done((bf16[128,384]{1,0:T(8,128)(2,1)S(1)}, bf16[128,384]{1,0:T(8,128)(2,1)S(1)}, u32[]{:S(2)}, u32[]{:S(2)}) %collective-permute-start.2) | collective-permute-done | bytes 98336 | tf_op jit(solution)/shard_map/ppermute | solution.py:242
  14.5 1.6 %collective-permute-start.3 = (bf16[128,384]{1,0:T(8,128)(2,1)S(1)}, bf16[128,384]{1,0:T(8,128)(2,1)S(1)}, u32[]{:S(2)}, u32[]{:S(2)}) collective-permute-start(bf16[128,384]{1,0:T(8,128)(2,1)S(1)} %collective-permute-done.2.refs_1_), channel_id=1, source_target_pairs={{0,4},{2,6},{4,0},{6,2},{8,12},{10,14},{12,8},{14,10},{16,20},{18,... | collective-permute-start | bytes 294920 | tf_op jit(solution)/shard_map/ppermute | solution.py:242
  16.1 0.0 collective-permute-done.7.refs_5_
  16.1 0.0 collective-permute-done.6.refs_2_
  16.1 0.1 shard_map.86.pack_ref
  16.2 0.1 collective-permute-start.9
  16.3 0.0 collective-permute-done.1.remote_ref.query_ref
  16.3 0.1 shard_map.83.bias_ref
  16.4 0.6 %shard_map.87 = (f32[256,384]{1,0:T(8,128)S(1)}, f32[256,768]{1,0:T(8,128)S(1)}) custom-call(bf16[144,384]{1,0:T(8,128)(2,1)S(1)} %shard_map.82.own_ref.query_ref, bf16[144,384]{1,0:T(8,128)(2,1)S(1)} %collective-permute-done.1.remote_ref.query_ref, f32[16,1024]{1,0:T(8,128)S(1)} %shard_map.83.bias_ref, bf16[768,384]{1,0:T(8,128)(2,1)S(1)} %shard_map.86.pack_ref), custom_call_target="tpu_custom_call" | custom-call | tf_op jit(solution)/shard_map/pallas_call | solution.py:338
  17.0 1.0 %collective-permute-done.5.refs_1_ = bf16[128,384]{1,0:T(8,128)(2,1)S(1)} collective-permute-done((bf16[128,384]{1,0:T(8,128)(2,1)S(1)}, bf16[128,384]{1,0:T(8,128)(2,1)S(1)}, u32[]{:S(2)}, u32[]{:S(2)}) %collective-permute-start.5) | collective-permute-done | bytes 98336 | tf_op jit(solution)/shard_map/ppermute | solution.py:242
  17.9 1.2 %collective-permute-done.3.refs_0_ = bf16[128,384]{1,0:T(8,128)(2,1)S(1)} collective-permute-done((bf16[128,384]{1,0:T(8,128)(2,1)S(1)}, bf16[128,384]{1,0:T(8,128)(2,1)S(1)}, u32[]{:S(2)}, u32[]{:S(2)}) %collective-permute-start.3) | collective-permute-done | bytes 98336 | tf_op jit(solution)/shard_map/ppermute | solution.py:242
  19.2 0.1 collective-permute-start.8
  19.3 0.0 collective-permute-done.9.pack_ref
  19.3 0.6 %shard_map.89 = (f32[256,384]{1,0:T(8,128)S(1)}, f32[256,768]{1,0:T(8,128)S(1)}) custom-call(bf16[144,384]{1,0:T(8,128)(2,1)S(1)} %shard_map.82.own_ref.query_ref, bf16[144,384]{1,0:T(8,128)(2,1)S(1)} %collective-permute-done.1.remote_ref.query_ref, f32[16,1024]{1,0:T(8,128)S(1)} %shard_map.83.bias_ref, ...), custom_call_target="tpu_custom_call" | custom-call | tf_op jit(solution)/shard_map/pallas_call | solution.py:338
  19.9 0.5 %shard_map.90 = (f32[256,384]{1,0:T(8,128)S(1)}, f32[256,768]{1,0:T(8,128)S(1)}) custom-call(bf16[144,384]{1,0:T(8,128)(2,1)S(1)} %shard_map.82.own_ref.query_ref, bf16[144,384]{1,0:T(8,128)(2,1)S(1)} %collective-permute-done.1.remote_ref.query_ref, f32[16,1024]{1,0:T(8,128)S(1)} %shard_map.83.bias_ref, bf16[256,384]{1,0:T(8,128)(2,1)S(1)} %shard_map.88.pack_ref, ...), custom_call_target="tpu_custom_call" | custom-call | tf_op jit(solution)/shard_map/pallas_call | solution.py:338
  20.4 0.3 %collective-permute-done.8.pack_ref = bf16[256,384]{1,0:T(8,128)(2,1)S(1)} collective-permute-done((bf16[256,384]{1,0:T(8,128)(2,1)S(1)}, bf16[256,384]{1,0:T(8,128)(2,1)S(1)}, u32[]{:S(2)}, u32[]{:S(2)}) %collective-permute-start.8) | collective-permute-done | bytes 196640 | tf_op jit(solution)/shard_map/ppermute | solution.py:242
  20.7 0.5 %shard_map.92 = bf16[144,384]{1,0:T(8,128)(2,1)S(1)} custom-call(bf16[144,384]{1,0:T(8,128)(2,1)S(1)} %collective-permute-done.1.remote_ref.query_ref, f32[16,1024]{1,0:T(8,128)S(1)} %shard_map.83.bias_ref, bf16[256,384]{1,0:T(8,128)(2,1)S(1)} %collective-permute-done.8.pack_ref, f32[256,384]{1,0:T(8,128)S(1)} %get-tuple-element.17.context_ref, ...), custom_call_target="tpu_custom_call" | custom-call | tf_op jit(solution)/shard_map/pallas_call | solution.py:361
  21.2 2.1 %collective-permute-start.10 = (bf16[144,384]{1,0:T(8,128)(2,1)S(1)}, bf16[144,384]{1,0:T(8,128)(2,1)S(1)}, u32[]{:S(2)}, u32[]{:S(2)}) collective-permute-start(bf16[144,384]{1,0:T(8,128)(2,1)S(1)} %shard_map.92), channel_id=1, source_target_pairs={{0,8},{2,10},{4,12},{6,14},{8,0},{10,2},{12,4},{14,6},{16,24},{18,... | collective-permute-start | bytes 331784 | tf_op jit(solution)/shard_map/ppermute | solution.py:242
  23.3 0.0 copy-done.3
  23.3 0.0 copy-done.4
  23.3 0.6 %shard_map.93.gate_ref = f32[16,384]{1,0:T(8,128)S(1)} custom-call(s32[2]{0:T(128)S(1)} %copy-done.4, f32[50,384]{1,0:T(8,128)S(1)} %copy-done.3), custom_call_target="tpu_custom_call" | custom-call | tf_op jit(solution)/shard_map/pallas_call | solution.py:377
  23.9 0.4 %shard_map.91 = (f32[128,384]{1,0:T(8,128)S(1)}, f32[16,384]{1,0:T(8,128)S(1)}) custom-call(bf16[144,384]{1,0:T(8,128)(2,1)S(1)} %shard_map.82.own_ref.query_ref, f32[16,1024]{1,0:T(8,128)S(1)} %shard_map.83.bias_ref, bf16[256,384]{1,0:T(8,128)(2,1)S(1)} %collective-permute-done.8.pack_ref, f32[256,384]{1,0:T(8,128)S(1)} %get-tuple-element.17.context_ref, ...), custom_call_target="tpu_custom_call" | custom-call | tf_op jit(solution)/shard_map/pallas_call | solution.py:361
  24.3 2.4 %collective-permute-done.10.packet_ref = bf16[144,384]{1,0:T(8,128)(2,1)S(1)} collective-permute-done((bf16[144,384]{1,0:T(8,128)(2,1)S(1)}, bf16[144,384]{1,0:T(8,128)(2,1)S(1)}, u32[]{:S(2)}, u32[]{:S(2)}) %collective-permute-start.10) | collective-permute-done | bytes 110624 | tf_op jit(solution)/shard_map/ppermute | solution.py:242
  26.7 0.8 %shard_map.94 = bf16[128,384]{1,0:T(8,128)(2,1)} custom-call(f32[128,384]{1,0:T(8,128)S(1)} %get-tuple-element.19.own_ref, f32[16,384]{1,0:T(8,128)S(1)} %get-tuple-element.20.lines_ref, bf16[144,384]{1,0:T(8,128)(2,1)S(1)} %collective-permute-done.10.packet_ref, f32[16,384]{1,0:T(8,128)S(1)} %shard_map.93.gate_ref), custom_call_target="tpu_custom_call" | custom-call | tf_op jit(solution)/shard_map/pallas_call | solution.py:386
  (8 shorter events, 0.0 us)
Async XLA Ops:
  0.0 5.0 %copy-start = (bf16[128,384]{1,0:T(8,128)(2,1)S(1)}, bf16[128,384]{1,0:T(8,128)(2,1)}, u32[]{:S(2)}) copy-start(bf16[128,384]{1,0:T(8,128)(2,1)} %key_ref.1) | copy-start | bytes 294916
  0.0 6.8 %copy-start.2 = (bf16[128,384]{1,0:T(8,128)(2,1)S(1)}, bf16[128,384]{1,0:T(8,128)(2,1)}, u32[]{:S(2)}) copy-start(bf16[128,384]{1,0:T(8,128)(2,1)} %refs_3_.1) | copy-start | bytes 294916
  0.0 12.6 %collective-permute-start.4 = (bf16[128,384]{1,0:T(8,128)(2,1)}, bf16[128,384]{1,0:T(8,128)(2,1)S(1)}, u32[]{:S(2)}, u32[]{:S(2)}) collective-permute-start(bf16[128,384]{1,0:T(8,128)(2,1)} %refs_3_.1), channel_id=1, source_target_pairs={{0,16},{2,18},{4,20},{6,22},{8,24},{10,26},{12,28},{14,30},{16,0},... | collective-permute-start | bytes 294920 | tf_op jit(solution)/shard_map/ppermute | solution.py:242
  5.2 3.1 %copy-start.6 = (f32[384]{0:T(512)S(1)}, f32[384]{0:T(512)}, u32[]{:S(2)}) copy-start(f32[384]{0:T(512)} %param.11) | copy-start | bytes 4612
  5.2 3.1 %copy-start.7 = (f32[384]{0:T(512)S(1)}, f32[384]{0:T(512)}, u32[]{:S(2)}) copy-start(f32[384]{0:T(512)} %param.12) | copy-start | bytes 4612
  5.2 3.6 %collective-permute-start = (f32[2,128]{1,0:T(2,128)S(1)}, f32[2,128]{1,0:T(2,128)S(1)}, u32[]{:S(2)}, u32[]{:S(2)}) collective-permute-start(f32[2,128]{1,0:T(2,128)S(1)} %pad_maximum_fusion.own_ref), channel_id=1, source_target_pairs={{0,1},{1,0},{2,3},{3,2},{4,5},{5,4},{6,7},{7,6},{8,9},{9,8},{10,11... | collective-permute-start | bytes 3080 | tf_op jit(solution)/shard_map/ppermute | solution.py:278
  6.8 9.3 %collective-permute-start.7 = (bf16[128,384]{1,0:T(8,128)(2,1)S(1)}, bf16[128,384]{1,0:T(8,128)(2,1)S(1)}, u32[]{:S(2)}, u32[]{:S(2)}) collective-permute-start(bf16[128,384]{1,0:T(8,128)(2,1)S(1)} %copy-done.2), channel_id=1, source_target_pairs={{0,4},{2,6},{4,0},{6,2},{8,12},{10,14},{12,8},{14,10},{16,20},{18,... | collective-permute-start | bytes 294920 | tf_op jit(solution)/shard_map/ppermute | solution.py:242
  8.3 2.6 %copy-start.1 = (bf16[128,384]{1,0:T(8,128)(2,1)S(1)}, bf16[128,384]{1,0:T(8,128)(2,1)}, u32[]{:S(2)}) copy-start(bf16[128,384]{1,0:T(8,128)(2,1)} %query_ref.1) | copy-start | bytes 294916
  8.3 2.5 %copy-start.5 = (s32[1,16]{1,0:T(1,128)S(1)}, s32[1,16]{1,0:T(1,128)}, u32[]{:S(2)}) copy-start(s32[1,16]{1,0:T(1,128)} %far_ref.1) | copy-start | bytes 196
  9.0 5.6 %collective-permute-start.2 = (bf16[128,384]{1,0:T(8,128)(2,1)S(1)}, bf16[128,384]{1,0:T(8,128)(2,1)S(1)}, u32[]{:S(2)}, u32[]{:S(2)}) collective-permute-start(bf16[128,384]{1,0:T(8,128)(2,1)S(1)} %shard_map.84.refs_0_), channel_id=1, source_target_pairs={{0,16},{2,18},{4,20},{6,22},{8,24},{10,26},{12,28},{14,30},{16,0},... | collective-permute-start | bytes 294920 | tf_op jit(solution)/shard_map/ppermute | solution.py:242
  9.1 7.1 %collective-permute-start.6 = (bf16[128,384]{1,0:T(8,128)(2,1)S(1)}, bf16[128,384]{1,0:T(8,128)(2,1)S(1)}, u32[]{:S(2)}, u32[]{:S(2)}) collective-permute-start(bf16[128,384]{1,0:T(8,128)(2,1)S(1)} %shard_map.84.refs_0_), channel_id=1, source_target_pairs={{0,4},{2,6},{4,0},{6,2},{8,12},{10,14},{12,8},{14,10},{16,20},{18,... | collective-permute-start | bytes 294920 | tf_op jit(solution)/shard_map/ppermute | solution.py:242
  11.0 5.3 %collective-permute-start.1 = (bf16[144,384]{1,0:T(8,128)(2,1)S(1)}, bf16[144,384]{1,0:T(8,128)(2,1)S(1)}, u32[]{:S(2)}, u32[]{:S(2)}) collective-permute-start(bf16[144,384]{1,0:T(8,128)(2,1)S(1)} %shard_map.82.own_ref.query_ref), channel_id=1, source_target_pairs={{0,8},{2,10},{4,12},{6,14},{8,0},{10,2},{12,4},{14,6},{16,24},{18,... | collective-permute-start | bytes 331784 | tf_op jit(solution)/shard_map/ppermute | solution.py:242
  12.6 5.3 %collective-permute-start.5 = (bf16[128,384]{1,0:T(8,128)(2,1)S(1)}, bf16[128,384]{1,0:T(8,128)(2,1)S(1)}, u32[]{:S(2)}, u32[]{:S(2)}) collective-permute-start(bf16[128,384]{1,0:T(8,128)(2,1)S(1)} %shard_map.85.refs_4_), channel_id=1, source_target_pairs={{0,4},{2,6},{4,0},{6,2},{8,12},{10,14},{12,8},{14,10},{16,20},{18,... | collective-permute-start | bytes 294920 | tf_op jit(solution)/shard_map/ppermute | solution.py:242
  14.5 4.6 %collective-permute-start.3 = (bf16[128,384]{1,0:T(8,128)(2,1)S(1)}, bf16[128,384]{1,0:T(8,128)(2,1)S(1)}, u32[]{:S(2)}, u32[]{:S(2)}) collective-permute-start(bf16[128,384]{1,0:T(8,128)(2,1)S(1)} %collective-permute-done.2.refs_1_), channel_id=1, source_target_pairs={{0,4},{2,6},{4,0},{6,2},{8,12},{10,14},{12,8},{14,10},{16,20},{18,... | collective-permute-start | bytes 294920 | tf_op jit(solution)/shard_map/ppermute | solution.py:242
  16.2 3.1 %collective-permute-start.9 = (bf16[768,384]{1,0:T(8,128)(2,1)S(1)}, bf16[768,384]{1,0:T(8,128)(2,1)S(1)}, u32[]{:S(2)}, u32[]{:S(2)}) collective-permute-start(bf16[768,384]{1,0:T(8,128)(2,1)S(1)} %shard_map.86.pack_ref), channel_id=1, source_target_pairs={{0,2},{2,0},{4,6},{6,4},{8,10},{10,8},{12,14},{14,12},{16,18},{18,... | collective-permute-start | bytes 1769480 | tf_op jit(solution)/shard_map/ppermute | solution.py:242
  19.2 1.5 %collective-permute-start.8 = (bf16[256,384]{1,0:T(8,128)(2,1)S(1)}, bf16[256,384]{1,0:T(8,128)(2,1)S(1)}, u32[]{:S(2)}, u32[]{:S(2)}) collective-permute-start(bf16[256,384]{1,0:T(8,128)(2,1)S(1)} %shard_map.88.pack_ref), channel_id=1, source_target_pairs={{0,2},{2,0},{4,6},{6,4},{8,10},{10,8},{12,14},{14,12},{16,18},{18,... | collective-permute-start | bytes 589832 | tf_op jit(solution)/shard_map/ppermute | solution.py:242
  20.7 2.6 %copy-start.3 = (f32[50,384]{1,0:T(8,128)S(1)}, f32[50,384]{1,0:T(8,128)}, u32[]{:S(2)}) copy-start(f32[50,384]{1,0:T(8,128)} %table_ref.1) | copy-start | bytes 230404
  20.7 2.6 %copy-start.4 = (s32[2]{0:T(128)S(1)}, s32[2]{0:T(128)}, u32[]{:S(2)}) copy-start(s32[2]{0:T(128)} %step_ref.1) | copy-start | bytes 28
  21.2 5.6 %collective-permute-start.10 = (bf16[144,384]{1,0:T(8,128)(2,1)S(1)}, bf16[144,384]{1,0:T(8,128)(2,1)S(1)}, u32[]{:S(2)}, u32[]{:S(2)}) collective-permute-start(bf16[144,384]{1,0:T(8,128)(2,1)S(1)} %shard_map.92), channel_id=1, source_target_pairs={{0,8},{2,10},{4,12},{6,14},{8,0},{10,2},{12,4},{14,6},{16,24},{18,... | collective-permute-start | bytes 331784 | tf_op jit(solution)/shard_map/ppermute | solution.py:242

commit v20 on v19

--- a/solution.py
+++ b/solution.py
@@ -37,9 +37,15 @@
     return jnp.concatenate(parts, axis=1)
 
 
-def key_kernel(full_width, key_ref, gain_ref, own_ref, other_ref, out_ref):
+def key_kernel(full_width, key_ref, gain_ref, own_ref, other_ref, out_ref, *piece_refs):
     total = own_ref[1:2, :] + other_ref[1:2, :]
-    out_ref[...] = normed(key_ref, factor_of(total, full_width), gain_ref)
+    key = normed(key_ref, factor_of(total, full_width), gain_ref)
+    out_ref[...] = key
+    low = 0
+    for piece_ref in piece_refs:
+        high = low + piece_ref.shape[1]
+        piece_ref[...] = key[:, low:high]
+        low = high
 
 
 def query_kernel(
@@ -80,9 +86,10 @@
     out_ref[...] = source_ref[...]
 
 
-def pack_kernel(held, *refs):
-    for place, source_ref in enumerate(refs[: 2 * held]):
-        refs[-1][place * HD : (place + 1) * HD, :] = source_ref[...]
+def pack_kernel(spots, *refs):
+    for (row, low), source_ref in zip(spots, refs):
+        rows, width = source_ref.shape
+        refs[-1][row : row + rows, low : low + width] = source_ref[...]
 
 
 def absorb(queries, pack_ref, biases, olds):
@@ -269,6 +276,17 @@
     key_gain = key_gain.reshape(1, width)
 
     far = bits[0]
+
+    def copied(source, flops):
+        return pl.pallas_call(
+            copy_kernel,
+            out_shape=jax.ShapeDtypeStruct(source.shape, source.dtype),
+            in_specs=[VMEM],
+            out_specs=VMEM,
+            compiler_params=params,
+            cost_estimate=cost(flops),
+        )(source)
+
     far_value = exchange(value_proj, far)
     query_f, key_f = query_proj.astype(jnp.float32), key_proj.astype(jnp.float32)
     sums = jnp.stack(
@@ -279,11 +297,14 @@
     else:
         sums = lax.psum(sums, "head")
         others = jnp.zeros_like(sums)
-    own_key = pl.pallas_call(
+    piece_widths = [width - HD, HD]
+    own_key, *own_pieces = pl.pallas_call(
         functools.partial(key_kernel, width * splits),
-        out_shape=jax.ShapeDtypeStruct((rows, width), jnp.bfloat16),
+        out_shape=[
+            jax.ShapeDtypeStruct((rows, piece), jnp.bfloat16) for piece in [width] + piece_widths
+        ],
         in_specs=[VMEM] * 4,
-        out_specs=VMEM,
+        out_specs=[VMEM] * 3,
         compiler_params=params,
     )(key_proj, key_gain, sums, others)
     near_values = gathered(value_proj, bits[1:])
@@ -295,19 +316,15 @@
         out_specs=VMEM,
         compiler_params=params,
     )(query_proj, query_gain, far_blocks, sums, others)
-    far_key = exchange(own_key, far)
+    far_pieces = [
+        copied(exchange(piece, far), flops) for piece, flops in zip(own_pieces, (4 * UNIT, 0))
+    ]
     queries = [query_packet, exchange(query_packet, query_mask)]
-    far_value = pl.pallas_call(
-        copy_kernel,
-        out_shape=jax.ShapeDtypeStruct((rows, width), jnp.bfloat16),
-        in_specs=[VMEM],
-        out_specs=VMEM,
-        compiler_params=params,
-        cost_estimate=cost(4 * UNIT),
-    )(far_value)
-    late_keys, late_values = gathered(far_key, bits[1:]), gathered(far_value, bits[1:])
+    far_value = copied(far_value, 4 * UNIT)
+    late_pieces = [gathered(piece, bits[1:]) for piece in far_pieces]
+    late_values = gathered(far_value, bits[1:])
     early = [0, far] + sorted(mask for mask in near_keys if mask)
-    late = sorted(mask ^ far for mask in late_keys if mask)
+    late = sorted(mask ^ far for mask in late_values if mask)
     early_masks = early + [mask ^ 1 for mask in early]
     all_masks = early_masks + late + [mask ^ 1 for mask in late]
     biases = pl.pallas_call(
@@ -319,20 +336,25 @@
     )(*queries)
 
     def packed(keys, values, flops, *after):
-        held = len(keys)
+        spots, sources = [], []
+        for place, parts in enumerate(keys + [[value] for value in values]):
+            low = 0
+            for part in parts:
+                spots.append((place * rows, low))
+                sources.append(part)
+                low += part.shape[1]
         return pl.pallas_call(
-            functools.partial(pack_kernel, held),
-            out_shape=jax.ShapeDtypeStruct((2 * held * rows, width), jnp.bfloat16),
-            in_specs=[VMEM] * (2 * held + len(after)),
+            functools.partial(pack_kernel, spots),
+            out_shape=jax.ShapeDtypeStruct((2 * len(keys) * rows, width), jnp.bfloat16),
+            in_specs=[VMEM] * (len(sources) + len(after)),
             out_specs=VMEM,
             compiler_params=params,
             cost_estimate=cost(flops),
-        )(*keys, *values, *after)
-
-    near_keys[far], near_values[far] = far_key, far_value
-    early_pack = packed(
-        [near_keys[mask] for mask in early], [near_values[mask] for mask in early], 0
-    )
+        )(*sources, *after)
+
+    near_values[far] = far_value
+    early_keys = [far_pieces if mask == far else [near_keys[mask]] for mask in early]
+    early_pack = packed(early_keys, [near_values[mask] for mask in early], 0)
 
     def step(first, pack, *state):
         return pl.pallas_call(
@@ -348,7 +370,7 @@
 
     state = step(0, early_pack)
     late_pack = packed(
-        [late_keys[mask ^ far] for mask in late],
+        [[pieces[mask ^ far] for pieces in late_pieces] for mask in late],
         [late_values[mask ^ far] for mask in late],
         12 * UNIT,
         state[1],

time: 27.7 us -> 29.6 us (1.069)
  starting transfers between devices: 15.1 us -> 17.4 us
  waiting for transfers between devices: 6.75 us -> 6.32 us
    ppermute x10 -> x12, starting transfers between devices: 13.5 us -> 15.8 us  [exchange(): return lax.ppermute(array, 'tm', [(i, i ^ mask) for i in range(count)])]
    ppermute x10 -> x12, waiting for transfers between devices: 6.23 us -> 5.78 us  [exchange(): return lax.ppermute(array, 'tm', [(i, i ^ mask) for i in range(count)])]
  transfers between devices with their start and end apart: 11 -> 13, of which waited for: 6 -> 6; matrix products, arithmetic and copies ran while one was open for 4% -> 4% of each run, Pallas kernels for 11% -> 11%
where the time goes in v20:
time: 29.6 us; the launch traced here: 29.5 us
  starting transfers between devices  17.4 us (59%)
  waiting for transfers between devices  6.32 us (21%)
  Pallas kernels  4.43 us (15%)
  other arithmetic  1.14 us (4%)
    ppermute x12, starting transfers between devices, exchange(): return lax.ppermute(array, 'tm', [(i, i ^ mask) for i in range(count)])  15.8 us
    ppermute x12, waiting for transfers between devices, exchange(): return lax.ppermute(array, 'tm', [(i, i ^ mask) for i in range(count)])  5.78 us
    pallas_call x3, Pallas kernels, step(): pl.pallas_call(functools.partial(step_kernel, first), out_shape=[jax.Shap...  1.69 us
    ppermute x1, starting transfers between devices, local(): others = lax.ppermute(sums, 'head', [(0, 1), (1, 0)])  1.58 us
    reduce_sum x1, other arithmetic, local(): jnp.sum(query_f * query_f, axis=-1)  1.02 us
    pallas_call x2, Pallas kernels, last(): pl.pallas_call(functools.partial(last_attention, place), out_shape=out_sh...  0.9 us
    pallas_call x1, Pallas kernels, local(): pl.pallas_call(merge_kernel, out_shape=jax.ShapeDtypeStruct((rows, width)...  0.85 us
  transfers between devices with their start and end apart: 13, of which 6 were waited for; matrix products, arithmetic and copies ran while one was open for 4% of the time, Pallas kernels for 11%

profile of v20, /device:TPU:0, one launch (start us, length us, event | category | flops | bytes accessed | tf_op | source)
XLA Modules:
  0.0 29.5 jit_solution(6423577224346392412)
XLA Ops:
  0.0 4.0 %collective-permute-start.6 = (bf16[128,384]{1,0:T(8,128)(2,1)}, bf16[128,384]{1,0:T(8,128)(2,1)S(1)}, u32[]{:S(2)}, u32[]{:S(2)}) collective-permute-start(bf16[128,384]{1,0:T(8,128)(2,1)} %refs_4_.1), channel_id=1, source_target_pairs={{0,16},{2,18},{4,20},{6,22},{8,24},{10,26},{12,28},{14,30},{16,0},... | collective-permute-start | bytes 294920 | tf_op jit(solution)/shard_map/ppermute | solution.py:249
  4.0 1.0 %multiply_reduce_fusion.1 = f32[128]{0:T(128)S(1)} fusion(bf16[128,384]{1,0:T(8,128)(2,1)} %query_ref.1), kind=kLoop, calls=%fused_computation.1 | loop fusion | flops 147328 | bytes 98816 | tf_op jit(solution)/shard_map/reduce_sum | solution.py:293
  5.1 0.0 copy-done
  5.1 0.0 copy-start.1
  5.1 0.1 multiply_reduce_fusion
  5.2 1.6 %collective-permute-start = (f32[2,128]{1,0:T(2,128)S(1)}, f32[2,128]{1,0:T(2,128)S(1)}, u32[]{:S(2)}, u32[]{:S(2)}) collective-permute-start(f32[2,128]{1,0:T(2,128)S(1)} %pad_maximum_fusion.own_ref), channel_id=1, source_target_pairs={{0,1},{1,0},{2,3},{3,2},{4,5},{5,4},{6,7},{7,6},{8,9},{9,8},{10,11... | collective-permute-start | bytes 3080 | tf_op jit(solution)/shard_map/ppermute | solution.py:296
  6.8 0.0 copy-done.2
  6.8 1.5 %collective-permute-start.9 = (bf16[128,384]{1,0:T(8,128)(2,1)S(1)}, bf16[128,384]{1,0:T(8,128)(2,1)S(1)}, u32[]{:S(2)}, u32[]{:S(2)}) collective-permute-start(bf16[128,384]{1,0:T(8,128)(2,1)S(1)} %copy-done.2), channel_id=1, source_target_pairs={{0,4},{2,6},{4,0},{6,2},{8,12},{10,14},{12,8},{14,10},{16,20},{18,... | collective-permute-start | bytes 294920 | tf_op jit(solution)/shard_map/ppermute | solution.py:249
  8.3 0.0 copy-done.6
  8.3 0.0 copy-done.7
  8.3 0.5 %collective-permute-done.other_ref = f32[2,128]{1,0:T(2,128)S(1)} collective-permute-done((f32[2,128]{1,0:T(2,128)S(1)}, f32[2,128]{1,0:T(2,128)S(1)}, u32[]{:S(2)}, u32[]{:S(2)}) %collective-permute-start) | collective-permute-done | bytes 1056 | tf_op jit(solution)/shard_map/ppermute | solution.py:296
  8.9 0.1 shard_map.84
  9.0 0.1 collective-permute-start.2
  9.1 1.8 %collective-permute-start.8 = (bf16[128,384]{1,0:T(8,128)(2,1)S(1)}, bf16[128,384]{1,0:T(8,128)(2,1)S(1)}, u32[]{:S(2)}, u32[]{:S(2)}) collective-permute-start(bf16[128,384]{1,0:T(8,128)(2,1)S(1)} %get-tuple-element.18.refs_0_), channel_id=1, source_target_pairs={{0,4},{2,6},{4,0},{6,2},{8,12},{10,14},{12,8},{14,10},{16,20},{18,... | collective-permute-start | bytes 294920 | tf_op jit(solution)/shard_map/ppermute | solution.py:249
  10.9 2.6 %collective-permute-start.4 = (bf16[128,128]{1,0:T(8,128)(2,1)S(1)}, bf16[128,128]{1,0:T(8,128)(2,1)S(1)}, u32[]{:S(2)}, u32[]{:S(2)}) collective-permute-start(bf16[128,128]{1,0:T(8,128)(2,1)S(1)} %get-tuple-element.17), channel_id=1, source_target_pairs={{0,16},{2,18},{4,20},{6,22},{8,24},{10,26},{12,28},{14,30},{16,0},... | collective-permute-start | bytes 98312 | tf_op jit(solution)/shard_map/ppermute | solution.py:249
  13.5 0.0 copy-done.1
  13.5 0.0 copy-done.5
  13.5 0.1 shard_map.82.own_ref.query_ref
  13.6 0.0 collective-permute-done.6.source_ref
  13.6 1.6 %collective-permute-start.1 = (bf16[144,384]{1,0:T(8,128)(2,1)S(1)}, bf16[144,384]{1,0:T(8,128)(2,1)S(1)}, u32[]{:S(2)}, u32[]{:S(2)}) collective-permute-start(bf16[144,384]{1,0:T(8,128)(2,1)S(1)} %shard_map.82.own_ref.query_ref), channel_id=1, source_target_pairs={{0,8},{2,10},{4,12},{6,14},{8,0},{10,2},{12,4},{14,6},{16,24},{18,... | collective-permute-start | bytes 331784 | tf_op jit(solution)/shard_map/ppermute | solution.py:249
  15.3 0.0 collective-permute-done.2.source_ref
  15.3 0.6 %collective-permute-start.7 = (bf16[128,384]{1,0:T(8,128)(2,1)S(1)}, bf16[128,384]{1,0:T(8,128)(2,1)S(1)}, u32[]{:S(2)}, u32[]{:S(2)}) collective-permute-start(bf16[128,384]{1,0:T(8,128)(2,1)S(1)} %shard_map.87.refs_5_), channel_id=1, source_target_pairs={{0,4},{2,6},{4,0},{6,2},{8,12},{10,14},{12,8},{14,10},{16,20},{18,... | collective-permute-start | bytes 294920 | tf_op jit(solution)/shard_map/ppermute | solution.py:249
  15.9 0.1 collective-permute-done.4.source_ref
  16.0 1.5 %collective-permute-start.3 = (bf16[128,256]{1,0:T(8,128)(2,1)S(1)}, bf16[128,256]{1,0:T(8,128)(2,1)S(1)}, u32[]{:S(2)}, u32[]{:S(2)}) collective-permute-start(bf16[128,256]{1,0:T(8,128)(2,1)S(1)} %shard_map.85.refs_1_), channel_id=1, source_target_pairs={{0,4},{2,6},{4,0},{6,2},{8,12},{10,14},{12,8},{14,10},{16,20},{18,... | collective-permute-start | bytes 196616 | tf_op jit(solution)/shard_map/ppermute | solution.py:249
  17.4 0.0 collective-permute-done.9.refs_6_
  17.4 0.6 %collective-permute-start.5 = (bf16[128,128]{1,0:T(8,128)(2,1)S(1)}, bf16[128,128]{1,0:T(8,128)(2,1)S(1)}, u32[]{:S(2)}, u32[]{:S(2)}) collective-permute-start(bf16[128,128]{1,0:T(8,128)(2,1)S(1)} %shard_map.86.refs_2_), channel_id=1, source_target_pairs={{0,4},{2,6},{4,0},{6,2},{8,12},{10,14},{12,8},{14,10},{16,20},{18,... | collective-permute-start | bytes 98312 | tf_op jit(solution)/shard_map/ppermute | solution.py:249
  18.0 0.0 collective-permute-done.8.refs_3_
  18.0 0.1 shard_map.88.pack_ref
  18.1 0.1 collective-permute-start.11
  18.2 0.3 collective-permute-done.1.remote_ref.query_ref
  18.4 0.1 shard_map.83.bias_ref
  18.5 0.6 %shard_map.89 = (f32[256,384]{1,0:T(8,128)S(1)}, f32[256,768]{1,0:T(8,128)S(1)}) custom-call(bf16[144,384]{1,0:T(8,128)(2,1)S(1)} %shard_map.82.own_ref.query_ref, bf16[144,384]{1,0:T(8,128)(2,1)S(1)} %collective-permute-done.1.remote_ref.query_ref, f32[16,1024]{1,0:T(8,128)S(1)} %shard_map.83.bias_ref, bf16[768,384]{1,0:T(8,128)(2,1)S(1)} %shard_map.88.pack_ref), custom_call_target="tpu_custom_call" | custom-call | tf_op jit(solution)/shard_map/pallas_call | solution.py:360
  19.1 2.3 %collective-permute-done.5.refs_1_ = bf16[128,128]{1,0:T(8,128)(2,1)S(1)} collective-permute-done((bf16[128,128]{1,0:T(8,128)(2,1)S(1)}, bf16[128,128]{1,0:T(8,128)(2,1)S(1)}, u32[]{:S(2)}, u32[]{:S(2)}) %collective-permute-start.5) | collective-permute-done | bytes 32800 | tf_op jit(solution)/shard_map/ppermute | solution.py:249
  21.4 0.0 collective-permute-done.3.refs_0_
  21.4 0.0 collective-permute-done.7.refs_2_
  21.4 0.1 collective-permute-start.10
  21.5 0.0 collective-permute-done.11.pack_ref
  21.5 0.6 %shard_map.91 = (f32[256,384]{1,0:T(8,128)S(1)}, f32[256,768]{1,0:T(8,128)S(1)}) custom-call(bf16[144,384]{1,0:T(8,128)(2,1)S(1)} %shard_map.82.own_ref.query_ref, bf16[144,384]{1,0:T(8,128)(2,1)S(1)} %collective-permute-done.1.remote_ref.query_ref, f32[16,1024]{1,0:T(8,128)S(1)} %shard_map.83.bias_ref, ...), custom_call_target="tpu_custom_call" | custom-call | tf_op jit(solution)/shard_map/pallas_call | solution.py:360
  22.1 0.5 %shard_map.92 = (f32[256,384]{1,0:T(8,128)S(1)}, f32[256,768]{1,0:T(8,128)S(1)}) custom-call(bf16[144,384]{1,0:T(8,128)(2,1)S(1)} %shard_map.82.own_ref.query_ref, bf16[144,384]{1,0:T(8,128)(2,1)S(1)} %collective-permute-done.1.remote_ref.query_ref, f32[16,1024]{1,0:T(8,128)S(1)} %shard_map.83.bias_ref, bf16[256,384]{1,0:T(8,128)(2,1)S(1)} %shard_map.90.pack_ref, ...), custom_call_target="tpu_custom_call" | custom-call | tf_op jit(solution)/shard_map/pallas_call | solution.py:360
  22.6 0.3 collective-permute-done.10.pack_ref
  22.9 0.5 %shard_map.94 = bf16[144,384]{1,0:T(8,128)(2,1)S(1)} custom-call(bf16[144,384]{1,0:T(8,128)(2,1)S(1)} %collective-permute-done.1.remote_ref.query_ref, f32[16,1024]{1,0:T(8,128)S(1)} %shard_map.83.bias_ref, bf16[256,384]{1,0:T(8,128)(2,1)S(1)} %collective-permute-done.10.pack_ref, f32[256,384]{1,0:T(8,128)S(1)} %get-tuple-element.23.context_ref, ...), custom_call_target="tpu_custom_call" | custom-call | tf_op jit(solution)/shard_map/pallas_call | solution.py:383
  23.4 1.4 %collective-permute-start.12 = (bf16[144,384]{1,0:T(8,128)(2,1)S(1)}, bf16[144,384]{1,0:T(8,128)(2,1)S(1)}, u32[]{:S(2)}, u32[]{:S(2)}) collective-permute-start(bf16[144,384]{1,0:T(8,128)(2,1)S(1)} %shard_map.94), channel_id=1, source_target_pairs={{0,8},{2,10},{4,12},{6,14},{8,0},{10,2},{12,4},{14,6},{16,24},{18,... | collective-permute-start | bytes 331784 | tf_op jit(solution)/shard_map/ppermute | solution.py:249
  24.7 0.0 copy-done.3
  24.7 0.0 copy-done.4
  24.7 0.6 %shard_map.95.gate_ref = f32[16,384]{1,0:T(8,128)S(1)} custom-call(s32[2]{0:T(128)S(1)} %copy-done.4, f32[50,384]{1,0:T(8,128)S(1)} %copy-done.3), custom_call_target="tpu_custom_call" | custom-call | tf_op jit(solution)/shard_map/pallas_call | solution.py:399
  25.3 0.4 %shard_map.93 = (f32[128,384]{1,0:T(8,128)S(1)}, f32[16,384]{1,0:T(8,128)S(1)}) custom-call(bf16[144,384]{1,0:T(8,128)(2,1)S(1)} %shard_map.82.own_ref.query_ref, f32[16,1024]{1,0:T(8,128)S(1)} %shard_map.83.bias_ref, bf16[256,384]{1,0:T(8,128)(2,1)S(1)} %collective-permute-done.10.pack_ref, f32[256,384]{1,0:T(8,128)S(1)} %get-tuple-element.23.context_ref, ...), custom_call_target="tpu_custom_call" | custom-call | tf_op jit(solution)/shard_map/pallas_call | solution.py:383
  25.8 2.9 %collective-permute-done.12.packet_ref = bf16[144,384]{1,0:T(8,128)(2,1)S(1)} collective-permute-done((bf16[144,384]{1,0:T(8,128)(2,1)S(1)}, bf16[144,384]{1,0:T(8,128)(2,1)S(1)}, u32[]{:S(2)}, u32[]{:S(2)}) %collective-permute-start.12) | collective-permute-done | bytes 110624 | tf_op jit(solution)/shard_map/ppermute | solution.py:249
  28.6 0.8 %shard_map.96 = bf16[128,384]{1,0:T(8,128)(2,1)} custom-call(f32[128,384]{1,0:T(8,128)S(1)} %get-tuple-element.25.own_ref, f32[16,384]{1,0:T(8,128)S(1)} %get-tuple-element.26.lines_ref, bf16[144,384]{1,0:T(8,128)(2,1)S(1)} %collective-permute-done.12.packet_ref, f32[16,384]{1,0:T(8,128)S(1)} %shard_map.95.gate_ref), custom_call_target="tpu_custom_call" | custom-call | tf_op jit(solution)/shard_map/pallas_call | solution.py:408
  (14 shorter events, 0.1 us)
Async XLA Ops:
  0.0 5.1 %copy-start = (bf16[128,384]{1,0:T(8,128)(2,1)S(1)}, bf16[128,384]{1,0:T(8,128)(2,1)}, u32[]{:S(2)}) copy-start(bf16[128,384]{1,0:T(8,128)(2,1)} %key_ref.1) | copy-start | bytes 294916
  0.0 6.8 %copy-start.2 = (bf16[128,384]{1,0:T(8,128)(2,1)S(1)}, bf16[128,384]{1,0:T(8,128)(2,1)}, u32[]{:S(2)}) copy-start(bf16[128,384]{1,0:T(8,128)(2,1)} %refs_4_.1) | copy-start | bytes 294916
  0.0 13.6 %collective-permute-start.6 = (bf16[128,384]{1,0:T(8,128)(2,1)}, bf16[128,384]{1,0:T(8,128)(2,1)S(1)}, u32[]{:S(2)}, u32[]{:S(2)}) collective-permute-start(bf16[128,384]{1,0:T(8,128)(2,1)} %refs_4_.1), channel_id=1, source_target_pairs={{0,16},{2,18},{4,20},{6,22},{8,24},{10,26},{12,28},{14,30},{16,0},... | collective-permute-start | bytes 294920 | tf_op jit(solution)/shard_map/ppermute | solution.py:249
  4.0 4.3 %copy-start.6 = (f32[384]{0:T(512)S(1)}, f32[384]{0:T(512)}, u32[]{:S(2)}) copy-start(f32[384]{0:T(512)} %param.12) | copy-start | bytes 4612
  4.0 4.3 %copy-start.7 = (f32[384]{0:T(512)S(1)}, f32[384]{0:T(512)}, u32[]{:S(2)}) copy-start(f32[384]{0:T(512)} %param.11) | copy-start | bytes 4612
  5.1 8.4 %copy-start.1 = (bf16[128,384]{1,0:T(8,128)(2,1)S(1)}, bf16[128,384]{1,0:T(8,128)(2,1)}, u32[]{:S(2)}) copy-start(bf16[128,384]{1,0:T(8,128)(2,1)} %query_ref.1) | copy-start | bytes 294916
  5.2 3.6 %collective-permute-start = (f32[2,128]{1,0:T(2,128)S(1)}, f32[2,128]{1,0:T(2,128)S(1)}, u32[]{:S(2)}, u32[]{:S(2)}) collective-permute-start(f32[2,128]{1,0:T(2,128)S(1)} %pad_maximum_fusion.own_ref), channel_id=1, source_target_pairs={{0,1},{1,0},{2,3},{3,2},{4,5},{5,4},{6,7},{7,6},{8,9},{9,8},{10,11... | collective-permute-start | bytes 3080 | tf_op jit(solution)/shard_map/ppermute | solution.py:296
  6.8 10.6 %collective-permute-start.9 = (bf16[128,384]{1,0:T(8,128)(2,1)S(1)}, bf16[128,384]{1,0:T(8,128)(2,1)S(1)}, u32[]{:S(2)}, u32[]{:S(2)}) collective-permute-start(bf16[128,384]{1,0:T(8,128)(2,1)S(1)} %copy-done.2), channel_id=1, source_target_pairs={{0,4},{2,6},{4,0},{6,2},{8,12},{10,14},{12,8},{14,10},{16,20},{18,... | collective-permute-start | bytes 294920 | tf_op jit(solution)/shard_map/ppermute | solution.py:249
  9.0 6.3 %collective-permute-start.2 = (bf16[128,256]{1,0:T(8,128)(2,1)S(1)}, bf16[128,256]{1,0:T(8,128)(2,1)S(1)}, u32[]{:S(2)}, u32[]{:S(2)}) collective-permute-start(bf16[128,256]{1,0:T(8,128)(2,1)S(1)} %get-tuple-element.16), channel_id=1, source_target_pairs={{0,16},{2,18},{4,20},{6,22},{8,24},{10,26},{12,28},{14,30},{16,0},... | collective-permute-start | bytes 196616 | tf_op jit(solution)/shard_map/ppermute | solution.py:249
  9.1 4.4 %copy-start.5 = (s32[1,16]{1,0:T(1,128)S(1)}, s32[1,16]{1,0:T(1,128)}, u32[]{:S(2)}) copy-start(s32[1,16]{1,0:T(1,128)} %far_ref.1) | copy-start | bytes 196
  9.1 8.9 %collective-permute-start.8 = (bf16[128,384]{1,0:T(8,128)(2,1)S(1)}, bf16[128,384]{1,0:T(8,128)(2,1)S(1)}, u32[]{:S(2)}, u32[]{:S(2)}) collective-permute-start(bf16[128,384]{1,0:T(8,128)(2,1)S(1)} %get-tuple-element.18.refs_0_), channel_id=1, source_target_pairs={{0,4},{2,6},{4,0},{6,2},{8,12},{10,14},{12,8},{14,10},{16,20},{18,... | collective-permute-start | bytes 294920 | tf_op jit(solution)/shard_map/ppermute | solution.py:249
  10.9 5.1 %collective-permute-start.4 = (bf16[128,128]{1,0:T(8,128)(2,1)S(1)}, bf16[128,128]{1,0:T(8,128)(2,1)S(1)}, u32[]{:S(2)}, u32[]{:S(2)}) collective-permute-start(bf16[128,128]{1,0:T(8,128)(2,1)S(1)} %get-tuple-element.17), channel_id=1, source_target_pairs={{0,16},{2,18},{4,20},{6,22},{8,24},{10,26},{12,28},{14,30},{16,0},... | collective-permute-start | bytes 98312 | tf_op jit(solution)/shard_map/ppermute | solution.py:249
  13.6 4.8 %collective-permute-start.1 = (bf16[144,384]{1,0:T(8,128)(2,1)S(1)}, bf16[144,384]{1,0:T(8,128)(2,1)S(1)}, u32[]{:S(2)}, u32[]{:S(2)}) collective-permute-start(bf16[144,384]{1,0:T(8,128)(2,1)S(1)} %shard_map.82.own_ref.query_ref), channel_id=1, source_target_pairs={{0,8},{2,10},{4,12},{6,14},{8,0},{10,2},{12,4},{14,6},{16,24},{18,... | collective-permute-start | bytes 331784 | tf_op jit(solution)/shard_map/ppermute | solution.py:249
  15.3 6.1 %collective-permute-start.7 = (bf16[128,384]{1,0:T(8,128)(2,1)S(1)}, bf16[128,384]{1,0:T(8,128)(2,1)S(1)}, u32[]{:S(2)}, u32[]{:S(2)}) collective-permute-start(bf16[128,384]{1,0:T(8,128)(2,1)S(1)} %shard_map.87.refs_5_), channel_id=1, source_target_pairs={{0,4},{2,6},{4,0},{6,2},{8,12},{10,14},{12,8},{14,10},{16,20},{18,... | collective-permute-start | bytes 294920 | tf_op jit(solution)/shard_map/ppermute | solution.py:249
  16.0 5.4 %collective-permute-start.3 = (bf16[128,256]{1,0:T(8,128)(2,1)S(1)}, bf16[128,256]{1,0:T(8,128)(2,1)S(1)}, u32[]{:S(2)}, u32[]{:S(2)}) collective-permute-start(bf16[128,256]{1,0:T(8,128)(2,1)S(1)} %shard_map.85.refs_1_), channel_id=1, source_target_pairs={{0,4},{2,6},{4,0},{6,2},{8,12},{10,14},{12,8},{14,10},{16,20},{18,... | collective-permute-start | bytes 196616 | tf_op jit(solution)/shard_map/ppermute | solution.py:249
  17.4 3.9 %collective-permute-start.5 = (bf16[128,128]{1,0:T(8,128)(2,1)S(1)}, bf16[128,128]{1,0:T(8,128)(2,1)S(1)}, u32[]{:S(2)}, u32[]{:S(2)}) collective-permute-start(bf16[128,128]{1,0:T(8,128)(2,1)S(1)} %shard_map.86.refs_2_), channel_id=1, source_target_pairs={{0,4},{2,6},{4,0},{6,2},{8,12},{10,14},{12,8},{14,10},{16,20},{18,... | collective-permute-start | bytes 98312 | tf_op jit(solution)/shard_map/ppermute | solution.py:249
  18.1 3.4 %collective-permute-start.11 = (bf16[768,384]{1,0:T(8,128)(2,1)S(1)}, bf16[768,384]{1,0:T(8,128)(2,1)S(1)}, u32[]{:S(2)}, u32[]{:S(2)}) collective-permute-start(bf16[768,384]{1,0:T(8,128)(2,1)S(1)} %shard_map.88.pack_ref), channel_id=1, source_target_pairs={{0,2},{2,0},{4,6},{6,4},{8,10},{10,8},{12,14},{14,12},{16,18},{18,... | collective-permute-start | bytes 1769480 | tf_op jit(solution)/shard_map/ppermute | solution.py:249
  21.4 1.5 %collective-permute-start.10 = (bf16[256,384]{1,0:T(8,128)(2,1)S(1)}, bf16[256,384]{1,0:T(8,128)(2,1)S(1)}, u32[]{:S(2)}, u32[]{:S(2)}) collective-permute-start(bf16[256,384]{1,0:T(8,128)(2,1)S(1)} %shard_map.90.pack_ref), channel_id=1, source_target_pairs={{0,2},{2,0},{4,6},{6,4},{8,10},{10,8},{12,14},{14,12},{16,18},{18,... | collective-permute-start | bytes 589832 | tf_op jit(solution)/shard_map/ppermute | solution.py:249
  22.9 1.8 %copy-start.3 = (f32[50,384]{1,0:T(8,128)S(1)}, f32[50,384]{1,0:T(8,128)}, u32[]{:S(2)}) copy-start(f32[50,384]{1,0:T(8,128)} %table_ref.1) | copy-start | bytes 230404
  22.9 1.8 %copy-start.4 = (s32[2]{0:T(128)S(1)}, s32[2]{0:T(128)}, u32[]{:S(2)}) copy-start(s32[2]{0:T(128)} %step_ref.1) | copy-start | bytes 28
  23.4 5.3 %collective-permute-start.12 = (bf16[144,384]{1,0:T(8,128)(2,1)S(1)}, bf16[144,384]{1,0:T(8,128)(2,1)S(1)}, u32[]{:S(2)}, u32[]{:S(2)}) collective-permute-start(bf16[144,384]{1,0:T(8,128)(2,1)S(1)} %shard_map.94), channel_id=1, source_target_pairs={{0,8},{2,10},{4,12},{6,14},{8,0},{10,2},{12,4},{14,6},{16,24},{18,... | collective-permute-start | bytes 331784 | tf_op jit(solution)/shard_map/ppermute | solution.py:249

commit v21 on v19

--- a/solution.py
+++ b/solution.py
@@ -38,7 +38,7 @@
 
 
 def key_kernel(full_width, key_ref, gain_ref, own_ref, other_ref, out_ref):
-    total = own_ref[1:2, :] + other_ref[1:2, :]
+    total = own_ref[...] + other_ref[...]
     out_ref[...] = normed(key_ref, factor_of(total, full_width), gain_ref)
 
 
@@ -51,7 +51,7 @@
     other_ref,
     query_out,
 ):
-    total = own_ref[0:1, :] + other_ref[0:1, :]
+    total = own_ref[...] + other_ref[...]
     query_out[:HD, :] = normed(query_ref, factor_of(total, full_width), gain_ref)
     far = far_ref[...].astype(jnp.float32)
     far = jnp.concatenate([far, jnp.full((1, HD - far.shape[1]), -1.0)], axis=1)
@@ -270,22 +270,23 @@
 
     far = bits[0]
     far_value = exchange(value_proj, far)
-    query_f, key_f = query_proj.astype(jnp.float32), key_proj.astype(jnp.float32)
-    sums = jnp.stack(
-        [jnp.sum(query_f * query_f, axis=-1), jnp.sum(key_f * key_f, axis=-1)], axis=0
-    )
-    if splits == 2:
-        others = lax.ppermute(sums, "head", [(0, 1), (1, 0)])
-    else:
-        sums = lax.psum(sums, "head")
-        others = jnp.zeros_like(sums)
+
+    def row_sums(source):
+        wide = source.astype(jnp.float32)
+        own = jnp.sum(wide * wide, axis=-1)[None, :]
+        if splits == 2:
+            return own, lax.ppermute(own, "head", [(0, 1), (1, 0)])
+        own = lax.psum(own, "head")
+        return own, jnp.zeros_like(own)
+
+    key_sums, query_sums = row_sums(key_proj), row_sums(query_proj)
     own_key = pl.pallas_call(
         functools.partial(key_kernel, width * splits),
         out_shape=jax.ShapeDtypeStruct((rows, width), jnp.bfloat16),
         in_specs=[VMEM] * 4,
         out_specs=VMEM,
         compiler_params=params,
-    )(key_proj, key_gain, sums, others)
+    )(key_proj, key_gain, *key_sums)
     near_values = gathered(value_proj, bits[1:])
     near_keys = gathered(own_key, bits[1:])
     query_packet = pl.pallas_call(
@@ -294,7 +295,7 @@
         in_specs=[VMEM] * 5,
         out_specs=VMEM,
         compiler_params=params,
-    )(query_proj, query_gain, far_blocks, sums, others)
+    )(query_proj, query_gain, far_blocks, *query_sums)
     far_key = exchange(own_key, far)
     queries = [query_packet, exchange(query_packet, query_mask)]
     far_value = pl.pallas_call(
@@ -303,7 +304,7 @@
         in_specs=[VMEM],
         out_specs=VMEM,
         compiler_params=params,
-        cost_estimate=cost(4 * UNIT),
+        cost_estimate=cost(UNIT),
     )(far_value)
     late_keys, late_values = gathered(far_key, bits[1:]), gathered(far_value, bits[1:])
     early = [0, far] + sorted(mask for mask in near_keys if mask)

time: 27.7 us -> 29.1 us (1.051)
  starting transfers between devices: 15.1 us -> 17.5 us
  waiting for transfers between devices: 6.75 us -> 5.75 us
    ppermute x1 -> x2, starting transfers between devices: 1.58 us -> 4.62 us  [row_sums(): return (own, lax.ppermute(own, 'head', [(0, 1), (1, 0)]))]
    ppermute x10, starting transfers between devices: 13.5 us -> 12.9 us  [exchange(): return lax.ppermute(array, 'tm', [(i, i ^ mask) for i in range(count)])]
    ppermute x1 -> x2, waiting for transfers between devices: 0.52 us -> 0.01 us  [row_sums(): return (own, lax.ppermute(own, 'head', [(0, 1), (1, 0)]))]
    ppermute x10, waiting for transfers between devices: 6.23 us -> 5.74 us  [exchange(): return lax.ppermute(array, 'tm', [(i, i ^ mask) for i in range(count)])]
  transfers between devices with their start and end apart: 11 -> 12, of which waited for: 6 -> 6; matrix products, arithmetic and copies ran while one was open for 4% -> 0% of each run, Pallas kernels for 11% -> 11%
where the time goes in v21:
time: 29.1 us; the launch traced here: 29 us
  starting transfers between devices  17.5 us (60%)
  waiting for transfers between devices  5.75 us (20%)
  Pallas kernels  4.43 us (15%)
  other arithmetic  1.17 us (4%)
    ppermute x10, starting transfers between devices, exchange(): return lax.ppermute(array, 'tm', [(i, i ^ mask) for i in range(count)])  12.9 us
    ppermute x10, waiting for transfers between devices, exchange(): return lax.ppermute(array, 'tm', [(i, i ^ mask) for i in range(count)])  5.74 us
    ppermute x2, starting transfers between devices, row_sums(): return (own, lax.ppermute(own, 'head', [(0, 1), (1, 0)]))  4.62 us
    pallas_call x3, Pallas kernels, step(): pl.pallas_call(functools.partial(step_kernel, first), out_shape=[jax.Shap...  1.7 us
    reduce_sum x2, other arithmetic, row_sums(): own = jnp.sum(wide * wide, axis=-1)[None, :]  1.17 us
    pallas_call x2, Pallas kernels, last(): pl.pallas_call(functools.partial(last_attention, place), out_shape=out_sh...  0.9 us
    pallas_call x1, Pallas kernels, local(): pl.pallas_call(merge_kernel, out_shape=jax.ShapeDtypeStruct((rows, width)...  0.85 us
  transfers between devices with their start and end apart: 12, of which 6 were waited for; matrix products, arithmetic and copies ran while one was open for 0% of the time, Pallas kernels for 11%

profile of v21, /device:TPU:0, one launch (start us, length us, event | category | flops | bytes accessed | tf_op | source)
XLA Modules:
  0.0 29.0 jit_solution(13672247189581748022)
XLA Ops:
  0.0 0.0 copy-start
  0.0 1.1 %multiply_reduce_fusion = f32[128]{0:T(128)S(1)} fusion(bf16[128,384]{1,0:T(8,128)(2,1)} %key_ref.1), kind=kLoop, calls=%fused_computation | loop fusion | flops 147328 | bytes 98816 | tf_op jit(solution)/shard_map/reduce_sum | solution.py:276
  1.1 3.0 %collective-permute-start.2 = (f32[1,128]{1,0:T(1,128)S(1)}, f32[1,128]{1,0:T(1,128)S(1)}, u32[]{:S(2)}, u32[]{:S(2)}) collective-permute-start(f32[1,128]{1,0:T(1,128)S(1)} %bitcast.4), channel_id=1, source_target_pairs={{0,1},{1,0},{2,3},{3,2},{4,5},{5,4},{6,7},{7,6},{8,9},{9,8},{10,11... | collective-permute-start | bytes 1544 | tf_op jit(solution)/shard_map/ppermute | solution.py:278
  4.1 2.6 %collective-permute-start.5 = (bf16[128,384]{1,0:T(8,128)(2,1)}, bf16[128,384]{1,0:T(8,128)(2,1)S(1)}, u32[]{:S(2)}, u32[]{:S(2)}) collective-permute-start(bf16[128,384]{1,0:T(8,128)(2,1)} %refs_3_.1), channel_id=1, source_target_pairs={{0,16},{2,18},{4,20},{6,22},{8,24},{10,26},{12,28},{14,30},{16,0},... | collective-permute-start | bytes 294920 | tf_op jit(solution)/shard_map/ppermute | solution.py:242
  6.7 0.0 copy-done.6
  6.7 0.0 collective-permute-done.2.other_ref
  6.7 0.0 copy-done
  6.7 0.1 shard_map.84.refs_0_
  6.8 0.0 copy-start.2
  6.9 2.1 %collective-permute-start.3 = (bf16[128,384]{1,0:T(8,128)(2,1)S(1)}, bf16[128,384]{1,0:T(8,128)(2,1)S(1)}, u32[]{:S(2)}, u32[]{:S(2)}) collective-permute-start(bf16[128,384]{1,0:T(8,128)(2,1)S(1)} %shard_map.84.refs_0_), channel_id=1, source_target_pairs={{0,16},{2,18},{4,20},{6,22},{8,24},{10,26},{12,28},{14,30},{16,0},... | collective-permute-start | bytes 294920 | tf_op jit(solution)/shard_map/ppermute | solution.py:242
  8.9 0.0 copy-done.1
  8.9 0.1 multiply_reduce_fusion.1
  9.0 0.0 copy-start.4
  9.0 1.6 %collective-permute-start = (f32[1,128]{1,0:T(1,128)S(1)}, f32[1,128]{1,0:T(1,128)S(1)}, u32[]{:S(2)}, u32[]{:S(2)}) collective-permute-start(f32[1,128]{1,0:T(1,128)S(1)} %bitcast.2), channel_id=1, source_target_pairs={{0,1},{1,0},{2,3},{3,2},{4,5},{5,4},{6,7},{7,6},{8,9},{9,8},{10,11... | collective-permute-start | bytes 1544 | tf_op jit(solution)/shard_map/ppermute | solution.py:278
  10.6 0.0 copy-done.2
  10.6 1.5 %collective-permute-start.8 = (bf16[128,384]{1,0:T(8,128)(2,1)S(1)}, bf16[128,384]{1,0:T(8,128)(2,1)S(1)}, u32[]{:S(2)}, u32[]{:S(2)}) collective-permute-start(bf16[128,384]{1,0:T(8,128)(2,1)S(1)} %copy-done.2), channel_id=1, source_target_pairs={{0,4},{2,6},{4,0},{6,2},{8,12},{10,14},{12,8},{14,10},{16,20},{18,... | collective-permute-start | bytes 294920 | tf_op jit(solution)/shard_map/ppermute | solution.py:242
  12.1 0.0 copy-done.7
  12.1 0.5 %collective-permute-start.7 = (bf16[128,384]{1,0:T(8,128)(2,1)S(1)}, bf16[128,384]{1,0:T(8,128)(2,1)S(1)}, u32[]{:S(2)}, u32[]{:S(2)}) collective-permute-start(bf16[128,384]{1,0:T(8,128)(2,1)S(1)} %shard_map.84.refs_0_), channel_id=1, source_target_pairs={{0,4},{2,6},{4,0},{6,2},{8,12},{10,14},{12,8},{14,10},{16,20},{18,... | collective-permute-start | bytes 294920 | tf_op jit(solution)/shard_map/ppermute | solution.py:242
  12.7 0.0 collective-permute-done.other_ref
  12.7 0.0 copy-done.4
  12.7 0.1 shard_map.82.own_ref.query_ref
  12.8 1.6 %collective-permute-start.1 = (bf16[144,384]{1,0:T(8,128)(2,1)S(1)}, bf16[144,384]{1,0:T(8,128)(2,1)S(1)}, u32[]{:S(2)}, u32[]{:S(2)}) collective-permute-start(bf16[144,384]{1,0:T(8,128)(2,1)S(1)} %shard_map.82.own_ref.query_ref), channel_id=1, source_target_pairs={{0,8},{2,10},{4,12},{6,14},{8,0},{10,2},{12,4},{14,6},{16,24},{18,... | collective-permute-start | bytes 331784 | tf_op jit(solution)/shard_map/ppermute | solution.py:242
  14.4 0.2 collective-permute-done.5.source_ref
  14.6 1.6 %collective-permute-start.6 = (bf16[128,384]{1,0:T(8,128)(2,1)S(1)}, bf16[128,384]{1,0:T(8,128)(2,1)S(1)}, u32[]{:S(2)}, u32[]{:S(2)}) collective-permute-start(bf16[128,384]{1,0:T(8,128)(2,1)S(1)} %shard_map.85.refs_4_), channel_id=1, source_target_pairs={{0,4},{2,6},{4,0},{6,2},{8,12},{10,14},{12,8},{14,10},{16,20},{18,... | collective-permute-start | bytes 294920 | tf_op jit(solution)/shard_map/ppermute | solution.py:242
  16.2 0.0 collective-permute-done.3.refs_1_
  16.2 1.2 %collective-permute-start.4 = (bf16[128,384]{1,0:T(8,128)(2,1)S(1)}, bf16[128,384]{1,0:T(8,128)(2,1)S(1)}, u32[]{:S(2)}, u32[]{:S(2)}) collective-permute-start(bf16[128,384]{1,0:T(8,128)(2,1)S(1)} %collective-permute-done.3.refs_1_), channel_id=1, source_target_pairs={{0,4},{2,6},{4,0},{6,2},{8,12},{10,14},{12,8},{14,10},{16,20},{18,... | collective-permute-start | bytes 294920 | tf_op jit(solution)/shard_map/ppermute | solution.py:242
  17.4 0.0 collective-permute-done.8.refs_5_
  17.4 0.0 collective-permute-done.7.refs_2_
  17.4 0.1 shard_map.86.pack_ref
  17.5 0.1 collective-permute-start.10
  17.5 0.1 collective-permute-done.1.remote_ref.query_ref
  17.6 0.1 shard_map.83.bias_ref
  17.7 0.6 %shard_map.87 = (f32[256,384]{1,0:T(8,128)S(1)}, f32[256,768]{1,0:T(8,128)S(1)}) custom-call(bf16[144,384]{1,0:T(8,128)(2,1)S(1)} %shard_map.82.own_ref.query_ref, bf16[144,384]{1,0:T(8,128)(2,1)S(1)} %collective-permute-done.1.remote_ref.query_ref, f32[16,1024]{1,0:T(8,128)S(1)} %shard_map.83.bias_ref, bf16[768,384]{1,0:T(8,128)(2,1)S(1)} %shard_map.86.pack_ref), custom_call_target="tpu_custom_call" | custom-call | tf_op jit(solution)/shard_map/pallas_call | solution.py:339
  18.3 1.5 %collective-permute-done.6.refs_1_ = bf16[128,384]{1,0:T(8,128)(2,1)S(1)} collective-permute-done((bf16[128,384]{1,0:T(8,128)(2,1)S(1)}, bf16[128,384]{1,0:T(8,128)(2,1)S(1)}, u32[]{:S(2)}, u32[]{:S(2)}) %collective-permute-start.6) | collective-permute-done | bytes 98336 | tf_op jit(solution)/shard_map/ppermute | solution.py:242
  19.8 1.1 %collective-permute-done.4.refs_0_ = bf16[128,384]{1,0:T(8,128)(2,1)S(1)} collective-permute-done((bf16[128,384]{1,0:T(8,128)(2,1)S(1)}, bf16[128,384]{1,0:T(8,128)(2,1)S(1)}, u32[]{:S(2)}, u32[]{:S(2)}) %collective-permute-start.4) | collective-permute-done | bytes 98336 | tf_op jit(solution)/shard_map/ppermute | solution.py:242
  20.9 0.1 collective-permute-start.9
  21.0 0.0 collective-permute-done.10.pack_ref
  21.0 0.7 %shard_map.89 = (f32[256,384]{1,0:T(8,128)S(1)}, f32[256,768]{1,0:T(8,128)S(1)}) custom-call(bf16[144,384]{1,0:T(8,128)(2,1)S(1)} %shard_map.82.own_ref.query_ref, bf16[144,384]{1,0:T(8,128)(2,1)S(1)} %collective-permute-done.1.remote_ref.query_ref, f32[16,1024]{1,0:T(8,128)S(1)} %shard_map.83.bias_ref, ...), custom_call_target="tpu_custom_call" | custom-call | tf_op jit(solution)/shard_map/pallas_call | solution.py:339
  21.7 0.5 %shard_map.90 = (f32[256,384]{1,0:T(8,128)S(1)}, f32[256,768]{1,0:T(8,128)S(1)}) custom-call(bf16[144,384]{1,0:T(8,128)(2,1)S(1)} %shard_map.82.own_ref.query_ref, bf16[144,384]{1,0:T(8,128)(2,1)S(1)} %collective-permute-done.1.remote_ref.query_ref, f32[16,1024]{1,0:T(8,128)S(1)} %shard_map.83.bias_ref, bf16[256,384]{1,0:T(8,128)(2,1)S(1)} %shard_map.88.pack_ref, ...), custom_call_target="tpu_custom_call" | custom-call | tf_op jit(solution)/shard_map/pallas_call | solution.py:339
  22.1 0.3 collective-permute-done.9.pack_ref
  22.4 0.5 %shard_map.92 = bf16[144,384]{1,0:T(8,128)(2,1)S(1)} custom-call(bf16[144,384]{1,0:T(8,128)(2,1)S(1)} %collective-permute-done.1.remote_ref.query_ref, f32[16,1024]{1,0:T(8,128)S(1)} %shard_map.83.bias_ref, bf16[256,384]{1,0:T(8,128)(2,1)S(1)} %collective-permute-done.9.pack_ref, f32[256,384]{1,0:T(8,128)S(1)} %get-tuple-element.17.context_ref, ...), custom_call_target="tpu_custom_call" | custom-call | tf_op jit(solution)/shard_map/pallas_call | solution.py:362
  22.9 1.6 %collective-permute-start.11 = (bf16[144,384]{1,0:T(8,128)(2,1)S(1)}, bf16[144,384]{1,0:T(8,128)(2,1)S(1)}, u32[]{:S(2)}, u32[]{:S(2)}) collective-permute-start(bf16[144,384]{1,0:T(8,128)(2,1)S(1)} %shard_map.92), channel_id=1, source_target_pairs={{0,8},{2,10},{4,12},{6,14},{8,0},{10,2},{12,4},{14,6},{16,24},{18,... | collective-permute-start | bytes 331784 | tf_op jit(solution)/shard_map/ppermute | solution.py:242
  24.5 0.0 copy-done.3
  24.5 0.0 copy-done.5
  24.5 0.6 %shard_map.93.gate_ref = f32[16,384]{1,0:T(8,128)S(1)} custom-call(s32[2]{0:T(128)S(1)} %copy-done.5, f32[50,384]{1,0:T(8,128)S(1)} %copy-done.3), custom_call_target="tpu_custom_call" | custom-call | tf_op jit(solution)/shard_map/pallas_call | solution.py:378
  25.1 0.4 %shard_map.91 = (f32[128,384]{1,0:T(8,128)S(1)}, f32[16,384]{1,0:T(8,128)S(1)}) custom-call(bf16[144,384]{1,0:T(8,128)(2,1)S(1)} %shard_map.82.own_ref.query_ref, f32[16,1024]{1,0:T(8,128)S(1)} %shard_map.83.bias_ref, bf16[256,384]{1,0:T(8,128)(2,1)S(1)} %collective-permute-done.9.pack_ref, f32[256,384]{1,0:T(8,128)S(1)} %get-tuple-element.17.context_ref, ...), custom_call_target="tpu_custom_call" | custom-call | tf_op jit(solution)/shard_map/pallas_call | solution.py:362
  25.6 2.6 %collective-permute-done.11.packet_ref = bf16[144,384]{1,0:T(8,128)(2,1)S(1)} collective-permute-done((bf16[144,384]{1,0:T(8,128)(2,1)S(1)}, bf16[144,384]{1,0:T(8,128)(2,1)S(1)}, u32[]{:S(2)}, u32[]{:S(2)}) %collective-permute-start.11) | collective-permute-done | bytes 110624 | tf_op jit(solution)/shard_map/ppermute | solution.py:242
  28.1 0.8 %shard_map.94 = bf16[128,384]{1,0:T(8,128)(2,1)} custom-call(f32[128,384]{1,0:T(8,128)S(1)} %get-tuple-element.19.own_ref, f32[16,384]{1,0:T(8,128)S(1)} %get-tuple-element.20.lines_ref, bf16[144,384]{1,0:T(8,128)(2,1)S(1)} %collective-permute-done.11.packet_ref, f32[16,384]{1,0:T(8,128)S(1)} %shard_map.93.gate_ref), custom_call_target="tpu_custom_call" | custom-call | tf_op jit(solution)/shard_map/pallas_call | solution.py:387
  (9 shorter events, 0.0 us)
Async XLA Ops:
  0.0 6.7 %copy-start = (bf16[128,384]{1,0:T(8,128)(2,1)S(1)}, bf16[128,384]{1,0:T(8,128)(2,1)}, u32[]{:S(2)}) copy-start(bf16[128,384]{1,0:T(8,128)(2,1)} %key_ref.1) | copy-start | bytes 294916
  0.0 6.7 %copy-start.6 = (f32[384]{0:T(512)S(1)}, f32[384]{0:T(512)}, u32[]{:S(2)}) copy-start(f32[384]{0:T(512)} %param.12) | copy-start | bytes 4612
  1.1 5.6 %collective-permute-start.2 = (f32[1,128]{1,0:T(1,128)S(1)}, f32[1,128]{1,0:T(1,128)S(1)}, u32[]{:S(2)}, u32[]{:S(2)}) collective-permute-start(f32[1,128]{1,0:T(1,128)S(1)} %bitcast.4), channel_id=1, source_target_pairs={{0,1},{1,0},{2,3},{3,2},{4,5},{5,4},{6,7},{7,6},{8,9},{9,8},{10,11... | collective-permute-start | bytes 1544 | tf_op jit(solution)/shard_map/ppermute | solution.py:278
  4.1 10.5 %collective-permute-start.5 = (bf16[128,384]{1,0:T(8,128)(2,1)}, bf16[128,384]{1,0:T(8,128)(2,1)S(1)}, u32[]{:S(2)}, u32[]{:S(2)}) collective-permute-start(bf16[128,384]{1,0:T(8,128)(2,1)} %refs_3_.1), channel_id=1, source_target_pairs={{0,16},{2,18},{4,20},{6,22},{8,24},{10,26},{12,28},{14,30},{16,0},... | collective-permute-start | bytes 294920 | tf_op jit(solution)/shard_map/ppermute | solution.py:242
  6.7 2.2 %copy-start.1 = (bf16[128,384]{1,0:T(8,128)(2,1)S(1)}, bf16[128,384]{1,0:T(8,128)(2,1)}, u32[]{:S(2)}) copy-start(bf16[128,384]{1,0:T(8,128)(2,1)} %query_ref.1) | copy-start | bytes 294916
  6.8 3.8 %copy-start.2 = (bf16[128,384]{1,0:T(8,128)(2,1)S(1)}, bf16[128,384]{1,0:T(8,128)(2,1)}, u32[]{:S(2)}) copy-start(bf16[128,384]{1,0:T(8,128)(2,1)} %refs_3_.1) | copy-start | bytes 294916
  6.9 9.3 %collective-permute-start.3 = (bf16[128,384]{1,0:T(8,128)(2,1)S(1)}, bf16[128,384]{1,0:T(8,128)(2,1)S(1)}, u32[]{:S(2)}, u32[]{:S(2)}) collective-permute-start(bf16[128,384]{1,0:T(8,128)(2,1)S(1)} %shard_map.84.refs_0_), channel_id=1, source_target_pairs={{0,16},{2,18},{4,20},{6,22},{8,24},{10,26},{12,28},{14,30},{16,0},... | collective-permute-start | bytes 294920 | tf_op jit(solution)/shard_map/ppermute | solution.py:242
  8.9 3.2 %copy-start.7 = (f32[384]{0:T(512)S(1)}, f32[384]{0:T(512)}, u32[]{:S(2)}) copy-start(f32[384]{0:T(512)} %param.11) | copy-start | bytes 4612
  9.0 3.6 %copy-start.4 = (s32[1,16]{1,0:T(1,128)S(1)}, s32[1,16]{1,0:T(1,128)}, u32[]{:S(2)}) copy-start(s32[1,16]{1,0:T(1,128)} %far_ref.1) | copy-start | bytes 196
  9.0 3.6 %collective-permute-start = (f32[1,128]{1,0:T(1,128)S(1)}, f32[1,128]{1,0:T(1,128)S(1)}, u32[]{:S(2)}, u32[]{:S(2)}) collective-permute-start(f32[1,128]{1,0:T(1,128)S(1)} %bitcast.2), channel_id=1, source_target_pairs={{0,1},{1,0},{2,3},{3,2},{4,5},{5,4},{6,7},{7,6},{8,9},{9,8},{10,11... | collective-permute-start | bytes 1544 | tf_op jit(solution)/shard_map/ppermute | solution.py:278
  10.6 6.8 %collective-permute-start.8 = (bf16[128,384]{1,0:T(8,128)(2,1)S(1)}, bf16[128,384]{1,0:T(8,128)(2,1)S(1)}, u32[]{:S(2)}, u32[]{:S(2)}) collective-permute-start(bf16[128,384]{1,0:T(8,128)(2,1)S(1)} %copy-done.2), channel_id=1, source_target_pairs={{0,4},{2,6},{4,0},{6,2},{8,12},{10,14},{12,8},{14,10},{16,20},{18,... | collective-permute-start | bytes 294920 | tf_op jit(solution)/shard_map/ppermute | solution.py:242
  12.1 5.3 %collective-permute-start.7 = (bf16[128,384]{1,0:T(8,128)(2,1)S(1)}, bf16[128,384]{1,0:T(8,128)(2,1)S(1)}, u32[]{:S(2)}, u32[]{:S(2)}) collective-permute-start(bf16[128,384]{1,0:T(8,128)(2,1)S(1)} %shard_map.84.refs_0_), channel_id=1, source_target_pairs={{0,4},{2,6},{4,0},{6,2},{8,12},{10,14},{12,8},{14,10},{16,20},{18,... | collective-permute-start | bytes 294920 | tf_op jit(solution)/shard_map/ppermute | solution.py:242
  12.8 4.8 %collective-permute-start.1 = (bf16[144,384]{1,0:T(8,128)(2,1)S(1)}, bf16[144,384]{1,0:T(8,128)(2,1)S(1)}, u32[]{:S(2)}, u32[]{:S(2)}) collective-permute-start(bf16[144,384]{1,0:T(8,128)(2,1)S(1)} %shard_map.82.own_ref.query_ref), channel_id=1, source_target_pairs={{0,8},{2,10},{4,12},{6,14},{8,0},{10,2},{12,4},{14,6},{16,24},{18,... | collective-permute-start | bytes 331784 | tf_op jit(solution)/shard_map/ppermute | solution.py:242
  14.6 5.2 %collective-permute-start.6 = (bf16[128,384]{1,0:T(8,128)(2,1)S(1)}, bf16[128,384]{1,0:T(8,128)(2,1)S(1)}, u32[]{:S(2)}, u32[]{:S(2)}) collective-permute-start(bf16[128,384]{1,0:T(8,128)(2,1)S(1)} %shard_map.85.refs_4_), channel_id=1, source_target_pairs={{0,4},{2,6},{4,0},{6,2},{8,12},{10,14},{12,8},{14,10},{16,20},{18,... | collective-permute-start | bytes 294920 | tf_op jit(solution)/shard_map/ppermute | solution.py:242
  16.2 4.7 %collective-permute-start.4 = (bf16[128,384]{1,0:T(8,128)(2,1)S(1)}, bf16[128,384]{1,0:T(8,128)(2,1)S(1)}, u32[]{:S(2)}, u32[]{:S(2)}) collective-permute-start(bf16[128,384]{1,0:T(8,128)(2,1)S(1)} %collective-permute-done.3.refs_1_), channel_id=1, source_target_pairs={{0,4},{2,6},{4,0},{6,2},{8,12},{10,14},{12,8},{14,10},{16,20},{18,... | collective-permute-start | bytes 294920 | tf_op jit(solution)/shard_map/ppermute | solution.py:242
  17.5 3.5 %collective-permute-start.10 = (bf16[768,384]{1,0:T(8,128)(2,1)S(1)}, bf16[768,384]{1,0:T(8,128)(2,1)S(1)}, u32[]{:S(2)}, u32[]{:S(2)}) collective-permute-start(bf16[768,384]{1,0:T(8,128)(2,1)S(1)} %shard_map.86.pack_ref), channel_id=1, source_target_pairs={{0,2},{2,0},{4,6},{6,4},{8,10},{10,8},{12,14},{14,12},{16,18},{18,... | collective-permute-start | bytes 1769480 | tf_op jit(solution)/shard_map/ppermute | solution.py:242
  20.9 1.5 %collective-permute-start.9 = (bf16[256,384]{1,0:T(8,128)(2,1)S(1)}, bf16[256,384]{1,0:T(8,128)(2,1)S(1)}, u32[]{:S(2)}, u32[]{:S(2)}) collective-permute-start(bf16[256,384]{1,0:T(8,128)(2,1)S(1)} %shard_map.88.pack_ref), channel_id=1, source_target_pairs={{0,2},{2,0},{4,6},{6,4},{8,10},{10,8},{12,14},{14,12},{16,18},{18,... | collective-permute-start | bytes 589832 | tf_op jit(solution)/shard_map/ppermute | solution.py:242
  22.4 2.1 %copy-start.3 = (f32[50,384]{1,0:T(8,128)S(1)}, f32[50,384]{1,0:T(8,128)}, u32[]{:S(2)}) copy-start(f32[50,384]{1,0:T(8,128)} %table_ref.1) | copy-start | bytes 230404
  22.4 2.1 %copy-start.5 = (s32[2]{0:T(128)S(1)}, s32[2]{0:T(128)}, u32[]{:S(2)}) copy-start(s32[2]{0:T(128)} %step_ref.1) | copy-start | bytes 28
  22.9 5.3 %collective-permute-start.11 = (bf16[144,384]{1,0:T(8,128)(2,1)S(1)}, bf16[144,384]{1,0:T(8,128)(2,1)S(1)}, u32[]{:S(2)}, u32[]{:S(2)}) collective-permute-start(bf16[144,384]{1,0:T(8,128)(2,1)S(1)} %shard_map.92), channel_id=1, source_target_pairs={{0,8},{2,10},{4,12},{6,14},{8,0},{10,2},{12,4},{14,6},{16,24},{18,... | collective-permute-start | bytes 331784 | tf_op jit(solution)/shard_map/ppermute | solution.py:242

commit v22 on v19

--- a/solution.py
+++ b/solution.py
@@ -268,7 +268,7 @@
     query_gain = query_gain.reshape(1, width)
     key_gain = key_gain.reshape(1, width)
 
-    far = bits[0]
+    far = bits[0] | query_mask
     far_value = exchange(value_proj, far)
     query_f, key_f = query_proj.astype(jnp.float32), key_proj.astype(jnp.float32)
     sums = jnp.stack(

time: 27.7 us -> 29.5 us (1.065)
  waiting for transfers between devices: 6.75 us -> 11 us
  starting transfers between devices: 15.1 us -> 12.1 us
  local copies, waits for them, and re-layouts: 0.04 us -> 0.39 us
    ppermute x10, waiting for transfers between devices: 6.23 us -> 10.5 us  [exchange(): return lax.ppermute(array, 'tm', [(i, i ^ mask) for i in range(count)])]
    ppermute x10, starting transfers between devices: 13.5 us -> 10.5 us  [exchange(): return lax.ppermute(array, 'tm', [(i, i ^ mask) for i in range(count)])]
    unnamed x16, local copies, waits for them, and re-layouts: 0.04 us -> 0.39 us
  transfers between devices with their start and end apart: 11 -> 11, of which waited for: 6 -> 5; matrix products, arithmetic and copies ran while one was open for 4% -> 4% of each run, Pallas kernels for 11% -> 11%
where the time goes in v22:
time: 29.5 us; the launch traced here: 29.3 us
  starting transfers between devices  12.1 us (41%)
  waiting for transfers between devices  11 us (37%)
  Pallas kernels  4.44 us (15%)
  other arithmetic  1.11 us (4%)
  local copies, waits for them, and re-layouts  0.39 us (1%)
    ppermute x10, starting transfers between devices, exchange(): return lax.ppermute(array, 'tm', [(i, i ^ mask) for i in range(count)])  10.5 us
    ppermute x10, waiting for transfers between devices, exchange(): return lax.ppermute(array, 'tm', [(i, i ^ mask) for i in range(count)])  10.5 us
    pallas_call x3, Pallas kernels, step(): pl.pallas_call(functools.partial(step_kernel, first), out_shape=[jax.Shap...  1.71 us
    ppermute x1, starting transfers between devices, local(): others = lax.ppermute(sums, 'head', [(0, 1), (1, 0)])  1.58 us
    reduce_sum x1, other arithmetic, local(): jnp.sum(query_f * query_f, axis=-1)  1 us
    pallas_call x2, Pallas kernels, last(): pl.pallas_call(functools.partial(last_attention, place), out_shape=out_sh...  0.9 us
    pallas_call x1, Pallas kernels, local(): pl.pallas_call(merge_kernel, out_shape=jax.ShapeDtypeStruct((rows, width)...  0.85 us
  transfers between devices with their start and end apart: 11, of which 5 were waited for; matrix products, arithmetic and copies ran while one was open for 4% of the time, Pallas kernels for 11%

profile of v22, /device:TPU:0, one launch (start us, length us, event | category | flops | bytes accessed | tf_op | source)
XLA Modules:
  0.0 29.3 jit_solution(16734178300260856899)
XLA Ops:
  0.0 0.0 copy-start
  0.0 5.0 %collective-permute-start.4 = (bf16[128,384]{1,0:T(8,128)(2,1)}, bf16[128,384]{1,0:T(8,128)(2,1)S(1)}, u32[]{:S(2)}, u32[]{:S(2)}) collective-permute-start(bf16[128,384]{1,0:T(8,128)(2,1)} %refs_3_.1), channel_id=1, source_target_pairs={{0,24},{2,26},{4,28},{6,30},{8,16},{10,18},{12,20},{14,22},{16,8},... | collective-permute-start | bytes 294920 | tf_op jit(solution)/shard_map/ppermute | solution.py:242
  5.1 1.0 %multiply_reduce_fusion.1 = f32[128]{0:T(128)S(1)} fusion(bf16[128,384]{1,0:T(8,128)(2,1)} %query_ref.1), kind=kLoop, calls=%fused_computation.1 | loop fusion | flops 147328 | bytes 98816 | tf_op jit(solution)/shard_map/reduce_sum | solution.py:275
  6.1 0.0 copy-done
  6.1 0.1 multiply_reduce_fusion
  6.2 0.0 copy-start.6
  6.2 0.0 copy-start.7
  6.2 1.6 %collective-permute-start = (f32[2,128]{1,0:T(2,128)S(1)}, f32[2,128]{1,0:T(2,128)S(1)}, u32[]{:S(2)}, u32[]{:S(2)}) collective-permute-start(f32[2,128]{1,0:T(2,128)S(1)} %pad_maximum_fusion.own_ref), channel_id=1, source_target_pairs={{0,1},{1,0},{2,3},{3,2},{4,5},{5,4},{6,7},{7,6},{8,9},{9,8},{10,11... | collective-permute-start | bytes 3080 | tf_op jit(solution)/shard_map/ppermute | solution.py:278
  7.8 0.0 copy-done.2
  7.8 1.5 %collective-permute-start.7 = (bf16[128,384]{1,0:T(8,128)(2,1)S(1)}, bf16[128,384]{1,0:T(8,128)(2,1)S(1)}, u32[]{:S(2)}, u32[]{:S(2)}) collective-permute-start(bf16[128,384]{1,0:T(8,128)(2,1)S(1)} %copy-done.2), channel_id=1, source_target_pairs={{0,4},{2,6},{4,0},{6,2},{8,12},{10,14},{12,8},{14,10},{16,20},{18,... | collective-permute-start | bytes 294920 | tf_op jit(solution)/shard_map/ppermute | solution.py:242
  9.3 0.0 copy-done.6
  9.3 0.0 copy-done.7
  9.3 0.0 copy-start.1
  9.3 0.0 copy-start.5
  9.3 0.5 %collective-permute-done.other_ref = f32[2,128]{1,0:T(2,128)S(1)} collective-permute-done((f32[2,128]{1,0:T(2,128)S(1)}, f32[2,128]{1,0:T(2,128)S(1)}, u32[]{:S(2)}, u32[]{:S(2)}) %collective-permute-start) | collective-permute-done | bytes 1056 | tf_op jit(solution)/shard_map/ppermute | solution.py:278
  9.9 0.1 shard_map.84.refs_0_
  10.0 0.1 collective-permute-start.2
  10.1 1.7 %collective-permute-start.6 = (bf16[128,384]{1,0:T(8,128)(2,1)S(1)}, bf16[128,384]{1,0:T(8,128)(2,1)S(1)}, u32[]{:S(2)}, u32[]{:S(2)}) collective-permute-start(bf16[128,384]{1,0:T(8,128)(2,1)S(1)} %shard_map.84.refs_0_), channel_id=1, source_target_pairs={{0,4},{2,6},{4,0},{6,2},{8,12},{10,14},{12,8},{14,10},{16,20},{18,... | collective-permute-start | bytes 294920 | tf_op jit(solution)/shard_map/ppermute | solution.py:242
  11.7 0.0 copy-done.1
  11.8 0.0 copy-done.5
  11.8 0.1 shard_map.82.own_ref.query_ref
  11.9 0.1 collective-permute-start.1
  12.0 0.0 collective-permute-done.4.source_ref
  12.0 0.5 %collective-permute-start.5 = (bf16[128,384]{1,0:T(8,128)(2,1)S(1)}, bf16[128,384]{1,0:T(8,128)(2,1)S(1)}, u32[]{:S(2)}, u32[]{:S(2)}) collective-permute-start(bf16[128,384]{1,0:T(8,128)(2,1)S(1)} %shard_map.85.refs_4_), channel_id=1, source_target_pairs={{0,4},{2,6},{4,0},{6,2},{8,12},{10,14},{12,8},{14,10},{16,20},{18,... | collective-permute-start | bytes 294920 | tf_op jit(solution)/shard_map/ppermute | solution.py:242
  12.4 4.1 %collective-permute-done.2.refs_1_ = bf16[128,384]{1,0:T(8,128)(2,1)S(1)} collective-permute-done((bf16[128,384]{1,0:T(8,128)(2,1)S(1)}, bf16[128,384]{1,0:T(8,128)(2,1)S(1)}, u32[]{:S(2)}, u32[]{:S(2)}) %collective-permute-start.2) | collective-permute-done | bytes 98336 | tf_op jit(solution)/shard_map/ppermute | solution.py:242
  16.6 1.5 %collective-permute-start.3 = (bf16[128,384]{1,0:T(8,128)(2,1)S(1)}, bf16[128,384]{1,0:T(8,128)(2,1)S(1)}, u32[]{:S(2)}, u32[]{:S(2)}) collective-permute-start(bf16[128,384]{1,0:T(8,128)(2,1)S(1)} %collective-permute-done.2.refs_1_), channel_id=1, source_target_pairs={{0,4},{2,6},{4,0},{6,2},{8,12},{10,14},{12,8},{14,10},{16,20},{18,... | collective-permute-start | bytes 294920 | tf_op jit(solution)/shard_map/ppermute | solution.py:242
  18.1 0.0 collective-permute-done.7.refs_5_
  18.1 0.0 collective-permute-done.6.refs_2_
  18.1 0.1 shard_map.86.pack_ref
  18.1 0.1 collective-permute-start.9
  18.2 0.0 collective-permute-done.1.remote_ref.query_ref
  18.2 0.1 shard_map.83.bias_ref
  18.3 0.6 %shard_map.87 = (f32[256,384]{1,0:T(8,128)S(1)}, f32[256,768]{1,0:T(8,128)S(1)}) custom-call(bf16[144,384]{1,0:T(8,128)(2,1)S(1)} %shard_map.82.own_ref.query_ref, bf16[144,384]{1,0:T(8,128)(2,1)S(1)} %collective-permute-done.1.remote_ref.query_ref, f32[16,1024]{1,0:T(8,128)S(1)} %shard_map.83.bias_ref, bf16[768,384]{1,0:T(8,128)(2,1)S(1)} %shard_map.86.pack_ref), custom_call_target="tpu_custom_call" | custom-call | tf_op jit(solution)/shard_map/pallas_call | solution.py:338
  18.9 0.0 collective-permute-done.5.refs_1_
  18.9 2.3 %collective-permute-done.3.refs_0_ = bf16[128,384]{1,0:T(8,128)(2,1)S(1)} collective-permute-done((bf16[128,384]{1,0:T(8,128)(2,1)S(1)}, bf16[128,384]{1,0:T(8,128)(2,1)S(1)}, u32[]{:S(2)}, u32[]{:S(2)}) %collective-permute-start.3) | collective-permute-done | bytes 98336 | tf_op jit(solution)/shard_map/ppermute | solution.py:242
  21.2 0.1 collective-permute-start.8
  21.3 0.0 collective-permute-done.9.pack_ref
  21.3 0.6 %shard_map.89 = (f32[256,384]{1,0:T(8,128)S(1)}, f32[256,768]{1,0:T(8,128)S(1)}) custom-call(bf16[144,384]{1,0:T(8,128)(2,1)S(1)} %shard_map.82.own_ref.query_ref, bf16[144,384]{1,0:T(8,128)(2,1)S(1)} %collective-permute-done.1.remote_ref.query_ref, f32[16,1024]{1,0:T(8,128)S(1)} %shard_map.83.bias_ref, ...), custom_call_target="tpu_custom_call" | custom-call | tf_op jit(solution)/shard_map/pallas_call | solution.py:338
  22.0 0.5 %shard_map.90 = (f32[256,384]{1,0:T(8,128)S(1)}, f32[256,768]{1,0:T(8,128)S(1)}) custom-call(bf16[144,384]{1,0:T(8,128)(2,1)S(1)} %shard_map.82.own_ref.query_ref, bf16[144,384]{1,0:T(8,128)(2,1)S(1)} %collective-permute-done.1.remote_ref.query_ref, f32[16,1024]{1,0:T(8,128)S(1)} %shard_map.83.bias_ref, bf16[256,384]{1,0:T(8,128)(2,1)S(1)} %shard_map.88.pack_ref, ...), custom_call_target="tpu_custom_call" | custom-call | tf_op jit(solution)/shard_map/pallas_call | solution.py:338
  22.4 0.3 collective-permute-done.8.pack_ref
  22.7 0.5 %shard_map.92 = bf16[144,384]{1,0:T(8,128)(2,1)S(1)} custom-call(bf16[144,384]{1,0:T(8,128)(2,1)S(1)} %collective-permute-done.1.remote_ref.query_ref, f32[16,1024]{1,0:T(8,128)S(1)} %shard_map.83.bias_ref, bf16[256,384]{1,0:T(8,128)(2,1)S(1)} %collective-permute-done.8.pack_ref, f32[256,384]{1,0:T(8,128)S(1)} %get-tuple-element.17.context_ref, ...), custom_call_target="tpu_custom_call" | custom-call | tf_op jit(solution)/shard_map/pallas_call | solution.py:361
  23.2 0.1 collective-permute-start.10
  23.3 0.3 %copy-done.3 = f32[50,384]{1,0:T(8,128)S(1)} copy-done((f32[50,384]{1,0:T(8,128)S(1)}, f32[50,384]{1,0:T(8,128)}, u32[]{:S(2)}) %copy-start.3) | copy-done | bytes 76824
  23.6 0.0 copy-done.4
  23.6 0.6 %shard_map.93.gate_ref = f32[16,384]{1,0:T(8,128)S(1)} custom-call(s32[2]{0:T(128)S(1)} %copy-done.4, f32[50,384]{1,0:T(8,128)S(1)} %copy-done.3), custom_call_target="tpu_custom_call" | custom-call | tf_op jit(solution)/shard_map/pallas_call | solution.py:377
  24.2 0.4 %shard_map.91 = (f32[128,384]{1,0:T(8,128)S(1)}, f32[16,384]{1,0:T(8,128)S(1)}) custom-call(bf16[144,384]{1,0:T(8,128)(2,1)S(1)} %shard_map.82.own_ref.query_ref, f32[16,1024]{1,0:T(8,128)S(1)} %shard_map.83.bias_ref, bf16[256,384]{1,0:T(8,128)(2,1)S(1)} %collective-permute-done.8.pack_ref, f32[256,384]{1,0:T(8,128)S(1)} %get-tuple-element.17.context_ref, ...), custom_call_target="tpu_custom_call" | custom-call | tf_op jit(solution)/shard_map/pallas_call | solution.py:361
  24.6 3.8 %collective-permute-done.10.packet_ref = bf16[144,384]{1,0:T(8,128)(2,1)S(1)} collective-permute-done((bf16[144,384]{1,0:T(8,128)(2,1)S(1)}, bf16[144,384]{1,0:T(8,128)(2,1)S(1)}, u32[]{:S(2)}, u32[]{:S(2)}) %collective-permute-start.10) | collective-permute-done | bytes 110624 | tf_op jit(solution)/shard_map/ppermute | solution.py:242
  28.5 0.8 %shard_map.94 = bf16[128,384]{1,0:T(8,128)(2,1)} custom-call(f32[128,384]{1,0:T(8,128)S(1)} %get-tuple-element.19.own_ref, f32[16,384]{1,0:T(8,128)S(1)} %get-tuple-element.20.lines_ref, bf16[144,384]{1,0:T(8,128)(2,1)S(1)} %collective-permute-done.10.packet_ref, f32[16,384]{1,0:T(8,128)S(1)} %shard_map.93.gate_ref), custom_call_target="tpu_custom_call" | custom-call | tf_op jit(solution)/shard_map/pallas_call | solution.py:386
  (8 shorter events, 0.0 us)
Async XLA Ops:
  0.0 6.1 %copy-start = (bf16[128,384]{1,0:T(8,128)(2,1)S(1)}, bf16[128,384]{1,0:T(8,128)(2,1)}, u32[]{:S(2)}) copy-start(bf16[128,384]{1,0:T(8,128)(2,1)} %key_ref.1) | copy-start | bytes 294916
  0.0 7.8 %copy-start.2 = (bf16[128,384]{1,0:T(8,128)(2,1)S(1)}, bf16[128,384]{1,0:T(8,128)(2,1)}, u32[]{:S(2)}) copy-start(bf16[128,384]{1,0:T(8,128)(2,1)} %refs_3_.1) | copy-start | bytes 294916
  0.0 12.0 %collective-permute-start.4 = (bf16[128,384]{1,0:T(8,128)(2,1)}, bf16[128,384]{1,0:T(8,128)(2,1)S(1)}, u32[]{:S(2)}, u32[]{:S(2)}) collective-permute-start(bf16[128,384]{1,0:T(8,128)(2,1)} %refs_3_.1), channel_id=1, source_target_pairs={{0,24},{2,26},{4,28},{6,30},{8,16},{10,18},{12,20},{14,22},{16,8},... | collective-permute-start | bytes 294920 | tf_op jit(solution)/shard_map/ppermute | solution.py:242
  6.2 3.1 %copy-start.6 = (f32[384]{0:T(512)S(1)}, f32[384]{0:T(512)}, u32[]{:S(2)}) copy-start(f32[384]{0:T(512)} %param.11) | copy-start | bytes 4612
  6.2 3.1 %copy-start.7 = (f32[384]{0:T(512)S(1)}, f32[384]{0:T(512)}, u32[]{:S(2)}) copy-start(f32[384]{0:T(512)} %param.12) | copy-start | bytes 4612
  6.2 3.6 %collective-permute-start = (f32[2,128]{1,0:T(2,128)S(1)}, f32[2,128]{1,0:T(2,128)S(1)}, u32[]{:S(2)}, u32[]{:S(2)}) collective-permute-start(f32[2,128]{1,0:T(2,128)S(1)} %pad_maximum_fusion.own_ref), channel_id=1, source_target_pairs={{0,1},{1,0},{2,3},{3,2},{4,5},{5,4},{6,7},{7,6},{8,9},{9,8},{10,11... | collective-permute-start | bytes 3080 | tf_op jit(solution)/shard_map/ppermute | solution.py:278
  7.8 10.2 %collective-permute-start.7 = (bf16[128,384]{1,0:T(8,128)(2,1)S(1)}, bf16[128,384]{1,0:T(8,128)(2,1)S(1)}, u32[]{:S(2)}, u32[]{:S(2)}) collective-permute-start(bf16[128,384]{1,0:T(8,128)(2,1)S(1)} %copy-done.2), channel_id=1, source_target_pairs={{0,4},{2,6},{4,0},{6,2},{8,12},{10,14},{12,8},{14,10},{16,20},{18,... | collective-permute-start | bytes 294920 | tf_op jit(solution)/shard_map/ppermute | solution.py:242
  9.3 2.4 %copy-start.1 = (bf16[128,384]{1,0:T(8,128)(2,1)S(1)}, bf16[128,384]{1,0:T(8,128)(2,1)}, u32[]{:S(2)}) copy-start(bf16[128,384]{1,0:T(8,128)(2,1)} %query_ref.1) | copy-start | bytes 294916
  9.3 2.4 %copy-start.5 = (s32[1,16]{1,0:T(1,128)S(1)}, s32[1,16]{1,0:T(1,128)}, u32[]{:S(2)}) copy-start(s32[1,16]{1,0:T(1,128)} %far_ref.1) | copy-start | bytes 196
  10.0 6.6 %collective-permute-start.2 = (bf16[128,384]{1,0:T(8,128)(2,1)S(1)}, bf16[128,384]{1,0:T(8,128)(2,1)S(1)}, u32[]{:S(2)}, u32[]{:S(2)}) collective-permute-start(bf16[128,384]{1,0:T(8,128)(2,1)S(1)} %shard_map.84.refs_0_), channel_id=1, source_target_pairs={{0,24},{2,26},{4,28},{6,30},{8,16},{10,18},{12,20},{14,22},{16,8},... | collective-permute-start | bytes 294920 | tf_op jit(solution)/shard_map/ppermute | solution.py:242
  10.1 8.0 %collective-permute-start.6 = (bf16[128,384]{1,0:T(8,128)(2,1)S(1)}, bf16[128,384]{1,0:T(8,128)(2,1)S(1)}, u32[]{:S(2)}, u32[]{:S(2)}) collective-permute-start(bf16[128,384]{1,0:T(8,128)(2,1)S(1)} %shard_map.84.refs_0_), channel_id=1, source_target_pairs={{0,4},{2,6},{4,0},{6,2},{8,12},{10,14},{12,8},{14,10},{16,20},{18,... | collective-permute-start | bytes 294920 | tf_op jit(solution)/shard_map/ppermute | solution.py:242
  11.9 6.3 %collective-permute-start.1 = (bf16[144,384]{1,0:T(8,128)(2,1)S(1)}, bf16[144,384]{1,0:T(8,128)(2,1)S(1)}, u32[]{:S(2)}, u32[]{:S(2)}) collective-permute-start(bf16[144,384]{1,0:T(8,128)(2,1)S(1)} %shard_map.82.own_ref.query_ref), channel_id=1, source_target_pairs={{0,8},{2,10},{4,12},{6,14},{8,0},{10,2},{12,4},{14,6},{16,24},{18,... | collective-permute-start | bytes 331784 | tf_op jit(solution)/shard_map/ppermute | solution.py:242
  12.0 6.9 %collective-permute-start.5 = (bf16[128,384]{1,0:T(8,128)(2,1)S(1)}, bf16[128,384]{1,0:T(8,128)(2,1)S(1)}, u32[]{:S(2)}, u32[]{:S(2)}) collective-permute-start(bf16[128,384]{1,0:T(8,128)(2,1)S(1)} %shard_map.85.refs_4_), channel_id=1, source_target_pairs={{0,4},{2,6},{4,0},{6,2},{8,12},{10,14},{12,8},{14,10},{16,20},{18,... | collective-permute-start | bytes 294920 | tf_op jit(solution)/shard_map/ppermute | solution.py:242
  16.6 4.6 %collective-permute-start.3 = (bf16[128,384]{1,0:T(8,128)(2,1)S(1)}, bf16[128,384]{1,0:T(8,128)(2,1)S(1)}, u32[]{:S(2)}, u32[]{:S(2)}) collective-permute-start(bf16[128,384]{1,0:T(8,128)(2,1)S(1)} %collective-permute-done.2.refs_1_), channel_id=1, source_target_pairs={{0,4},{2,6},{4,0},{6,2},{8,12},{10,14},{12,8},{14,10},{16,20},{18,... | collective-permute-start | bytes 294920 | tf_op jit(solution)/shard_map/ppermute | solution.py:242
  18.1 3.2 %collective-permute-start.9 = (bf16[768,384]{1,0:T(8,128)(2,1)S(1)}, bf16[768,384]{1,0:T(8,128)(2,1)S(1)}, u32[]{:S(2)}, u32[]{:S(2)}) collective-permute-start(bf16[768,384]{1,0:T(8,128)(2,1)S(1)} %shard_map.86.pack_ref), channel_id=1, source_target_pairs={{0,2},{2,0},{4,6},{6,4},{8,10},{10,8},{12,14},{14,12},{16,18},{18,... | collective-permute-start | bytes 1769480 | tf_op jit(solution)/shard_map/ppermute | solution.py:242
  21.2 1.5 %collective-permute-start.8 = (bf16[256,384]{1,0:T(8,128)(2,1)S(1)}, bf16[256,384]{1,0:T(8,128)(2,1)S(1)}, u32[]{:S(2)}, u32[]{:S(2)}) collective-permute-start(bf16[256,384]{1,0:T(8,128)(2,1)S(1)} %shard_map.88.pack_ref), channel_id=1, source_target_pairs={{0,2},{2,0},{4,6},{6,4},{8,10},{10,8},{12,14},{14,12},{16,18},{18,... | collective-permute-start | bytes 589832 | tf_op jit(solution)/shard_map/ppermute | solution.py:242
  22.7 0.9 %copy-start.3 = (f32[50,384]{1,0:T(8,128)S(1)}, f32[50,384]{1,0:T(8,128)}, u32[]{:S(2)}) copy-start(f32[50,384]{1,0:T(8,128)} %table_ref.1) | copy-start | bytes 230404
  22.7 0.9 %copy-start.4 = (s32[2]{0:T(128)S(1)}, s32[2]{0:T(128)}, u32[]{:S(2)}) copy-start(s32[2]{0:T(128)} %step_ref.1) | copy-start | bytes 28
  23.2 5.3 %collective-permute-start.10 = (bf16[144,384]{1,0:T(8,128)(2,1)S(1)}, bf16[144,384]{1,0:T(8,128)(2,1)S(1)}, u32[]{:S(2)}, u32[]{:S(2)}) collective-permute-start(bf16[144,384]{1,0:T(8,128)(2,1)S(1)} %shard_map.92), channel_id=1, source_target_pairs={{0,8},{2,10},{4,12},{6,14},{8,0},{10,2},{12,4},{14,6},{16,24},{18,... | collective-permute-start | bytes 331784 | tf_op jit(solution)/shard_map/ppermute | solution.py:242

commit v23 on v19

--- a/solution.py
+++ b/solution.py
@@ -213,7 +213,7 @@
     out_ref[rows:, :] = jnp.broadcast_to(table_ref[pl.ds(last, 1), :], (rows, out_ref.shape[1]))
 
 
-def merge_kernel(own_ref, lines_ref, packet_ref, gate_ref, out_ref):
+def merge_kernel(own_ref, lines_ref, packet_ref, gate_ref, out_hbm, out_ref, sems):
     rows, width = own_ref.shape
     pieces = packet_ref[rows:, :].astype(jnp.float32)
     own_top, own_total = lines_ref[0:1, :], lines_ref[8:9, :]
@@ -226,6 +226,7 @@
     start = lax.axis_index("tm") * rows
     first_rows = (start // FRAME_TOK + 1) * FRAME_TOK - start
     row_ids = lax.broadcasted_iota(jnp.int32, (rows, 1), 0)
+    copies = []
     for low in range(0, width, HD):
         high = low + HD
         context = own_ref[:, low:high] * spread(own_share[:, low:high])
@@ -235,6 +236,12 @@
             row_ids < first_rows, gate_ref[0:1, low:high], gate_ref[8:9, low:high]
         )
         out_ref[:, low:high] = (context * gate).astype(jnp.bfloat16)
+        part = (slice(None), pl.ds(low, HD))
+        copy = pltpu.make_async_copy(out_ref.at[part], out_hbm.at[part], sems.at[low // HD])
+        copy.start()
+        copies.append(copy)
+    for copy in copies:
+        copy.wait()
 
 
 def exchange(array, mask):
@@ -387,7 +394,11 @@
         merge_kernel,
         out_shape=jax.ShapeDtypeStruct((rows, width), jnp.bfloat16),
         in_specs=[VMEM] * 4,
-        out_specs=VMEM,
+        out_specs=ANY,
+        scratch_shapes=[
+            pltpu.VMEM((rows, width), jnp.bfloat16),
+            pltpu.SemaphoreType.DMA((width // HD,)),
+        ],
         compiler_params=params,
     )(own, own_lines, packet, gates)
 

time: 27.7 us -> 27.7 us (level)
  no operation moved by 1% of the time
where the time goes in v23:
time: 27.7 us; the launch traced here: 27.6 us
  starting transfers between devices  15.1 us (55%)
  waiting for transfers between devices  6.75 us (24%)
  Pallas kernels  4.42 us (16%)
  other arithmetic  1.11 us (4%)
    ppermute x10, starting transfers between devices, exchange(): return lax.ppermute(array, 'tm', [(i, i ^ mask) for i in range(count)])  13.5 us
    ppermute x10, waiting for transfers between devices, exchange(): return lax.ppermute(array, 'tm', [(i, i ^ mask) for i in range(count)])  6.23 us
    pallas_call x3, Pallas kernels, step(): pl.pallas_call(functools.partial(step_kernel, first), out_shape=[jax.Shap...  1.69 us
    ppermute x1, starting transfers between devices, local(): others = lax.ppermute(sums, 'head', [(0, 1), (1, 0)])  1.58 us
    reduce_sum x1, other arithmetic, local(): jnp.sum(query_f * query_f, axis=-1)  1 us
    pallas_call x2, Pallas kernels, last(): pl.pallas_call(functools.partial(last_attention, place), out_shape=out_sh...  0.9 us
    pallas_call x1, Pallas kernels, local(): pl.pallas_call(merge_kernel, out_shape=jax.ShapeDtypeStruct((rows, width)...  0.85 us
    pallas_call x1, Pallas kernels, local(): pl.pallas_call(gate_kernel, out_shape=jax.ShapeDtypeStruct((16, width), j...  0.57 us
  transfers between devices with their start and end apart: 11, of which 6 were waited for; matrix products, arithmetic and copies ran while one was open for 4% of the time, Pallas kernels for 11%

profile of v23, /device:TPU:0, one launch (start us, length us, event | category | flops | bytes accessed | tf_op | source)
XLA Modules:
  0.0 27.6 jit_solution(3389610814080990071)
XLA Ops:
  0.0 0.0 copy-start
  0.0 4.0 %collective-permute-start.4 = (bf16[128,384]{1,0:T(8,128)(2,1)}, bf16[128,384]{1,0:T(8,128)(2,1)S(1)}, u32[]{:S(2)}, u32[]{:S(2)}) collective-permute-start(bf16[128,384]{1,0:T(8,128)(2,1)} %refs_3_.1), channel_id=1, source_target_pairs={{0,16},{2,18},{4,20},{6,22},{8,24},{10,26},{12,28},{14,30},{16,0},... | collective-permute-start | bytes 294920 | tf_op jit(solution)/shard_map/ppermute | solution.py:249
  4.0 1.0 %multiply_reduce_fusion.1 = f32[128]{0:T(128)S(1)} fusion(bf16[128,384]{1,0:T(8,128)(2,1)} %query_ref.1), kind=kLoop, calls=%fused_computation.1 | loop fusion | flops 147328 | bytes 98816 | tf_op jit(solution)/shard_map/reduce_sum | solution.py:282
  5.0 0.0 copy-done
  5.1 0.1 multiply_reduce_fusion
  5.2 0.0 copy-start.6
  5.2 0.0 copy-start.7
  5.2 1.6 %collective-permute-start = (f32[2,128]{1,0:T(2,128)S(1)}, f32[2,128]{1,0:T(2,128)S(1)}, u32[]{:S(2)}, u32[]{:S(2)}) collective-permute-start(f32[2,128]{1,0:T(2,128)S(1)} %pad_maximum_fusion.own_ref), channel_id=1, source_target_pairs={{0,1},{1,0},{2,3},{3,2},{4,5},{5,4},{6,7},{7,6},{8,9},{9,8},{10,11... | collective-permute-start | bytes 3080 | tf_op jit(solution)/shard_map/ppermute | solution.py:285
  6.8 0.0 copy-done.2
  6.8 1.5 %collective-permute-start.7 = (bf16[128,384]{1,0:T(8,128)(2,1)S(1)}, bf16[128,384]{1,0:T(8,128)(2,1)S(1)}, u32[]{:S(2)}, u32[]{:S(2)}) collective-permute-start(bf16[128,384]{1,0:T(8,128)(2,1)S(1)} %copy-done.2), channel_id=1, source_target_pairs={{0,4},{2,6},{4,0},{6,2},{8,12},{10,14},{12,8},{14,10},{16,20},{18,... | collective-permute-start | bytes 294920 | tf_op jit(solution)/shard_map/ppermute | solution.py:249
  8.3 0.0 copy-done.6
  8.3 0.0 copy-done.7
  8.3 0.0 copy-start.1
  8.3 0.0 copy-start.5
  8.3 0.5 %collective-permute-done.other_ref = f32[2,128]{1,0:T(2,128)S(1)} collective-permute-done((f32[2,128]{1,0:T(2,128)S(1)}, f32[2,128]{1,0:T(2,128)S(1)}, u32[]{:S(2)}, u32[]{:S(2)}) %collective-permute-start) | collective-permute-done | bytes 1056 | tf_op jit(solution)/shard_map/ppermute | solution.py:285
  8.8 0.1 shard_map.84.refs_0_
  9.0 0.1 collective-permute-start.2
  9.1 1.8 %collective-permute-start.6 = (bf16[128,384]{1,0:T(8,128)(2,1)S(1)}, bf16[128,384]{1,0:T(8,128)(2,1)S(1)}, u32[]{:S(2)}, u32[]{:S(2)}) collective-permute-start(bf16[128,384]{1,0:T(8,128)(2,1)S(1)} %shard_map.84.refs_0_), channel_id=1, source_target_pairs={{0,4},{2,6},{4,0},{6,2},{8,12},{10,14},{12,8},{14,10},{16,20},{18,... | collective-permute-start | bytes 294920 | tf_op jit(solution)/shard_map/ppermute | solution.py:249
  10.8 0.0 copy-done.1
  10.9 0.0 copy-done.5
  10.9 0.1 shard_map.82.own_ref.query_ref
  11.0 1.6 %collective-permute-start.1 = (bf16[144,384]{1,0:T(8,128)(2,1)S(1)}, bf16[144,384]{1,0:T(8,128)(2,1)S(1)}, u32[]{:S(2)}, u32[]{:S(2)}) collective-permute-start(bf16[144,384]{1,0:T(8,128)(2,1)S(1)} %shard_map.82.own_ref.query_ref), channel_id=1, source_target_pairs={{0,8},{2,10},{4,12},{6,14},{8,0},{10,2},{12,4},{14,6},{16,24},{18,... | collective-permute-start | bytes 331784 | tf_op jit(solution)/shard_map/ppermute | solution.py:249
  12.6 0.0 collective-permute-done.4.source_ref
  12.6 0.6 %collective-permute-start.5 = (bf16[128,384]{1,0:T(8,128)(2,1)S(1)}, bf16[128,384]{1,0:T(8,128)(2,1)S(1)}, u32[]{:S(2)}, u32[]{:S(2)}) collective-permute-start(bf16[128,384]{1,0:T(8,128)(2,1)S(1)} %shard_map.85.refs_4_), channel_id=1, source_target_pairs={{0,4},{2,6},{4,0},{6,2},{8,12},{10,14},{12,8},{14,10},{16,20},{18,... | collective-permute-start | bytes 294920 | tf_op jit(solution)/shard_map/ppermute | solution.py:249
  13.2 1.3 %collective-permute-done.2.refs_1_ = bf16[128,384]{1,0:T(8,128)(2,1)S(1)} collective-permute-done((bf16[128,384]{1,0:T(8,128)(2,1)S(1)}, bf16[128,384]{1,0:T(8,128)(2,1)S(1)}, u32[]{:S(2)}, u32[]{:S(2)}) %collective-permute-start.2) | collective-permute-done | bytes 98336 | tf_op jit(solution)/shard_map/ppermute | solution.py:249
  14.5 1.6 %collective-permute-start.3 = (bf16[128,384]{1,0:T(8,128)(2,1)S(1)}, bf16[128,384]{1,0:T(8,128)(2,1)S(1)}, u32[]{:S(2)}, u32[]{:S(2)}) collective-permute-start(bf16[128,384]{1,0:T(8,128)(2,1)S(1)} %collective-permute-done.2.refs_1_), channel_id=1, source_target_pairs={{0,4},{2,6},{4,0},{6,2},{8,12},{10,14},{12,8},{14,10},{16,20},{18,... | collective-permute-start | bytes 294920 | tf_op jit(solution)/shard_map/ppermute | solution.py:249
  16.1 0.0 collective-permute-done.7.refs_5_
  16.1 0.0 collective-permute-done.6.refs_2_
  16.1 0.1 shard_map.86.pack_ref
  16.2 0.1 collective-permute-start.9
  16.3 0.0 collective-permute-done.1.remote_ref.query_ref
  16.3 0.1 shard_map.83.bias_ref
  16.4 0.6 %shard_map.87 = (f32[256,384]{1,0:T(8,128)S(1)}, f32[256,768]{1,0:T(8,128)S(1)}) custom-call(bf16[144,384]{1,0:T(8,128)(2,1)S(1)} %shard_map.82.own_ref.query_ref, bf16[144,384]{1,0:T(8,128)(2,1)S(1)} %collective-permute-done.1.remote_ref.query_ref, f32[16,1024]{1,0:T(8,128)S(1)} %shard_map.83.bias_ref, bf16[768,384]{1,0:T(8,128)(2,1)S(1)} %shard_map.86.pack_ref), custom_call_target="tpu_custom_call" | custom-call | tf_op jit(solution)/shard_map/pallas_call | solution.py:345
  17.0 1.0 %collective-permute-done.5.refs_1_ = bf16[128,384]{1,0:T(8,128)(2,1)S(1)} collective-permute-done((bf16[128,384]{1,0:T(8,128)(2,1)S(1)}, bf16[128,384]{1,0:T(8,128)(2,1)S(1)}, u32[]{:S(2)}, u32[]{:S(2)}) %collective-permute-start.5) | collective-permute-done | bytes 98336 | tf_op jit(solution)/shard_map/ppermute | solution.py:249
  17.9 1.2 %collective-permute-done.3.refs_0_ = bf16[128,384]{1,0:T(8,128)(2,1)S(1)} collective-permute-done((bf16[128,384]{1,0:T(8,128)(2,1)S(1)}, bf16[128,384]{1,0:T(8,128)(2,1)S(1)}, u32[]{:S(2)}, u32[]{:S(2)}) %collective-permute-start.3) | collective-permute-done | bytes 98336 | tf_op jit(solution)/shard_map/ppermute | solution.py:249
  19.2 0.1 collective-permute-start.8
  19.3 0.0 collective-permute-done.9.pack_ref
  19.3 0.6 %shard_map.89 = (f32[256,384]{1,0:T(8,128)S(1)}, f32[256,768]{1,0:T(8,128)S(1)}) custom-call(bf16[144,384]{1,0:T(8,128)(2,1)S(1)} %shard_map.82.own_ref.query_ref, bf16[144,384]{1,0:T(8,128)(2,1)S(1)} %collective-permute-done.1.remote_ref.query_ref, f32[16,1024]{1,0:T(8,128)S(1)} %shard_map.83.bias_ref, ...), custom_call_target="tpu_custom_call" | custom-call | tf_op jit(solution)/shard_map/pallas_call | solution.py:345
  19.9 0.5 %shard_map.90 = (f32[256,384]{1,0:T(8,128)S(1)}, f32[256,768]{1,0:T(8,128)S(1)}) custom-call(bf16[144,384]{1,0:T(8,128)(2,1)S(1)} %shard_map.82.own_ref.query_ref, bf16[144,384]{1,0:T(8,128)(2,1)S(1)} %collective-permute-done.1.remote_ref.query_ref, f32[16,1024]{1,0:T(8,128)S(1)} %shard_map.83.bias_ref, bf16[256,384]{1,0:T(8,128)(2,1)S(1)} %shard_map.88.pack_ref, ...), custom_call_target="tpu_custom_call" | custom-call | tf_op jit(solution)/shard_map/pallas_call | solution.py:345
  20.4 0.3 %collective-permute-done.8.pack_ref = bf16[256,384]{1,0:T(8,128)(2,1)S(1)} collective-permute-done((bf16[256,384]{1,0:T(8,128)(2,1)S(1)}, bf16[256,384]{1,0:T(8,128)(2,1)S(1)}, u32[]{:S(2)}, u32[]{:S(2)}) %collective-permute-start.8) | collective-permute-done | bytes 196640 | tf_op jit(solution)/shard_map/ppermute | solution.py:249
  20.7 0.5 %shard_map.92 = bf16[144,384]{1,0:T(8,128)(2,1)S(1)} custom-call(bf16[144,384]{1,0:T(8,128)(2,1)S(1)} %collective-permute-done.1.remote_ref.query_ref, f32[16,1024]{1,0:T(8,128)S(1)} %shard_map.83.bias_ref, bf16[256,384]{1,0:T(8,128)(2,1)S(1)} %collective-permute-done.8.pack_ref, f32[256,384]{1,0:T(8,128)S(1)} %get-tuple-element.17.context_ref, ...), custom_call_target="tpu_custom_call" | custom-call | tf_op jit(solution)/shard_map/pallas_call | solution.py:368
  21.2 2.1 %collective-permute-start.10 = (bf16[144,384]{1,0:T(8,128)(2,1)S(1)}, bf16[144,384]{1,0:T(8,128)(2,1)S(1)}, u32[]{:S(2)}, u32[]{:S(2)}) collective-permute-start(bf16[144,384]{1,0:T(8,128)(2,1)S(1)} %shard_map.92), channel_id=1, source_target_pairs={{0,8},{2,10},{4,12},{6,14},{8,0},{10,2},{12,4},{14,6},{16,24},{18,... | collective-permute-start | bytes 331784 | tf_op jit(solution)/shard_map/ppermute | solution.py:249
  23.3 0.0 copy-done.3
  23.3 0.0 copy-done.4
  23.3 0.6 %shard_map.93.gate_ref = f32[16,384]{1,0:T(8,128)S(1)} custom-call(s32[2]{0:T(128)S(1)} %copy-done.4, f32[50,384]{1,0:T(8,128)S(1)} %copy-done.3), custom_call_target="tpu_custom_call" | custom-call | tf_op jit(solution)/shard_map/pallas_call | solution.py:384
  23.9 0.4 %shard_map.91 = (f32[128,384]{1,0:T(8,128)S(1)}, f32[16,384]{1,0:T(8,128)S(1)}) custom-call(bf16[144,384]{1,0:T(8,128)(2,1)S(1)} %shard_map.82.own_ref.query_ref, f32[16,1024]{1,0:T(8,128)S(1)} %shard_map.83.bias_ref, bf16[256,384]{1,0:T(8,128)(2,1)S(1)} %collective-permute-done.8.pack_ref, f32[256,384]{1,0:T(8,128)S(1)} %get-tuple-element.17.context_ref, ...), custom_call_target="tpu_custom_call" | custom-call | tf_op jit(solution)/shard_map/pallas_call | solution.py:368
  24.3 2.4 %collective-permute-done.10.packet_ref = bf16[144,384]{1,0:T(8,128)(2,1)S(1)} collective-permute-done((bf16[144,384]{1,0:T(8,128)(2,1)S(1)}, bf16[144,384]{1,0:T(8,128)(2,1)S(1)}, u32[]{:S(2)}, u32[]{:S(2)}) %collective-permute-start.10) | collective-permute-done | bytes 110624 | tf_op jit(solution)/shard_map/ppermute | solution.py:249
  26.7 0.8 %shard_map.94 = bf16[128,384]{1,0:T(8,128)(2,1)} custom-call(f32[128,384]{1,0:T(8,128)S(1)} %get-tuple-element.19.own_ref, f32[16,384]{1,0:T(8,128)S(1)} %get-tuple-element.20.lines_ref, bf16[144,384]{1,0:T(8,128)(2,1)S(1)} %collective-permute-done.10.packet_ref, f32[16,384]{1,0:T(8,128)S(1)} %shard_map.93.gate_ref), custom_call_target="tpu_custom_call" | custom-call | tf_op jit(solution)/shard_map/pallas_call | solution.py:393
  (8 shorter events, 0.0 us)
Async XLA Ops:
  0.0 5.0 %copy-start = (bf16[128,384]{1,0:T(8,128)(2,1)S(1)}, bf16[128,384]{1,0:T(8,128)(2,1)}, u32[]{:S(2)}) copy-start(bf16[128,384]{1,0:T(8,128)(2,1)} %key_ref.1) | copy-start | bytes 294916
  0.0 6.8 %copy-start.2 = (bf16[128,384]{1,0:T(8,128)(2,1)S(1)}, bf16[128,384]{1,0:T(8,128)(2,1)}, u32[]{:S(2)}) copy-start(bf16[128,384]{1,0:T(8,128)(2,1)} %refs_3_.1) | copy-start | bytes 294916
  0.0 12.6 %collective-permute-start.4 = (bf16[128,384]{1,0:T(8,128)(2,1)}, bf16[128,384]{1,0:T(8,128)(2,1)S(1)}, u32[]{:S(2)}, u32[]{:S(2)}) collective-permute-start(bf16[128,384]{1,0:T(8,128)(2,1)} %refs_3_.1), channel_id=1, source_target_pairs={{0,16},{2,18},{4,20},{6,22},{8,24},{10,26},{12,28},{14,30},{16,0},... | collective-permute-start | bytes 294920 | tf_op jit(solution)/shard_map/ppermute | solution.py:249
  5.2 3.1 %copy-start.6 = (f32[384]{0:T(512)S(1)}, f32[384]{0:T(512)}, u32[]{:S(2)}) copy-start(f32[384]{0:T(512)} %param.11) | copy-start | bytes 4612
  5.2 3.1 %copy-start.7 = (f32[384]{0:T(512)S(1)}, f32[384]{0:T(512)}, u32[]{:S(2)}) copy-start(f32[384]{0:T(512)} %param.12) | copy-start | bytes 4612
  5.2 3.6 %collective-permute-start = (f32[2,128]{1,0:T(2,128)S(1)}, f32[2,128]{1,0:T(2,128)S(1)}, u32[]{:S(2)}, u32[]{:S(2)}) collective-permute-start(f32[2,128]{1,0:T(2,128)S(1)} %pad_maximum_fusion.own_ref), channel_id=1, source_target_pairs={{0,1},{1,0},{2,3},{3,2},{4,5},{5,4},{6,7},{7,6},{8,9},{9,8},{10,11... | collective-permute-start | bytes 3080 | tf_op jit(solution)/shard_map/ppermute | solution.py:285
  6.8 9.3 %collective-permute-start.7 = (bf16[128,384]{1,0:T(8,128)(2,1)S(1)}, bf16[128,384]{1,0:T(8,128)(2,1)S(1)}, u32[]{:S(2)}, u32[]{:S(2)}) collective-permute-start(bf16[128,384]{1,0:T(8,128)(2,1)S(1)} %copy-done.2), channel_id=1, source_target_pairs={{0,4},{2,6},{4,0},{6,2},{8,12},{10,14},{12,8},{14,10},{16,20},{18,... | collective-permute-start | bytes 294920 | tf_op jit(solution)/shard_map/ppermute | solution.py:249
  8.3 2.6 %copy-start.1 = (bf16[128,384]{1,0:T(8,128)(2,1)S(1)}, bf16[128,384]{1,0:T(8,128)(2,1)}, u32[]{:S(2)}) copy-start(bf16[128,384]{1,0:T(8,128)(2,1)} %query_ref.1) | copy-start | bytes 294916
  8.3 2.5 %copy-start.5 = (s32[1,16]{1,0:T(1,128)S(1)}, s32[1,16]{1,0:T(1,128)}, u32[]{:S(2)}) copy-start(s32[1,16]{1,0:T(1,128)} %far_ref.1) | copy-start | bytes 196
  9.0 5.6 %collective-permute-start.2 = (bf16[128,384]{1,0:T(8,128)(2,1)S(1)}, bf16[128,384]{1,0:T(8,128)(2,1)S(1)}, u32[]{:S(2)}, u32[]{:S(2)}) collective-permute-start(bf16[128,384]{1,0:T(8,128)(2,1)S(1)} %shard_map.84.refs_0_), channel_id=1, source_target_pairs={{0,16},{2,18},{4,20},{6,22},{8,24},{10,26},{12,28},{14,30},{16,0},... | collective-permute-start | bytes 294920 | tf_op jit(solution)/shard_map/ppermute | solution.py:249
  9.1 7.1 %collective-permute-start.6 = (bf16[128,384]{1,0:T(8,128)(2,1)S(1)}, bf16[128,384]{1,0:T(8,128)(2,1)S(1)}, u32[]{:S(2)}, u32[]{:S(2)}) collective-permute-start(bf16[128,384]{1,0:T(8,128)(2,1)S(1)} %shard_map.84.refs_0_), channel_id=1, source_target_pairs={{0,4},{2,6},{4,0},{6,2},{8,12},{10,14},{12,8},{14,10},{16,20},{18,... | collective-permute-start | bytes 294920 | tf_op jit(solution)/shard_map/ppermute | solution.py:249
  11.0 5.3 %collective-permute-start.1 = (bf16[144,384]{1,0:T(8,128)(2,1)S(1)}, bf16[144,384]{1,0:T(8,128)(2,1)S(1)}, u32[]{:S(2)}, u32[]{:S(2)}) collective-permute-start(bf16[144,384]{1,0:T(8,128)(2,1)S(1)} %shard_map.82.own_ref.query_ref), channel_id=1, source_target_pairs={{0,8},{2,10},{4,12},{6,14},{8,0},{10,2},{12,4},{14,6},{16,24},{18,... | collective-permute-start | bytes 331784 | tf_op jit(solution)/shard_map/ppermute | solution.py:249
  12.6 5.3 %collective-permute-start.5 = (bf16[128,384]{1,0:T(8,128)(2,1)S(1)}, bf16[128,384]{1,0:T(8,128)(2,1)S(1)}, u32[]{:S(2)}, u32[]{:S(2)}) collective-permute-start(bf16[128,384]{1,0:T(8,128)(2,1)S(1)} %shard_map.85.refs_4_), channel_id=1, source_target_pairs={{0,4},{2,6},{4,0},{6,2},{8,12},{10,14},{12,8},{14,10},{16,20},{18,... | collective-permute-start | bytes 294920 | tf_op jit(solution)/shard_map/ppermute | solution.py:249
  14.5 4.6 %collective-permute-start.3 = (bf16[128,384]{1,0:T(8,128)(2,1)S(1)}, bf16[128,384]{1,0:T(8,128)(2,1)S(1)}, u32[]{:S(2)}, u32[]{:S(2)}) collective-permute-start(bf16[128,384]{1,0:T(8,128)(2,1)S(1)} %collective-permute-done.2.refs_1_), channel_id=1, source_target_pairs={{0,4},{2,6},{4,0},{6,2},{8,12},{10,14},{12,8},{14,10},{16,20},{18,... | collective-permute-start | bytes 294920 | tf_op jit(solution)/shard_map/ppermute | solution.py:249
  16.2 3.1 %collective-permute-start.9 = (bf16[768,384]{1,0:T(8,128)(2,1)S(1)}, bf16[768,384]{1,0:T(8,128)(2,1)S(1)}, u32[]{:S(2)}, u32[]{:S(2)}) collective-permute-start(bf16[768,384]{1,0:T(8,128)(2,1)S(1)} %shard_map.86.pack_ref), channel_id=1, source_target_pairs={{0,2},{2,0},{4,6},{6,4},{8,10},{10,8},{12,14},{14,12},{16,18},{18,... | collective-permute-start | bytes 1769480 | tf_op jit(solution)/shard_map/ppermute | solution.py:249
  19.2 1.5 %collective-permute-start.8 = (bf16[256,384]{1,0:T(8,128)(2,1)S(1)}, bf16[256,384]{1,0:T(8,128)(2,1)S(1)}, u32[]{:S(2)}, u32[]{:S(2)}) collective-permute-start(bf16[256,384]{1,0:T(8,128)(2,1)S(1)} %shard_map.88.pack_ref), channel_id=1, source_target_pairs={{0,2},{2,0},{4,6},{6,4},{8,10},{10,8},{12,14},{14,12},{16,18},{18,... | collective-permute-start | bytes 589832 | tf_op jit(solution)/shard_map/ppermute | solution.py:249
  20.7 2.6 %copy-start.3 = (f32[50,384]{1,0:T(8,128)S(1)}, f32[50,384]{1,0:T(8,128)}, u32[]{:S(2)}) copy-start(f32[50,384]{1,0:T(8,128)} %table_ref.1) | copy-start | bytes 230404
  20.7 2.6 %copy-start.4 = (s32[2]{0:T(128)S(1)}, s32[2]{0:T(128)}, u32[]{:S(2)}) copy-start(s32[2]{0:T(128)} %step_ref.1) | copy-start | bytes 28
  21.2 5.6 %collective-permute-start.10 = (bf16[144,384]{1,0:T(8,128)(2,1)S(1)}, bf16[144,384]{1,0:T(8,128)(2,1)S(1)}, u32[]{:S(2)}, u32[]{:S(2)}) collective-permute-start(bf16[144,384]{1,0:T(8,128)(2,1)S(1)} %shard_map.92), channel_id=1, source_target_pairs={{0,8},{2,10},{4,12},{6,14},{8,0},{10,2},{12,4},{14,6},{16,24},{18,... | collective-permute-start | bytes 331784 | tf_op jit(solution)/shard_map/ppermute | solution.py:249

commit v24 on v23

--- a/solution.py
+++ b/solution.py
@@ -223,15 +223,19 @@
     own_share, other_share = jnp.exp2(own_top - top), jnp.exp2(other_top - top)
     scale = 1.0 / (own_total * own_share + other_total * other_share)
     own_share, other_share = own_share * scale, other_share * scale
+    shares = [share[:, low : low + HD] for share in (own_share, other_share) for low in range(0, width, HD)]
+    shares += [jnp.zeros((1, HD), jnp.float32)] * (-len(shares) % 8)
+    columns = jnp.concatenate(shares, axis=0).T
     start = lax.axis_index("tm") * rows
     first_rows = (start // FRAME_TOK + 1) * FRAME_TOK - start
     row_ids = lax.broadcasted_iota(jnp.int32, (rows, 1), 0)
     copies = []
     for low in range(0, width, HD):
         high = low + HD
-        context = own_ref[:, low:high] * spread(own_share[:, low:high])
+        context = own_ref[:, low:high] * columns[:, low // HD : low // HD + 1]
         other = packet_ref[:rows, low:high].astype(jnp.float32)
-        context += other * spread(other_share[:, low:high])
+        spot = (width + low) // HD
+        context += other * columns[:, spot : spot + 1]
         gate = jnp.where(
             row_ids < first_rows, gate_ref[0:1, low:high], gate_ref[8:9, low:high]
         )

time: 27.7 us -> 27.9 us (level)
  no operation moved by 1% of the time
where the time goes in v24:
time: 27.9 us; the launch traced here: 27.7 us
  starting transfers between devices  15.1 us (54%)
  waiting for transfers between devices  6.75 us (24%)
  Pallas kernels  4.55 us (16%)
  other arithmetic  1.11 us (4%)
    ppermute x10, starting transfers between devices, exchange(): return lax.ppermute(array, 'tm', [(i, i ^ mask) for i in range(count)])  13.5 us
    ppermute x10, waiting for transfers between devices, exchange(): return lax.ppermute(array, 'tm', [(i, i ^ mask) for i in range(count)])  6.23 us
    pallas_call x3, Pallas kernels, step(): pl.pallas_call(functools.partial(step_kernel, first), out_shape=[jax.Shap...  1.69 us
    ppermute x1, starting transfers between devices, local(): others = lax.ppermute(sums, 'head', [(0, 1), (1, 0)])  1.58 us
    reduce_sum x1, other arithmetic, local(): jnp.sum(query_f * query_f, axis=-1)  1 us
    pallas_call x1, Pallas kernels, local(): pl.pallas_call(merge_kernel, out_shape=jax.ShapeDtypeStruct((rows, width)...  0.98 us
    pallas_call x2, Pallas kernels, last(): pl.pallas_call(functools.partial(last_attention, place), out_shape=out_sh...  0.9 us
    pallas_call x1, Pallas kernels, local(): pl.pallas_call(gate_kernel, out_shape=jax.ShapeDtypeStruct((16, width), j...  0.57 us
  transfers between devices with their start and end apart: 11, of which 6 were waited for; matrix products, arithmetic and copies ran while one was open for 4% of the time, Pallas kernels for 11%

profile of v24, /device:TPU:0, one launch (start us, length us, event | category | flops | bytes accessed | tf_op | source)
XLA Modules:
  0.0 27.7 jit_solution(12556271736106139509)
XLA Ops:
  0.0 0.0 copy-start
  0.0 4.0 %collective-permute-start.4 = (bf16[128,384]{1,0:T(8,128)(2,1)}, bf16[128,384]{1,0:T(8,128)(2,1)S(1)}, u32[]{:S(2)}, u32[]{:S(2)}) collective-permute-start(bf16[128,384]{1,0:T(8,128)(2,1)} %refs_3_.1), channel_id=1, source_target_pairs={{0,16},{2,18},{4,20},{6,22},{8,24},{10,26},{12,28},{14,30},{16,0},... | collective-permute-start | bytes 294920 | tf_op jit(solution)/shard_map/ppermute | solution.py:253
  4.0 1.0 %multiply_reduce_fusion.1 = f32[128]{0:T(128)S(1)} fusion(bf16[128,384]{1,0:T(8,128)(2,1)} %query_ref.1), kind=kLoop, calls=%fused_computation.1 | loop fusion | flops 147328 | bytes 98816 | tf_op jit(solution)/shard_map/reduce_sum | solution.py:286
  5.0 0.0 copy-done
  5.1 0.1 multiply_reduce_fusion
  5.2 0.0 copy-start.6
  5.2 0.0 copy-start.7
  5.2 1.6 %collective-permute-start = (f32[2,128]{1,0:T(2,128)S(1)}, f32[2,128]{1,0:T(2,128)S(1)}, u32[]{:S(2)}, u32[]{:S(2)}) collective-permute-start(f32[2,128]{1,0:T(2,128)S(1)} %pad_maximum_fusion.own_ref), channel_id=1, source_target_pairs={{0,1},{1,0},{2,3},{3,2},{4,5},{5,4},{6,7},{7,6},{8,9},{9,8},{10,11... | collective-permute-start | bytes 3080 | tf_op jit(solution)/shard_map/ppermute | solution.py:289
  6.8 0.0 copy-done.2
  6.8 1.5 %collective-permute-start.7 = (bf16[128,384]{1,0:T(8,128)(2,1)S(1)}, bf16[128,384]{1,0:T(8,128)(2,1)S(1)}, u32[]{:S(2)}, u32[]{:S(2)}) collective-permute-start(bf16[128,384]{1,0:T(8,128)(2,1)S(1)} %copy-done.2), channel_id=1, source_target_pairs={{0,4},{2,6},{4,0},{6,2},{8,12},{10,14},{12,8},{14,10},{16,20},{18,... | collective-permute-start | bytes 294920 | tf_op jit(solution)/shard_map/ppermute | solution.py:253
  8.3 0.0 copy-done.6
  8.3 0.0 copy-done.7
  8.3 0.0 copy-start.1
  8.3 0.0 copy-start.5
  8.3 0.5 %collective-permute-done.other_ref = f32[2,128]{1,0:T(2,128)S(1)} collective-permute-done((f32[2,128]{1,0:T(2,128)S(1)}, f32[2,128]{1,0:T(2,128)S(1)}, u32[]{:S(2)}, u32[]{:S(2)}) %collective-permute-start) | collective-permute-done | bytes 1056 | tf_op jit(solution)/shard_map/ppermute | solution.py:289
  8.8 0.1 shard_map.84.refs_0_
  9.0 0.1 collective-permute-start.2
  9.1 1.8 %collective-permute-start.6 = (bf16[128,384]{1,0:T(8,128)(2,1)S(1)}, bf16[128,384]{1,0:T(8,128)(2,1)S(1)}, u32[]{:S(2)}, u32[]{:S(2)}) collective-permute-start(bf16[128,384]{1,0:T(8,128)(2,1)S(1)} %shard_map.84.refs_0_), channel_id=1, source_target_pairs={{0,4},{2,6},{4,0},{6,2},{8,12},{10,14},{12,8},{14,10},{16,20},{18,... | collective-permute-start | bytes 294920 | tf_op jit(solution)/shard_map/ppermute | solution.py:253
  10.8 0.0 copy-done.1
  10.9 0.0 copy-done.5
  10.9 0.1 shard_map.82.own_ref.query_ref
  11.0 1.6 %collective-permute-start.1 = (bf16[144,384]{1,0:T(8,128)(2,1)S(1)}, bf16[144,384]{1,0:T(8,128)(2,1)S(1)}, u32[]{:S(2)}, u32[]{:S(2)}) collective-permute-start(bf16[144,384]{1,0:T(8,128)(2,1)S(1)} %shard_map.82.own_ref.query_ref), channel_id=1, source_target_pairs={{0,8},{2,10},{4,12},{6,14},{8,0},{10,2},{12,4},{14,6},{16,24},{18,... | collective-permute-start | bytes 331784 | tf_op jit(solution)/shard_map/ppermute | solution.py:253
  12.6 0.0 collective-permute-done.4.source_ref
  12.6 0.6 %collective-permute-start.5 = (bf16[128,384]{1,0:T(8,128)(2,1)S(1)}, bf16[128,384]{1,0:T(8,128)(2,1)S(1)}, u32[]{:S(2)}, u32[]{:S(2)}) collective-permute-start(bf16[128,384]{1,0:T(8,128)(2,1)S(1)} %shard_map.85.refs_4_), channel_id=1, source_target_pairs={{0,4},{2,6},{4,0},{6,2},{8,12},{10,14},{12,8},{14,10},{16,20},{18,... | collective-permute-start | bytes 294920 | tf_op jit(solution)/shard_map/ppermute | solution.py:253
  13.2 1.3 %collective-permute-done.2.refs_1_ = bf16[128,384]{1,0:T(8,128)(2,1)S(1)} collective-permute-done((bf16[128,384]{1,0:T(8,128)(2,1)S(1)}, bf16[128,384]{1,0:T(8,128)(2,1)S(1)}, u32[]{:S(2)}, u32[]{:S(2)}) %collective-permute-start.2) | collective-permute-done | bytes 98336 | tf_op jit(solution)/shard_map/ppermute | solution.py:253
  14.5 1.6 %collective-permute-start.3 = (bf16[128,384]{1,0:T(8,128)(2,1)S(1)}, bf16[128,384]{1,0:T(8,128)(2,1)S(1)}, u32[]{:S(2)}, u32[]{:S(2)}) collective-permute-start(bf16[128,384]{1,0:T(8,128)(2,1)S(1)} %collective-permute-done.2.refs_1_), channel_id=1, source_target_pairs={{0,4},{2,6},{4,0},{6,2},{8,12},{10,14},{12,8},{14,10},{16,20},{18,... | collective-permute-start | bytes 294920 | tf_op jit(solution)/shard_map/ppermute | solution.py:253
  16.1 0.0 collective-permute-done.7.refs_5_
  16.1 0.0 collective-permute-done.6.refs_2_
  16.1 0.1 shard_map.86.pack_ref
  16.2 0.1 collective-permute-start.9
  16.3 0.0 collective-permute-done.1.remote_ref.query_ref
  16.3 0.1 shard_map.83.bias_ref
  16.4 0.6 %shard_map.87 = (f32[256,384]{1,0:T(8,128)S(1)}, f32[256,768]{1,0:T(8,128)S(1)}) custom-call(bf16[144,384]{1,0:T(8,128)(2,1)S(1)} %shard_map.82.own_ref.query_ref, bf16[144,384]{1,0:T(8,128)(2,1)S(1)} %collective-permute-done.1.remote_ref.query_ref, f32[16,1024]{1,0:T(8,128)S(1)} %shard_map.83.bias_ref, bf16[768,384]{1,0:T(8,128)(2,1)S(1)} %shard_map.86.pack_ref), custom_call_target="tpu_custom_call" | custom-call | tf_op jit(solution)/shard_map/pallas_call | solution.py:349
  17.0 1.0 %collective-permute-done.5.refs_1_ = bf16[128,384]{1,0:T(8,128)(2,1)S(1)} collective-permute-done((bf16[128,384]{1,0:T(8,128)(2,1)S(1)}, bf16[128,384]{1,0:T(8,128)(2,1)S(1)}, u32[]{:S(2)}, u32[]{:S(2)}) %collective-permute-start.5) | collective-permute-done | bytes 98336 | tf_op jit(solution)/shard_map/ppermute | solution.py:253
  17.9 1.2 %collective-permute-done.3.refs_0_ = bf16[128,384]{1,0:T(8,128)(2,1)S(1)} collective-permute-done((bf16[128,384]{1,0:T(8,128)(2,1)S(1)}, bf16[128,384]{1,0:T(8,128)(2,1)S(1)}, u32[]{:S(2)}, u32[]{:S(2)}) %collective-permute-start.3) | collective-permute-done | bytes 98336 | tf_op jit(solution)/shard_map/ppermute | solution.py:253
  19.2 0.1 collective-permute-start.8
  19.3 0.0 collective-permute-done.9.pack_ref
  19.3 0.6 %shard_map.89 = (f32[256,384]{1,0:T(8,128)S(1)}, f32[256,768]{1,0:T(8,128)S(1)}) custom-call(bf16[144,384]{1,0:T(8,128)(2,1)S(1)} %shard_map.82.own_ref.query_ref, bf16[144,384]{1,0:T(8,128)(2,1)S(1)} %collective-permute-done.1.remote_ref.query_ref, f32[16,1024]{1,0:T(8,128)S(1)} %shard_map.83.bias_ref, ...), custom_call_target="tpu_custom_call" | custom-call | tf_op jit(solution)/shard_map/pallas_call | solution.py:349
  19.9 0.5 %shard_map.90 = (f32[256,384]{1,0:T(8,128)S(1)}, f32[256,768]{1,0:T(8,128)S(1)}) custom-call(bf16[144,384]{1,0:T(8,128)(2,1)S(1)} %shard_map.82.own_ref.query_ref, bf16[144,384]{1,0:T(8,128)(2,1)S(1)} %collective-permute-done.1.remote_ref.query_ref, f32[16,1024]{1,0:T(8,128)S(1)} %shard_map.83.bias_ref, bf16[256,384]{1,0:T(8,128)(2,1)S(1)} %shard_map.88.pack_ref, ...), custom_call_target="tpu_custom_call" | custom-call | tf_op jit(solution)/shard_map/pallas_call | solution.py:349
  20.4 0.3 %collective-permute-done.8.pack_ref = bf16[256,384]{1,0:T(8,128)(2,1)S(1)} collective-permute-done((bf16[256,384]{1,0:T(8,128)(2,1)S(1)}, bf16[256,384]{1,0:T(8,128)(2,1)S(1)}, u32[]{:S(2)}, u32[]{:S(2)}) %collective-permute-start.8) | collective-permute-done | bytes 196640 | tf_op jit(solution)/shard_map/ppermute | solution.py:253
  20.7 0.5 %shard_map.92 = bf16[144,384]{1,0:T(8,128)(2,1)S(1)} custom-call(bf16[144,384]{1,0:T(8,128)(2,1)S(1)} %collective-permute-done.1.remote_ref.query_ref, f32[16,1024]{1,0:T(8,128)S(1)} %shard_map.83.bias_ref, bf16[256,384]{1,0:T(8,128)(2,1)S(1)} %collective-permute-done.8.pack_ref, f32[256,384]{1,0:T(8,128)S(1)} %get-tuple-element.17.context_ref, ...), custom_call_target="tpu_custom_call" | custom-call | tf_op jit(solution)/shard_map/pallas_call | solution.py:372
  21.2 2.1 %collective-permute-start.10 = (bf16[144,384]{1,0:T(8,128)(2,1)S(1)}, bf16[144,384]{1,0:T(8,128)(2,1)S(1)}, u32[]{:S(2)}, u32[]{:S(2)}) collective-permute-start(bf16[144,384]{1,0:T(8,128)(2,1)S(1)} %shard_map.92), channel_id=1, source_target_pairs={{0,8},{2,10},{4,12},{6,14},{8,0},{10,2},{12,4},{14,6},{16,24},{18,... | collective-permute-start | bytes 331784 | tf_op jit(solution)/shard_map/ppermute | solution.py:253
  23.3 0.0 copy-done.3
  23.3 0.0 copy-done.4
  23.3 0.6 %shard_map.93.gate_ref = f32[16,384]{1,0:T(8,128)S(1)} custom-call(s32[2]{0:T(128)S(1)} %copy-done.4, f32[50,384]{1,0:T(8,128)S(1)} %copy-done.3), custom_call_target="tpu_custom_call" | custom-call | tf_op jit(solution)/shard_map/pallas_call | solution.py:388
  23.9 0.4 %shard_map.91 = (f32[128,384]{1,0:T(8,128)S(1)}, f32[16,384]{1,0:T(8,128)S(1)}) custom-call(bf16[144,384]{1,0:T(8,128)(2,1)S(1)} %shard_map.82.own_ref.query_ref, f32[16,1024]{1,0:T(8,128)S(1)} %shard_map.83.bias_ref, bf16[256,384]{1,0:T(8,128)(2,1)S(1)} %collective-permute-done.8.pack_ref, f32[256,384]{1,0:T(8,128)S(1)} %get-tuple-element.17.context_ref, ...), custom_call_target="tpu_custom_call" | custom-call | tf_op jit(solution)/shard_map/pallas_call | solution.py:372
  24.3 2.4 %collective-permute-done.10.packet_ref = bf16[144,384]{1,0:T(8,128)(2,1)S(1)} collective-permute-done((bf16[144,384]{1,0:T(8,128)(2,1)S(1)}, bf16[144,384]{1,0:T(8,128)(2,1)S(1)}, u32[]{:S(2)}, u32[]{:S(2)}) %collective-permute-start.10) | collective-permute-done | bytes 110624 | tf_op jit(solution)/shard_map/ppermute | solution.py:253
  26.7 1.0 %shard_map.94 = bf16[128,384]{1,0:T(8,128)(2,1)} custom-call(f32[128,384]{1,0:T(8,128)S(1)} %get-tuple-element.19.own_ref, f32[16,384]{1,0:T(8,128)S(1)} %get-tuple-element.20.lines_ref, bf16[144,384]{1,0:T(8,128)(2,1)S(1)} %collective-permute-done.10.packet_ref, f32[16,384]{1,0:T(8,128)S(1)} %shard_map.93.gate_ref), custom_call_target="tpu_custom_call" | custom-call | tf_op jit(solution)/shard_map/pallas_call | solution.py:397
  (8 shorter events, 0.0 us)
Async XLA Ops:
  0.0 5.0 %copy-start = (bf16[128,384]{1,0:T(8,128)(2,1)S(1)}, bf16[128,384]{1,0:T(8,128)(2,1)}, u32[]{:S(2)}) copy-start(bf16[128,384]{1,0:T(8,128)(2,1)} %key_ref.1) | copy-start | bytes 294916
  0.0 6.8 %copy-start.2 = (bf16[128,384]{1,0:T(8,128)(2,1)S(1)}, bf16[128,384]{1,0:T(8,128)(2,1)}, u32[]{:S(2)}) copy-start(bf16[128,384]{1,0:T(8,128)(2,1)} %refs_3_.1) | copy-start | bytes 294916
  0.0 12.6 %collective-permute-start.4 = (bf16[128,384]{1,0:T(8,128)(2,1)}, bf16[128,384]{1,0:T(8,128)(2,1)S(1)}, u32[]{:S(2)}, u32[]{:S(2)}) collective-permute-start(bf16[128,384]{1,0:T(8,128)(2,1)} %refs_3_.1), channel_id=1, source_target_pairs={{0,16},{2,18},{4,20},{6,22},{8,24},{10,26},{12,28},{14,30},{16,0},... | collective-permute-start | bytes 294920 | tf_op jit(solution)/shard_map/ppermute | solution.py:253
  5.2 3.1 %copy-start.6 = (f32[384]{0:T(512)S(1)}, f32[384]{0:T(512)}, u32[]{:S(2)}) copy-start(f32[384]{0:T(512)} %param.11) | copy-start | bytes 4612
  5.2 3.1 %copy-start.7 = (f32[384]{0:T(512)S(1)}, f32[384]{0:T(512)}, u32[]{:S(2)}) copy-start(f32[384]{0:T(512)} %param.12) | copy-start | bytes 4612
  5.2 3.6 %collective-permute-start = (f32[2,128]{1,0:T(2,128)S(1)}, f32[2,128]{1,0:T(2,128)S(1)}, u32[]{:S(2)}, u32[]{:S(2)}) collective-permute-start(f32[2,128]{1,0:T(2,128)S(1)} %pad_maximum_fusion.own_ref), channel_id=1, source_target_pairs={{0,1},{1,0},{2,3},{3,2},{4,5},{5,4},{6,7},{7,6},{8,9},{9,8},{10,11... | collective-permute-start | bytes 3080 | tf_op jit(solution)/shard_map/ppermute | solution.py:289
  6.8 9.3 %collective-permute-start.7 = (bf16[128,384]{1,0:T(8,128)(2,1)S(1)}, bf16[128,384]{1,0:T(8,128)(2,1)S(1)}, u32[]{:S(2)}, u32[]{:S(2)}) collective-permute-start(bf16[128,384]{1,0:T(8,128)(2,1)S(1)} %copy-done.2), channel_id=1, source_target_pairs={{0,4},{2,6},{4,0},{6,2},{8,12},{10,14},{12,8},{14,10},{16,20},{18,... | collective-permute-start | bytes 294920 | tf_op jit(solution)/shard_map/ppermute | solution.py:253
  8.3 2.6 %copy-start.1 = (bf16[128,384]{1,0:T(8,128)(2,1)S(1)}, bf16[128,384]{1,0:T(8,128)(2,1)}, u32[]{:S(2)}) copy-start(bf16[128,384]{1,0:T(8,128)(2,1)} %query_ref.1) | copy-start | bytes 294916
  8.3 2.5 %copy-start.5 = (s32[1,16]{1,0:T(1,128)S(1)}, s32[1,16]{1,0:T(1,128)}, u32[]{:S(2)}) copy-start(s32[1,16]{1,0:T(1,128)} %far_ref.1) | copy-start | bytes 196
  9.0 5.6 %collective-permute-start.2 = (bf16[128,384]{1,0:T(8,128)(2,1)S(1)}, bf16[128,384]{1,0:T(8,128)(2,1)S(1)}, u32[]{:S(2)}, u32[]{:S(2)}) collective-permute-start(bf16[128,384]{1,0:T(8,128)(2,1)S(1)} %shard_map.84.refs_0_), channel_id=1, source_target_pairs={{0,16},{2,18},{4,20},{6,22},{8,24},{10,26},{12,28},{14,30},{16,0},... | collective-permute-start | bytes 294920 | tf_op jit(solution)/shard_map/ppermute | solution.py:253
  9.1 7.1 %collective-permute-start.6 = (bf16[128,384]{1,0:T(8,128)(2,1)S(1)}, bf16[128,384]{1,0:T(8,128)(2,1)S(1)}, u32[]{:S(2)}, u32[]{:S(2)}) collective-permute-start(bf16[128,384]{1,0:T(8,128)(2,1)S(1)} %shard_map.84.refs_0_), channel_id=1, source_target_pairs={{0,4},{2,6},{4,0},{6,2},{8,12},{10,14},{12,8},{14,10},{16,20},{18,... | collective-permute-start | bytes 294920 | tf_op jit(solution)/shard_map/ppermute | solution.py:253
  11.0 5.3 %collective-permute-start.1 = (bf16[144,384]{1,0:T(8,128)(2,1)S(1)}, bf16[144,384]{1,0:T(8,128)(2,1)S(1)}, u32[]{:S(2)}, u32[]{:S(2)}) collective-permute-start(bf16[144,384]{1,0:T(8,128)(2,1)S(1)} %shard_map.82.own_ref.query_ref), channel_id=1, source_target_pairs={{0,8},{2,10},{4,12},{6,14},{8,0},{10,2},{12,4},{14,6},{16,24},{18,... | collective-permute-start | bytes 331784 | tf_op jit(solution)/shard_map/ppermute | solution.py:253
  12.6 5.3 %collective-permute-start.5 = (bf16[128,384]{1,0:T(8,128)(2,1)S(1)}, bf16[128,384]{1,0:T(8,128)(2,1)S(1)}, u32[]{:S(2)}, u32[]{:S(2)}) collective-permute-start(bf16[128,384]{1,0:T(8,128)(2,1)S(1)} %shard_map.85.refs_4_), channel_id=1, source_target_pairs={{0,4},{2,6},{4,0},{6,2},{8,12},{10,14},{12,8},{14,10},{16,20},{18,... | collective-permute-start | bytes 294920 | tf_op jit(solution)/shard_map/ppermute | solution.py:253
  14.5 4.6 %collective-permute-start.3 = (bf16[128,384]{1,0:T(8,128)(2,1)S(1)}, bf16[128,384]{1,0:T(8,128)(2,1)S(1)}, u32[]{:S(2)}, u32[]{:S(2)}) collective-permute-start(bf16[128,384]{1,0:T(8,128)(2,1)S(1)} %collective-permute-done.2.refs_1_), channel_id=1, source_target_pairs={{0,4},{2,6},{4,0},{6,2},{8,12},{10,14},{12,8},{14,10},{16,20},{18,... | collective-permute-start | bytes 294920 | tf_op jit(solution)/shard_map/ppermute | solution.py:253
  16.2 3.1 %collective-permute-start.9 = (bf16[768,384]{1,0:T(8,128)(2,1)S(1)}, bf16[768,384]{1,0:T(8,128)(2,1)S(1)}, u32[]{:S(2)}, u32[]{:S(2)}) collective-permute-start(bf16[768,384]{1,0:T(8,128)(2,1)S(1)} %shard_map.86.pack_ref), channel_id=1, source_target_pairs={{0,2},{2,0},{4,6},{6,4},{8,10},{10,8},{12,14},{14,12},{16,18},{18,... | collective-permute-start | bytes 1769480 | tf_op jit(solution)/shard_map/ppermute | solution.py:253
  19.2 1.5 %collective-permute-start.8 = (bf16[256,384]{1,0:T(8,128)(2,1)S(1)}, bf16[256,384]{1,0:T(8,128)(2,1)S(1)}, u32[]{:S(2)}, u32[]{:S(2)}) collective-permute-start(bf16[256,384]{1,0:T(8,128)(2,1)S(1)} %shard_map.88.pack_ref), channel_id=1, source_target_pairs={{0,2},{2,0},{4,6},{6,4},{8,10},{10,8},{12,14},{14,12},{16,18},{18,... | collective-permute-start | bytes 589832 | tf_op jit(solution)/shard_map/ppermute | solution.py:253
  20.7 2.6 %copy-start.3 = (f32[50,384]{1,0:T(8,128)S(1)}, f32[50,384]{1,0:T(8,128)}, u32[]{:S(2)}) copy-start(f32[50,384]{1,0:T(8,128)} %table_ref.1) | copy-start | bytes 230404
  20.7 2.6 %copy-start.4 = (s32[2]{0:T(128)S(1)}, s32[2]{0:T(128)}, u32[]{:S(2)}) copy-start(s32[2]{0:T(128)} %step_ref.1) | copy-start | bytes 28
  21.2 5.6 %collective-permute-start.10 = (bf16[144,384]{1,0:T(8,128)(2,1)S(1)}, bf16[144,384]{1,0:T(8,128)(2,1)S(1)}, u32[]{:S(2)}, u32[]{:S(2)}) collective-permute-start(bf16[144,384]{1,0:T(8,128)(2,1)S(1)} %shard_map.92), channel_id=1, source_target_pairs={{0,8},{2,10},{4,12},{6,14},{8,0},{10,2},{12,4},{14,6},{16,24},{18,... | collective-permute-start | bytes 331784 | tf_op jit(solution)/shard_map/ppermute | solution.py:253
